TPU v7x, 32 devices: a whole 2x2x4 slice. The times are simulated.
32 devices in a mesh: leaf: 8 (over z, x), col: 4 (over y, core).
Axes of the slice: x: 2, y: 2, z: 4, core: 2. Of those that a mesh axis runs over, the one named last changes fastest.
Arguments:
- leaf_rhs: bfloat16 [256, 256, 512], P('leaf', None, 'col'), may hold values from -6 to 6
- leaf_lower_inv: bfloat16 [256, 256, 256], P(('leaf', 'col')), may hold values from -0.375 to 0.375
- leaf_lower_panels: bfloat16 [256, 3, 256, 256], P(('leaf', 'col')), may hold values from -0.03125 to 0.03125
- leaf_upper_inv: bfloat16 [256, 256, 256], P(('leaf', 'col')), may hold values from -0.375 to 0.375
- leaf_upper_panels: bfloat16 [256, 3, 256, 256], P(('leaf', 'col')), may hold values from -0.21875 to 0.21875
- ancestors: int32 [256, 3], P(('leaf', 'col')), may hold values from 0 to 3
- sep_rhs: bfloat16 [8, 256, 512], P('leaf', None, 'col'), may hold values from -6 to 6
- sep_lower_inv: bfloat16 [8, 256, 256], P('leaf'), may hold values from -0.375 to 0.375
- sep_lower_panels: bfloat16 [8, 2, 256, 256], P('leaf'), may hold values from -0.109375 to 0.109375
- sep_upper_inv: bfloat16 [8, 256, 256], P('leaf'), may hold values from -0.375 to 0.375
- sep_upper_panels: bfloat16 [8, 2, 256, 256], P('leaf'), may hold values from -0.21875 to 0.21875
Outputs:
- leaf_solution: bfloat16 [256, 256, 512], P('leaf', None, 'col')
- sep_solution: bfloat16 [8, 256, 512], P('leaf', None, 'col')
Inputs may be any that keep to these rules, and one draw needn't show every extreme that they name: `ancestors`: 0 marks an empty slot; a value m names the separator of level m above the supernode's subtree; a row may name a level more than once.
All inputs are finite; a program needn't handle non-finite values.
Results may differ from a plain program's by a relative error of at most 0.022.
Values may be sent and summed in bfloat16 or wider, within the bound.
No kernel may reach another device: no remote copies, remote signals or barrier semaphores. Data moves between devices by JAX's collectives and lax.ppermute only.
A program may use at most 128 MiB of HBM per device.

v0:
```python
import jax
import jax.numpy as jnp
from jax import lax
from jax.sharding import PartitionSpec as P

HIGH = lax.Precision.HIGHEST


def from_partner(value, axis, bit):
    mask = 2**bit
    pairs = [(source, source ^ mask) for source in range(lax.axis_size(axis))]
    return lax.ppermute(value, axis, pairs)


def on_device(
    leaf_rhs,
    leaf_lower_inv,
    leaf_lower_panels,
    leaf_upper_inv,
    leaf_upper_panels,
    ancestors,
    sep_rhs,
    sep_lower_inv,
    sep_lower_panels,
    sep_upper_inv,
    sep_upper_panels,
):
    levels = lax.axis_size("leaf").bit_length() - 1
    device = lax.axis_index("leaf")
    heights = jnp.arange(1, levels + 1, dtype=jnp.int32)
    onehot = (ancestors[:, :, None] == heights[None, None, :]).astype(jnp.bfloat16)
    rhs_cols = sep_rhs.shape[2]
    block_rows = leaf_rhs.shape[1]
    owned_rhs = lax.all_to_all(leaf_rhs, "col", split_axis=0, concat_axis=2, tiled=True)
    leaf_value = jnp.einsum(
        "kbc,kcr->kbr", leaf_lower_inv, owned_rhs, preferred_element_type=jnp.float32
    ).astype(jnp.bfloat16)
    products = jnp.einsum(
        "kabc,kcr->kabr", leaf_lower_panels, leaf_value, preferred_element_type=jnp.float32
    )
    partial_value = jnp.einsum(
        "kal,kabr->lbr", onehot.astype(jnp.float32), products, precision=HIGH
    )
    pending = lax.psum_scatter(partial_value, "col", scatter_dimension=2, tiled=True)
    own_rhs = sep_rhs[0].astype(jnp.float32)
    own_forward = jnp.zeros((block_rows, rhs_cols), jnp.bfloat16)
    for height in range(1, levels + 1):
        summed = pending[height - 1]
        for bit_index in range(height):
            summed = summed + from_partner(summed, "leaf", bit_index)
        is_owner = device % 2**height == 2 ** (height - 1)
        sep_input = (own_rhs - summed).astype(jnp.bfloat16)
        sep_value = jnp.dot(sep_lower_inv[0], sep_input, preferred_element_type=jnp.float32).astype(
            jnp.bfloat16
        )
        own_forward = jnp.where(is_owner, sep_value, own_forward)
        if height < levels:
            update = jnp.einsum(
                "ibc,cr->ibr",
                sep_lower_panels[0, : levels - height],
                sep_value,
                preferred_element_type=jnp.float32,
            )
            masked_update = jnp.where(is_owner, update, 0.0)
            pending = pending.at[height:].add(masked_update)
    solved = jnp.zeros((levels, block_rows, rhs_cols), jnp.bfloat16)
    own_solution = jnp.zeros((block_rows, rhs_cols), jnp.bfloat16)
    for height in range(levels, 0, -1):
        is_owner = device % 2**height == 2 ** (height - 1)
        remaining = own_forward.astype(jnp.float32)
        if height < levels:
            remaining = remaining - jnp.einsum(
                "ibc,icr->br",
                sep_upper_panels[0, : levels - height],
                solved[height:],
                preferred_element_type=jnp.float32,
            )
        sep_rest = remaining.astype(jnp.bfloat16)
        sep_value = jnp.dot(sep_upper_inv[0], sep_rest, preferred_element_type=jnp.float32).astype(
            jnp.bfloat16
        )
        own_solution = jnp.where(is_owner, sep_value, own_solution)
        spread = jnp.where(is_owner, sep_value, jnp.zeros_like(sep_value))
        for bit_index in range(height):
            spread = spread + from_partner(spread, "leaf", bit_index)
        solved = solved.at[height - 1].set(spread)
    gathered = lax.all_gather(solved, "col", axis=2, tiled=True)
    picked = jnp.einsum(
        "kal,lbr->kabr", onehot, gathered, preferred_element_type=jnp.float32
    ).astype(jnp.bfloat16)
    update = jnp.einsum(
        "kabc,kacr->kbr", leaf_upper_panels, picked, preferred_element_type=jnp.float32
    )
    leaf_rest = (leaf_value.astype(jnp.float32) - update).astype(jnp.bfloat16)
    leaf_result = jnp.einsum(
        "kbc,kcr->kbr", leaf_upper_inv, leaf_rest, preferred_element_type=jnp.float32
    ).astype(jnp.bfloat16)
    leaf_solution = lax.all_to_all(leaf_result, "col", split_axis=2, concat_axis=0, tiled=True)
    return (leaf_solution, own_solution[None])


def solution(mesh):
    placed = (
        P("leaf", None, "col"),
        P(("leaf", "col"), None, None),
        P(("leaf", "col"), None, None, None),
        P(("leaf", "col"), None, None),
        P(("leaf", "col"), None, None, None),
        P(("leaf", "col"), None),
        P("leaf", None, "col"),
        P("leaf", None, None),
        P("leaf", None, None, None),
        P("leaf", None, None),
        P("leaf", None, None, None),
    )
    return jax.shard_map(
        on_device,
        mesh=mesh,
        in_specs=placed,
        out_specs=(P("leaf", None, "col"), P("leaf", None, "col")),
        check_vma=False,
    )
```

profile of v0, /device:TPU:0, one launch (start us, length us, event | category | flops | bytes accessed | tf_op | source)
XLA Modules:
  0.0 363.6 jit_solution(16980417630803602139)
XLA Ops:
  7.2 4.7 %all-to-all-start = ((bf16[32,256,128]{2,1,0:T(8,128)(2,1)}), bf16[32,256,128]{2,1,0:T(8,128)(2,1)}, u32[]{:S(2)}, u32[]{:S(2)}) async-start(bf16[32,256,128]{2,1,0:T(8,128)(2,1)} %param.21), calls=%async_computation | async-start | bytes 4194304 | tf_op jit(solution)/shard_map/all_to_all | solution.py:34
  12.0 26.3 %all-to-all-done = bf16[32,256,128]{2,1,0:T(8,128)(2,1)} async-done(((bf16[32,256,128]{2,1,0:T(8,128)(2,1)}), bf16[32,256,128]{2,1,0:T(8,128)(2,1)}, u32[]{:S(2)}, u32[]{:S(2)}) %all-to-all-start) | async-done | bytes 2097184 | tf_op jit(solution)/shard_map/all_to_all | solution.py:34
  38.3 4.5 %copy.56 = bf16[4,8,256,128]{3,0,2,1:T(4,128)(2,1)} copy(bf16[4,8,256,128]{3,2,1,0:T(8,128)(2,1)} %bitcast) | data formatting | bytes 4194304 | tf_op jit(solution)/shard_map/all_to_all | solution.py:34
  42.8 4.1 %all_to_all.29 = bf16[8,256,512]{2,1,0:T(8,128)(2,1)} reshape(bf16[8,256,4,128]{3,2,1,0:T(4,128)(2,1)} %bitcast.163) | data formatting | bytes 4194304 | tf_op jit(solution)/shard_map/all_to_all | solution.py:34
  46.9 2.6 convolution_convert_fusion
  49.6 1.3 copy-done.2
  50.9 6.4 %fusion.5 = f32[8,512,3,256]{3,1,2,0:T(8,128)} fusion(bf16[8,3,256,256]{3,2,1,0:T(8,128)(2,1)S(1)} %copy-done, bf16[8,256,512]{2,1,0:T(8,128)(2,1)S(1)} %convolution_convert_fusion), kind=kOutput, calls=%fused_computation.7 | convolution fusion | flops 1610612736 | bytes 17825792 | tf_op jit(solution)/shard_map/kabc,kcr->kabr/dot_general | solution.py:38
  57.3 12.9 %copy.35 = f32[8,512,3,256]{1,0,2,3:T(8,128)} copy(f32[8,512,3,256]{3,1,2,0:T(8,128)} %fusion.5) | data formatting | bytes 25165824 | tf_op jit(solution)/shard_map/kabc,kcr->kabr/dot_general | solution.py:38
  70.2 9.3 %fusion.7 = f32[3,256,512]{2,0,1:T(4,128)S(1)} fusion(f32[8,512,3,256]{1,0,2,3:T(8,128)} %copy.35, s32[8,3]{0,1:T(4,128)S(1)} %copy-done.9, s32[3]{0:T(128)S(1)} %iota_add_fusion), kind=kOutput, calls=%fused_computation.12 | convolution fusion | flops 113246280 | bytes 14155884 | tf_op jit(solution)/shard_map/kal,kabr->lbr/dot_general | solution.py:41
  79.5 32.4 %copy.42 = f32[3,256,512]{0,1,2:T(8,128)} copy(f32[3,256,512]{2,0,1:T(4,128)S(1)} %fusion.7) | data formatting | bytes 3145728
  111.9 42.8 %reshape.186 = f32[512,768]{1,0:T(8,128)} reshape(f32[512,256,3]{2,1,0:T(8,128)} %bitcast.41) | data formatting | bytes 3145728
  154.8 29.5 %reduce-scatter.4.cloned.1.call-done = f32[128,768]{1,0:T(8,128)} async-done(((f32[512,768]{1,0:T(8,128)}), f32[128,768]{1,0:T(8,128)}) %reduce-scatter.4.cloned.1.call-update) | async-done | bytes 393232
  184.2 18.0 %reshape.187 = f32[128,256,3]{2,1,0:T(8,128)} reshape(f32[128,768]{1,0:T(8,128)} %reduce-scatter.4.cloned.1.call-done) | data formatting | bytes 786432
  202.2 10.0 %copy.46 = f32[1,256,128]{1,2,0:T(8,128)S(1)} copy(f32[1,256,128]{0,1,2:T(8,128)} %bitcast.161) | data formatting | bytes 262144
  212.2 1.5 collective-permute-start
  213.8 12.8 %slice.136 = f32[2,256,128]{0,1,2:T(8,128)} slice(f32[3,256,128]{0,1,2:T(8,128)} %bitcast.162), slice={[1:3], [0:256], [0:128]} | slice | bytes 524288 | tf_op jit(solution)/shard_map/slice.106
  226.6 10.2 %copy.45 = f32[2,256,128]{1,2,0:T(8,128)S(1)} copy(f32[2,256,128]{0,1,2:T(8,128)} %slice.136) | data formatting | bytes 524288
  237.3 0.6 collective-permute-start.1
  237.9 4.4 %collective-permute-done.1 = f32[256,128]{0,1:T(8,128)S(1)} collective-permute-done((f32[256,128]{0,1:T(8,128)S(1)}, f32[256,128]{0,1:T(8,128)S(1)}, u32[]{:S(2)}, u32[]{:S(2)}) %collective-permute-start.1) | collective-permute-done | bytes 131104 | tf_op jit(solution)/shard_map/ppermute | solution.py:12
  242.4 1.6 collective-permute-start.2
  243.9 3.5 collective-permute-done.2
  247.8 0.6 collective-permute-start.3
  248.4 4.4 %collective-permute-done.3 = f32[256,128]{0,1:T(8,128)S(1)} collective-permute-done((f32[256,128]{0,1:T(8,128)S(1)}, f32[256,128]{0,1:T(8,128)S(1)}, u32[]{:S(2)}, u32[]{:S(2)}) %collective-permute-start.3) | collective-permute-done | bytes 131104 | tf_op jit(solution)/shard_map/ppermute | solution.py:12
  252.9 1.6 collective-permute-start.4
  254.4 4.9 %collective-permute-done.4 = f32[256,128]{0,1:T(8,128)S(1)} collective-permute-done((f32[256,128]{0,1:T(8,128)S(1)}, f32[256,128]{0,1:T(8,128)S(1)}, u32[]{:S(2)}, u32[]{:S(2)}) %collective-permute-start.4) | collective-permute-done | bytes 131104 | tf_op jit(solution)/shard_map/ppermute | solution.py:12
  259.3 1.6 collective-permute-start.5
  260.9 5.7 %collective-permute-done.5 = f32[256,128]{0,1:T(8,128)S(1)} collective-permute-done((f32[256,128]{0,1:T(8,128)S(1)}, f32[256,128]{0,1:T(8,128)S(1)}, u32[]{:S(2)}, u32[]{:S(2)}) %collective-permute-start.5) | collective-permute-done | bytes 131104 | tf_op jit(solution)/shard_map/ppermute | solution.py:12
  267.1 0.6 collective-permute-start.6
  267.7 3.7 %collective-permute-done.6 = bf16[256,128]{0,1:T(8,128)(2,1)S(1)} collective-permute-done((bf16[256,128]{0,1:T(8,128)(2,1)S(1)}, bf16[256,128]{0,1:T(8,128)(2,1)S(1)}, u32[]{:S(2)}, u32[]{:S(2)}) %collective-permute-start.6) | collective-permute-done | bytes 65568 | tf_op jit(solution)/shard_map/ppermute | solution.py:12
  271.6 4.1 %collective-permute-done.7 = bf16[256,128]{0,1:T(8,128)(2,1)S(1)} collective-permute-done((bf16[256,128]{0,1:T(8,128)(2,1)S(1)}, bf16[256,128]{0,1:T(8,128)(2,1)S(1)}, u32[]{:S(2)}, u32[]{:S(2)}) %collective-permute-start.7) | collective-permute-done | bytes 65568 | tf_op jit(solution)/shard_map/ppermute | solution.py:12
  275.8 1.1 collective-permute-start.8
  276.9 4.4 %collective-permute-done.8 = bf16[256,128]{0,1:T(8,128)(2,1)S(1)} collective-permute-done((bf16[256,128]{0,1:T(8,128)(2,1)S(1)}, bf16[256,128]{0,1:T(8,128)(2,1)S(1)}, u32[]{:S(2)}, u32[]{:S(2)}) %collective-permute-start.8) | collective-permute-done | bytes 65568 | tf_op jit(solution)/shard_map/ppermute | solution.py:12
  281.3 0.3 broadcast_select_fusion.1
  281.6 0.6 collective-permute-start.9
  282.2 3.8 %collective-permute-done.9 = bf16[256,128]{0,1:T(8,128)(2,1)S(1)} collective-permute-done((bf16[256,128]{0,1:T(8,128)(2,1)S(1)}, bf16[256,128]{0,1:T(8,128)(2,1)S(1)}, u32[]{:S(2)}, u32[]{:S(2)}) %collective-permute-start.9) | collective-permute-done | bytes 65568 | tf_op jit(solution)/shard_map/ppermute | solution.py:12
  286.1 4.2 %collective-permute-done.10 = bf16[256,128]{0,1:T(8,128)(2,1)S(1)} collective-permute-done((bf16[256,128]{0,1:T(8,128)(2,1)S(1)}, bf16[256,128]{0,1:T(8,128)(2,1)S(1)}, u32[]{:S(2)}, u32[]{:S(2)}) %collective-permute-start.10) | collective-permute-done | bytes 65568 | tf_op jit(solution)/shard_map/ppermute | solution.py:12
  290.3 0.4 select_bitcast_fusion
  290.7 0.6 collective-permute-start.11
  291.3 3.8 %collective-permute-done.11 = bf16[256,128]{0,1:T(8,128)(2,1)S(1)} collective-permute-done((bf16[256,128]{0,1:T(8,128)(2,1)S(1)}, bf16[256,128]{0,1:T(8,128)(2,1)S(1)}, u32[]{:S(2)}, u32[]{:S(2)}) %collective-permute-start.11) | collective-permute-done | bytes 65568 | tf_op jit(solution)/shard_map/ppermute | solution.py:12
  295.1 7.6 %all_gather.3 = bf16[3,256,512]{1,2,0:T(8,128)(2,1)S(1)} all-gather(bf16[3,256,128]{1,2,0:T(8,128)(2,1)S(1)} %bitcast_dynamic-update-slice_fusion), channel_id=1, replica_groups=mesh['leaf'=8,'col'=4] {'col'}, dimensions={2}, use_global_device_ids=true | all-gather | bytes 983040 | tf_op jit(solution)/shard_map/all_gather | solution.py:87
  302.8 1.0 copy.38
  303.7 4.5 %fusion.54 = bf16[8,3,256,512]{3,0,2,1:T(8,128)(2,1)} fusion(bf16[3,256,512,1]{2,0,1,3:T(4,128)(2,1)S(1)} %copy.38, s32[8,3]{0,1:T(4,128)S(1)} %copy-done.9, s32[3]{0:T(128)S(1)} %iota_add_fusion), kind=kOutput, calls=%fused_computation.71 | convolution fusion | flops 18874440 | bytes 7077996 | tf_op jit(solution)/shard_map/kal,lbr->kabr/dot_general | solution.py:88
  308.3 9.7 %convert_bitcast_fusion = bf16[8,256,512]{1,2,0:T(8,128)(2,1)} fusion(bf16[8,256,256]{2,1,0:T(8,128)(2,1)} %param.24, bf16[8,256,512]{2,1,0:T(8,128)(2,1)S(1)} %copy-done.3, bf16[8,3,256,256]{3,2,1,0:T(8,128)(2,1)} %param.25, bf16[8,3,256,512]{3,0,2,1:T(8,128)(2,1)} %fusion.54), kind=kOutput, calls=%fused_computation.10 | convolution fusion | flops 2151677952 | bytes 14680064 | tf_op jit(solution)/shard_map/kbc,kcr->kbr/dot_general | solution.py:95
  317.9 4.1 %copy.31 = bf16[8,256,512]{1,0,2:T(8,128)(2,1)} copy(bf16[8,256,512]{1,2,0:T(8,128)(2,1)} %convert_bitcast_fusion) | data formatting | bytes 4194304 | tf_op jit(solution)/shard_map/convert_element_type | solution.py:97
  322.0 4.5 %all-to-all-start.1 = ((bf16[8,256,512]{1,0,2:T(8,128)(2,1)}), bf16[8,256,512]{1,0,2:T(8,128)(2,1)}, u32[]{:S(2)}, u32[]{:S(2)}) async-start(bf16[8,256,512]{1,0,2:T(8,128)(2,1)} %copy.31), calls=%async_computation.1 | async-start | bytes 4194304 | tf_op jit(solution)/shard_map/all_to_all | solution.py:98
  326.5 0.7 copy.33
  327.2 25.0 %all-to-all-done.1 = bf16[8,256,512]{1,0,2:T(8,128)(2,1)} async-done(((bf16[8,256,512]{1,0,2:T(8,128)(2,1)}), bf16[8,256,512]{1,0,2:T(8,128)(2,1)}, u32[]{:S(2)}, u32[]{:S(2)}) %all-to-all-start.1) | async-done | bytes 2097184 | tf_op jit(solution)/shard_map/all_to_all | solution.py:98
  352.2 4.5 %copy.32 = bf16[4,8,256,128]{3,2,1,0:T(8,128)(2,1)} copy(bf16[4,8,256,128]{2,1,3,0:T(8,128)(2,1)} %bitcast.37) | data formatting | bytes 4194304 | tf_op jit(solution)/shard_map/all_to_all | solution.py:98
  (43 shorter events, 1.9 us)
Async XLA Ops:
  7.2 43.7 %copy-start = (bf16[8,3,256,256]{3,2,1,0:T(8,128)(2,1)S(1)}, bf16[8,3,256,256]{3,2,1,0:T(8,128)(2,1)}, u32[]{:S(2)}) copy-start(bf16[8,3,256,256]{3,2,1,0:T(8,128)(2,1)} %param.23) | copy-start | bytes 9437188
  7.2 31.1 %all-to-all-start = ((bf16[32,256,128]{2,1,0:T(8,128)(2,1)}), bf16[32,256,128]{2,1,0:T(8,128)(2,1)}, u32[]{:S(2)}, u32[]{:S(2)}) async-start(bf16[32,256,128]{2,1,0:T(8,128)(2,1)} %param.21), calls=%async_computation | async-start | bytes 4194304 | tf_op jit(solution)/shard_map/all_to_all | solution.py:34
  11.9 172.3 %reduce-scatter.4.cloned.1.call-start = ((), (), s32[]{:S(2)}) async-start(), calls=%async_computation.3 | async-start | bytes 1966080
  49.6 1.3 copy-start.2
  57.3 12.9 %copy-start.9 = (s32[8,3]{0,1:T(4,128)S(1)}, s32[8,3]{0,1:T(4,128)}, u32[]{:S(2)}) copy-start(s32[8,3]{0,1:T(4,128)} %param.26) | copy-start | bytes 292
  202.2 11.5 %copy-start.8 = (bf16[1,256,128]{2,1,0:T(8,128)(2,1)S(1)}, bf16[1,256,128]{2,1,0:T(8,128)(2,1)}, u32[]{:S(2)}) copy-start(bf16[1,256,128]{2,1,0:T(8,128)(2,1)} %param.27) | copy-start | bytes 196612
  212.2 24.6 %collective-permute-start = (f32[256,128]{0,1:T(8,128)S(1)}, f32[256,128]{0,1:T(8,128)S(1)}, u32[]{:S(2)}, u32[]{:S(2)}) collective-permute-start(f32[256,128]{0,1:T(8,128)S(1)} %bitcast.166), channel_id=1, source_target_pairs={{0,4},{4,0},{8,12},{12,8},{16,20},{20,16},{24,28},{28,24},{1,5},{5... | collective-permute-start | bytes 393224 | tf_op jit(solution)/shard_map/ppermute | solution.py:12
  226.6 10.2 %copy-start.5 = (bf16[1,256,256]{2,1,0:T(8,128)(2,1)S(1)}, bf16[1,256,256]{2,1,0:T(8,128)(2,1)}, u32[]{:S(2)}) copy-start(bf16[1,256,256]{2,1,0:T(8,128)(2,1)} %param.28) | copy-start | bytes 393220
  226.6 10.4 %copy-start.6 = (bf16[1,2,256,256]{3,2,1,0:T(8,128)(2,1)S(1)}, bf16[1,2,256,256]{3,2,1,0:T(8,128)(2,1)}, u32[]{:S(2)}) copy-start(bf16[1,2,256,256]{3,2,1,0:T(8,128)(2,1)} %param.29) | copy-start | bytes 786436
  236.8 30.0 %copy-start.4 = (bf16[1,256,256]{2,1,0:T(8,128)(2,1)S(1)}, bf16[1,256,256]{2,1,0:T(8,128)(2,1)}, u32[]{:S(2)}) copy-start(bf16[1,256,256]{2,1,0:T(8,128)(2,1)} %param.30) | copy-start | bytes 393220
  236.8 44.5 %copy-start.7 = (bf16[1,2,256,256]{3,2,1,0:T(8,128)(2,1)S(1)}, bf16[1,2,256,256]{3,2,1,0:T(8,128)(2,1)}, u32[]{:S(2)}) copy-start(bf16[1,2,256,256]{3,2,1,0:T(8,128)(2,1)} %param.31) | copy-start | bytes 786436
  237.3 5.0 %collective-permute-start.1 = (f32[256,128]{0,1:T(8,128)S(1)}, f32[256,128]{0,1:T(8,128)S(1)}, u32[]{:S(2)}, u32[]{:S(2)}) collective-permute-start(f32[256,128]{0,1:T(8,128)S(1)} %slice_bitcast_fusion), channel_id=1, source_target_pairs={{0,4},{4,0},{8,12},{12,8},{16,20},{20,16},{24,28},{28,24},{1,5},{5... | collective-permute-start | bytes 393224 | tf_op jit(solution)/shard_map/ppermute | solution.py:12
  242.4 5.0 %collective-permute-start.2 = (f32[256,128]{0,1:T(8,128)S(1)}, f32[256,128]{0,1:T(8,128)S(1)}, u32[]{:S(2)}, u32[]{:S(2)}) collective-permute-start(f32[256,128]{0,1:T(8,128)S(1)} %fusion.60), channel_id=1, source_target_pairs={{0,8},{4,12},{8,0},{12,4},{16,24},{20,28},{24,16},{28,20},{1,9},{5... | collective-permute-start | bytes 393224 | tf_op jit(solution)/shard_map/ppermute | solution.py:12
  247.8 5.0 %collective-permute-start.3 = (f32[256,128]{0,1:T(8,128)S(1)}, f32[256,128]{0,1:T(8,128)S(1)}, u32[]{:S(2)}, u32[]{:S(2)}) collective-permute-start(f32[256,128]{0,1:T(8,128)S(1)} %fusion.14), channel_id=1, source_target_pairs={{0,4},{4,0},{8,12},{12,8},{16,20},{20,16},{24,28},{28,24},{1,5},{5... | collective-permute-start | bytes 393224 | tf_op jit(solution)/shard_map/ppermute | solution.py:12
  252.9 6.4 %collective-permute-start.4 = (f32[256,128]{0,1:T(8,128)S(1)}, f32[256,128]{0,1:T(8,128)S(1)}, u32[]{:S(2)}, u32[]{:S(2)}) collective-permute-start(f32[256,128]{0,1:T(8,128)S(1)} %add.89), channel_id=1, source_target_pairs={{0,8},{4,12},{8,0},{12,4},{16,24},{20,28},{24,16},{28,20},{1,9},{5... | collective-permute-start | bytes 393224 | tf_op jit(solution)/shard_map/ppermute | solution.py:12
  259.3 7.3 %collective-permute-start.5 = (f32[256,128]{0,1:T(8,128)S(1)}, f32[256,128]{0,1:T(8,128)S(1)}, u32[]{:S(2)}, u32[]{:S(2)}) collective-permute-start(f32[256,128]{0,1:T(8,128)S(1)} %add.90), channel_id=1, source_target_pairs={{0,16},{4,20},{8,24},{12,28},{16,0},{20,4},{24,8},{28,12},{1,17},{... | collective-permute-start | bytes 393224 | tf_op jit(solution)/shard_map/ppermute | solution.py:12
  267.1 4.3 %collective-permute-start.6 = (bf16[256,128]{0,1:T(8,128)(2,1)S(1)}, bf16[256,128]{0,1:T(8,128)(2,1)S(1)}, u32[]{:S(2)}, u32[]{:S(2)}) collective-permute-start(bf16[256,128]{0,1:T(8,128)(2,1)S(1)} %fusion.22), channel_id=1, source_target_pairs={{0,4},{4,0},{8,12},{12,8},{16,20},{20,16},{24,28},{28,24},{1,5},{5... | collective-permute-start | bytes 196616 | tf_op jit(solution)/shard_map/ppermute | solution.py:12
  271.4 4.3 %collective-permute-start.7 = (bf16[256,128]{0,1:T(8,128)(2,1)S(1)}, bf16[256,128]{0,1:T(8,128)(2,1)S(1)}, u32[]{:S(2)}, u32[]{:S(2)}) collective-permute-start(bf16[256,128]{0,1:T(8,128)(2,1)S(1)} %add.92), channel_id=1, source_target_pairs={{0,8},{4,12},{8,0},{12,4},{16,24},{20,28},{24,16},{28,20},{1,9},{5... | collective-permute-start | bytes 196616 | tf_op jit(solution)/shard_map/ppermute | solution.py:12
  275.8 5.5 %collective-permute-start.8 = (bf16[256,128]{0,1:T(8,128)(2,1)S(1)}, bf16[256,128]{0,1:T(8,128)(2,1)S(1)}, u32[]{:S(2)}, u32[]{:S(2)}) collective-permute-start(bf16[256,128]{0,1:T(8,128)(2,1)S(1)} %add.93), channel_id=1, source_target_pairs={{0,16},{4,20},{8,24},{12,28},{16,0},{20,4},{24,8},{28,12},{1,17},{... | collective-permute-start | bytes 196616 | tf_op jit(solution)/shard_map/ppermute | solution.py:12
  281.6 4.3 %collective-permute-start.9 = (bf16[256,128]{0,1:T(8,128)(2,1)S(1)}, bf16[256,128]{0,1:T(8,128)(2,1)S(1)}, u32[]{:S(2)}, u32[]{:S(2)}) collective-permute-start(bf16[256,128]{0,1:T(8,128)(2,1)S(1)} %get-tuple-element.66), channel_id=1, source_target_pairs={{0,4},{4,0},{8,12},{12,8},{16,20},{20,16},{24,28},{28,24},{1,5},{5... | collective-permute-start | bytes 196616 | tf_op jit(solution)/shard_map/ppermute | solution.py:12
  286.0 4.3 %collective-permute-start.10 = (bf16[256,128]{0,1:T(8,128)(2,1)S(1)}, bf16[256,128]{0,1:T(8,128)(2,1)S(1)}, u32[]{:S(2)}, u32[]{:S(2)}) collective-permute-start(bf16[256,128]{0,1:T(8,128)(2,1)S(1)} %add.95), channel_id=1, source_target_pairs={{0,8},{4,12},{8,0},{12,4},{16,24},{20,28},{24,16},{28,20},{1,9},{5... | collective-permute-start | bytes 196616 | tf_op jit(solution)/shard_map/ppermute | solution.py:12
  290.7 4.3 %collective-permute-start.11 = (bf16[256,128]{0,1:T(8,128)(2,1)S(1)}, bf16[256,128]{0,1:T(8,128)(2,1)S(1)}, u32[]{:S(2)}, u32[]{:S(2)}) collective-permute-start(bf16[256,128]{0,1:T(8,128)(2,1)S(1)} %get-tuple-element.65), channel_id=1, source_target_pairs={{0,4},{4,0},{8,12},{12,8},{16,20},{20,16},{24,28},{28,24},{1,5},{5... | collective-permute-start | bytes 196616 | tf_op jit(solution)/shard_map/ppermute | solution.py:12
  303.7 4.6 %copy-start.3 = (bf16[8,256,512]{2,1,0:T(8,128)(2,1)S(1)}, bf16[8,256,512]{2,1,0:T(8,128)(2,1)}, u32[]{:S(2)}) copy-start(bf16[8,256,512]{2,1,0:T(8,128)(2,1)} %copy-done.2) | copy-start | bytes 6291460
  322.0 30.2 %all-to-all-start.1 = ((bf16[8,256,512]{1,0,2:T(8,128)(2,1)}), bf16[8,256,512]{1,0,2:T(8,128)(2,1)}, u32[]{:S(2)}, u32[]{:S(2)}) async-start(bf16[8,256,512]{1,0,2:T(8,128)(2,1)} %copy.31), calls=%async_computation.1 | async-start | bytes 4194304 | tf_op jit(solution)/shard_map/all_to_all | solution.py:98
  326.5 30.3 %copy-start.1 = (bf16[8,3,256,256]{3,2,1,0:T(8,128)(2,1)S(1)}, bf16[8,3,256,256]{3,2,1,0:T(8,128)(2,1)}, u32[]{:S(2)}) copy-start(bf16[8,3,256,256]{3,2,1,0:T(8,128)(2,1)} %param.23) | copy-start | bytes 9437188
Sparse Core Ops, SparseCore 0:
  154.9 29.2 reduce-scatter.3
where the time goes:
time: 365 us; the launch traced here: 364 us
  local copies, waits for them, and re-layouts  159 us (44%)
  waiting for transfers between devices  128 us (35%)
  matrix products  34.5 us (9%)
  starting transfers between devices  19.8 us (5%)
  between operations  14.3 us (4%)
  blocking collectives  7.65 us (2%)
    unnamed x27, local copies, waits for them, and re-layouts  116 us
    ppermute x12, waiting for transfers between devices, from_partner(): return lax.ppermute(value, axis, pairs)  46.9 us
    unnamed x2, waiting for transfers between devices  29.5 us
    all_to_all x1, waiting for transfers between devices, on_device(): lax.all_to_all(leaf_rhs, 'col', split_axis=0, concat_axis=2, tiled=True)  26.3 us
    all_to_all x1, waiting for transfers between devices, on_device(): lax.all_to_all(leaf_result, 'col', split_axis=2, concat_axis=0, tiled=True)  25 us
    dot_general x1, local copies, waits for them, and re-layouts, on_device(): jnp.einsum('kabc,kcr->kabr', leaf_lower_panels, leaf_value, preferred_ele...  12.9 us
    another operation x1, local copies, waits for them, and re-layouts  12.8 us
    ppermute x12, starting transfers between devices, from_partner(): return lax.ppermute(value, axis, pairs)  10.6 us
  transfers between devices with their start and end apart: 15, of which 14 were waited for; matrix products, arithmetic and copies ran while one was open for 7% of the time, Pallas kernels for 0%

commit v1 on v0

v1 whole, which is shorter than its diff:
```python
import functools

import jax
import jax.numpy as jnp
from jax import lax
from jax.experimental import pallas as pl
from jax.experimental.pallas import tpu as pltpu
from jax.sharding import PartitionSpec as P

F32 = jnp.float32
BF16 = jnp.bfloat16
VMEM_LIMIT = 48 * 2**20


def swap(value, axis, mask):
    pairs = [(source, source ^ mask) for source in range(lax.axis_size(axis))]
    return lax.ppermute(value, axis, pairs)


def dot(left, right):
    return jnp.dot(left, right, preferred_element_type=F32)


def params():
    return pltpu.CompilerParams(vmem_limit_bytes=VMEM_LIMIT)


def cost(flops, moved):
    return pl.CostEstimate(flops=flops, bytes_accessed=moved, transcendentals=0)


def forward_kernel(levels, offsets, ancestors, rhs, inv, panels, start, value, total, held):
    step = pl.program_id(0)
    slots = panels.shape[1]

    @pl.when(step == 0)
    def _():
        held[...] = start[...]

    solved = dot(inv[0], rhs[0]).astype(BF16)
    value[0] = solved
    products = [dot(panels[0, slot], solved) for slot in range(slots)]
    for level in range(levels):
        add = None
        for slot in range(slots):
            chosen = (ancestors[step, slot] == level + 1).astype(F32)
            term = products[slot] * chosen
            add = term if add is None else add + term
        held[level] += add

    @pl.when(step == pl.num_programs(0) - 1)
    def _():
        total[...] = held[...].astype(total.dtype)


def forward(offset, ancestors, rhs, inv, panels, start, out_dtype):
    count, size, _ = inv.shape
    slots = panels.shape[1]
    levels, _, cols = start.shape
    return pl.pallas_call(
        functools.partial(forward_kernel, levels),
        grid_spec=pltpu.PrefetchScalarGridSpec(
            num_scalar_prefetch=2,
            grid=(count,),
            in_specs=[
                pl.BlockSpec((1, size, cols), lambda i, offsets, _: (offsets[0] + i, 0, 0)),
                pl.BlockSpec((1, size, size), lambda i, *_: (i, 0, 0)),
                pl.BlockSpec((1, slots, size, size), lambda i, *_: (i, 0, 0, 0)),
                pl.BlockSpec((levels, size, cols), lambda i, *_: (0, 0, 0)),
            ],
            out_specs=[
                pl.BlockSpec((1, size, cols), lambda i, *_: (i, 0, 0)),
                pl.BlockSpec((levels, size, cols), lambda i, *_: (0, 0, 0)),
            ],
            scratch_shapes=[pltpu.VMEM((levels, size, cols), F32)],
        ),
        out_shape=[
            jax.ShapeDtypeStruct((count, size, cols), BF16),
            jax.ShapeDtypeStruct((levels, size, cols), out_dtype),
        ],
        compiler_params=params(),
        cost_estimate=cost(
            2 * count * (1 + slots) * size * size * cols,
            2 * count * size * ((1 + slots) * size + 2 * cols),
        ),
        name="leaf_forward",
    )(offset, ancestors, rhs, inv, panels, start)


def backward_kernel(ancestors, value, inv, panels, paths, result):
    step = pl.program_id(0)
    rest = value[0].astype(F32)
    for slot in range(panels.shape[1]):
        level = ancestors[step, slot]
        picked = paths[jnp.maximum(level - 1, 0)]
        picked = jnp.where(level > 0, picked, jnp.zeros_like(picked))
        rest = rest - dot(panels[0, slot], picked)
    result[0] = dot(inv[0], rest.astype(BF16)).astype(BF16)


def backward(ancestors, value, inv, panels, paths):
    count, size, _ = inv.shape
    slots = panels.shape[1]
    levels, _, cols = paths.shape
    return pl.pallas_call(
        backward_kernel,
        grid_spec=pltpu.PrefetchScalarGridSpec(
            num_scalar_prefetch=1,
            grid=(count,),
            in_specs=[
                pl.BlockSpec((1, size, cols), lambda i, *_: (i, 0, 0)),
                pl.BlockSpec((1, size, size), lambda i, *_: (i, 0, 0)),
                pl.BlockSpec((1, slots, size, size), lambda i, *_: (i, 0, 0, 0)),
                pl.BlockSpec((levels, size, cols), lambda i, *_: (0, 0, 0)),
            ],
            out_specs=pl.BlockSpec((1, size, cols), lambda i, *_: (i, 0, 0)),
        ),
        out_shape=jax.ShapeDtypeStruct((count, size, cols), BF16),
        compiler_params=params(),
        cost_estimate=cost(
            2 * count * (1 + slots) * size * size * cols,
            2 * count * size * ((1 + slots) * size + 2 * cols),
        ),
        name="leaf_backward",
    )(ancestors, value, inv, panels, paths)


def climb_kernel(mine, theirs, factors, solved, passed):
    pending = mine[0].astype(F32) + theirs[0].astype(F32)
    value = dot(factors[0], (-pending).astype(BF16)).astype(BF16)
    solved[...] = value
    for above in range(passed.shape[0]):
        carried = mine[above + 1].astype(F32) + theirs[above + 1].astype(F32)
        passed[above] = (carried + dot(factors[2 + 2 * above], value)).astype(BF16)


def climb(mine, theirs, factors):
    levels, size, cols = mine.shape
    return pl.pallas_call(
        climb_kernel,
        out_shape=[
            jax.ShapeDtypeStruct((size, cols), BF16),
            jax.ShapeDtypeStruct((levels - 1, size, cols), BF16),
        ],
        compiler_params=params(),
        cost_estimate=cost(2 * levels * size * size * cols, 2 * levels * size * (size + 4 * cols)),
        name="climb",
    )(mine, theirs, factors)


def descend_kernel(levels, mine, theirs, *refs):
    factors, values, paths = refs[:levels], refs[levels : 2 * levels - 1], refs[-1]
    pending = mine[0].astype(F32) + theirs[0].astype(F32)
    top = dot(factors[levels - 1][0], (-pending).astype(BF16)).astype(BF16)
    for level in range(levels - 1, -1, -1):
        rest = top if level == levels - 1 else values[level][...]
        if level < levels - 1:
            rest = rest.astype(F32)
            for above in range(levels - 1 - level):
                rest = rest - dot(factors[level][3 + 2 * above], paths[level + 1 + above])
            rest = rest.astype(BF16)
        paths[level] = dot(factors[level][1], rest).astype(BF16)


def descend(mine, theirs, factors, values):
    levels = len(factors)
    _, size, cols = mine.shape
    return pl.pallas_call(
        functools.partial(descend_kernel, levels),
        out_shape=jax.ShapeDtypeStruct((levels, size, cols), BF16),
        compiler_params=params(),
        cost_estimate=cost(
            levels * (levels + 3) * size * size * cols, levels * (levels + 3) * size * size
        ),
        name="descend",
    )(mine, theirs, *factors, *values)


def along_path(own, levels, device):
    chosen = []
    for level in range(1, levels + 1):
        block = own[: 2 + 2 * (levels - level)]
        owner = 2 ** (level - 1)
        holders = {owner}
        for bit in reversed(range(level)):
            targets = {holder ^ 2**bit for holder in holders}
            groups = range(0, lax.axis_size("leaf"), 2**level)
            pairs = [(group + holder, group + (holder ^ 2**bit)) for group in groups for holder in sorted(holders)]
            arrived = lax.ppermute(block, "leaf", pairs)
            place = device % 2**level
            took = functools.reduce(jnp.logical_or, [place == target for target in sorted(targets)])
            block = jnp.where(took, arrived, block)
            holders |= targets
        chosen.append(block)
    return chosen


def on_device(
    leaf_rhs,
    leaf_lower_inv,
    leaf_lower_panels,
    leaf_upper_inv,
    leaf_upper_panels,
    ancestors,
    sep_rhs,
    sep_lower_inv,
    sep_lower_panels,
    sep_upper_inv,
    sep_upper_panels,
):
    levels = lax.axis_size("leaf").bit_length() - 1
    device = lax.axis_index("leaf")
    place = lax.axis_index("col")
    low, high = place % 2, place // 2
    count = leaf_lower_inv.shape[0]
    _, size, cols = leaf_rhs.shape

    first_rows = high * 2 * count + low * count
    second_rows = high * 2 * count + (1 - low) * count
    far_first_rows = (1 - high) * 2 * count + low * count
    far_second_rows = (1 - high) * 2 * count + (1 - low) * count
    far_first = swap(lax.dynamic_slice_in_dim(leaf_rhs, far_first_rows, count, 0), "col", 2)
    far_second = swap(lax.dynamic_slice_in_dim(leaf_rhs, far_second_rows, count, 0), "col", 2)
    near_ancestors = swap(ancestors, "col", 1)
    near_lower_inv = swap(leaf_lower_inv, "col", 1)
    near_lower_panels = swap(leaf_lower_panels, "col", 1)
    near_upper_inv = swap(leaf_upper_inv, "col", 1)
    near_upper_panels = swap(leaf_upper_panels, "col", 1)

    pieces = [sep_lower_inv, sep_upper_inv]
    for above in range(levels - 1):
        pieces += [sep_lower_panels[:, above], sep_upper_panels[:, above]]
    path_factors = along_path(jnp.concatenate(pieces, axis=0), levels, device)

    owned = [device % 2**level == 2 ** (level - 1) for level in range(1, levels + 1)]
    negated = -sep_rhs[0].astype(F32)
    start_own = jnp.stack([jnp.where(is_owner, negated, 0.0) for is_owner in owned])
    start_far = jnp.zeros_like(start_own)
    zero = jnp.zeros((1,), jnp.int32)

    def at(rows):
        return jnp.reshape(rows, (1,)).astype(jnp.int32)

    value_first, total = forward(
        at(first_rows), ancestors, leaf_rhs, leaf_lower_inv, leaf_lower_panels, start_own, F32
    )
    value_second, own_total = forward(
        at(second_rows), near_ancestors, leaf_rhs, near_lower_inv, near_lower_panels, total, F32
    )
    far_value_first, total = forward(
        zero, ancestors, far_first, leaf_lower_inv, leaf_lower_panels, start_far, F32
    )
    far_value_second, far_total = forward(
        zero, near_ancestors, far_second, near_lower_inv, near_lower_panels, total, BF16
    )

    mine = (own_total + swap(far_total, "col", 2).astype(F32)).astype(BF16)
    values = []
    for level in range(1, levels):
        theirs = swap(mine, "leaf", 2 ** (level - 1))
        solved, mine = climb(mine, theirs, path_factors[level - 1])
        values.append(solved)
    theirs = swap(mine, "leaf", 2 ** (levels - 1))
    paths = descend(mine, theirs, path_factors, values)
    far_paths = swap(paths, "col", 2)

    own_solution = jnp.zeros((size, cols), BF16)
    for level in range(levels):
        own_solution = jnp.where(owned[level], paths[level], own_solution)

    sent_first = backward(ancestors, far_value_first, leaf_upper_inv, leaf_upper_panels, far_paths)
    sent_second = backward(
        near_ancestors, far_value_second, near_upper_inv, near_upper_panels, far_paths
    )
    got_first = swap(sent_first, "col", 2)
    got_second = swap(sent_second, "col", 2)
    own_first = backward(ancestors, value_first, leaf_upper_inv, leaf_upper_panels, paths)
    own_second = backward(near_ancestors, value_second, near_upper_inv, near_upper_panels, paths)

    solution_rows = jnp.zeros(leaf_rhs.shape, BF16)
    for rows, part in (
        (first_rows, own_first),
        (second_rows, own_second),
        (far_first_rows, got_first),
        (far_second_rows, got_second),
    ):
        solution_rows = lax.dynamic_update_slice_in_dim(solution_rows, part, rows, 0)
    return (solution_rows, own_solution[None])


def solution(mesh):
    placed = (
        P("leaf", None, "col"),
        P(("leaf", "col"), None, None),
        P(("leaf", "col"), None, None, None),
        P(("leaf", "col"), None, None),
        P(("leaf", "col"), None, None, None),
        P(("leaf", "col"), None),
        P("leaf", None, "col"),
        P("leaf", None, None),
        P("leaf", None, None, None),
        P("leaf", None, None),
        P("leaf", None, None, None),
    )
    return jax.shard_map(
        on_device,
        mesh=mesh,
        in_specs=placed,
        out_specs=(P("leaf", None, "col"), P("leaf", None, "col")),
        check_vma=False,
    )
```

time: 365 us -> 145 us (0.40)
  local copies, waits for them, and re-layouts: 159 us -> 21.1 us
  waiting for transfers between devices: 128 us -> 29.4 us
  Pallas kernels: 0 us -> 58.4 us
  matrix products: 34.5 us -> 0 us
  between operations: 14.3 us -> 1.17 us
  starting transfers between devices: 19.8 us -> 28.1 us
  blocking collectives: 7.65 us -> 0 us
  other arithmetic: 0.16 us -> 5.51 us
    unnamed x27 -> x53, local copies, waits for them, and re-layouts: 116 us -> 13.9 us
    pallas_call x0 -> x11, Pallas kernels: none -> 58.4 us  [the longest x4 28.4 us: forward(): pl.pallas_call(functools.partial(forward_kernel, levels), grid_spec=pltpu...]
    all_to_all x2 -> x0, waiting for transfers between devices: 51.3 us -> none  [the longest x1 26.3 us: on_device(): lax.all_to_all(leaf_rhs, 'col', split_axis=0, concat_axis=2, tiled=True)]
    dot_general x13 -> x0, matrix products: 34.5 us -> none  [the longest x1 9.66 us: on_device(): jnp.einsum('kbc,kcr->kbr', leaf_upper_inv, leaf_rest, preferred_element_t...]
    unnamed x2 -> x0, waiting for transfers between devices: 29.5 us -> none
    ppermute x12 -> x20, waiting for transfers between devices: 46.9 us -> 29.4 us  [the longest x14 25.1 us: swap(): return lax.ppermute(value, axis, pairs)]
    ppermute x12 -> x20, starting transfers between devices: 10.6 us -> 28.1 us  [the longest x14 14.1 us: swap(): return lax.ppermute(value, axis, pairs)]
    all_to_all x3 -> x0, local copies, waits for them, and re-layouts: 13.2 us -> none  [the longest x2 8.65 us: on_device(): lax.all_to_all(leaf_rhs, 'col', split_axis=0, concat_axis=2, tiled=True)]
  transfers between devices with their start and end apart: 15 -> 20, of which waited for: 14 -> 6; matrix products, arithmetic and copies ran while one was open for 7% -> 13% of each run, Pallas kernels for 0% -> 41%
where the time goes in v1:
time: 145 us; the launch traced here: 144 us
  Pallas kernels  58.4 us (40%)
  waiting for transfers between devices  29.4 us (20%)
  starting transfers between devices  28.1 us (19%)
  local copies, waits for them, and re-layouts  21.1 us (15%)
  other arithmetic  5.51 us (4%)
    pallas_call x4, Pallas kernels, forward(): pl.pallas_call(functools.partial(forward_kernel, levels), grid_spec=pltpu...  28.4 us
    pallas_call x4, Pallas kernels, backward(): pl.pallas_call(backward_kernel, grid_spec=pltpu.PrefetchScalarGridSpec(nu...  28 us
    ppermute x14, waiting for transfers between devices, swap(): return lax.ppermute(value, axis, pairs)  25.1 us
    ppermute x14, starting transfers between devices, swap(): return lax.ppermute(value, axis, pairs)  14.1 us
    ppermute x6, starting transfers between devices, along_path(): arrived = lax.ppermute(block, 'leaf', pairs)  14 us
    unnamed x53, local copies, waits for them, and re-layouts  13.9 us
    ppermute x6, waiting for transfers between devices, along_path(): arrived = lax.ppermute(block, 'leaf', pairs)  4.25 us
    concatenate x2, local copies, waits for them, and re-layouts, on_device(): path_factors = along_path(jnp.concatenate(pieces, axis=0), levels, device)  3.19 us
  transfers between devices with their start and end apart: 20, of which 6 were waited for; matrix products, arithmetic and copies ran while one was open for 13% of the time, Pallas kernels for 41%

profile of v1, /device:TPU:0, one launch (start us, length us, event | category | flops | bytes accessed | tf_op | source)
XLA Modules:
  0.0 143.7 jit_solution(3582681975848167664)
XLA Ops:
  0.7 0.5 collective-permute-start.2
  1.2 1.6 %constant_dynamic-update-slice_fusion.5 = (bf16[2,256,256]{2,1,0:T(8,128)(2,1)}, bf16[6,256,256]{2,1,0:T(8,128)(2,1)}) fusion(bf16[1,256,256]{2,1,0:T(8,128)(2,1)} %param.18), kind=kLoop, calls=%fused_computation.25 | loop fusion | bytes 393216
  2.8 1.6 %constant_dynamic-update-slice_fusion.4 = (bf16[2,256,256]{2,1,0:T(8,128)(2,1)}, bf16[6,256,256]{2,1,0:T(8,128)(2,1)}) fusion(bf16[2,256,256]{2,1,0:T(8,128)(2,1)} %get-tuple-element.30, bf16[1,256,256]{2,1,0:T(8,128)(2,1)} %param.20, bf16[6,256,256]{2,1,0:T(8,128)(2,1)} %get-tuple-element.31), kind=kLoop, calls=%fused_computation.24 | loop fusion | bytes 393216 | tf_op jit(solution)/shard_map/concatenate | solution.py:233
  4.4 1.3 collective-permute-start.12
  5.8 2.3 %constant_dynamic-slice_fusion = (bf16[8,256,128]{2,1,0:T(8,128)(2,1)}, bf16[8,256,128]{2,1,0:T(8,128)(2,1)}) fusion(bf16[32,256,128]{2,1,0:T(8,128)(2,1)} %rhs.3, s32[]{:T(128)S(6)} %select_n.143, s32[]{:T(128)S(6)} %select_n.142), kind=kLoop, calls=%fused_computation.30 | loop fusion | bytes 2097160 | tf_op jit(solution)/shard_map/dynamic_slice | solution.py:222
  8.1 2.7 %collective-permute-start.4 = (bf16[8,256,128]{2,1,0:T(8,128)(2,1)}, bf16[8,256,128]{2,1,0:T(8,128)(2,1)}, u32[]{:S(2)}, u32[]{:S(2)}) collective-permute-start(bf16[8,256,128]{2,1,0:T(8,128)(2,1)} %get-tuple-element.26), channel_id=1, source_target_pairs={{0,2},{1,3},{2,0},{3,1},{4,6},{5,7},{6,4},{7,5},{8,10},{9,11},{10,... | collective-permute-start | bytes 1572872 | tf_op jit(solution)/shard_map/ppermute | solution.py:17
  11.4 1.7 %constant_dynamic-update-slice_fusion.1 = bf16[6,256,256]{2,1,0:T(8,128)(2,1)} fusion(bf16[6,256,256]{2,1,0:T(8,128)(2,1)} %get-tuple-element.29, bf16[1,2,256,256]{3,2,1,0:T(8,128)(2,1)} %param.19), kind=kLoop, calls=%fused_computation.21 | loop fusion | bytes 262144
  13.1 1.0 slice_bitcast_fusion
  14.1 0.6 copy-done.21
  14.7 0.9 pad_maximum_fusion
  15.6 0.9 fusion.2
  16.6 1.7 %broadcast_select_fusion.3 = bf16[2,256,256]{2,1,0:T(8,128)(2,1)} fusion(bf16[2,256,256]{2,1,0:T(8,128)(2,1)} %collective-permute-done.12, bf16[2,256,256]{2,1,0:T(8,128)(2,1)} %get-tuple-element.28, pred[]{:T(512)S(6)} %eq.66), kind=kLoop, calls=%fused_computation.6 | loop fusion | flops 131072 | bytes 786433 | tf_op jit(solution)/shard_map/jit(_where)/select_n | solution.py:192
  18.3 4.2 %collective-permute-start.13 = (bf16[2,256,256]{2,1,0:T(8,128)(2,1)}, bf16[2,256,256]{2,1,0:T(8,128)(2,1)}, u32[]{:S(2)}, u32[]{:S(2)}) collective-permute-start(bf16[2,256,256]{2,1,0:T(8,128)(2,1)} %broadcast_select_fusion.3), channel_id=1, source_target_pairs={{0,8},{16,24},{1,9},{17,25},{2,10},{18,26},{3,11},{19,27}} | collective-permute-start | bytes 786440 | tf_op jit(solution)/shard_map/ppermute | solution.py:189
  22.6 1.6 %constant_dynamic-update-slice_fusion = bf16[6,256,256]{2,1,0:T(8,128)(2,1)} fusion(bf16[6,256,256]{2,1,0:T(8,128)(2,1)} %constant_dynamic-update-slice_fusion.1, bf16[1,2,256,256]{3,2,1,0:T(8,128)(2,1)} %param.21), kind=kLoop, calls=%fused_computation.20 | loop fusion | bytes 262144
  24.2 4.2 %collective-permute-done.13 = bf16[2,256,256]{2,1,0:T(8,128)(2,1)} collective-permute-done((bf16[2,256,256]{2,1,0:T(8,128)(2,1)}, bf16[2,256,256]{2,1,0:T(8,128)(2,1)}, u32[]{:S(2)}, u32[]{:S(2)}) %collective-permute-start.13) | collective-permute-done | bytes 262176 | tf_op jit(solution)/shard_map/ppermute | solution.py:189
  28.8 7.1 %leaf_forward.4 = (bf16[8,256,128]{2,1,0:T(8,128)(2,1)S(1)}, f32[3,256,128]{2,1,0:T(8,128)S(1)}) custom-call(s32[1]{0:T(128)} %bitcast.offsets, s32[8,3]{1,0:T(8,128)S(1)} %copy.16.ancestors, bf16[32,256,128]{2,1,0:T(8,128)(2,1)S(1)} %copy-done, bf16[8,256,256]{2,1,0:T(8,128)(2,1)S(1)} %copy-done.3, bf16[8,3,256,256]{3,2,1,0:T(8,128)(2,1)} %panels.5, ...), custom_call_target="tpu_custom_call" | custom-call | flops 536870912 | bytes 5242880 | tf_op jit(solution)/shard_map/leaf_forward/pallas_call | solution.py:60
  36.0 0.8 copy-done.4
  36.8 0.7 copy-done.12
  37.5 1.6 %bitcast_dynamic-update-slice_fusion.1 = bf16[6,256,256]{2,1,0:T(8,128)(2,1)} fusion(bf16[6,256,256]{2,1,0:T(8,128)(2,1)} %constant_dynamic-update-slice_fusion, bf16[1,2,256,256]{3,2,1,0:T(8,128)(2,1)} %param.19), kind=kLoop, calls=%fused_computation.10 | loop fusion | bytes 262144
  39.1 1.3 collective-permute-start.9
  40.4 1.6 %bitcast_dynamic-update-slice_fusion = bf16[6,256,256]{2,1,0:T(8,128)(2,1)} fusion(bf16[6,256,256]{2,1,0:T(8,128)(2,1)} %bitcast_dynamic-update-slice_fusion.1, bf16[1,2,256,256]{3,2,1,0:T(8,128)(2,1)} %param.21), kind=kLoop, calls=%fused_computation.9 | loop fusion | bytes 262144 | tf_op jit(solution)/shard_map/concatenate | solution.py:233
  42.0 1.9 %copy-done.1 = bf16[8,3,256,256]{3,2,1,0:T(8,128)(2,1)S(1)} copy-done((bf16[8,3,256,256]{3,2,1,0:T(8,128)(2,1)S(1)}, bf16[8,3,256,256]{3,2,1,0:T(8,128)(2,1)}, u32[]{:S(2)}) %copy-start.1) | copy-done | bytes 3145752
  43.9 6.4 %leaf_forward.6 = (bf16[8,256,128]{2,1,0:T(8,128)(2,1)S(1)}, f32[3,256,128]{2,1,0:T(8,128)S(1)}) custom-call(s32[1]{0:T(128)} %constant.86.clone.1.offsets, s32[8,3]{1,0:T(8,128)S(1)} %copy.16.ancestors, bf16[8,256,128]{2,1,0:T(8,128)(2,1)} %collective-permute-done.4.rhs, bf16[8,256,256]{2,1,0:T(8,128)(2,1)S(1)} %copy-done.3, ...), custom_call_target="tpu_custom_call" | custom-call | flops 536870912 | bytes 5242880 | tf_op jit(solution)/shard_map/leaf_forward/pallas_call | solution.py:60
  50.3 1.3 collective-permute-start.7
  51.6 1.0 broadcast_select_fusion.4
  52.7 4.6 %collective-permute-start.14 = (bf16[2,256,256]{2,1,0:T(8,128)(2,1)S(1)}, bf16[2,256,256]{2,1,0:T(8,128)(2,1)S(1)}, u32[]{:S(2)}, u32[]{:S(2)}) collective-permute-start(bf16[2,256,256]{2,1,0:T(8,128)(2,1)S(1)} %broadcast_select_fusion.4), channel_id=1, source_target_pairs={{0,4},{8,12},{16,20},{24,28},{1,5},{9,13},{17,21},{25,29},{2,6},{1... | collective-permute-start | bytes 786440 | tf_op jit(solution)/shard_map/ppermute | solution.py:189
  57.4 7.5 %leaf_forward.7 = (bf16[8,256,128]{2,1,0:T(8,128)(2,1)S(1)}, bf16[3,256,128]{2,1,0:T(8,128)(2,1)S(1)}) custom-call(s32[1]{0:T(128)} %constant.86.clone.1.offsets, s32[8,3]{1,0:T(8,128)S(1)} %collective-permute-done.ancestors, bf16[8,256,128]{2,1,0:T(8,128)(2,1)} %collective-permute-done.3.rhs, bf16[8,256,256]{2,1,0:T(8,128)(2,1)} %collective-permute-done.1.inv, ...), custom_call_target="tpu_custom_call" | custom-call | flops 536870912 | bytes 5242880 | tf_op jit(solution)/shard_map/leaf_forward/pallas_call | solution.py:60
  64.9 1.6 %collective-permute-start.5 = (bf16[3,256,128]{2,1,0:T(8,128)(2,1)S(1)}, bf16[3,256,128]{2,1,0:T(8,128)(2,1)S(1)}, u32[]{:S(2)}, u32[]{:S(2)}) collective-permute-start(bf16[3,256,128]{2,1,0:T(8,128)(2,1)S(1)} %get-tuple-element.18), channel_id=1, source_target_pairs={{0,2},{1,3},{2,0},{3,1},{4,6},{5,7},{6,4},{7,5},{8,10},{9,11},{10,... | collective-permute-start | bytes 589832 | tf_op jit(solution)/shard_map/ppermute | solution.py:17
  66.7 7.4 %leaf_forward.5 = (bf16[8,256,128]{2,1,0:T(8,128)(2,1)S(1)}, f32[3,256,128]{2,1,0:T(8,128)S(1)}) custom-call(s32[1]{0:T(128)} %bitcast.1.offsets, s32[8,3]{1,0:T(8,128)S(1)} %collective-permute-done.ancestors, bf16[32,256,128]{2,1,0:T(8,128)(2,1)S(1)} %copy-done, bf16[8,256,256]{2,1,0:T(8,128)(2,1)} %collective-permute-done.1.inv, ...), custom_call_target="tpu_custom_call" | custom-call | flops 536870912 | bytes 5242880 | tf_op jit(solution)/shard_map/leaf_forward/pallas_call | solution.py:60
  74.1 0.8 copy-done.10
  74.9 1.3 collective-permute-start.10
  76.5 15.4 %collective-permute-done.6.theirs = bf16[3,256,128]{2,1,0:T(8,128)(2,1)S(1)} collective-permute-done((bf16[3,256,128]{2,1,0:T(8,128)(2,1)S(1)}, bf16[3,256,128]{2,1,0:T(8,128)(2,1)S(1)}, u32[]{:S(2)}, u32[]{:S(2)}) %collective-permute-start.6) | collective-permute-done | bytes 196640 | tf_op jit(solution)/shard_map/ppermute | solution.py:17
  92.3 2.7 %collective-permute-start.8 = (bf16[2,256,128]{2,1,0:T(8,128)(2,1)S(1)}, bf16[2,256,128]{2,1,0:T(8,128)(2,1)S(1)}, u32[]{:S(2)}, u32[]{:S(2)}) collective-permute-start(bf16[2,256,128]{2,1,0:T(8,128)(2,1)S(1)} %get-tuple-element.19.mine), channel_id=1, source_target_pairs={{0,8},{4,12},{8,0},{12,4},{16,24},{20,28},{24,16},{28,20},{1,9},{5... | collective-permute-start | bytes 393224 | tf_op jit(solution)/shard_map/ppermute | solution.py:17
  95.1 2.9 %collective-permute-done.8.theirs = bf16[2,256,128]{2,1,0:T(8,128)(2,1)S(1)} collective-permute-done((bf16[2,256,128]{2,1,0:T(8,128)(2,1)S(1)}, bf16[2,256,128]{2,1,0:T(8,128)(2,1)S(1)}, u32[]{:S(2)}, u32[]{:S(2)}) %collective-permute-start.8) | collective-permute-done | bytes 131104 | tf_op jit(solution)/shard_map/ppermute | solution.py:17
  98.4 2.7 %collective-permute-start.11 = (bf16[1,256,128]{2,1,0:T(8,128)(2,1)S(1)}, bf16[1,256,128]{2,1,0:T(8,128)(2,1)S(1)}, u32[]{:S(2)}, u32[]{:S(2)}) collective-permute-start(bf16[1,256,128]{2,1,0:T(8,128)(2,1)S(1)} %get-tuple-element.20.mine), channel_id=1, source_target_pairs={{0,16},{4,20},{8,24},{12,28},{16,0},{20,4},{24,8},{28,12},{1,17},{... | collective-permute-start | bytes 196616 | tf_op jit(solution)/shard_map/ppermute | solution.py:17
  101.1 2.5 %collective-permute-done.11.theirs = bf16[1,256,128]{2,1,0:T(8,128)(2,1)S(1)} collective-permute-done((bf16[1,256,128]{2,1,0:T(8,128)(2,1)S(1)}, bf16[1,256,128]{2,1,0:T(8,128)(2,1)S(1)}, u32[]{:S(2)}, u32[]{:S(2)}) %collective-permute-start.11) | collective-permute-done | bytes 65568 | tf_op jit(solution)/shard_map/ppermute | solution.py:17
  103.7 1.1 descend.1.paths
  104.8 0.6 collective-permute-start.17
  105.4 1.0 copy-done.5
  106.4 6.7 %leaf_backward.4 = bf16[8,256,128]{2,1,0:T(8,128)(2,1)S(1)} custom-call(s32[8,3]{1,0:T(8,128)S(1)} %copy.16.ancestors, bf16[8,256,128]{2,1,0:T(8,128)(2,1)S(1)} %copy-done.5, bf16[8,256,256]{2,1,0:T(8,128)(2,1)} %inv.7, bf16[8,3,256,256]{3,2,1,0:T(8,128)(2,1)S(1)} %copy-done.2, bf16[3,256,128]{2,1,0:T(8,128)(2,1)S(1)} %descend.1.paths), custom_call_target="tpu_custom_call" | custom-call | flops 536870912 | bytes 5242880 | tf_op jit(solution)/shard_map/leaf_backward/pallas_call | solution.py:105
  113.1 6.7 %leaf_backward.6 = bf16[8,256,128]{2,1,0:T(8,128)(2,1)S(1)} custom-call(s32[8,3]{1,0:T(8,128)S(1)} %copy.16.ancestors, bf16[8,256,128]{2,1,0:T(8,128)(2,1)S(1)} %copy-done.7, bf16[8,256,256]{2,1,0:T(8,128)(2,1)} %inv.7, bf16[8,3,256,256]{3,2,1,0:T(8,128)(2,1)S(1)} %copy-done.2, bf16[3,256,128]{2,1,0:T(8,128)(2,1)S(1)} %collective-permute-done.17.paths), custom_call_target="tpu_custom_call" | custom-call | flops 536870912 | bytes 5242880 | tf_op jit(solution)/shard_map/leaf_backward/pallas_call | solution.py:105
  119.8 1.6 %collective-permute-start.18 = (bf16[8,256,128]{2,1,0:T(8,128)(2,1)S(1)}, bf16[8,256,128]{2,1,0:T(8,128)(2,1)S(1)}, u32[]{:S(2)}, u32[]{:S(2)}) collective-permute-start(bf16[8,256,128]{2,1,0:T(8,128)(2,1)S(1)} %leaf_backward.6), channel_id=1, source_target_pairs={{0,2},{1,3},{2,0},{3,1},{4,6},{5,7},{6,4},{7,5},{8,10},{9,11},{10,... | collective-permute-start | bytes 1572872 | tf_op jit(solution)/shard_map/ppermute | solution.py:17
  122.0 7.3 %leaf_backward.7 = bf16[8,256,128]{2,1,0:T(8,128)(2,1)S(1)} custom-call(s32[8,3]{1,0:T(8,128)S(1)} %collective-permute-done.ancestors, bf16[8,256,128]{2,1,0:T(8,128)(2,1)S(1)} %copy-done.9, bf16[8,256,256]{2,1,0:T(8,128)(2,1)} %collective-permute-done.15.inv, bf16[8,3,256,256]{3,2,1,0:T(8,128)(2,1)} %collective-permute-done.16.panels, ...), custom_call_target="tpu_custom_call" | custom-call | flops 536870912 | bytes 5242880 | tf_op jit(solution)/shard_map/leaf_backward/pallas_call | solution.py:105
  129.4 0.6 collective-permute-start.19
  129.9 7.3 %leaf_backward.5 = bf16[8,256,128]{2,1,0:T(8,128)(2,1)S(1)} custom-call(s32[8,3]{1,0:T(8,128)S(1)} %collective-permute-done.ancestors, bf16[8,256,128]{2,1,0:T(8,128)(2,1)S(1)} %copy-done.11, bf16[8,256,256]{2,1,0:T(8,128)(2,1)} %collective-permute-done.15.inv, bf16[8,3,256,256]{3,2,1,0:T(8,128)(2,1)} %collective-permute-done.16.panels, ...), custom_call_target="tpu_custom_call" | custom-call | flops 536870912 | bytes 5242880 | tf_op jit(solution)/shard_map/leaf_backward/pallas_call | solution.py:105
  137.3 0.6 fusion.4
  138.1 4.2 %collective-permute-done.19 = bf16[8,256,128]{2,1,0:T(8,128)(2,1)S(1)} collective-permute-done((bf16[8,256,128]{2,1,0:T(8,128)(2,1)S(1)}, bf16[8,256,128]{2,1,0:T(8,128)(2,1)S(1)}, u32[]{:S(2)}, u32[]{:S(2)}) %collective-permute-start.19) | collective-permute-done | bytes 524320 | tf_op jit(solution)/shard_map/ppermute | solution.py:17
  142.4 1.3 copy-done.14
  (77 shorter events, 3.5 us)
Async XLA Ops:
  0.6 14.1 %copy-start.15 = (bf16[1,256,256]{2,1,0:T(8,128)(2,1)S(1)}, bf16[1,256,256]{2,1,0:T(8,128)(2,1)}, u32[]{:S(2)}) copy-start(bf16[1,256,256]{2,1,0:T(8,128)(2,1)} %param.18) | copy-start | bytes 393220
  0.6 14.1 %copy-start.17 = (bf16[1,256,256]{2,1,0:T(8,128)(2,1)S(1)}, bf16[1,256,256]{2,1,0:T(8,128)(2,1)}, u32[]{:S(2)}) copy-start(bf16[1,256,256]{2,1,0:T(8,128)(2,1)} %param.20) | copy-start | bytes 393220
  0.7 10.1 %copy-start.23 = (s32[8,3]{0,1:T(4,128)S(1)}, s32[8,3]{0,1:T(4,128)}, u32[]{:S(2)}) copy-start(s32[8,3]{0,1:T(4,128)} %param.16) | copy-start | bytes 292
  0.7 10.3 %copy-start.3 = (bf16[8,256,256]{2,1,0:T(8,128)(2,1)S(1)}, bf16[8,256,256]{2,1,0:T(8,128)(2,1)}, u32[]{:S(2)}) copy-start(bf16[8,256,256]{2,1,0:T(8,128)(2,1)} %inv.5) | copy-start | bytes 3145732
  0.7 52.1 %collective-permute-start.2 = (bf16[8,3,256,256]{3,2,1,0:T(8,128)(2,1)}, bf16[8,3,256,256]{3,2,1,0:T(8,128)(2,1)}, u32[]{:S(2)}, u32[]{:S(2)}) collective-permute-start(bf16[8,3,256,256]{3,2,1,0:T(8,128)(2,1)} %panels.5), channel_id=1, source_target_pairs={{0,1},{1,0},{2,3},{3,2},{4,5},{5,4},{6,7},{7,6},{8,9},{9,8},{10,11... | collective-permute-start | bytes 9437192 | tf_op jit(solution)/shard_map/ppermute | solution.py:17
  4.4 12.1 %collective-permute-start.12 = (bf16[2,256,256]{2,1,0:T(8,128)(2,1)}, bf16[2,256,256]{2,1,0:T(8,128)(2,1)}, u32[]{:S(2)}, u32[]{:S(2)}) collective-permute-start(bf16[2,256,256]{2,1,0:T(8,128)(2,1)} %get-tuple-element.28), channel_id=1, source_target_pairs={{16,0},{17,1},{18,2},{19,3}} | collective-permute-start | bytes 786440 | tf_op jit(solution)/shard_map/ppermute | solution.py:189
  8.1 31.0 %collective-permute-start.4 = (bf16[8,256,128]{2,1,0:T(8,128)(2,1)}, bf16[8,256,128]{2,1,0:T(8,128)(2,1)}, u32[]{:S(2)}, u32[]{:S(2)}) collective-permute-start(bf16[8,256,128]{2,1,0:T(8,128)(2,1)} %get-tuple-element.26), channel_id=1, source_target_pairs={{0,2},{1,3},{2,0},{3,1},{4,6},{5,7},{6,4},{7,5},{8,10},{9,11},{10,... | collective-permute-start | bytes 1572872 | tf_op jit(solution)/shard_map/ppermute | solution.py:17
  10.9 7.5 %collective-permute-start = (s32[8,3]{1,0:T(8,128)S(1)}, s32[8,3]{1,0:T(8,128)S(1)}, u32[]{:S(2)}, u32[]{:S(2)}) collective-permute-start(s32[8,3]{1,0:T(8,128)S(1)} %copy.16.ancestors), channel_id=1, source_target_pairs={{0,1},{1,0},{2,3},{3,2},{4,5},{5,4},{6,7},{7,6},{8,9},{9,8},{10,11... | collective-permute-start | bytes 296 | tf_op jit(solution)/shard_map/ppermute | solution.py:17
  10.9 41.7 %collective-permute-start.1 = (bf16[8,256,256]{2,1,0:T(8,128)(2,1)S(1)}, bf16[8,256,256]{2,1,0:T(8,128)(2,1)}, u32[]{:S(2)}, u32[]{:S(2)}) collective-permute-start(bf16[8,256,256]{2,1,0:T(8,128)(2,1)S(1)} %copy-done.3), channel_id=1, source_target_pairs={{0,1},{1,0},{2,3},{3,2},{4,5},{5,4},{6,7},{7,6},{8,9},{9,8},{10,11... | collective-permute-start | bytes 3145736 | tf_op jit(solution)/shard_map/ppermute | solution.py:17
  11.4 17.4 %copy-start = (bf16[32,256,128]{2,1,0:T(8,128)(2,1)S(1)}, bf16[32,256,128]{2,1,0:T(8,128)(2,1)}, u32[]{:S(2)}) copy-start(bf16[32,256,128]{2,1,0:T(8,128)(2,1)} %rhs.3) | copy-start | bytes 6291460
  14.1 0.7 copy-start.21
  14.1 8.5 %copy-start.19 = (bf16[1,256,256]{2,1,0:T(8,128)(2,1)}, bf16[1,256,256]{2,1,0:T(8,128)(2,1)S(1)}, u32[]{:S(2)}) copy-start(bf16[1,256,256]{2,1,0:T(8,128)(2,1)S(1)} %get-tuple-element.35) | copy-start | bytes 393220
  16.6 105.4 %collective-permute-start.16 = (bf16[8,3,256,256]{3,2,1,0:T(8,128)(2,1)}, bf16[8,3,256,256]{3,2,1,0:T(8,128)(2,1)}, u32[]{:S(2)}, u32[]{:S(2)}) collective-permute-start(bf16[8,3,256,256]{3,2,1,0:T(8,128)(2,1)} %panels.7), channel_id=1, source_target_pairs={{0,1},{1,0},{2,3},{3,2},{4,5},{5,4},{6,7},{7,6},{8,9},{9,8},{10,11... | collective-permute-start | bytes 9437192 | tf_op jit(solution)/shard_map/ppermute | solution.py:17
  18.3 10.0 %collective-permute-start.13 = (bf16[2,256,256]{2,1,0:T(8,128)(2,1)}, bf16[2,256,256]{2,1,0:T(8,128)(2,1)}, u32[]{:S(2)}, u32[]{:S(2)}) collective-permute-start(bf16[2,256,256]{2,1,0:T(8,128)(2,1)} %broadcast_select_fusion.3), channel_id=1, source_target_pairs={{0,8},{16,24},{1,9},{17,25},{2,10},{18,26},{3,11},{19,27}} | collective-permute-start | bytes 786440 | tf_op jit(solution)/shard_map/ppermute | solution.py:189
  28.3 22.0 %collective-permute-start.3 = (bf16[8,256,128]{2,1,0:T(8,128)(2,1)}, bf16[8,256,128]{2,1,0:T(8,128)(2,1)}, u32[]{:S(2)}, u32[]{:S(2)}) collective-permute-start(bf16[8,256,128]{2,1,0:T(8,128)(2,1)} %get-tuple-element.27), channel_id=1, source_target_pairs={{0,2},{1,3},{2,0},{3,1},{4,6},{5,7},{6,4},{7,5},{8,10},{9,11},{10,... | collective-permute-start | bytes 1572872 | tf_op jit(solution)/shard_map/ppermute | solution.py:17
  36.0 0.8 copy-start.4
  36.8 0.7 copy-start.12
  39.1 25.9 %collective-permute-start.9 = (bf16[4,256,256]{2,1,0:T(8,128)(2,1)}, bf16[4,256,256]{2,1,0:T(8,128)(2,1)S(1)}, u32[]{:S(2)}, u32[]{:S(2)}) collective-permute-start(bf16[4,256,256]{2,1,0:T(8,128)(2,1)} %pad_maximum_fusion), channel_id=1, source_target_pairs={{8,0},{24,16},{9,1},{25,17},{10,2},{26,18},{11,3},{27,19}} | collective-permute-start | bytes 1572872 | tf_op jit(solution)/shard_map/ppermute | solution.py:189
  42.0 1.9 %copy-start.1 = (bf16[8,3,256,256]{3,2,1,0:T(8,128)(2,1)S(1)}, bf16[8,3,256,256]{3,2,1,0:T(8,128)(2,1)}, u32[]{:S(2)}) copy-start(bf16[8,3,256,256]{3,2,1,0:T(8,128)(2,1)} %panels.5) | copy-start | bytes 9437188
  50.3 2.3 %copy-start.6 = (bf16[8,256,128]{2,1,0:T(8,128)(2,1)}, bf16[8,256,128]{2,1,0:T(8,128)(2,1)S(1)}, u32[]{:S(2)}) copy-start(bf16[8,256,128]{2,1,0:T(8,128)(2,1)S(1)} %get-tuple-element.24.value) | copy-start | bytes 1572868
  50.3 25.9 %collective-permute-start.7 = (bf16[6,256,256]{2,1,0:T(8,128)(2,1)}, bf16[6,256,256]{2,1,0:T(8,128)(2,1)S(1)}, u32[]{:S(2)}, u32[]{:S(2)}) collective-permute-start(bf16[6,256,256]{2,1,0:T(8,128)(2,1)} %bitcast_dynamic-update-slice_fusion), channel_id=1, source_target_pairs={{4,0},{12,8},{20,16},{28,24},{5,1},{13,9},{21,17},{29,25},{6,2},{1... | collective-permute-start | bytes 2359304 | tf_op jit(solution)/shard_map/ppermute | solution.py:189
  52.6 69.3 %collective-permute-start.15 = (bf16[8,256,256]{2,1,0:T(8,128)(2,1)}, bf16[8,256,256]{2,1,0:T(8,128)(2,1)}, u32[]{:S(2)}, u32[]{:S(2)}) collective-permute-start(bf16[8,256,256]{2,1,0:T(8,128)(2,1)} %inv.7), channel_id=1, source_target_pairs={{0,1},{1,0},{2,3},{3,2},{4,5},{5,4},{6,7},{7,6},{8,9},{9,8},{10,11... | collective-permute-start | bytes 3145736 | tf_op jit(solution)/shard_map/ppermute | solution.py:17
  52.7 48.4 %collective-permute-start.14 = (bf16[2,256,256]{2,1,0:T(8,128)(2,1)S(1)}, bf16[2,256,256]{2,1,0:T(8,128)(2,1)S(1)}, u32[]{:S(2)}, u32[]{:S(2)}) collective-permute-start(bf16[2,256,256]{2,1,0:T(8,128)(2,1)S(1)} %broadcast_select_fusion.4), channel_id=1, source_target_pairs={{0,4},{8,12},{16,20},{24,28},{1,5},{9,13},{17,21},{25,29},{2,6},{1... | collective-permute-start | bytes 786440 | tf_op jit(solution)/shard_map/ppermute | solution.py:189
  57.3 9.2 %copy-start.16 = (bf16[1,256,256]{2,1,0:T(8,128)(2,1)S(1)}, bf16[1,256,256]{2,1,0:T(8,128)(2,1)}, u32[]{:S(2)}) copy-start(bf16[1,256,256]{2,1,0:T(8,128)(2,1)} %param.18) | copy-start | bytes 393220
  57.4 9.2 %copy-start.18 = (bf16[1,256,256]{2,1,0:T(8,128)(2,1)S(1)}, bf16[1,256,256]{2,1,0:T(8,128)(2,1)}, u32[]{:S(2)}) copy-start(bf16[1,256,256]{2,1,0:T(8,128)(2,1)} %param.20) | copy-start | bytes 393220
  57.4 9.2 %copy-start.20 = (bf16[1,256,256]{2,1,0:T(8,128)(2,1)S(1)}, bf16[1,256,256]{2,1,0:T(8,128)(2,1)}, u32[]{:S(2)}) copy-start(bf16[1,256,256]{2,1,0:T(8,128)(2,1)} %copy-done.19) | copy-start | bytes 393220
  57.4 9.2 %copy-start.22 = (bf16[1,256,256]{2,1,0:T(8,128)(2,1)S(1)}, bf16[1,256,256]{2,1,0:T(8,128)(2,1)}, u32[]{:S(2)}) copy-start(bf16[1,256,256]{2,1,0:T(8,128)(2,1)} %copy-done.21) | copy-start | bytes 393220
  57.4 9.3 %copy-start.13 = (f32[3,256,128]{2,1,0:T(8,128)S(1)}, f32[3,256,128]{2,1,0:T(8,128)}, u32[]{:S(2)}) copy-start(f32[3,256,128]{2,1,0:T(8,128)} %copy-done.12) | copy-start | bytes 1179652
  64.9 9.1 %copy-start.8 = (bf16[8,256,128]{2,1,0:T(8,128)(2,1)}, bf16[8,256,128]{2,1,0:T(8,128)(2,1)S(1)}, u32[]{:S(2)}) copy-start(bf16[8,256,128]{2,1,0:T(8,128)(2,1)S(1)} %get-tuple-element.25.value) | copy-start | bytes 1572868
  64.9 9.9 %collective-permute-start.5 = (bf16[3,256,128]{2,1,0:T(8,128)(2,1)S(1)}, bf16[3,256,128]{2,1,0:T(8,128)(2,1)S(1)}, u32[]{:S(2)}, u32[]{:S(2)}) collective-permute-start(bf16[3,256,128]{2,1,0:T(8,128)(2,1)S(1)} %get-tuple-element.18), channel_id=1, source_target_pairs={{0,2},{1,3},{2,0},{3,1},{4,6},{5,7},{6,4},{7,5},{8,10},{9,11},{10,... | collective-permute-start | bytes 589832 | tf_op jit(solution)/shard_map/ppermute | solution.py:17
  74.1 0.8 copy-start.10
  74.9 20.1 %collective-permute-start.10 = (bf16[4,256,256]{2,1,0:T(8,128)(2,1)S(1)}, bf16[4,256,256]{2,1,0:T(8,128)(2,1)S(1)}, u32[]{:S(2)}, u32[]{:S(2)}) collective-permute-start(bf16[4,256,256]{2,1,0:T(8,128)(2,1)S(1)} %broadcast_select_fusion.1), channel_id=1, source_target_pairs={{0,4},{8,12},{16,20},{24,28},{1,5},{9,13},{17,21},{25,29},{2,6},{1... | collective-permute-start | bytes 1572872 | tf_op jit(solution)/shard_map/ppermute | solution.py:189
  76.3 15.6 %collective-permute-start.6 = (bf16[3,256,128]{2,1,0:T(8,128)(2,1)S(1)}, bf16[3,256,128]{2,1,0:T(8,128)(2,1)S(1)}, u32[]{:S(2)}, u32[]{:S(2)}) collective-permute-start(bf16[3,256,128]{2,1,0:T(8,128)(2,1)S(1)} %add_convert_fusion.mine), channel_id=1, source_target_pairs={{0,4},{4,0},{8,12},{12,8},{16,20},{20,16},{24,28},{28,24},{1,5},{5... | collective-permute-start | bytes 589832 | tf_op jit(solution)/shard_map/ppermute | solution.py:17
  92.3 5.8 %collective-permute-start.8 = (bf16[2,256,128]{2,1,0:T(8,128)(2,1)S(1)}, bf16[2,256,128]{2,1,0:T(8,128)(2,1)S(1)}, u32[]{:S(2)}, u32[]{:S(2)}) collective-permute-start(bf16[2,256,128]{2,1,0:T(8,128)(2,1)S(1)} %get-tuple-element.19.mine), channel_id=1, source_target_pairs={{0,8},{4,12},{8,0},{12,4},{16,24},{20,28},{24,16},{28,20},{1,9},{5... | collective-permute-start | bytes 393224 | tf_op jit(solution)/shard_map/ppermute | solution.py:17
  95.1 10.2 %copy-start.2 = (bf16[8,3,256,256]{3,2,1,0:T(8,128)(2,1)S(1)}, bf16[8,3,256,256]{3,2,1,0:T(8,128)(2,1)}, u32[]{:S(2)}) copy-start(bf16[8,3,256,256]{3,2,1,0:T(8,128)(2,1)} %panels.7) | copy-start | bytes 9437188
  98.4 5.2 %collective-permute-start.11 = (bf16[1,256,128]{2,1,0:T(8,128)(2,1)S(1)}, bf16[1,256,128]{2,1,0:T(8,128)(2,1)S(1)}, u32[]{:S(2)}, u32[]{:S(2)}) collective-permute-start(bf16[1,256,128]{2,1,0:T(8,128)(2,1)S(1)} %get-tuple-element.20.mine), channel_id=1, source_target_pairs={{0,16},{4,20},{8,24},{12,28},{16,0},{20,4},{24,8},{28,12},{1,17},{... | collective-permute-start | bytes 196616 | tf_op jit(solution)/shard_map/ppermute | solution.py:17
  104.8 8.3 %collective-permute-start.17 = (bf16[3,256,128]{2,1,0:T(8,128)(2,1)S(1)}, bf16[3,256,128]{2,1,0:T(8,128)(2,1)S(1)}, u32[]{:S(2)}, u32[]{:S(2)}) collective-permute-start(bf16[3,256,128]{2,1,0:T(8,128)(2,1)S(1)} %descend.1.paths), channel_id=1, source_target_pairs={{0,2},{1,3},{2,0},{3,1},{4,6},{5,7},{6,4},{7,5},{8,10},{9,11},{10,... | collective-permute-start | bytes 589832 | tf_op jit(solution)/shard_map/ppermute | solution.py:17
  105.4 1.0 copy-start.5
  106.4 6.7 %copy-start.7 = (bf16[8,256,128]{2,1,0:T(8,128)(2,1)S(1)}, bf16[8,256,128]{2,1,0:T(8,128)(2,1)}, u32[]{:S(2)}) copy-start(bf16[8,256,128]{2,1,0:T(8,128)(2,1)} %copy-done.6) | copy-start | bytes 1572868
  119.8 2.2 %copy-start.9 = (bf16[8,256,128]{2,1,0:T(8,128)(2,1)S(1)}, bf16[8,256,128]{2,1,0:T(8,128)(2,1)}, u32[]{:S(2)}) copy-start(bf16[8,256,128]{2,1,0:T(8,128)(2,1)} %copy-done.8) | copy-start | bytes 1572868
  119.8 18.2 %collective-permute-start.18 = (bf16[8,256,128]{2,1,0:T(8,128)(2,1)S(1)}, bf16[8,256,128]{2,1,0:T(8,128)(2,1)S(1)}, u32[]{:S(2)}, u32[]{:S(2)}) collective-permute-start(bf16[8,256,128]{2,1,0:T(8,128)(2,1)S(1)} %leaf_backward.6), channel_id=1, source_target_pairs={{0,2},{1,3},{2,0},{3,1},{4,6},{5,7},{6,4},{7,5},{8,10},{9,11},{10,... | collective-permute-start | bytes 1572872 | tf_op jit(solution)/shard_map/ppermute | solution.py:17
  122.0 7.9 %copy-start.11 = (bf16[8,256,128]{2,1,0:T(8,128)(2,1)S(1)}, bf16[8,256,128]{2,1,0:T(8,128)(2,1)}, u32[]{:S(2)}) copy-start(bf16[8,256,128]{2,1,0:T(8,128)(2,1)} %copy-done.10) | copy-start | bytes 1572868
  129.4 12.9 %collective-permute-start.19 = (bf16[8,256,128]{2,1,0:T(8,128)(2,1)S(1)}, bf16[8,256,128]{2,1,0:T(8,128)(2,1)S(1)}, u32[]{:S(2)}, u32[]{:S(2)}) collective-permute-start(bf16[8,256,128]{2,1,0:T(8,128)(2,1)S(1)} %leaf_backward.7), channel_id=1, source_target_pairs={{0,2},{1,3},{2,0},{3,1},{4,6},{5,7},{6,4},{7,5},{8,10},{9,11},{10,... | collective-permute-start | bytes 1572872 | tf_op jit(solution)/shard_map/ppermute | solution.py:17
  142.3 1.3 copy-start.14

commit v2 on v0

v2 whole, which is shorter than its diff:
```python
import functools

import jax
import jax.numpy as jnp
from jax import lax
from jax.experimental import pallas as pl
from jax.experimental.pallas import tpu as pltpu
from jax.sharding import PartitionSpec as P

F32 = jnp.float32
BF16 = jnp.bfloat16
FORWARD_VMEM = 60 * 2**20
LEAF_VMEM = 10 * 2**20
TREE_VMEM = 6 * 2**20
BATCH = 4
PART = 3


def swap(value, axis, mask):
    pairs = [(source, source ^ mask) for source in range(lax.axis_size(axis))]
    return lax.ppermute(value, axis, pairs)


def dot(left, right):
    return jnp.dot(left, right, preferred_element_type=F32)


def cost(flops, moved):
    return pl.CostEstimate(flops=flops, bytes_accessed=moved, transcendentals=0)


def forward_kernel(first, last, scalars, ancestors, rhs, far, inv, panels, start, *refs):
    if last:
        value, own_total, far_total, solved, held, sems = refs
    else:
        value, total, solved, held, sems = refs
    step, steps = pl.program_id(0), pl.num_programs(0)
    batch, slots = panels.shape[:2]
    levels, _, both = held.shape
    cols = both // 2

    def leaving(leaf):
        return pltpu.make_async_copy(solved.at[leaf], value.at[leaf], sems.at[leaf])

    @pl.when(step == 0)
    def _():
        if first:
            for level in range(levels):
                held[level, :, :cols] = start[0].astype(F32) * -(scalars[2] == level + 1).astype(F32)
                held[level, :, cols:] = jnp.zeros((held.shape[1], cols), F32)
        else:
            held[...] = start[...]

    values = []
    for leaf in range(batch):
        columns = jnp.concatenate([rhs[leaf], far[leaf]], axis=1)
        values.append(dot(inv[leaf], columns).astype(BF16))
        solved[step * batch + leaf] = values[leaf]
        leaving(step * batch + leaf).start()
    sums = [None] * levels
    for leaf in range(batch):
        for slot in range(slots):
            product = dot(panels[leaf, slot], values[leaf])
            named = ancestors[step * batch + leaf, slot]
            for level in range(levels):
                term = product * (named == level + 1).astype(F32)
                sums[level] = term if sums[level] is None else sums[level] + term
    for level in range(levels):
        held[level] += sums[level]

    @pl.when(step == steps - 1)
    def _():
        if last:
            own_total[...] = held[:, :, :cols]
            far_total[...] = held[:, :, cols:].astype(BF16)
        else:
            total[...] = held[...]
        for leaf in range(solved.shape[0]):
            leaving(leaf).wait()


def forward(levels, scalars, which, ancestors, inv, panels, rhs, far, start, first, last):
    count, size, _ = inv.shape
    cols = rhs.shape[2]
    slots = panels.shape[1]
    batch = min(BATCH, count)
    whole = lambda i, *_: (0, 0, 0)
    if last:
        sums = [jax.ShapeDtypeStruct((levels, size, cols), F32), jax.ShapeDtypeStruct((levels, size, cols), BF16)]
    else:
        sums = [jax.ShapeDtypeStruct((levels, size, 2 * cols), F32)]
    return pl.pallas_call(
        functools.partial(forward_kernel, first, last),
        grid_spec=pltpu.PrefetchScalarGridSpec(
            num_scalar_prefetch=2,
            grid=(count // batch,),
            in_specs=[
                pl.BlockSpec((batch, size, cols), lambda i, scalars, _: (scalars[which] // batch + i, 0, 0)),
                pl.BlockSpec((batch, size, cols), lambda i, *_: (i, 0, 0)),
                pl.BlockSpec((batch, size, size), lambda i, *_: (i, 0, 0)),
                pl.BlockSpec((batch, slots, size, size), lambda i, *_: (i, 0, 0, 0)),
                pl.BlockSpec(start.shape, whole),
            ],
            out_specs=[pl.BlockSpec(memory_space=pl.ANY)] + [pl.BlockSpec(part.shape, whole) for part in sums],
            scratch_shapes=[
                pltpu.VMEM((count, size, 2 * cols), BF16),
                pltpu.VMEM((levels, size, 2 * cols), F32),
                pltpu.SemaphoreType.DMA((count,)),
            ],
        ),
        out_shape=[jax.ShapeDtypeStruct((count, size, 2 * cols), BF16)] + sums,
        compiler_params=pltpu.CompilerParams(vmem_limit_bytes=FORWARD_VMEM),
        cost_estimate=cost(0, 0),
        name="leaf_forward",
    )(scalars, ancestors, rhs, far, inv, panels, start)


def solve_leaves(base, step, batch, ancestors, value, inv, panels, paths):
    leaves = [step * batch + index for index in range(batch)]
    rests = []
    for leaf in leaves:
        update = None
        for slot in range(panels.shape[1]):
            level = ancestors[base + leaf, slot]
            picked = paths[jnp.maximum(level - 1, 0)]
            picked = jnp.where(level > 0, picked, jnp.zeros_like(picked))
            term = dot(panels[leaf, slot], picked)
            update = term if update is None else update + term
        rests.append((value[leaf].astype(F32) - update).astype(BF16))
    return [dot(inv[leaf], rest).astype(BF16) for leaf, rest in zip(leaves, rests)]


def send_kernel(base, ancestors, value, inv, panels, paths, result):
    count = result.shape[0]
    batch = min(BATCH, count)

    @pl.loop(0, count // batch)
    def _(step):
        solutions = solve_leaves(base, step, batch, ancestors, value, inv, panels, paths)
        for index, solution_block in enumerate(solutions):
            result[step * batch + index] = solution_block


def solve_far(ancestors, inv, panels, value, paths, base, count):
    size, cols = paths.shape[1:]

    def part(array):
        block = (count,) + array.shape[1:]
        return pl.BlockSpec(block, lambda i: (base // count,) + (0,) * (array.ndim - 1))

    return pl.pallas_call(
        functools.partial(send_kernel, base),
        grid=(1,),
        in_specs=[
            pl.BlockSpec(memory_space=pltpu.SMEM),
            pl.BlockSpec((count, size, cols), lambda i: (base // count, 0, 1)),
            part(inv),
            part(panels),
            pl.BlockSpec(paths.shape, lambda i: (0, 0, 0)),
        ],
        out_specs=pl.BlockSpec((count, size, cols), lambda i: (0, 0, 0)),
        out_shape=jax.ShapeDtypeStruct((count, size, cols), BF16),
        compiler_params=pltpu.CompilerParams(vmem_limit_bytes=LEAF_VMEM),
        cost_estimate=cost(0, 0),
        name="solve_far",
    )(ancestors, value, inv, panels, paths)


def keep_kernel(which, scalars, ancestors, value, inv, panels, paths, *refs):
    result, solved, sems = refs[-3:]
    step, steps = pl.program_id(0), pl.num_programs(0)
    batch = value.shape[0]

    def leaving(leaf):
        return pltpu.make_async_copy(solved.at[leaf], result.at[scalars[which] + leaf], sems.at[leaf])

    for index, solution_block in enumerate(solve_leaves(step * batch, 0, batch, ancestors, value, inv, panels, paths)):
        solved[step * batch + index] = solution_block
        leaving(step * batch + index).start()

    @pl.when(step == steps - 1)
    def _():
        for leaf in range(solved.shape[0]):
            leaving(leaf).wait()


def solve_own(scalars, which, ancestors, inv, panels, value, paths, rows, into=None):
    size, cols = paths.shape[1:]
    count, slots = panels.shape[:2]
    batch = min(BATCH, count)
    extra = [] if into is None else [into]
    hbm, smem = pl.BlockSpec(memory_space=pl.ANY), pl.BlockSpec(memory_space=pltpu.SMEM)
    return pl.pallas_call(
        functools.partial(keep_kernel, which),
        grid=(count // batch,),
        in_specs=[
            smem,
            smem,
            pl.BlockSpec((batch, size, cols), lambda i: (i, 0, 0)),
            pl.BlockSpec((batch, size, size), lambda i: (i, 0, 0)),
            pl.BlockSpec((batch, slots, size, size), lambda i: (i, 0, 0, 0)),
            pl.BlockSpec(paths.shape, lambda i: (0, 0, 0)),
        ]
        + [hbm] * len(extra),
        out_specs=hbm,
        out_shape=jax.ShapeDtypeStruct((rows, size, cols), BF16),
        scratch_shapes=[pltpu.VMEM((count, size, cols), BF16), pltpu.SemaphoreType.DMA((count,))],
        input_output_aliases={} if into is None else {6: 0},
        compiler_params=pltpu.CompilerParams(vmem_limit_bytes=LEAF_VMEM),
        cost_estimate=cost(0, 0),
        name="solve_own",
    )(scalars, ancestors, value, inv, panels, paths, *extra)


def place_kernel(scalars, part, whole, result):
    result[...] = part[...]


def place_rows(scalars, which, offset, part, whole):
    count, size, cols = part.shape
    return pl.pallas_call(
        place_kernel,
        grid_spec=pltpu.PrefetchScalarGridSpec(
            num_scalar_prefetch=1,
            grid=(1,),
            in_specs=[pl.BlockSpec(part.shape, lambda i, _: (0, 0, 0)), pl.BlockSpec(memory_space=pl.ANY)],
            out_specs=pl.BlockSpec(part.shape, lambda i, scalars: ((scalars[which] + offset) // count, 0, 0)),
        ),
        out_shape=jax.ShapeDtypeStruct(whole.shape, whole.dtype),
        input_output_aliases={2: 0},
        compiler_params=pltpu.CompilerParams(vmem_limit_bytes=LEAF_VMEM),
        cost_estimate=cost(0, 0),
        name="place_rows",
    )(scalars, part, whole)


def combine_kernel(lower_inv, lower_panels, upper_inv, upper_panels, blocks, *parts):
    made = [dot(upper_inv[0], lower_inv[0]).astype(BF16)]
    for slot in range(blocks.shape[0] // 2):
        made.append(dot(lower_panels[0, slot], lower_inv[0]).astype(BF16))
        made.append(dot(upper_inv[0], upper_panels[0, slot]).astype(BF16))
    for index, block in enumerate(made):
        blocks[index] = block
    for part in parts:
        for index in range(part.shape[0]):
            part[index] = made.pop(0)


def combine(lower_inv, lower_panels, upper_inv, upper_panels):
    size = lower_inv.shape[1]
    total = 1 + 2 * lower_panels.shape[1]
    counts = [total] + [min(PART, total - begin) for begin in range(0, total, PART)]
    blocks, *parts = pl.pallas_call(
        combine_kernel,
        out_shape=[jax.ShapeDtypeStruct((blocks, size, size), BF16) for blocks in counts],
        compiler_params=pltpu.CompilerParams(vmem_limit_bytes=TREE_VMEM),
        cost_estimate=cost(2**20, 2**20),
        name="combine",
    )(lower_inv, lower_panels, upper_inv, upper_panels)
    return blocks, parts


def sort_kernel(parts, flags, mine, *refs):
    theirs, factors, rest = refs[:parts], refs[parts], refs[parts + 1 :]

    @pl.when(flags[0] == 1)
    def _():
        factors[...] = mine[...]
        for onward in rest:
            begin = 0
            for part in theirs:
                for index in range(min(part.shape[0], onward.shape[0] - begin)):
                    onward[begin + index] = part[index]
                begin += part.shape[0]

    @pl.when(flags[0] == 0)
    def _():
        begin = 0
        for part in theirs:
            factors[begin : begin + part.shape[0]] = part[...]
            begin += part.shape[0]
        for onward in rest:
            onward[...] = mine[: onward.shape[0]]


def sort(bit, mine, theirs):
    memory = pl.BlockSpec(memory_space=pltpu.VMEM)
    shapes = [jax.ShapeDtypeStruct(mine.shape, BF16)]
    if mine.shape[0] > 1:
        shapes.append(jax.ShapeDtypeStruct((mine.shape[0] - 2,) + mine.shape[1:], BF16))
        shapes.append(jax.ShapeDtypeStruct((1,) + mine.shape[1:], BF16))
    return pl.pallas_call(
        functools.partial(sort_kernel, len(theirs)),
        in_specs=[pl.BlockSpec(memory_space=pltpu.SMEM), memory] + [memory] * len(theirs),
        out_specs=[memory] * len(shapes),
        out_shape=shapes,
        compiler_params=pltpu.CompilerParams(vmem_limit_bytes=TREE_VMEM),
        cost_estimate=cost(2**20, 2**20),
        name="sort",
    )(jnp.reshape(bit, (1,)).astype(jnp.int32), mine, *theirs)


def pick_kernel(flags, *refs):
    sources, chosen = refs[:-1], refs[-1]
    for index, source in enumerate(sources):

        @pl.when(flags[0] == index)
        def _(source=source):
            chosen[...] = source[...]


def pick(index, sources):
    shape = (1,) + sources[0].shape[1:]
    return pl.pallas_call(
        pick_kernel,
        grid=(1,),
        in_specs=[pl.BlockSpec(memory_space=pltpu.SMEM)] + [pl.BlockSpec(shape, lambda i: (0, 0, 0))] * len(sources),
        out_specs=pl.BlockSpec(shape, lambda i: (0, 0, 0)),
        out_shape=jax.ShapeDtypeStruct(shape, BF16),
        compiler_params=pltpu.CompilerParams(vmem_limit_bytes=TREE_VMEM),
        cost_estimate=cost(2**20, 2**20),
        name="pick",
    )(jnp.reshape(index, (1,)).astype(jnp.int32), *sources)


def from_owners(value, level, hop):
    owner = 2 ** (level - 1)
    pairs = [
        (group + owner + index, group + (owner + index ^ hop))
        for group in range(0, lax.axis_size("leaf"), 2**level)
        for index in range(2)
    ]
    return lax.ppermute(value, "leaf", pairs)


def after(value, *earlier):
    return lax.optimization_barrier((value, *earlier))[0]


def climb_kernel(mine, theirs, factors, part, passed):
    entered = (-(mine[0].astype(F32) + theirs[0].astype(F32))).astype(BF16)
    for above in range(passed.shape[0]):
        carried = mine[above + 1].astype(F32) + theirs[above + 1].astype(F32)
        passed[above] = (carried + dot(factors[1 + 2 * above], entered)).astype(BF16)
    part[...] = dot(factors[0], entered)


def climb(mine, theirs, factors):
    levels, size, cols = mine.shape
    return pl.pallas_call(
        climb_kernel,
        out_shape=[
            jax.ShapeDtypeStruct((size, cols), F32),
            jax.ShapeDtypeStruct((levels - 1, size, cols), BF16),
        ],
        compiler_params=pltpu.CompilerParams(vmem_limit_bytes=TREE_VMEM),
        cost_estimate=cost(2**20, 2**20),
        name="climb",
    )(mine, theirs, factors)


def descend_kernel(levels, mine, theirs, *refs):
    factors, parts, paths = refs[:levels], refs[levels : 2 * levels - 1], refs[-1]
    entered = (-(mine[0].astype(F32) + theirs[0].astype(F32))).astype(BF16)
    paths[levels - 1] = dot(factors[levels - 1][0], entered).astype(BF16)
    for level in range(levels - 2, -1, -1):
        rest = parts[level][...]
        for above in reversed(range(levels - 1 - level)):
            rest = rest - dot(factors[level][2 + 2 * above], paths[level + 1 + above])
        paths[level] = rest.astype(BF16)


def descend(mine, theirs, factors, parts):
    levels = len(factors)
    _, size, cols = mine.shape
    return pl.pallas_call(
        functools.partial(descend_kernel, levels),
        out_shape=jax.ShapeDtypeStruct((levels, size, cols), BF16),
        compiler_params=pltpu.CompilerParams(vmem_limit_bytes=TREE_VMEM),
        cost_estimate=cost(2**20, 2**20),
        name="descend",
    )(mine, theirs, *factors, *parts)


def on_device(
    leaf_rhs,
    leaf_lower_inv,
    leaf_lower_panels,
    leaf_upper_inv,
    leaf_upper_panels,
    ancestors,
    sep_rhs,
    sep_lower_inv,
    sep_lower_panels,
    sep_upper_inv,
    sep_upper_panels,
):
    levels = lax.axis_size("leaf").bit_length() - 1
    device = lax.axis_index("leaf")
    place = lax.axis_index("col")
    low, high = place % 2, place // 2
    count = leaf_lower_inv.shape[0]
    rows, size, cols = leaf_rhs.shape

    first = high * 2 * count + low * count
    second = high * 2 * count + (1 - low) * count
    owned = [device % 2**level == 2 ** (level - 1) for level in range(1, levels + 1)]
    own_level = sum(jnp.where(is_owner, level, 0) for level, is_owner in enumerate(owned, 1))

    away = (1 - high) * 2 * count
    scalars = jnp.stack([first, second, own_level, away + low * count, away + (1 - low) * count]).astype(jnp.int32)
    half = count // 2
    sent = lax.optimization_barrier(
        [lax.dynamic_slice_in_dim(leaf_rhs, away + part * count, count, 0) for part in (low, 1 - low)]
    )
    far_rhs = [swap(part, "col", 2) for part in sent]

    near_ancestors = swap(ancestors, "col", 1)
    near_lower_inv = swap(leaf_lower_inv, "col", 1)
    near_lower_panels = swap(leaf_lower_panels, "col", 1)
    local = (ancestors, leaf_lower_inv, leaf_lower_panels)
    near = (near_ancestors, near_lower_inv, near_lower_panels)

    blocks, pieces = combine(after(sep_lower_inv, *sent), sep_lower_panels, sep_upper_inv, sep_upper_panels)

    start = after(sep_rhs, *near)
    value_1, total = forward(levels, scalars, 0, *local, leaf_rhs, far_rhs[0], start, True, False)
    arrived = [swap(piece, "leaf", 1) for piece in pieces]
    found, *onward = sort(device % 2, blocks, after(arrived, total))
    factors = [found]
    total = after(total, found)
    value_2, own_total, far_total = forward(levels, scalars, 1, *near, leaf_rhs, far_rhs[1], total, False, True)

    if levels == 3:
        from_top = [from_owners(onward[1], levels, hop) for hop in (4, 6)]
        far_total = after(far_total, *from_top)
    mine = (own_total + swap(far_total, "col", 2).astype(F32)).astype(BF16)
    parts = []
    for level in range(1, levels + 1):
        theirs = swap(mine, "leaf", 2 ** (level - 1))
        if onward:
            arrived = swap(onward[0], "leaf", 2**level)
            before = onward[0]
            found, *onward = sort(device // 2**level % 2, before, [arrived])
            factors.append(found)
            theirs = after(theirs, found)
            top = None
            if levels == 3:
                top = pick(device // 2 % 4, [*from_top, before, arrived])
                factors.append(top)
                onward = []
        elif level == 2:
            theirs = after(theirs, top)
        if level < levels:
            part, mine = climb(mine, theirs, factors[level - 1])
            parts.append(part)
        if level == 1:
            near_upper_inv = swap(after(leaf_upper_inv, mine), "col", 1)
            near_upper_panels = swap(after(leaf_upper_panels, mine), "col", 1)
    paths = descend(mine, theirs, factors, parts)
    far_paths = swap(paths, "col", 2)

    own_solution = jnp.zeros((size, cols), BF16)
    for level in range(levels):
        own_solution = jnp.where(owned[level], paths[level], own_solution)

    local = (ancestors, leaf_upper_inv, leaf_upper_panels)
    near = (near_ancestors, near_upper_inv, near_upper_panels)
    leaf_solution = solve_own(scalars, 0, *local, value_1, paths, rows)
    far_paths = after(far_paths, leaf_solution)
    returning = [
        (3, 0, solve_far(*local, value_1, far_paths, 0, count)),
        (4, 0, solve_far(*near, value_2, far_paths, 0, half)),
        (4, half, solve_far(*near, value_2, far_paths, half, half)),
    ]
    leaf_solution = solve_own(scalars, 1, *near, value_2, paths, rows, leaf_solution)
    for which, offset, part in returning:
        leaf_solution = place_rows(scalars, which, offset, swap(part, "col", 2), leaf_solution)
    return (leaf_solution, own_solution[None])


def solution(mesh):
    placed = (
        P("leaf", None, "col"),
        P(("leaf", "col"), None, None),
        P(("leaf", "col"), None, None, None),
        P(("leaf", "col"), None, None),
        P(("leaf", "col"), None, None, None),
        P(("leaf", "col"), None),
        P("leaf", None, "col"),
        P("leaf", None, None),
        P("leaf", None, None, None),
        P("leaf", None, None),
        P("leaf", None, None, None),
    )
    return jax.shard_map(
        on_device,
        mesh=mesh,
        in_specs=placed,
        out_specs=(P("leaf", None, "col"), P("leaf", None, "col")),
        check_vma=False,
    )
```

time: 365 us -> 104 us (0.28)
  local copies, waits for them, and re-layouts: 159 us -> 14.1 us
  waiting for transfers between devices: 128 us -> 31.3 us
  matrix products: 34.5 us -> 0 us
  Pallas kernels: 0 us -> 32.7 us
  between operations: 14.3 us -> 0.93 us
  blocking collectives: 7.65 us -> 0 us
    unnamed x27 -> x59, local copies, waits for them, and re-layouts: 116 us -> 11.3 us
    all_to_all x2 -> x0, waiting for transfers between devices: 51.3 us -> none  [the longest x1 26.3 us: on_device(): lax.all_to_all(leaf_rhs, 'col', split_axis=0, concat_axis=2, tiled=True)]
    dot_general x13 -> x0, matrix products: 34.5 us -> none  [the longest x1 9.66 us: on_device(): jnp.einsum('kbc,kcr->kbr', leaf_upper_inv, leaf_rest, preferred_element_t...]
    pallas_call x0 -> x17, Pallas kernels: none -> 32.7 us  [the longest x2 12.6 us: forward(): pl.pallas_call(functools.partial(forward_kernel, first, last), grid_spec=...]
    unnamed x2 -> x0, waiting for transfers between devices: 29.5 us -> none
    ppermute x12 -> x20, waiting for transfers between devices: 46.9 us -> 31.3 us  [the longest x18 31.3 us: swap(): return lax.ppermute(value, axis, pairs)]
    all_to_all x3 -> x0, local copies, waits for them, and re-layouts: 13.2 us -> none  [the longest x2 8.65 us: on_device(): lax.all_to_all(leaf_rhs, 'col', split_axis=0, concat_axis=2, tiled=True)]
    dot_general x1 -> x0, local copies, waits for them, and re-layouts: 12.9 us -> none  [on_device(): jnp.einsum('kabc,kcr->kabr', leaf_lower_panels, leaf_value, preferred_ele...]
  transfers between devices with their start and end apart: 15 -> 20, of which waited for: 14 -> 11; matrix products, arithmetic and copies ran while one was open for 7% -> 4% of each run, Pallas kernels for 0% -> 30%
where the time goes in v2:
time: 104 us; the launch traced here: 103 us
  Pallas kernels  32.7 us (31%)
  waiting for transfers between devices  31.3 us (30%)
  starting transfers between devices  22.4 us (22%)
  local copies, waits for them, and re-layouts  14.1 us (14%)
  other arithmetic  1.69 us (2%)
    ppermute x18, waiting for transfers between devices, swap(): return lax.ppermute(value, axis, pairs)  31.3 us
    ppermute x18, starting transfers between devices, swap(): return lax.ppermute(value, axis, pairs)  20.4 us
    pallas_call x2, Pallas kernels, forward(): pl.pallas_call(functools.partial(forward_kernel, first, last), grid_spec=...  12.6 us
    unnamed x59, local copies, waits for them, and re-layouts  11.3 us
    pallas_call x2, Pallas kernels, solve_own(): pl.pallas_call(functools.partial(keep_kernel, which), grid=(count // batc...  6.3 us
    pallas_call x3, Pallas kernels, solve_far(): pl.pallas_call(functools.partial(send_kernel, base), grid=(1,), in_specs=...  5.9 us
    pallas_call x3, Pallas kernels, place_rows(): pl.pallas_call(place_kernel, grid_spec=pltpu.PrefetchScalarGridSpec(num_s...  3.88 us
    pallas_call x2, Pallas kernels, climb(): pl.pallas_call(climb_kernel, out_shape=[jax.ShapeDtypeStruct((size, cols)...  2.13 us
  transfers between devices with their start and end apart: 20, of which 11 were waited for; matrix products, arithmetic and copies ran while one was open for 4% of the time, Pallas kernels for 30%

profile of v2, /device:TPU:0, one launch (start us, length us, event | category | flops | bytes accessed | tf_op | source)
XLA Modules:
  0.0 103.1 jit_solution(9515925887737123622)
XLA Ops:
  1.3 2.1 %constant_dynamic-slice_fusion = (bf16[8,256,128]{2,1,0:T(8,128)(2,1)S(1)}, bf16[8,256,128]{2,1,0:T(8,128)(2,1)}) fusion(bf16[32,256,128]{2,1,0:T(8,128)(2,1)} %rhs.3, s32[]{:T(128)S(6)} %select_n.85, s32[]{:T(128)S(6)} %select_n.84), kind=kLoop, calls=%fused_computation.4 | loop fusion | bytes 2097160 | tf_op jit(solution)/shard_map/dynamic_slice | solution.py:414
  3.4 2.9 %collective-permute-start.4 = (bf16[8,256,128]{2,1,0:T(8,128)(2,1)}, bf16[8,256,128]{2,1,0:T(8,128)(2,1)}, u32[]{:S(2)}, u32[]{:S(2)}) collective-permute-start(bf16[8,256,128]{2,1,0:T(8,128)(2,1)} %get-tuple-element.32), channel_id=1, source_target_pairs={{0,2},{1,3},{2,0},{3,1},{4,6},{5,7},{6,4},{7,5},{8,10},{9,11},{10,... | collective-permute-start | bytes 1572872 | tf_op jit(solution)/shard_map/ppermute | solution.py:21
  6.7 1.6 %collective-permute-start.5 = (bf16[3,256,256]{2,1,0:T(8,128)(2,1)S(1)}, bf16[3,256,256]{2,1,0:T(8,128)(2,1)S(1)}, u32[]{:S(2)}, u32[]{:S(2)}) collective-permute-start(bf16[3,256,256]{2,1,0:T(8,128)(2,1)S(1)} %get-tuple-element.37), channel_id=1, source_target_pairs={{0,4},{4,0},{8,12},{12,8},{16,20},{20,16},{24,28},{28,24},{1,5},{5... | collective-permute-start | bytes 1179656 | tf_op jit(solution)/shard_map/ppermute | solution.py:21
  8.3 1.2 %collective-permute-done.ancestors = s32[8,3]{1,0:T(8,128)S(1)} collective-permute-done((s32[8,3]{1,0:T(8,128)S(1)}, s32[8,3]{1,0:T(8,128)S(1)}, u32[]{:S(2)}, u32[]{:S(2)}) %collective-permute-start) | collective-permute-done | bytes 128 | tf_op jit(solution)/shard_map/ppermute | solution.py:21
  9.5 1.4 %collective-permute-start.1 = (bf16[8,256,128]{2,1,0:T(8,128)(2,1)S(1)}, bf16[8,256,128]{2,1,0:T(8,128)(2,1)S(1)}, u32[]{:S(2)}, u32[]{:S(2)}) collective-permute-start(bf16[8,256,128]{2,1,0:T(8,128)(2,1)S(1)} %get-tuple-element.31), channel_id=1, source_target_pairs={{0,2},{1,3},{2,0},{3,1},{4,6},{5,7},{6,4},{7,5},{8,10},{9,11},{10,... | collective-permute-start | bytes 1572872 | tf_op jit(solution)/shard_map/ppermute | solution.py:21
  11.2 0.7 stack.23.scalars
  11.9 7.5 %collective-permute-done.4.far = bf16[8,256,128]{2,1,0:T(8,128)(2,1)} collective-permute-done((bf16[8,256,128]{2,1,0:T(8,128)(2,1)}, bf16[8,256,128]{2,1,0:T(8,128)(2,1)}, u32[]{:S(2)}, u32[]{:S(2)}) %collective-permute-start.4) | collective-permute-done | bytes 524320 | tf_op jit(solution)/shard_map/ppermute | solution.py:21
  19.3 6.2 %leaf_forward.2 = (bf16[8,256,256]{2,1,0:T(8,128)(2,1)}, f32[3,256,256]{2,1,0:T(8,128)}) custom-call(s32[5]{0:T(128)} %stack.23.scalars, s32[8,3]{1,0:T(8,128)} %copy-done.24, bf16[32,256,128]{2,1,0:T(8,128)(2,1)} %rhs.3, bf16[8,256,128]{2,1,0:T(8,128)(2,1)} %collective-permute-done.4.far, bf16[8,256,256]{2,1,0:T(8,128)(2,1)} %inv.3, ...), custom_call_target="tpu_custom_call" | custom-call | tf_op jit(solution)/shard_map/leaf_forward/pallas_call | solution.py:92
  25.7 0.7 collective-permute-start.8
  26.3 1.3 %collective-permute-start.7 = (bf16[1,256,256]{2,1,0:T(8,128)(2,1)S(1)}, bf16[1,256,256]{2,1,0:T(8,128)(2,1)S(1)}, u32[]{:S(2)}, u32[]{:S(2)}) collective-permute-start(bf16[1,256,256]{2,1,0:T(8,128)(2,1)S(1)} %get-tuple-element.46), channel_id=1, source_target_pairs={{16,0},{20,4},{17,1},{21,5},{18,2},{22,6},{19,3},{23,7}} | collective-permute-start | bytes 393224 | tf_op jit(solution)/shard_map/ppermute | solution.py:333
  27.6 2.3 %collective-permute-done.1.far = bf16[8,256,128]{2,1,0:T(8,128)(2,1)S(1)} collective-permute-done((bf16[8,256,128]{2,1,0:T(8,128)(2,1)S(1)}, bf16[8,256,128]{2,1,0:T(8,128)(2,1)S(1)}, u32[]{:S(2)}, u32[]{:S(2)}) %collective-permute-start.1) | collective-permute-done | bytes 524320 | tf_op jit(solution)/shard_map/ppermute | solution.py:21
  29.9 0.8 copy-done.27
  30.7 6.4 %leaf_forward.3 = (bf16[8,256,256]{2,1,0:T(8,128)(2,1)}, f32[3,256,128]{2,1,0:T(8,128)}, bf16[3,256,128]{2,1,0:T(8,128)(2,1)}) custom-call(s32[5]{0:T(128)} %stack.23.scalars, s32[8,3]{1,0:T(8,128)} %copy-done.22, bf16[32,256,128]{2,1,0:T(8,128)(2,1)} %rhs.3, bf16[8,256,128]{2,1,0:T(8,128)(2,1)} %copy-done.27, ...), custom_call_target="tpu_custom_call" | custom-call | tf_op jit(solution)/shard_map/leaf_forward/pallas_call | solution.py:92
  37.2 0.7 copy-done.14
  38.5 1.8 %collective-permute-start.9 = (bf16[3,256,128]{2,1,0:T(8,128)(2,1)}, bf16[3,256,128]{2,1,0:T(8,128)(2,1)S(1)}, u32[]{:S(2)}, u32[]{:S(2)}) collective-permute-start(bf16[3,256,128]{2,1,0:T(8,128)(2,1)} %get-tuple-element.47), channel_id=1, source_target_pairs={{0,2},{1,3},{2,0},{3,1},{4,6},{5,7},{6,4},{7,5},{8,10},{9,11},{10,... | collective-permute-start | bytes 589832 | tf_op jit(solution)/shard_map/ppermute | solution.py:21
  40.3 1.6 %collective-permute-start.11 = (bf16[3,256,256]{2,1,0:T(8,128)(2,1)S(1)}, bf16[3,256,256]{2,1,0:T(8,128)(2,1)S(1)}, u32[]{:S(2)}, u32[]{:S(2)}) collective-permute-start(bf16[3,256,256]{2,1,0:T(8,128)(2,1)S(1)} %get-tuple-element.48.mine.refs_2_), channel_id=1, source_target_pairs={{0,8},{4,12},{8,0},{12,4},{16,24},{20,28},{24,16},{28,20},{1,9},{5... | collective-permute-start | bytes 1179656 | tf_op jit(solution)/shard_map/ppermute | solution.py:21
  41.8 3.3 %collective-permute-done.9 = bf16[3,256,128]{2,1,0:T(8,128)(2,1)S(1)} collective-permute-done((bf16[3,256,128]{2,1,0:T(8,128)(2,1)}, bf16[3,256,128]{2,1,0:T(8,128)(2,1)S(1)}, u32[]{:S(2)}, u32[]{:S(2)}) %collective-permute-start.9) | collective-permute-done | bytes 196640 | tf_op jit(solution)/shard_map/ppermute | solution.py:21
  45.1 1.0 %add_convert_fusion.mine = bf16[3,256,128]{2,1,0:T(8,128)(2,1)S(1)} fusion(f32[3,256,128]{2,1,0:T(8,128)} %get-tuple-element.44, bf16[3,256,128]{2,1,0:T(8,128)(2,1)S(1)} %collective-permute-done.9), kind=kLoop, calls=%fused_computation | loop fusion | flops 294912 | bytes 786432 | tf_op jit(solution)/shard_map/convert_element_type | solution.py:437
  46.1 1.5 %collective-permute-start.10 = (bf16[3,256,128]{2,1,0:T(8,128)(2,1)S(1)}, bf16[3,256,128]{2,1,0:T(8,128)(2,1)S(1)}, u32[]{:S(2)}, u32[]{:S(2)}) collective-permute-start(bf16[3,256,128]{2,1,0:T(8,128)(2,1)S(1)} %add_convert_fusion.mine), channel_id=1, source_target_pairs={{0,4},{4,0},{8,12},{12,8},{16,20},{20,16},{24,28},{28,24},{1,5},{5... | collective-permute-start | bytes 589832 | tf_op jit(solution)/shard_map/ppermute | solution.py:21
  47.6 2.6 %collective-permute-done.11.refs_0_.refs_3_ = bf16[3,256,256]{2,1,0:T(8,128)(2,1)S(1)} collective-permute-done((bf16[3,256,256]{2,1,0:T(8,128)(2,1)S(1)}, bf16[3,256,256]{2,1,0:T(8,128)(2,1)S(1)}, u32[]{:S(2)}, u32[]{:S(2)}) %collective-permute-start.11) | collective-permute-done | bytes 393248 | tf_op jit(solution)/shard_map/ppermute | solution.py:21
  50.2 0.9 sort.3
  51.1 0.8 collective-permute-done.10.theirs
  51.9 0.9 climb.2
  54.0 1.5 %collective-permute-start.14 = (bf16[2,256,128]{2,1,0:T(8,128)(2,1)}, bf16[2,256,128]{2,1,0:T(8,128)(2,1)}, u32[]{:S(2)}, u32[]{:S(2)}) collective-permute-start(bf16[2,256,128]{2,1,0:T(8,128)(2,1)} %get-tuple-element.51.mine), channel_id=1, source_target_pairs={{0,8},{4,12},{8,0},{12,4},{16,24},{20,28},{24,16},{28,20},{1,9},{5... | collective-permute-start | bytes 393224 | tf_op jit(solution)/shard_map/ppermute | solution.py:21
  55.5 1.1 %copy-done.9 = bf16[3,256,256]{2,1,0:T(8,128)(2,1)S(1)} copy-done((bf16[3,256,256]{2,1,0:T(8,128)(2,1)S(1)}, bf16[3,256,256]{2,1,0:T(8,128)(2,1)}, u32[]{:S(2)}) %copy-start.9) | copy-done | bytes 393240
  56.6 1.0 copy-done.11
  57.6 0.9 copy-done.15
  58.5 0.9 copy-done.17
  59.7 1.2 %climb.3 = (f32[256,128]{1,0:T(8,128)S(1)}, bf16[1,256,128]{2,1,0:T(8,128)(2,1)S(1)}) custom-call(bf16[2,256,128]{2,1,0:T(8,128)(2,1)} %get-tuple-element.51.mine, bf16[2,256,128]{2,1,0:T(8,128)(2,1)} %collective-permute-done.14.theirs, bf16[3,256,256]{2,1,0:T(8,128)(2,1)S(1)} %get-tuple-element.49.factors.refs_1_), custom_call_target="tpu_custom_call" | custom-call | flops 1048576 | bytes 1048576 | tf_op jit(solution)/shard_map/climb/pallas_call | solution.py:350
  60.9 2.6 %collective-permute-start.15 = (bf16[1,256,128]{2,1,0:T(8,128)(2,1)S(1)}, bf16[1,256,128]{2,1,0:T(8,128)(2,1)S(1)}, u32[]{:S(2)}, u32[]{:S(2)}) collective-permute-start(bf16[1,256,128]{2,1,0:T(8,128)(2,1)S(1)} %get-tuple-element.55.mine), channel_id=1, source_target_pairs={{0,16},{4,20},{8,24},{12,28},{16,0},{20,4},{24,8},{28,12},{1,17},{... | collective-permute-start | bytes 196616 | tf_op jit(solution)/shard_map/ppermute | solution.py:21
  63.5 2.7 %collective-permute-done.15.theirs = bf16[1,256,128]{2,1,0:T(8,128)(2,1)S(1)} collective-permute-done((bf16[1,256,128]{2,1,0:T(8,128)(2,1)S(1)}, bf16[1,256,128]{2,1,0:T(8,128)(2,1)S(1)}, u32[]{:S(2)}, u32[]{:S(2)}) %collective-permute-start.15) | collective-permute-done | bytes 65568 | tf_op jit(solution)/shard_map/ppermute | solution.py:21
  66.1 1.1 %copy-done.7 = bf16[5,256,256]{2,1,0:T(8,128)(2,1)S(1)} copy-done((bf16[5,256,256]{2,1,0:T(8,128)(2,1)S(1)}, bf16[5,256,256]{2,1,0:T(8,128)(2,1)}, u32[]{:S(2)}) %copy-start.7) | copy-done | bytes 655384
  67.2 0.9 copy-done.19
  68.7 1.5 %collective-permute-start.16 = (bf16[3,256,128]{2,1,0:T(8,128)(2,1)S(1)}, bf16[3,256,128]{2,1,0:T(8,128)(2,1)S(1)}, u32[]{:S(2)}, u32[]{:S(2)}) collective-permute-start(bf16[3,256,128]{2,1,0:T(8,128)(2,1)S(1)} %descend.1.paths), channel_id=1, source_target_pairs={{0,2},{1,3},{2,0},{3,1},{4,6},{5,7},{6,4},{7,5},{8,10},{9,11},{10,... | collective-permute-start | bytes 589832 | tf_op jit(solution)/shard_map/ppermute | solution.py:21
  70.3 1.2 %copy-done.2 = bf16[8,256,256]{2,1,0:T(8,128)(2,1)S(1)} copy-done((bf16[8,256,256]{2,1,0:T(8,128)(2,1)S(1)}, bf16[8,256,256]{2,1,0:T(8,128)(2,1)}, u32[]{:S(2)}) %copy-start.2) | copy-done | bytes 1048600
  71.5 1.2 %copy-done.4 = bf16[8,256,256]{2,1,0:T(8,128)(2,1)S(1)} copy-done((bf16[8,256,256]{2,1,0:T(8,128)(2,1)S(1)}, bf16[8,256,256]{2,1,0:T(8,128)(2,1)}, u32[]{:S(2)}) %copy-start.4) | copy-done | bytes 1048600
  72.7 2.9 %solve_own.2.refs_0_ = bf16[32,256,128]{2,1,0:T(8,128)(2,1)} custom-call(s32[5]{0:T(128)S(1)} %copy-done.26, s32[8,3]{1,0:T(8,128)S(1)} %copy-done.25, bf16[8,256,256]{2,1,0:T(8,128)(2,1)S(1)} %copy-done.4, bf16[8,256,256]{2,1,0:T(8,128)(2,1)S(1)} %copy-done.2, bf16[8,3,256,256]{3,2,1,0:T(8,128)(2,1)S(1)} %copy-done, bf16[3,256,128]{2,1,0:T(8,128)(2,1)S(1)} %descend.1.paths), custom_call_target="tpu_custom_call" | custom-call | tf_op jit(solution)/shard_map/solve_own/pallas_call | solution.py:193
  75.7 2.2 %solve_far.5 = bf16[8,256,128]{2,1,0:T(8,128)(2,1)S(1)} custom-call(s32[8,3]{1,0:T(8,128)S(1)} %copy-done.25, bf16[8,256,256]{2,1,0:T(8,128)(2,1)S(1)} %copy-done.5, bf16[8,256,256]{2,1,0:T(8,128)(2,1)S(1)} %copy-done.3, bf16[8,3,256,256]{3,2,1,0:T(8,128)(2,1)S(1)} %copy-done, bf16[3,256,128]{2,1,0:T(8,128)(2,1)S(1)} %collective-permute-done.16.paths), custom_call_target="tpu_custom_call" | custom-call | tf_op jit(solution)/shard_map/solve_far/pallas_call | solution.py:151
  78.5 1.9 %solve_far.4 = bf16[4,256,128]{2,1,0:T(8,128)(2,1)S(1)} custom-call(s32[8,3]{1,0:T(8,128)S(1)} %copy-done.23, bf16[8,256,256]{2,1,0:T(8,128)(2,1)S(1)} %copy-done.1, bf16[8,256,256]{2,1,0:T(8,128)(2,1)} %collective-permute-done.12.inv, bf16[8,3,256,256]{3,2,1,0:T(8,128)(2,1)S(1)} %collective-permute-done.13.panels, ...), custom_call_target="tpu_custom_call" | custom-call | tf_op jit(solution)/shard_map/solve_far/pallas_call | solution.py:151
  80.4 1.5 %collective-permute-start.18 = (bf16[4,256,128]{2,1,0:T(8,128)(2,1)S(1)}, bf16[4,256,128]{2,1,0:T(8,128)(2,1)S(1)}, u32[]{:S(2)}, u32[]{:S(2)}) collective-permute-start(bf16[4,256,128]{2,1,0:T(8,128)(2,1)S(1)} %solve_far.4), channel_id=1, source_target_pairs={{0,2},{1,3},{2,0},{3,1},{4,6},{5,7},{6,4},{7,5},{8,10},{9,11},{10,... | collective-permute-start | bytes 786440 | tf_op jit(solution)/shard_map/ppermute | solution.py:21
  81.9 1.9 %solve_far.3 = bf16[4,256,128]{2,1,0:T(8,128)(2,1)S(1)} custom-call(s32[8,3]{1,0:T(8,128)S(1)} %copy-done.23, bf16[8,256,256]{2,1,0:T(8,128)(2,1)S(1)} %copy-done.1, bf16[8,256,256]{2,1,0:T(8,128)(2,1)} %collective-permute-done.12.inv, bf16[8,3,256,256]{3,2,1,0:T(8,128)(2,1)S(1)} %collective-permute-done.13.panels, ...), custom_call_target="tpu_custom_call" | custom-call | tf_op jit(solution)/shard_map/solve_far/pallas_call | solution.py:151
  85.1 3.4 %solve_own.3.whole = bf16[32,256,128]{2,1,0:T(8,128)(2,1)} custom-call(s32[5]{0:T(128)S(1)} %copy-done.26, s32[8,3]{1,0:T(8,128)S(1)} %copy-done.23, bf16[8,256,256]{2,1,0:T(8,128)(2,1)S(1)} %copy-done.1, bf16[8,256,256]{2,1,0:T(8,128)(2,1)} %collective-permute-done.12.inv, ...), custom_call_target="tpu_custom_call", output_to_operand_aliasing={{}: (6, {})} | custom-call | tf_op jit(solution)/shard_map/solve_own/pallas_call | solution.py:193
  88.5 4.3 %collective-permute-done.19.part = bf16[8,256,128]{2,1,0:T(8,128)(2,1)S(1)} collective-permute-done((bf16[8,256,128]{2,1,0:T(8,128)(2,1)S(1)}, bf16[8,256,128]{2,1,0:T(8,128)(2,1)S(1)}, u32[]{:S(2)}, u32[]{:S(2)}) %collective-permute-start.19) | collective-permute-done | bytes 524320 | tf_op jit(solution)/shard_map/ppermute | solution.py:21
  92.8 1.4 %place_rows.3.whole = bf16[32,256,128]{2,1,0:T(8,128)(2,1)} custom-call(s32[5]{0:T(128)S(1)} %copy-done.26, bf16[8,256,128]{2,1,0:T(8,128)(2,1)S(1)} %collective-permute-done.19.part, bf16[32,256,128]{2,1,0:T(8,128)(2,1)} %solve_own.3.whole), custom_call_target="tpu_custom_call", output_to_operand_aliasing={{}: (2, {})} | custom-call | tf_op jit(solution)/shard_map/place_rows/pallas_call | solution.py:221
  94.2 4.3 %collective-permute-done.18.part = bf16[4,256,128]{2,1,0:T(8,128)(2,1)S(1)} collective-permute-done((bf16[4,256,128]{2,1,0:T(8,128)(2,1)S(1)}, bf16[4,256,128]{2,1,0:T(8,128)(2,1)S(1)}, u32[]{:S(2)}, u32[]{:S(2)}) %collective-permute-start.18) | collective-permute-done | bytes 262176 | tf_op jit(solution)/shard_map/ppermute | solution.py:21
  98.4 1.3 %place_rows.4.whole = bf16[32,256,128]{2,1,0:T(8,128)(2,1)} custom-call(s32[5]{0:T(128)S(1)} %copy-done.26, bf16[4,256,128]{2,1,0:T(8,128)(2,1)S(1)} %collective-permute-done.18.part, bf16[32,256,128]{2,1,0:T(8,128)(2,1)} %place_rows.3.whole), custom_call_target="tpu_custom_call", output_to_operand_aliasing={{}: (2, {})} | custom-call | tf_op jit(solution)/shard_map/place_rows/pallas_call | solution.py:221
  99.7 2.2 %collective-permute-done.17.part = bf16[4,256,128]{2,1,0:T(8,128)(2,1)S(1)} collective-permute-done((bf16[4,256,128]{2,1,0:T(8,128)(2,1)S(1)}, bf16[4,256,128]{2,1,0:T(8,128)(2,1)S(1)}, u32[]{:S(2)}, u32[]{:S(2)}) %collective-permute-start.17) | collective-permute-done | bytes 262176 | tf_op jit(solution)/shard_map/ppermute | solution.py:21
  101.8 1.3 %place_rows.5 = bf16[32,256,128]{2,1,0:T(8,128)(2,1)} custom-call(s32[5]{0:T(128)S(1)} %copy-done.26, bf16[4,256,128]{2,1,0:T(8,128)(2,1)S(1)} %collective-permute-done.17.part, bf16[32,256,128]{2,1,0:T(8,128)(2,1)} %place_rows.4.whole), custom_call_target="tpu_custom_call", output_to_operand_aliasing={{}: (2, {})} | custom-call | tf_op jit(solution)/shard_map/place_rows/pallas_call | solution.py:221
  (72 shorter events, 6.2 us)
Async XLA Ops:
  0.6 5.7 %copy-start.20 = (bf16[1,256,256]{2,1,0:T(8,128)(2,1)S(1)}, bf16[1,256,256]{2,1,0:T(8,128)(2,1)}, u32[]{:S(2)}) copy-start(bf16[1,256,256]{2,1,0:T(8,128)(2,1)} %lower_inv) | copy-start | bytes 393220
  0.6 5.7 %copy-start.13 = (bf16[1,2,256,256]{3,2,1,0:T(8,128)(2,1)S(1)}, bf16[1,2,256,256]{3,2,1,0:T(8,128)(2,1)}, u32[]{:S(2)}) copy-start(bf16[1,2,256,256]{3,2,1,0:T(8,128)(2,1)} %upper_panels.1) | copy-start | bytes 786436
  0.7 5.7 %copy-start.21 = (bf16[1,256,256]{2,1,0:T(8,128)(2,1)S(1)}, bf16[1,256,256]{2,1,0:T(8,128)(2,1)}, u32[]{:S(2)}) copy-start(bf16[1,256,256]{2,1,0:T(8,128)(2,1)} %upper_inv.1) | copy-start | bytes 393220
  0.7 5.7 %copy-start.12 = (bf16[1,2,256,256]{3,2,1,0:T(8,128)(2,1)S(1)}, bf16[1,2,256,256]{3,2,1,0:T(8,128)(2,1)}, u32[]{:S(2)}) copy-start(bf16[1,2,256,256]{3,2,1,0:T(8,128)(2,1)} %lower_panels.1) | copy-start | bytes 786436
  0.7 7.6 %copy-start.28 = (s32[8,3]{0,1:T(4,128)S(1)}, s32[8,3]{0,1:T(4,128)}, u32[]{:S(2)}) copy-start(s32[8,3]{0,1:T(4,128)} %param.16) | copy-start | bytes 292
  0.7 11.2 %collective-permute-start.3 = (bf16[8,3,256,256]{3,2,1,0:T(8,128)(2,1)}, bf16[8,3,256,256]{3,2,1,0:T(8,128)(2,1)}, u32[]{:S(2)}, u32[]{:S(2)}) collective-permute-start(bf16[8,3,256,256]{3,2,1,0:T(8,128)(2,1)} %panels.3), channel_id=1, source_target_pairs={{0,1},{1,0},{2,3},{3,2},{4,5},{5,4},{6,7},{7,6},{8,9},{9,8},{10,11... | collective-permute-start | bytes 9437192 | tf_op jit(solution)/shard_map/ppermute | solution.py:21
  1.2 9.7 %collective-permute-start.2 = (bf16[8,256,256]{2,1,0:T(8,128)(2,1)}, bf16[8,256,256]{2,1,0:T(8,128)(2,1)}, u32[]{:S(2)}, u32[]{:S(2)}) collective-permute-start(bf16[8,256,256]{2,1,0:T(8,128)(2,1)} %inv.3), channel_id=1, source_target_pairs={{0,1},{1,0},{2,3},{3,2},{4,5},{5,4},{6,7},{7,6},{8,9},{9,8},{10,11... | collective-permute-start | bytes 3145736 | tf_op jit(solution)/shard_map/ppermute | solution.py:21
  3.4 16.0 %collective-permute-start.4 = (bf16[8,256,128]{2,1,0:T(8,128)(2,1)}, bf16[8,256,128]{2,1,0:T(8,128)(2,1)}, u32[]{:S(2)}, u32[]{:S(2)}) collective-permute-start(bf16[8,256,128]{2,1,0:T(8,128)(2,1)} %get-tuple-element.32), channel_id=1, source_target_pairs={{0,2},{1,3},{2,0},{3,1},{4,6},{5,7},{6,4},{7,5},{8,10},{9,11},{10,... | collective-permute-start | bytes 1572872 | tf_op jit(solution)/shard_map/ppermute | solution.py:21
  6.7 18.9 %collective-permute-start.5 = (bf16[3,256,256]{2,1,0:T(8,128)(2,1)S(1)}, bf16[3,256,256]{2,1,0:T(8,128)(2,1)S(1)}, u32[]{:S(2)}, u32[]{:S(2)}) collective-permute-start(bf16[3,256,256]{2,1,0:T(8,128)(2,1)S(1)} %get-tuple-element.37), channel_id=1, source_target_pairs={{0,4},{4,0},{8,12},{12,8},{16,20},{20,16},{24,28},{28,24},{1,5},{5... | collective-permute-start | bytes 1179656 | tf_op jit(solution)/shard_map/ppermute | solution.py:21
  8.3 11.0 %copy-start.24 = (s32[8,3]{1,0:T(8,128)}, s32[8,3]{1,0:T(8,128)S(1)}, u32[]{:S(2)}) copy-start(s32[8,3]{1,0:T(8,128)S(1)} %copy.17.ancestors) | copy-start | bytes 292
  8.3 1.2 %collective-permute-start = (s32[8,3]{1,0:T(8,128)S(1)}, s32[8,3]{1,0:T(8,128)S(1)}, u32[]{:S(2)}, u32[]{:S(2)}) collective-permute-start(s32[8,3]{1,0:T(8,128)S(1)} %copy.17.ancestors), channel_id=1, source_target_pairs={{0,1},{1,0},{2,3},{3,2},{4,5},{5,4},{6,7},{7,6},{8,9},{9,8},{10,11... | collective-permute-start | bytes 296 | tf_op jit(solution)/shard_map/ppermute | solution.py:21
  9.5 16.0 %copy-start.22 = (s32[8,3]{1,0:T(8,128)}, s32[8,3]{1,0:T(8,128)S(1)}, u32[]{:S(2)}) copy-start(s32[8,3]{1,0:T(8,128)S(1)} %collective-permute-done.ancestors) | copy-start | bytes 292
  9.5 20.4 %collective-permute-start.1 = (bf16[8,256,128]{2,1,0:T(8,128)(2,1)S(1)}, bf16[8,256,128]{2,1,0:T(8,128)(2,1)S(1)}, u32[]{:S(2)}, u32[]{:S(2)}) collective-permute-start(bf16[8,256,128]{2,1,0:T(8,128)(2,1)S(1)} %get-tuple-element.31), channel_id=1, source_target_pairs={{0,2},{1,3},{2,0},{3,1},{4,6},{5,7},{6,4},{7,5},{8,10},{9,11},{10,... | collective-permute-start | bytes 1572872 | tf_op jit(solution)/shard_map/ppermute | solution.py:21
  10.9 14.6 %collective-permute-start.6 = (bf16[2,256,256]{2,1,0:T(8,128)(2,1)S(1)}, bf16[2,256,256]{2,1,0:T(8,128)(2,1)S(1)}, u32[]{:S(2)}, u32[]{:S(2)}) collective-permute-start(bf16[2,256,256]{2,1,0:T(8,128)(2,1)S(1)} %get-tuple-element.38), channel_id=1, source_target_pairs={{0,4},{4,0},{8,12},{12,8},{16,20},{20,16},{24,28},{28,24},{1,5},{5... | collective-permute-start | bytes 786440 | tf_op jit(solution)/shard_map/ppermute | solution.py:21
  25.6 24.6 %copy-start.8 = (bf16[3,256,256]{2,1,0:T(8,128)(2,1)}, bf16[3,256,256]{2,1,0:T(8,128)(2,1)S(1)}, u32[]{:S(2)}) copy-start(bf16[3,256,256]{2,1,0:T(8,128)(2,1)S(1)} %get-tuple-element.48.mine.refs_2_) | copy-start | bytes 1179652
  25.6 26.2 %copy-start.6 = (bf16[5,256,256]{2,1,0:T(8,128)(2,1)}, bf16[5,256,256]{2,1,0:T(8,128)(2,1)S(1)}, u32[]{:S(2)}) copy-start(bf16[5,256,256]{2,1,0:T(8,128)(2,1)S(1)} %get-tuple-element.41.factors.refs_0_) | copy-start | bytes 1966084
  25.7 11.5 %collective-permute-start.8 = (bf16[1,256,256]{2,1,0:T(8,128)(2,1)S(1)}, bf16[1,256,256]{2,1,0:T(8,128)(2,1)S(1)}, u32[]{:S(2)}, u32[]{:S(2)}) collective-permute-start(bf16[1,256,256]{2,1,0:T(8,128)(2,1)S(1)} %get-tuple-element.46), channel_id=1, source_target_pairs={{16,8},{20,12},{17,9},{21,13},{18,10},{22,14},{19,11},{23,15}} | collective-permute-start | bytes 393224 | tf_op jit(solution)/shard_map/ppermute | solution.py:333
  26.3 11.5 %collective-permute-start.7 = (bf16[1,256,256]{2,1,0:T(8,128)(2,1)S(1)}, bf16[1,256,256]{2,1,0:T(8,128)(2,1)S(1)}, u32[]{:S(2)}, u32[]{:S(2)}) collective-permute-start(bf16[1,256,256]{2,1,0:T(8,128)(2,1)S(1)} %get-tuple-element.46), channel_id=1, source_target_pairs={{16,0},{20,4},{17,1},{21,5},{18,2},{22,6},{19,3},{23,7}} | collective-permute-start | bytes 393224 | tf_op jit(solution)/shard_map/ppermute | solution.py:333
  29.9 0.8 copy-start.27
  37.2 0.7 copy-start.14
  38.5 6.6 %collective-permute-start.9 = (bf16[3,256,128]{2,1,0:T(8,128)(2,1)}, bf16[3,256,128]{2,1,0:T(8,128)(2,1)S(1)}, u32[]{:S(2)}, u32[]{:S(2)}) collective-permute-start(bf16[3,256,128]{2,1,0:T(8,128)(2,1)} %get-tuple-element.47), channel_id=1, source_target_pairs={{0,2},{1,3},{2,0},{3,1},{4,6},{5,7},{6,4},{7,5},{8,10},{9,11},{10,... | collective-permute-start | bytes 589832 | tf_op jit(solution)/shard_map/ppermute | solution.py:21
  40.3 10.0 %collective-permute-start.11 = (bf16[3,256,256]{2,1,0:T(8,128)(2,1)S(1)}, bf16[3,256,256]{2,1,0:T(8,128)(2,1)S(1)}, u32[]{:S(2)}, u32[]{:S(2)}) collective-permute-start(bf16[3,256,256]{2,1,0:T(8,128)(2,1)S(1)} %get-tuple-element.48.mine.refs_2_), channel_id=1, source_target_pairs={{0,8},{4,12},{8,0},{12,4},{16,24},{20,28},{24,16},{28,20},{1,9},{5... | collective-permute-start | bytes 1179656 | tf_op jit(solution)/shard_map/ppermute | solution.py:21
  46.1 5.7 %collective-permute-start.10 = (bf16[3,256,128]{2,1,0:T(8,128)(2,1)S(1)}, bf16[3,256,128]{2,1,0:T(8,128)(2,1)S(1)}, u32[]{:S(2)}, u32[]{:S(2)}) collective-permute-start(bf16[3,256,128]{2,1,0:T(8,128)(2,1)S(1)} %add_convert_fusion.mine), channel_id=1, source_target_pairs={{0,4},{4,0},{8,12},{12,8},{16,20},{20,16},{24,28},{28,24},{1,5},{5... | collective-permute-start | bytes 589832 | tf_op jit(solution)/shard_map/ppermute | solution.py:21
  50.2 2.6 %copy-start.10 = (bf16[3,256,256]{2,1,0:T(8,128)(2,1)}, bf16[3,256,256]{2,1,0:T(8,128)(2,1)S(1)}, u32[]{:S(2)}) copy-start(bf16[3,256,256]{2,1,0:T(8,128)(2,1)S(1)} %collective-permute-done.11.refs_0_.refs_3_) | copy-start | bytes 1179652
  51.9 18.4 %copy-start.25 = (s32[8,3]{1,0:T(8,128)S(1)}, s32[8,3]{1,0:T(8,128)}, u32[]{:S(2)}) copy-start(s32[8,3]{1,0:T(8,128)} %copy-done.24) | copy-start | bytes 292
  51.9 18.4 %copy-start.26 = (s32[5]{0:T(128)S(1)}, s32[5]{0:T(128)}, u32[]{:S(2)}) copy-start(s32[5]{0:T(128)} %stack.23.scalars) | copy-start | bytes 64
  52.8 0.7 copy-start.18
  53.5 25.0 %collective-permute-start.13 = (bf16[8,3,256,256]{3,2,1,0:T(8,128)(2,1)}, bf16[8,3,256,256]{3,2,1,0:T(8,128)(2,1)S(1)}, u32[]{:S(2)}, u32[]{:S(2)}) collective-permute-start(bf16[8,3,256,256]{3,2,1,0:T(8,128)(2,1)} %panels.5), channel_id=1, source_target_pairs={{0,1},{1,0},{2,3},{3,2},{4,5},{5,4},{6,7},{7,6},{8,9},{9,8},{10,11... | collective-permute-start | bytes 9437192 | tf_op jit(solution)/shard_map/ppermute | solution.py:21
  53.5 25.0 %collective-permute-start.12 = (bf16[8,256,256]{2,1,0:T(8,128)(2,1)}, bf16[8,256,256]{2,1,0:T(8,128)(2,1)}, u32[]{:S(2)}, u32[]{:S(2)}) collective-permute-start(bf16[8,256,256]{2,1,0:T(8,128)(2,1)} %inv.5), channel_id=1, source_target_pairs={{0,1},{1,0},{2,3},{3,2},{4,5},{5,4},{6,7},{7,6},{8,9},{9,8},{10,11... | collective-permute-start | bytes 3145736 | tf_op jit(solution)/shard_map/ppermute | solution.py:21
  54.0 5.7 %collective-permute-start.14 = (bf16[2,256,128]{2,1,0:T(8,128)(2,1)}, bf16[2,256,128]{2,1,0:T(8,128)(2,1)}, u32[]{:S(2)}, u32[]{:S(2)}) collective-permute-start(bf16[2,256,128]{2,1,0:T(8,128)(2,1)} %get-tuple-element.51.mine), channel_id=1, source_target_pairs={{0,8},{4,12},{8,0},{12,4},{16,24},{20,28},{24,16},{28,20},{1,9},{5... | collective-permute-start | bytes 393224 | tf_op jit(solution)/shard_map/ppermute | solution.py:21
  55.5 14.8 %copy-start = (bf16[8,3,256,256]{3,2,1,0:T(8,128)(2,1)S(1)}, bf16[8,3,256,256]{3,2,1,0:T(8,128)(2,1)}, u32[]{:S(2)}) copy-start(bf16[8,3,256,256]{3,2,1,0:T(8,128)(2,1)} %panels.5) | copy-start | bytes 9437188
  55.5 1.1 %copy-start.9 = (bf16[3,256,256]{2,1,0:T(8,128)(2,1)S(1)}, bf16[3,256,256]{2,1,0:T(8,128)(2,1)}, u32[]{:S(2)}) copy-start(bf16[3,256,256]{2,1,0:T(8,128)(2,1)} %copy-done.8) | copy-start | bytes 1179652
  56.6 1.0 copy-start.11
  57.6 0.9 copy-start.15
  58.5 0.9 copy-start.17
  60.9 5.2 %collective-permute-start.15 = (bf16[1,256,128]{2,1,0:T(8,128)(2,1)S(1)}, bf16[1,256,128]{2,1,0:T(8,128)(2,1)S(1)}, u32[]{:S(2)}, u32[]{:S(2)}) collective-permute-start(bf16[1,256,128]{2,1,0:T(8,128)(2,1)S(1)} %get-tuple-element.55.mine), channel_id=1, source_target_pairs={{0,16},{4,20},{8,24},{12,28},{16,0},{20,4},{24,8},{28,12},{1,17},{... | collective-permute-start | bytes 196616 | tf_op jit(solution)/shard_map/ppermute | solution.py:21
  66.1 1.1 %copy-start.7 = (bf16[5,256,256]{2,1,0:T(8,128)(2,1)S(1)}, bf16[5,256,256]{2,1,0:T(8,128)(2,1)}, u32[]{:S(2)}) copy-start(bf16[5,256,256]{2,1,0:T(8,128)(2,1)} %copy-done.6) | copy-start | bytes 1966084
  67.2 0.9 copy-start.19
  68.7 6.9 %collective-permute-start.16 = (bf16[3,256,128]{2,1,0:T(8,128)(2,1)S(1)}, bf16[3,256,128]{2,1,0:T(8,128)(2,1)S(1)}, u32[]{:S(2)}, u32[]{:S(2)}) collective-permute-start(bf16[3,256,128]{2,1,0:T(8,128)(2,1)S(1)} %descend.1.paths), channel_id=1, source_target_pairs={{0,2},{1,3},{2,0},{3,1},{4,6},{5,7},{6,4},{7,5},{8,10},{9,11},{10,... | collective-permute-start | bytes 589832 | tf_op jit(solution)/shard_map/ppermute | solution.py:21
  70.3 1.2 %copy-start.2 = (bf16[8,256,256]{2,1,0:T(8,128)(2,1)S(1)}, bf16[8,256,256]{2,1,0:T(8,128)(2,1)}, u32[]{:S(2)}) copy-start(bf16[8,256,256]{2,1,0:T(8,128)(2,1)} %inv.5) | copy-start | bytes 3145732
  71.5 1.2 %copy-start.4 = (bf16[8,256,256]{2,1,0:T(8,128)(2,1)S(1)}, bf16[8,256,256]{2,1,0:T(8,128)(2,1)}, u32[]{:S(2)}) copy-start(bf16[8,256,256]{2,1,0:T(8,128)(2,1)} %get-tuple-element.58.value) | copy-start | bytes 3145732
  72.7 3.0 %copy-start.3 = (bf16[8,256,256]{2,1,0:T(8,128)(2,1)S(1)}, bf16[8,256,256]{2,1,0:T(8,128)(2,1)}, u32[]{:S(2)}) copy-start(bf16[8,256,256]{2,1,0:T(8,128)(2,1)} %inv.5) | copy-start | bytes 3145732
  72.7 3.0 %copy-start.5 = (bf16[8,256,256]{2,1,0:T(8,128)(2,1)S(1)}, bf16[8,256,256]{2,1,0:T(8,128)(2,1)}, u32[]{:S(2)}) copy-start(bf16[8,256,256]{2,1,0:T(8,128)(2,1)} %get-tuple-element.58.value) | copy-start | bytes 3145732
  75.7 2.9 %copy-start.1 = (bf16[8,256,256]{2,1,0:T(8,128)(2,1)S(1)}, bf16[8,256,256]{2,1,0:T(8,128)(2,1)}, u32[]{:S(2)}) copy-start(bf16[8,256,256]{2,1,0:T(8,128)(2,1)} %get-tuple-element.43.value) | copy-start | bytes 3145732
  75.7 2.9 %copy-start.23 = (s32[8,3]{1,0:T(8,128)S(1)}, s32[8,3]{1,0:T(8,128)}, u32[]{:S(2)}) copy-start(s32[8,3]{1,0:T(8,128)} %copy-done.22) | copy-start | bytes 292
  77.9 14.9 %collective-permute-start.19 = (bf16[8,256,128]{2,1,0:T(8,128)(2,1)S(1)}, bf16[8,256,128]{2,1,0:T(8,128)(2,1)S(1)}, u32[]{:S(2)}, u32[]{:S(2)}) collective-permute-start(bf16[8,256,128]{2,1,0:T(8,128)(2,1)S(1)} %solve_far.5), channel_id=1, source_target_pairs={{0,2},{1,3},{2,0},{3,1},{4,6},{5,7},{6,4},{7,5},{8,10},{9,11},{10,... | collective-permute-start | bytes 1572872 | tf_op jit(solution)/shard_map/ppermute | solution.py:21
  80.4 18.0 %collective-permute-start.18 = (bf16[4,256,128]{2,1,0:T(8,128)(2,1)S(1)}, bf16[4,256,128]{2,1,0:T(8,128)(2,1)S(1)}, u32[]{:S(2)}, u32[]{:S(2)}) collective-permute-start(bf16[4,256,128]{2,1,0:T(8,128)(2,1)S(1)} %solve_far.4), channel_id=1, source_target_pairs={{0,2},{1,3},{2,0},{3,1},{4,6},{5,7},{6,4},{7,5},{8,10},{9,11},{10,... | collective-permute-start | bytes 786440 | tf_op jit(solution)/shard_map/ppermute | solution.py:21
  83.8 18.0 %collective-permute-start.17 = (bf16[4,256,128]{2,1,0:T(8,128)(2,1)S(1)}, bf16[4,256,128]{2,1,0:T(8,128)(2,1)S(1)}, u32[]{:S(2)}, u32[]{:S(2)}) collective-permute-start(bf16[4,256,128]{2,1,0:T(8,128)(2,1)S(1)} %solve_far.3), channel_id=1, source_target_pairs={{0,2},{1,3},{2,0},{3,1},{4,6},{5,7},{6,4},{7,5},{8,10},{9,11},{10,... | collective-permute-start | bytes 786440 | tf_op jit(solution)/shard_map/ppermute | solution.py:21
  (1 other events, 0.6 us)

commit v3 on v2

--- a/solution.py
+++ b/solution.py
@@ -71,7 +71,7 @@
     @pl.when(step == steps - 1)
     def _():
         if last:
-            own_total[...] = held[:, :, :cols]
+            own_total[...] = held[:, :, :cols].astype(BF16)
             far_total[...] = held[:, :, cols:].astype(BF16)
         else:
             total[...] = held[...]
@@ -86,7 +86,7 @@
     batch = min(BATCH, count)
     whole = lambda i, *_: (0, 0, 0)
     if last:
-        sums = [jax.ShapeDtypeStruct((levels, size, cols), F32), jax.ShapeDtypeStruct((levels, size, cols), BF16)]
+        sums = [jax.ShapeDtypeStruct((levels, size, cols), BF16)] * 2
     else:
         sums = [jax.ShapeDtypeStruct((levels, size, 2 * cols), F32)]
     return pl.pallas_call(
@@ -131,34 +131,33 @@
 
 
 def send_kernel(base, ancestors, value, inv, panels, paths, result):
-    count = result.shape[0]
+    step = pl.program_id(0)
+    batch = result.shape[0]
+    solutions = solve_leaves(base + step * batch, 0, batch, ancestors, value, inv, panels, paths)
+    for index, solution_block in enumerate(solutions):
+        result[index] = solution_block
+
+
+def solve_far(ancestors, inv, panels, value, paths, base, count):
+    levels, size, cols = paths.shape[0], paths.shape[1], paths.shape[2] // 2
     batch = min(BATCH, count)
-
-    @pl.loop(0, count // batch)
-    def _(step):
-        solutions = solve_leaves(base, step, batch, ancestors, value, inv, panels, paths)
-        for index, solution_block in enumerate(solutions):
-            result[step * batch + index] = solution_block
-
-
-def solve_far(ancestors, inv, panels, value, paths, base, count):
-    size, cols = paths.shape[1:]
+    ahead = base // batch
 
     def part(array):
-        block = (count,) + array.shape[1:]
-        return pl.BlockSpec(block, lambda i: (base // count,) + (0,) * (array.ndim - 1))
+        block = (batch,) + array.shape[1:]
+        return pl.BlockSpec(block, lambda i: (ahead + i,) + (0,) * (array.ndim - 1))
 
     return pl.pallas_call(
         functools.partial(send_kernel, base),
-        grid=(1,),
+        grid=(count // batch,),
         in_specs=[
             pl.BlockSpec(memory_space=pltpu.SMEM),
-            pl.BlockSpec((count, size, cols), lambda i: (base // count, 0, 1)),
+            pl.BlockSpec((batch, size, cols), lambda i: (ahead + i, 0, 1)),
             part(inv),
             part(panels),
-            pl.BlockSpec(paths.shape, lambda i: (0, 0, 0)),
+            pl.BlockSpec((levels, size, cols), lambda i: (0, 0, 1)),
         ],
-        out_specs=pl.BlockSpec((count, size, cols), lambda i: (0, 0, 0)),
+        out_specs=pl.BlockSpec((batch, size, cols), lambda i: (i, 0, 0)),
         out_shape=jax.ShapeDtypeStruct((count, size, cols), BF16),
         compiler_params=pltpu.CompilerParams(vmem_limit_bytes=LEAF_VMEM),
         cost_estimate=cost(0, 0),
@@ -185,7 +184,7 @@
 
 
 def solve_own(scalars, which, ancestors, inv, panels, value, paths, rows, into=None):
-    size, cols = paths.shape[1:]
+    levels, size, cols = paths.shape[0], paths.shape[1], paths.shape[2] // 2
     count, slots = panels.shape[:2]
     batch = min(BATCH, count)
     extra = [] if into is None else [into]
@@ -199,7 +198,7 @@
             pl.BlockSpec((batch, size, cols), lambda i: (i, 0, 0)),
             pl.BlockSpec((batch, size, size), lambda i: (i, 0, 0)),
             pl.BlockSpec((batch, slots, size, size), lambda i: (i, 0, 0, 0)),
-            pl.BlockSpec(paths.shape, lambda i: (0, 0, 0)),
+            pl.BlockSpec((levels, size, cols), lambda i: (0, 0, 0)),
         ]
         + [hbm] * len(extra),
         out_specs=hbm,
@@ -260,40 +259,31 @@
     return blocks, parts
 
 
-def sort_kernel(parts, flags, mine, *refs):
-    theirs, factors, rest = refs[:parts], refs[parts], refs[parts + 1 :]
-
-    @pl.when(flags[0] == 1)
+def sort_kernel(parts, wanted, flags, mine, *refs):
+    theirs, chosen = refs[:parts], refs[parts:]
+
+    @pl.when(flags[0] == wanted)
     def _():
-        factors[...] = mine[...]
-        for onward in rest:
+        for out in chosen:
+            out[...] = mine[: out.shape[0]]
+
+    @pl.when(flags[0] != wanted)
+    def _():
+        for out in chosen:
             begin = 0
             for part in theirs:
-                for index in range(min(part.shape[0], onward.shape[0] - begin)):
-                    onward[begin + index] = part[index]
+                for index in range(min(part.shape[0], out.shape[0] - begin)):
+                    out[begin + index] = part[index]
                 begin += part.shape[0]
 
-    @pl.when(flags[0] == 0)
-    def _():
-        begin = 0
-        for part in theirs:
-            factors[begin : begin + part.shape[0]] = part[...]
-            begin += part.shape[0]
-        for onward in rest:
-            onward[...] = mine[: onward.shape[0]]
-
-
-def sort(bit, mine, theirs):
+
+def sort(bit, wanted, mine, theirs, counts):
     memory = pl.BlockSpec(memory_space=pltpu.VMEM)
-    shapes = [jax.ShapeDtypeStruct(mine.shape, BF16)]
-    if mine.shape[0] > 1:
-        shapes.append(jax.ShapeDtypeStruct((mine.shape[0] - 2,) + mine.shape[1:], BF16))
-        shapes.append(jax.ShapeDtypeStruct((1,) + mine.shape[1:], BF16))
-    return pl.pallas_call(
-        functools.partial(sort_kernel, len(theirs)),
+    return pl.pallas_call(
+        functools.partial(sort_kernel, len(theirs), wanted),
         in_specs=[pl.BlockSpec(memory_space=pltpu.SMEM), memory] + [memory] * len(theirs),
-        out_specs=[memory] * len(shapes),
-        out_shape=shapes,
+        out_specs=[memory] * len(counts),
+        out_shape=[jax.ShapeDtypeStruct((count,) + mine.shape[1:], BF16) for count in counts],
         compiler_params=pltpu.CompilerParams(vmem_limit_bytes=TREE_VMEM),
         cost_estimate=cost(2**20, 2**20),
         name="sort",
@@ -301,22 +291,23 @@
 
 
 def pick_kernel(flags, *refs):
-    sources, chosen = refs[:-1], refs[-1]
+    sources, chosen, sem = refs[:-2], refs[-2], refs[-1]
     for index, source in enumerate(sources):
 
         @pl.when(flags[0] == index)
         def _(source=source):
-            chosen[...] = source[...]
+            copy = pltpu.make_async_copy(source.at[:1], chosen, sem)
+            copy.start()
+            copy.wait()
 
 
 def pick(index, sources):
-    shape = (1,) + sources[0].shape[1:]
     return pl.pallas_call(
         pick_kernel,
-        grid=(1,),
-        in_specs=[pl.BlockSpec(memory_space=pltpu.SMEM)] + [pl.BlockSpec(shape, lambda i: (0, 0, 0))] * len(sources),
-        out_specs=pl.BlockSpec(shape, lambda i: (0, 0, 0)),
-        out_shape=jax.ShapeDtypeStruct(shape, BF16),
+        in_specs=[pl.BlockSpec(memory_space=pltpu.SMEM)] + [pl.BlockSpec(memory_space=pl.ANY)] * len(sources),
+        out_specs=pl.BlockSpec(memory_space=pltpu.VMEM),
+        out_shape=jax.ShapeDtypeStruct((1,) + sources[0].shape[1:], BF16),
+        scratch_shapes=[pltpu.SemaphoreType.DMA],
         compiler_params=pltpu.CompilerParams(vmem_limit_bytes=TREE_VMEM),
         cost_estimate=cost(2**20, 2**20),
         name="pick",
@@ -337,21 +328,26 @@
     return lax.optimization_barrier((value, *earlier))[0]
 
 
-def climb_kernel(mine, theirs, factors, part, passed):
-    entered = (-(mine[0].astype(F32) + theirs[0].astype(F32))).astype(BF16)
+def climb_kernel(mine, theirs, factors, passed, entered, *both):
+    here = (-(mine[0].astype(F32) + theirs[0].astype(F32))).astype(BF16)
     for above in range(passed.shape[0]):
         carried = mine[above + 1].astype(F32) + theirs[above + 1].astype(F32)
-        passed[above] = (carried + dot(factors[1 + 2 * above], entered)).astype(BF16)
-    part[...] = dot(factors[0], entered)
+        passed[above] = (carried + dot(factors[1 + 2 * above], here)).astype(BF16)
+    entered[0] = here
+    if passed.shape[0] == 1:
+        entered[1] = passed[0]
 
 
 def climb(mine, theirs, factors):
     levels, size, cols = mine.shape
+    vmem = pl.BlockSpec(memory_space=pltpu.VMEM)
     return pl.pallas_call(
         climb_kernel,
+        in_specs=[vmem] * 3,
+        out_specs=[vmem] * 2,
         out_shape=[
-            jax.ShapeDtypeStruct((size, cols), F32),
             jax.ShapeDtypeStruct((levels - 1, size, cols), BF16),
+            jax.ShapeDtypeStruct((2 if levels == 2 else 1, size, cols), BF16),
         ],
         compiler_params=pltpu.CompilerParams(vmem_limit_bytes=TREE_VMEM),
         cost_estimate=cost(2**20, 2**20),
@@ -359,27 +355,78 @@
     )(mine, theirs, factors)
 
 
-def descend_kernel(levels, mine, theirs, *refs):
-    factors, parts, paths = refs[:levels], refs[levels : 2 * levels - 1], refs[-1]
-    entered = (-(mine[0].astype(F32) + theirs[0].astype(F32))).astype(BF16)
-    paths[levels - 1] = dot(factors[levels - 1][0], entered).astype(BF16)
+def hold_kernel(below, factors, next_factors, *refs):
+    refs, (kept, inputs, onward) = refs[:-3], refs[-3:]
+    begin = 0
+    if below == 1:
+        begin = refs[0].shape[0]
+        kept[:begin] = refs[0][...]
+        cols = refs[2].shape[2]
+        if inputs.shape[0] > 1:
+            inputs[:-1] = refs[1][...]
+        inputs[inputs.shape[0] - 1, :, :cols] = refs[2][0]
+        inputs[inputs.shape[0] - 1, :, cols:] = refs[3][0]
+    else:
+        inputs[...] = jnp.zeros(inputs.shape, BF16)
+    count = factors.shape[0] // 2
+    for above in range(count):
+        kept[begin + above] = factors[2 + 2 * above]
+    kept[begin + count] = factors[0]
+    onward[...] = next_factors[...]
+
+
+def hold(level, factors, next_factors, before):
+    size = factors.shape[1]
+    vmem = pl.BlockSpec(memory_space=pltpu.VMEM)
+    blocks = factors.shape[0] // 2 + 1 + (before[0].shape[0] if before else 0)
+    cols = 2 * before[2].shape[2] if before else size
+    *held, onward = pl.pallas_call(
+        functools.partial(hold_kernel, len(before) // 4),
+        in_specs=[vmem] * (2 + len(before)),
+        out_specs=[vmem] * 3,
+        out_shape=[
+            jax.ShapeDtypeStruct((blocks, size, size), BF16),
+            jax.ShapeDtypeStruct((max(level - 1, 1), size, cols), BF16),
+            jax.ShapeDtypeStruct(next_factors.shape, BF16),
+        ],
+        compiler_params=pltpu.CompilerParams(vmem_limit_bytes=TREE_VMEM),
+        cost_estimate=cost(2**20, 2**20),
+        name="hold",
+    )(factors, next_factors, *before)
+    return held, onward
+
+
+def descend_kernel(own, far, theirs, across, top, kept, inputs, paths):
+    levels = paths.shape[0]
+    entered = [own[1].astype(F32) + theirs[0].astype(F32), far[1].astype(F32) + across[0].astype(F32)]
+    entered = (-jnp.concatenate(entered, axis=1)).astype(BF16)
+    paths[levels - 1] = dot(top[0], entered).astype(BF16)
+    end = kept.shape[0]
     for level in range(levels - 2, -1, -1):
-        rest = parts[level][...]
-        for above in reversed(range(levels - 1 - level)):
-            rest = rest - dot(factors[level][2 + 2 * above], paths[level + 1 + above])
+        count = levels - 1 - level
+        end -= count + 1
+        if level == levels - 2:
+            entered = jnp.concatenate([own[0], far[0]], axis=1)
+        else:
+            entered = inputs[level]
+        rest = dot(kept[end + count], entered)
+        for above in reversed(range(count)):
+            rest = rest - dot(kept[end + above], paths[level + 1 + above])
         paths[level] = rest.astype(BF16)
 
 
-def descend(mine, theirs, factors, parts):
-    levels = len(factors)
-    _, size, cols = mine.shape
-    return pl.pallas_call(
-        functools.partial(descend_kernel, levels),
-        out_shape=jax.ShapeDtypeStruct((levels, size, cols), BF16),
+def descend(levels, own, far, theirs, across, top, kept, inputs):
+    _, size, cols = own.shape
+    vmem = pl.BlockSpec(memory_space=pltpu.VMEM)
+    return pl.pallas_call(
+        descend_kernel,
+        in_specs=[vmem] * 7,
+        out_specs=vmem,
+        out_shape=jax.ShapeDtypeStruct((levels, size, 2 * cols), BF16),
         compiler_params=pltpu.CompilerParams(vmem_limit_bytes=TREE_VMEM),
         cost_estimate=cost(2**20, 2**20),
         name="descend",
-    )(mine, theirs, *factors, *parts)
+    )(own, far, theirs, across, top, kept, inputs)
 
 
 def on_device(
@@ -410,9 +457,8 @@
     away = (1 - high) * 2 * count
     scalars = jnp.stack([first, second, own_level, away + low * count, away + (1 - low) * count]).astype(jnp.int32)
     half = count // 2
-    sent = lax.optimization_barrier(
-        [lax.dynamic_slice_in_dim(leaf_rhs, away + part * count, count, 0) for part in (low, 1 - low)]
-    )
+    sent = [lax.dynamic_slice_in_dim(leaf_rhs, away + low * count, count, 0)]
+    sent.append(lax.dynamic_slice_in_dim(after(leaf_rhs, sent[0]), away + (1 - low) * count, count, 0))
     far_rhs = [swap(part, "col", 2) for part in sent]
 
     near_ancestors = swap(ancestors, "col", 1)
@@ -426,52 +472,60 @@
     start = after(sep_rhs, *near)
     value_1, total = forward(levels, scalars, 0, *local, leaf_rhs, far_rhs[0], start, True, False)
     arrived = [swap(piece, "leaf", 1) for piece in pieces]
-    found, *onward = sort(device % 2, blocks, after(arrived, total))
-    factors = [found]
-    total = after(total, found)
+    count_above = blocks.shape[0] - 2
+    onward = sort(device % 2, 0, blocks, after(arrived, total), (count_above, 1)) if levels > 1 else []
+    total = after(total, *onward)
     value_2, own_total, far_total = forward(levels, scalars, 1, *near, leaf_rhs, far_rhs[1], total, False, True)
 
     if levels == 3:
         from_top = [from_owners(onward[1], levels, hop) for hop in (4, 6)]
         far_total = after(far_total, *from_top)
-    mine = (own_total + swap(far_total, "col", 2).astype(F32)).astype(BF16)
-    parts = []
-    for level in range(1, levels + 1):
+    mine = (own_total.astype(F32) + swap(far_total, "col", 2).astype(F32)).astype(BF16)
+    if levels == 3:
+        from_top = pick(device // 2 % 2, from_top)
+        mine = after(mine, from_top)
+    (factors,) = sort(device % 2, 1, blocks, after(arrived, mine), (blocks.shape[0],))
+    held = []
+    for level in range(1, levels):
         theirs = swap(mine, "leaf", 2 ** (level - 1))
-        if onward:
-            arrived = swap(onward[0], "leaf", 2**level)
-            before = onward[0]
-            found, *onward = sort(device // 2**level % 2, before, [arrived])
-            factors.append(found)
-            theirs = after(theirs, found)
-            top = None
-            if levels == 3:
-                top = pick(device // 2 % 4, [*from_top, before, arrived])
-                factors.append(top)
-                onward = []
-        elif level == 2:
+        here = onward[0]
+        if levels != 3 or level == 1:
+            arrived = swap(here, "leaf", 2**level)
+            (following,) = sort(device // 2**level % 2, 1, here, [arrived], (here.shape[0],))
+        if level < levels - 1 and levels != 3:
+            onward = sort(device // 2**level % 2, 0, here, [arrived], (here.shape[0] - 2, 1))
+        if levels == 3 and level == 1:
+            (candidate,) = sort(device // 2 % 2, 0, here, [arrived], (1,))
+            theirs = after(theirs, following, candidate)
+            top = pick(device // 4 % 2, [from_top, candidate])
+        elif levels == 3:
+            following = top
             theirs = after(theirs, top)
-        if level < levels:
-            part, mine = climb(mine, theirs, factors[level - 1])
-            parts.append(part)
+        else:
+            theirs = after(theirs, following)
+        passed, entered = climb(mine, theirs, factors)
         if level == 1:
-            near_upper_inv = swap(after(leaf_upper_inv, mine), "col", 1)
-            near_upper_panels = swap(after(leaf_upper_panels, mine), "col", 1)
-    paths = descend(mine, theirs, factors, parts)
-    far_paths = swap(paths, "col", 2)
+            near_upper_inv = swap(after(leaf_upper_inv, passed), "col", 1)
+            near_upper_panels = swap(after(leaf_upper_panels, passed), "col", 1)
+        held, following = hold(level, after(factors, passed), following, [*held, own, far] if level > 1 else [])
+        mine, factors, own, far = passed, following, entered, swap(entered, "col", 2)
+    theirs = swap(mine, "leaf", 2 ** (levels - 1))
+    hop = 2 ** (levels - 1) * lax.axis_size("col") + 2
+    pairs = [(source, source ^ hop) for source in range(lax.axis_size("leaf") * lax.axis_size("col"))]
+    across = lax.ppermute(mine, ("leaf", "col"), pairs)
+    paths = descend(levels, own, far, theirs, across, factors, *held)
 
     own_solution = jnp.zeros((size, cols), BF16)
     for level in range(levels):
-        own_solution = jnp.where(owned[level], paths[level], own_solution)
+        own_solution = jnp.where(owned[level], paths[level, :, :cols], own_solution)
 
     local = (ancestors, leaf_upper_inv, leaf_upper_panels)
     near = (near_ancestors, near_upper_inv, near_upper_panels)
     leaf_solution = solve_own(scalars, 0, *local, value_1, paths, rows)
-    far_paths = after(far_paths, leaf_solution)
     returning = [
-        (3, 0, solve_far(*local, value_1, far_paths, 0, count)),
-        (4, 0, solve_far(*near, value_2, far_paths, 0, half)),
-        (4, half, solve_far(*near, value_2, far_paths, half, half)),
+        (3, 0, solve_far(*local, value_1, paths, 0, count)),
+        (4, 0, solve_far(*near, value_2, paths, 0, half)),
+        (4, half, solve_far(*near, value_2, paths, half, half)),
     ]
     leaf_solution = solve_own(scalars, 1, *near, value_2, paths, rows, leaf_solution)
     for which, offset, part in returning:

time: 104 us -> 98.9 us (0.951)
  local copies, waits for them, and re-layouts: 14.1 us -> 8.74 us
  waiting for transfers between devices: 31.3 us -> 29.2 us
  Pallas kernels: 32.7 us -> 34.3 us
  starting transfers between devices: 22.4 us -> 23.5 us
    unnamed x59 -> x43, local copies, waits for them, and re-layouts: 11.3 us -> 4.34 us
    ppermute x18 -> x19, waiting for transfers between devices: 31.3 us -> 26.4 us  [swap(): return lax.ppermute(value, axis, pairs)]
    ppermute x0 -> x1, starting transfers between devices: none -> 3.2 us  [on_device(): across = lax.ppermute(mine, ('leaf', 'col'), pairs)]
    ppermute x0 -> x1, waiting for transfers between devices: none -> 2.85 us  [on_device(): across = lax.ppermute(mine, ('leaf', 'col'), pairs)]
    ppermute x18 -> x19, starting transfers between devices: 20.4 us -> 18.4 us  [swap(): return lax.ppermute(value, axis, pairs)]
    dynamic_slice x1 -> x2, local copies, waits for them, and re-layouts: 2.08 us -> 3.8 us  [the longest x1 1.91 us: on_device(): lax.dynamic_slice_in_dim(after(leaf_rhs, sent[0]), away + (1 - low) * cou...]
    pallas_call x9 -> x14, Pallas kernels: 9.62 us -> 10.3 us  [the longest x3 7.03 us: solve_far(): pl.pallas_call(functools.partial(send_kernel, base), grid=(count // batch...]
  transfers between devices with their start and end apart: 20 -> 22, of which waited for: 11 -> 11; matrix products, arithmetic and copies ran while one was open for 4% -> 6% of each run, Pallas kernels for 30% -> 33%
where the time goes in v3:
time: 98.9 us; the launch traced here: 98.4 us
  Pallas kernels  34.3 us (35%)
  waiting for transfers between devices  29.2 us (30%)
  starting transfers between devices  23.5 us (24%)
  local copies, waits for them, and re-layouts  8.74 us (9%)
  other arithmetic  1.63 us (2%)
  between operations  0.99 us (1%)
    ppermute x19, waiting for transfers between devices, swap(): return lax.ppermute(value, axis, pairs)  26.4 us
    ppermute x19, starting transfers between devices, swap(): return lax.ppermute(value, axis, pairs)  18.4 us
    pallas_call x2, Pallas kernels, forward(): pl.pallas_call(functools.partial(forward_kernel, first, last), grid_spec=...  12.5 us
    pallas_call x2, Pallas kernels, solve_own(): pl.pallas_call(functools.partial(keep_kernel, which), grid=(count // batc...  7.29 us
    pallas_call x3, Pallas kernels, solve_far(): pl.pallas_call(functools.partial(send_kernel, base), grid=(count // batch...  7.03 us
    unnamed x43, local copies, waits for them, and re-layouts  4.34 us
    pallas_call x3, Pallas kernels, place_rows(): pl.pallas_call(place_kernel, grid_spec=pltpu.PrefetchScalarGridSpec(num_s...  3.88 us
    ppermute x1, starting transfers between devices, on_device(): across = lax.ppermute(mine, ('leaf', 'col'), pairs)  3.2 us
  transfers between devices with their start and end apart: 22, of which 11 were waited for; matrix products, arithmetic and copies ran while one was open for 6% of the time, Pallas kernels for 33%

profile of v3, /device:TPU:0, one launch (start us, length us, event | category | flops | bytes accessed | tf_op | source)
XLA Modules:
  0.0 98.4 jit_solution(15583890743320748846)
XLA Ops:
  0.7 0.5 collective-permute-start.3
  1.3 1.9 %constant_dynamic-slice_fusion.1 = bf16[8,256,128]{2,1,0:T(8,128)(2,1)} fusion(bf16[32,256,128]{2,1,0:T(8,128)(2,1)} %rhs.3, s32[]{:T(128)S(6)} %select_n.94), kind=kLoop, calls=%fused_computation.5 | loop fusion | bytes 1048580 | tf_op jit(solution)/shard_map/dynamic_slice | solution.py:460
  3.2 2.9 %collective-permute-start.4 = (bf16[8,256,128]{2,1,0:T(8,128)(2,1)}, bf16[8,256,128]{2,1,0:T(8,128)(2,1)}, u32[]{:S(2)}, u32[]{:S(2)}) collective-permute-start(bf16[8,256,128]{2,1,0:T(8,128)(2,1)} %constant_dynamic-slice_fusion.1), channel_id=1, source_target_pairs={{0,2},{1,3},{2,0},{3,1},{4,6},{5,7},{6,4},{7,5},{8,10},{9,11},{10,... | collective-permute-start | bytes 1572872 | tf_op jit(solution)/shard_map/ppermute | solution.py:21
  6.1 1.9 %constant_dynamic-slice_fusion = bf16[8,256,128]{2,1,0:T(8,128)(2,1)} fusion(bf16[32,256,128]{2,1,0:T(8,128)(2,1)} %rhs.3, s32[]{:T(128)S(6)} %select_n.95), kind=kLoop, calls=%fused_computation.4 | loop fusion | bytes 1048580 | tf_op jit(solution)/shard_map/dynamic_slice | solution.py:461
  8.4 1.6 %collective-permute-start.5 = (bf16[3,256,256]{2,1,0:T(8,128)(2,1)S(1)}, bf16[3,256,256]{2,1,0:T(8,128)(2,1)S(1)}, u32[]{:S(2)}, u32[]{:S(2)}) collective-permute-start(bf16[3,256,256]{2,1,0:T(8,128)(2,1)S(1)} %get-tuple-element.43), channel_id=1, source_target_pairs={{0,4},{4,0},{8,12},{12,8},{16,20},{20,16},{24,28},{28,24},{1,5},{5... | collective-permute-start | bytes 1179656 | tf_op jit(solution)/shard_map/ppermute | solution.py:21
  10.0 1.2 %collective-permute-done.ancestors = s32[8,3]{1,0:T(8,128)S(1)} collective-permute-done((s32[8,3]{1,0:T(8,128)S(1)}, s32[8,3]{1,0:T(8,128)S(1)}, u32[]{:S(2)}, u32[]{:S(2)}) %collective-permute-start) | collective-permute-done | bytes 128 | tf_op jit(solution)/shard_map/ppermute | solution.py:21
  11.7 0.7 collective-permute-start.6
  12.4 0.6 stack.23.scalars
  13.0 6.2 %collective-permute-done.4.far = bf16[8,256,128]{2,1,0:T(8,128)(2,1)} collective-permute-done((bf16[8,256,128]{2,1,0:T(8,128)(2,1)}, bf16[8,256,128]{2,1,0:T(8,128)(2,1)}, u32[]{:S(2)}, u32[]{:S(2)}) %collective-permute-start.4) | collective-permute-done | bytes 524320 | tf_op jit(solution)/shard_map/ppermute | solution.py:21
  19.1 6.2 %leaf_forward.2 = (bf16[8,256,256]{2,1,0:T(8,128)(2,1)}, f32[3,256,256]{2,1,0:T(8,128)}) custom-call(s32[5]{0:T(128)} %stack.23.scalars, s32[8,3]{1,0:T(8,128)} %copy-done.14, bf16[32,256,128]{2,1,0:T(8,128)(2,1)} %rhs.3, bf16[8,256,128]{2,1,0:T(8,128)(2,1)} %collective-permute-done.4.far, bf16[8,256,256]{2,1,0:T(8,128)(2,1)} %inv.3, ...), custom_call_target="tpu_custom_call" | custom-call | tf_op jit(solution)/shard_map/leaf_forward/pallas_call | solution.py:92
  25.4 0.7 collective-permute-start.8
  26.1 1.3 %collective-permute-start.7 = (bf16[1,256,256]{2,1,0:T(8,128)(2,1)S(1)}, bf16[1,256,256]{2,1,0:T(8,128)(2,1)S(1)}, u32[]{:S(2)}, u32[]{:S(2)}) collective-permute-start(bf16[1,256,256]{2,1,0:T(8,128)(2,1)S(1)} %get-tuple-element.48), channel_id=1, source_target_pairs={{16,0},{20,4},{17,1},{21,5},{18,2},{22,6},{19,3},{23,7}} | collective-permute-start | bytes 393224 | tf_op jit(solution)/shard_map/ppermute | solution.py:324
  27.4 2.4 %collective-permute-done.1.far = bf16[8,256,128]{2,1,0:T(8,128)(2,1)} collective-permute-done((bf16[8,256,128]{2,1,0:T(8,128)(2,1)}, bf16[8,256,128]{2,1,0:T(8,128)(2,1)}, u32[]{:S(2)}, u32[]{:S(2)}) %collective-permute-start.1) | collective-permute-done | bytes 524320 | tf_op jit(solution)/shard_map/ppermute | solution.py:21
  29.8 6.3 %leaf_forward.3 = (bf16[8,256,256]{2,1,0:T(8,128)(2,1)}, bf16[3,256,128]{2,1,0:T(8,128)(2,1)}, bf16[3,256,128]{2,1,0:T(8,128)(2,1)}) custom-call(s32[5]{0:T(128)} %stack.23.scalars, s32[8,3]{1,0:T(8,128)} %copy-done.12, bf16[32,256,128]{2,1,0:T(8,128)(2,1)} %rhs.3, bf16[8,256,128]{2,1,0:T(8,128)(2,1)} %collective-permute-done.1.far, ...), custom_call_target="tpu_custom_call" | custom-call | tf_op jit(solution)/shard_map/leaf_forward/pallas_call | solution.py:92
  36.2 1.8 %collective-permute-start.9 = (bf16[3,256,128]{2,1,0:T(8,128)(2,1)}, bf16[3,256,128]{2,1,0:T(8,128)(2,1)S(1)}, u32[]{:S(2)}, u32[]{:S(2)}) collective-permute-start(bf16[3,256,128]{2,1,0:T(8,128)(2,1)} %get-tuple-element.53), channel_id=1, source_target_pairs={{0,2},{1,3},{2,0},{3,1},{4,6},{5,7},{6,4},{7,5},{8,10},{9,11},{10,... | collective-permute-start | bytes 589832 | tf_op jit(solution)/shard_map/ppermute | solution.py:21
  38.0 1.6 %collective-permute-start.11 = (bf16[3,256,256]{2,1,0:T(8,128)(2,1)S(1)}, bf16[3,256,256]{2,1,0:T(8,128)(2,1)S(1)}, u32[]{:S(2)}, u32[]{:S(2)}) collective-permute-start(bf16[3,256,256]{2,1,0:T(8,128)(2,1)S(1)} %get-tuple-element.47.mine), channel_id=1, source_target_pairs={{0,8},{4,12},{8,0},{12,4},{16,24},{20,28},{24,16},{28,20},{1,9},{5... | collective-permute-start | bytes 1179656 | tf_op jit(solution)/shard_map/ppermute | solution.py:21
  39.7 0.7 copy-done.6
  40.4 2.4 %collective-permute-done.9 = bf16[3,256,128]{2,1,0:T(8,128)(2,1)S(1)} collective-permute-done((bf16[3,256,128]{2,1,0:T(8,128)(2,1)}, bf16[3,256,128]{2,1,0:T(8,128)(2,1)S(1)}, u32[]{:S(2)}, u32[]{:S(2)}) %collective-permute-start.9) | collective-permute-done | bytes 196640 | tf_op jit(solution)/shard_map/ppermute | solution.py:21
  42.8 1.0 add_convert_fusion.mine
  43.8 1.5 %collective-permute-start.10 = (bf16[3,256,128]{2,1,0:T(8,128)(2,1)S(1)}, bf16[3,256,128]{2,1,0:T(8,128)(2,1)S(1)}, u32[]{:S(2)}, u32[]{:S(2)}) collective-permute-start(bf16[3,256,128]{2,1,0:T(8,128)(2,1)S(1)} %add_convert_fusion.mine), channel_id=1, source_target_pairs={{0,4},{4,0},{8,12},{12,8},{16,20},{20,16},{24,28},{28,24},{1,5},{5... | collective-permute-start | bytes 589832 | tf_op jit(solution)/shard_map/ppermute | solution.py:21
  45.3 2.6 %collective-permute-done.11.refs_0_ = bf16[3,256,256]{2,1,0:T(8,128)(2,1)S(1)} collective-permute-done((bf16[3,256,256]{2,1,0:T(8,128)(2,1)S(1)}, bf16[3,256,256]{2,1,0:T(8,128)(2,1)S(1)}, u32[]{:S(2)}, u32[]{:S(2)}) %collective-permute-start.11) | collective-permute-done | bytes 393248 | tf_op jit(solution)/shard_map/ppermute | solution.py:21
  48.0 1.5 %collective-permute-done.10.theirs = bf16[3,256,128]{2,1,0:T(8,128)(2,1)S(1)} collective-permute-done((bf16[3,256,128]{2,1,0:T(8,128)(2,1)S(1)}, bf16[3,256,128]{2,1,0:T(8,128)(2,1)S(1)}, u32[]{:S(2)}, u32[]{:S(2)}) %collective-permute-start.10) | collective-permute-done | bytes 196640 | tf_op jit(solution)/shard_map/ppermute | solution.py:21
  49.5 0.9 climb.2
  50.4 0.6 copy-done.16
  51.5 1.5 %collective-permute-start.14 = (bf16[2,256,128]{2,1,0:T(8,128)(2,1)}, bf16[2,256,128]{2,1,0:T(8,128)(2,1)}, u32[]{:S(2)}, u32[]{:S(2)}) collective-permute-start(bf16[2,256,128]{2,1,0:T(8,128)(2,1)} %get-tuple-element.58.mine), channel_id=1, source_target_pairs={{0,8},{4,12},{8,0},{12,4},{16,24},{20,28},{24,16},{28,20},{1,9},{5... | collective-permute-start | bytes 393224 | tf_op jit(solution)/shard_map/ppermute | solution.py:21
  53.0 0.9 copy-done.5
  53.9 0.9 copy-done.7
  55.0 1.6 %collective-permute-start.18 = (bf16[1,256,128]{2,1,0:T(8,128)(2,1)}, bf16[1,256,128]{2,1,0:T(8,128)(2,1)S(1)}, u32[]{:S(2)}, u32[]{:S(2)}) collective-permute-start(bf16[1,256,128]{2,1,0:T(8,128)(2,1)} %copy-done.16), channel_id=1, source_target_pairs={{0,2},{1,3},{2,0},{3,1},{4,6},{5,7},{6,4},{7,5},{8,10},{9,11},{10,... | collective-permute-start | bytes 196616 | tf_op jit(solution)/shard_map/ppermute | solution.py:21
  56.6 1.1 %copy-done.2 = bf16[5,256,256]{2,1,0:T(8,128)(2,1)S(1)} copy-done((bf16[5,256,256]{2,1,0:T(8,128)(2,1)S(1)}, bf16[5,256,256]{2,1,0:T(8,128)(2,1)}, u32[]{:S(2)}) %copy-start.2) | copy-done | bytes 655384
  57.8 1.2 %climb.3 = (bf16[1,256,128]{2,1,0:T(8,128)(2,1)S(1)}, bf16[2,256,128]{2,1,0:T(8,128)(2,1)S(1)}) custom-call(bf16[2,256,128]{2,1,0:T(8,128)(2,1)} %get-tuple-element.58.mine, bf16[2,256,128]{2,1,0:T(8,128)(2,1)} %collective-permute-done.14.theirs, bf16[3,256,256]{2,1,0:T(8,128)(2,1)S(1)} %get-tuple-element.66.factors), custom_call_target="tpu_custom_call" | custom-call | flops 1048576 | bytes 1048576 | tf_op jit(solution)/shard_map/climb/pallas_call | solution.py:344
  59.0 0.9 collective-permute-start.15
  59.9 3.2 %collective-permute-start.17 = (bf16[1,256,128]{2,1,0:T(8,128)(2,1)S(1)}, bf16[1,256,128]{2,1,0:T(8,128)(2,1)S(1)}, u32[]{:S(2)}, u32[]{:S(2)}) collective-permute-start(bf16[1,256,128]{2,1,0:T(8,128)(2,1)S(1)} %get-tuple-element.65), channel_id=1, source_target_pairs={{0,18},{1,19},{2,16},{3,17},{4,22},{5,23},{6,20},{7,21},{8,26},{9,... | collective-permute-start | bytes 196616 | tf_op jit(solution)/shard_map/ppermute | solution.py:515
  63.5 2.9 %collective-permute-done.17.across = bf16[1,256,128]{2,1,0:T(8,128)(2,1)S(1)} collective-permute-done((bf16[1,256,128]{2,1,0:T(8,128)(2,1)S(1)}, bf16[1,256,128]{2,1,0:T(8,128)(2,1)S(1)}, u32[]{:S(2)}, u32[]{:S(2)}) %collective-permute-start.17) | collective-permute-done | bytes 65568 | tf_op jit(solution)/shard_map/ppermute | solution.py:515
  66.4 2.8 %collective-permute-done.16.theirs = bf16[1,256,128]{2,1,0:T(8,128)(2,1)S(1)} collective-permute-done((bf16[1,256,128]{2,1,0:T(8,128)(2,1)S(1)}, bf16[1,256,128]{2,1,0:T(8,128)(2,1)S(1)}, u32[]{:S(2)}, u32[]{:S(2)}) %collective-permute-start.16) | collective-permute-done | bytes 65568 | tf_op jit(solution)/shard_map/ppermute | solution.py:21
  69.2 0.6 descend.1.paths
  69.8 3.3 %solve_far.5 = bf16[8,256,128]{2,1,0:T(8,128)(2,1)S(1)} custom-call(s32[8,3]{1,0:T(8,128)S(1)} %copy-done.15, bf16[8,256,256]{2,1,0:T(8,128)(2,1)S(1)} %copy-done.3, bf16[8,256,256]{2,1,0:T(8,128)(2,1)} %inv.5, bf16[8,3,256,256]{3,2,1,0:T(8,128)(2,1)} %panels.5, bf16[3,256,256]{2,1,0:T(8,128)(2,1)S(1)} %descend.1.paths), custom_call_target="tpu_custom_call" | custom-call | tf_op jit(solution)/shard_map/solve_far/pallas_call | solution.py:150
  73.4 1.9 %solve_far.4 = bf16[4,256,128]{2,1,0:T(8,128)(2,1)S(1)} custom-call(s32[8,3]{1,0:T(8,128)S(1)} %copy-done.13, bf16[8,256,256]{2,1,0:T(8,128)(2,1)S(1)} %copy-done, bf16[8,256,256]{2,1,0:T(8,128)(2,1)} %collective-permute-done.12.inv, bf16[8,3,256,256]{3,2,1,0:T(8,128)(2,1)S(1)} %collective-permute-done.13.panels, bf16[3,256,256]{2,1,0:T(8,128)(2,1)S(1)} %descend.1.paths), custom_call_target="tpu_custom_call" | custom-call | tf_op jit(solution)/shard_map/solve_far/pallas_call | solution.py:150
  75.3 1.9 %collective-permute-start.20 = (bf16[4,256,128]{2,1,0:T(8,128)(2,1)S(1)}, bf16[4,256,128]{2,1,0:T(8,128)(2,1)S(1)}, u32[]{:S(2)}, u32[]{:S(2)}) collective-permute-start(bf16[4,256,128]{2,1,0:T(8,128)(2,1)S(1)} %solve_far.4), channel_id=1, source_target_pairs={{0,2},{1,3},{2,0},{3,1},{4,6},{5,7},{6,4},{7,5},{8,10},{9,11},{10,... | collective-permute-start | bytes 786440 | tf_op jit(solution)/shard_map/ppermute | solution.py:21
  77.2 1.9 %solve_far.3 = bf16[4,256,128]{2,1,0:T(8,128)(2,1)S(1)} custom-call(s32[8,3]{1,0:T(8,128)S(1)} %copy-done.13, bf16[8,256,256]{2,1,0:T(8,128)(2,1)S(1)} %copy-done, bf16[8,256,256]{2,1,0:T(8,128)(2,1)} %collective-permute-done.12.inv, bf16[8,3,256,256]{3,2,1,0:T(8,128)(2,1)S(1)} %collective-permute-done.13.panels, bf16[3,256,256]{2,1,0:T(8,128)(2,1)S(1)} %descend.1.paths), custom_call_target="tpu_custom_call" | custom-call | tf_op jit(solution)/shard_map/solve_far/pallas_call | solution.py:150
  79.3 3.9 %solve_own.2.refs_0_ = bf16[32,256,128]{2,1,0:T(8,128)(2,1)} custom-call(s32[5]{0:T(128)S(1)} %copy-done.18, s32[8,3]{1,0:T(8,128)S(1)} %copy-done.15, bf16[8,256,256]{2,1,0:T(8,128)(2,1)S(1)} %copy-done.3, bf16[8,256,256]{2,1,0:T(8,128)(2,1)} %inv.5, bf16[8,3,256,256]{3,2,1,0:T(8,128)(2,1)} %panels.5, bf16[3,256,256]{2,1,0:T(8,128)(2,1)S(1)} %descend.1.paths), custom_call_target="tpu_custom_call" | custom-call | tf_op jit(solution)/shard_map/solve_own/pallas_call | solution.py:192
  83.2 0.6 fusion.1
  83.9 3.4 %solve_own.3.whole = bf16[32,256,128]{2,1,0:T(8,128)(2,1)} custom-call(s32[5]{0:T(128)S(1)} %copy-done.18, s32[8,3]{1,0:T(8,128)S(1)} %copy-done.13, bf16[8,256,256]{2,1,0:T(8,128)(2,1)S(1)} %copy-done, bf16[8,256,256]{2,1,0:T(8,128)(2,1)} %collective-permute-done.12.inv, ...), custom_call_target="tpu_custom_call", output_to_operand_aliasing={{}: (6, {})} | custom-call | tf_op jit(solution)/shard_map/solve_own/pallas_call | solution.py:192
  87.3 0.8 collective-permute-done.21.part
  88.1 1.4 %place_rows.3.whole = bf16[32,256,128]{2,1,0:T(8,128)(2,1)} custom-call(s32[5]{0:T(128)S(1)} %copy-done.18, bf16[8,256,128]{2,1,0:T(8,128)(2,1)S(1)} %collective-permute-done.21.part, bf16[32,256,128]{2,1,0:T(8,128)(2,1)} %solve_own.3.whole), custom_call_target="tpu_custom_call", output_to_operand_aliasing={{}: (2, {})} | custom-call | tf_op jit(solution)/shard_map/place_rows/pallas_call | solution.py:220
  89.4 4.3 %collective-permute-done.20.part = bf16[4,256,128]{2,1,0:T(8,128)(2,1)S(1)} collective-permute-done((bf16[4,256,128]{2,1,0:T(8,128)(2,1)S(1)}, bf16[4,256,128]{2,1,0:T(8,128)(2,1)S(1)}, u32[]{:S(2)}, u32[]{:S(2)}) %collective-permute-start.20) | collective-permute-done | bytes 262176 | tf_op jit(solution)/shard_map/ppermute | solution.py:21
  93.7 1.3 %place_rows.4.whole = bf16[32,256,128]{2,1,0:T(8,128)(2,1)} custom-call(s32[5]{0:T(128)S(1)} %copy-done.18, bf16[4,256,128]{2,1,0:T(8,128)(2,1)S(1)} %collective-permute-done.20.part, bf16[32,256,128]{2,1,0:T(8,128)(2,1)} %place_rows.3.whole), custom_call_target="tpu_custom_call", output_to_operand_aliasing={{}: (2, {})} | custom-call | tf_op jit(solution)/shard_map/place_rows/pallas_call | solution.py:220
  95.0 2.2 %collective-permute-done.19.part = bf16[4,256,128]{2,1,0:T(8,128)(2,1)S(1)} collective-permute-done((bf16[4,256,128]{2,1,0:T(8,128)(2,1)S(1)}, bf16[4,256,128]{2,1,0:T(8,128)(2,1)S(1)}, u32[]{:S(2)}, u32[]{:S(2)}) %collective-permute-start.19) | collective-permute-done | bytes 262176 | tf_op jit(solution)/shard_map/ppermute | solution.py:21
  97.1 1.3 %place_rows.5 = bf16[32,256,128]{2,1,0:T(8,128)(2,1)} custom-call(s32[5]{0:T(128)S(1)} %copy-done.18, bf16[4,256,128]{2,1,0:T(8,128)(2,1)S(1)} %collective-permute-done.19.part, bf16[32,256,128]{2,1,0:T(8,128)(2,1)} %place_rows.4.whole), custom_call_target="tpu_custom_call", output_to_operand_aliasing={{}: (2, {})} | custom-call | tf_op jit(solution)/shard_map/place_rows/pallas_call | solution.py:220
  (66 shorter events, 3.0 us)
Async XLA Ops:
  0.6 7.4 %copy-start.10 = (bf16[1,256,256]{2,1,0:T(8,128)(2,1)S(1)}, bf16[1,256,256]{2,1,0:T(8,128)(2,1)}, u32[]{:S(2)}) copy-start(bf16[1,256,256]{2,1,0:T(8,128)(2,1)} %lower_inv) | copy-start | bytes 393220
  0.6 7.4 %copy-start.9 = (bf16[1,2,256,256]{3,2,1,0:T(8,128)(2,1)S(1)}, bf16[1,2,256,256]{3,2,1,0:T(8,128)(2,1)}, u32[]{:S(2)}) copy-start(bf16[1,2,256,256]{3,2,1,0:T(8,128)(2,1)} %upper_panels.1) | copy-start | bytes 786436
  0.7 7.4 %copy-start.11 = (bf16[1,256,256]{2,1,0:T(8,128)(2,1)S(1)}, bf16[1,256,256]{2,1,0:T(8,128)(2,1)}, u32[]{:S(2)}) copy-start(bf16[1,256,256]{2,1,0:T(8,128)(2,1)} %upper_inv.1) | copy-start | bytes 393220
  0.7 7.4 %copy-start.8 = (bf16[1,2,256,256]{3,2,1,0:T(8,128)(2,1)S(1)}, bf16[1,2,256,256]{3,2,1,0:T(8,128)(2,1)}, u32[]{:S(2)}) copy-start(bf16[1,2,256,256]{3,2,1,0:T(8,128)(2,1)} %lower_panels.1) | copy-start | bytes 786436
  0.7 9.3 %copy-start.20 = (s32[8,3]{0,1:T(4,128)S(1)}, s32[8,3]{0,1:T(4,128)}, u32[]{:S(2)}) copy-start(s32[8,3]{0,1:T(4,128)} %param.16) | copy-start | bytes 292
  0.7 12.3 %collective-permute-start.3 = (bf16[8,3,256,256]{3,2,1,0:T(8,128)(2,1)}, bf16[8,3,256,256]{3,2,1,0:T(8,128)(2,1)}, u32[]{:S(2)}, u32[]{:S(2)}) collective-permute-start(bf16[8,3,256,256]{3,2,1,0:T(8,128)(2,1)} %panels.3), channel_id=1, source_target_pairs={{0,1},{1,0},{2,3},{3,2},{4,5},{5,4},{6,7},{7,6},{8,9},{9,8},{10,11... | collective-permute-start | bytes 9437192 | tf_op jit(solution)/shard_map/ppermute | solution.py:21
  1.2 10.5 %collective-permute-start.2 = (bf16[8,256,256]{2,1,0:T(8,128)(2,1)}, bf16[8,256,256]{2,1,0:T(8,128)(2,1)S(1)}, u32[]{:S(2)}, u32[]{:S(2)}) collective-permute-start(bf16[8,256,256]{2,1,0:T(8,128)(2,1)} %inv.3), channel_id=1, source_target_pairs={{0,1},{1,0},{2,3},{3,2},{4,5},{5,4},{6,7},{7,6},{8,9},{9,8},{10,11... | collective-permute-start | bytes 3145736 | tf_op jit(solution)/shard_map/ppermute | solution.py:21
  3.2 16.0 %collective-permute-start.4 = (bf16[8,256,128]{2,1,0:T(8,128)(2,1)}, bf16[8,256,128]{2,1,0:T(8,128)(2,1)}, u32[]{:S(2)}, u32[]{:S(2)}) collective-permute-start(bf16[8,256,128]{2,1,0:T(8,128)(2,1)} %constant_dynamic-slice_fusion.1), channel_id=1, source_target_pairs={{0,2},{1,3},{2,0},{3,1},{4,6},{5,7},{6,4},{7,5},{8,10},{9,11},{10,... | collective-permute-start | bytes 1572872 | tf_op jit(solution)/shard_map/ppermute | solution.py:21
  8.4 17.0 %collective-permute-start.5 = (bf16[3,256,256]{2,1,0:T(8,128)(2,1)S(1)}, bf16[3,256,256]{2,1,0:T(8,128)(2,1)S(1)}, u32[]{:S(2)}, u32[]{:S(2)}) collective-permute-start(bf16[3,256,256]{2,1,0:T(8,128)(2,1)S(1)} %get-tuple-element.43), channel_id=1, source_target_pairs={{0,4},{4,0},{8,12},{12,8},{16,20},{20,16},{24,28},{28,24},{1,5},{5... | collective-permute-start | bytes 1179656 | tf_op jit(solution)/shard_map/ppermute | solution.py:21
  10.0 9.1 %copy-start.14 = (s32[8,3]{1,0:T(8,128)}, s32[8,3]{1,0:T(8,128)S(1)}, u32[]{:S(2)}) copy-start(s32[8,3]{1,0:T(8,128)S(1)} %copy.17.ancestors) | copy-start | bytes 292
  10.0 1.2 %collective-permute-start = (s32[8,3]{1,0:T(8,128)S(1)}, s32[8,3]{1,0:T(8,128)S(1)}, u32[]{:S(2)}, u32[]{:S(2)}) collective-permute-start(s32[8,3]{1,0:T(8,128)S(1)} %copy.17.ancestors), channel_id=1, source_target_pairs={{0,1},{1,0},{2,3},{3,2},{4,5},{5,4},{6,7},{7,6},{8,9},{9,8},{10,11... | collective-permute-start | bytes 296 | tf_op jit(solution)/shard_map/ppermute | solution.py:21
  11.2 14.1 %copy-start.12 = (s32[8,3]{1,0:T(8,128)}, s32[8,3]{1,0:T(8,128)S(1)}, u32[]{:S(2)}) copy-start(s32[8,3]{1,0:T(8,128)S(1)} %collective-permute-done.ancestors) | copy-start | bytes 292
  11.2 18.6 %collective-permute-start.1 = (bf16[8,256,128]{2,1,0:T(8,128)(2,1)}, bf16[8,256,128]{2,1,0:T(8,128)(2,1)}, u32[]{:S(2)}, u32[]{:S(2)}) collective-permute-start(bf16[8,256,128]{2,1,0:T(8,128)(2,1)} %constant_dynamic-slice_fusion), channel_id=1, source_target_pairs={{0,2},{1,3},{2,0},{3,1},{4,6},{5,7},{6,4},{7,5},{8,10},{9,11},{10,... | collective-permute-start | bytes 1572872 | tf_op jit(solution)/shard_map/ppermute | solution.py:21
  11.7 13.6 %copy-start.19 = (bf16[8,256,256]{2,1,0:T(8,128)(2,1)}, bf16[8,256,256]{2,1,0:T(8,128)(2,1)S(1)}, u32[]{:S(2)}) copy-start(bf16[8,256,256]{2,1,0:T(8,128)(2,1)S(1)} %collective-permute-done.2.inv) | copy-start | bytes 3145732
  11.7 13.6 %collective-permute-start.6 = (bf16[2,256,256]{2,1,0:T(8,128)(2,1)S(1)}, bf16[2,256,256]{2,1,0:T(8,128)(2,1)S(1)}, u32[]{:S(2)}, u32[]{:S(2)}) collective-permute-start(bf16[2,256,256]{2,1,0:T(8,128)(2,1)S(1)} %get-tuple-element.44), channel_id=1, source_target_pairs={{0,4},{4,0},{8,12},{12,8},{16,20},{20,16},{24,28},{28,24},{1,5},{5... | collective-permute-start | bytes 786440 | tf_op jit(solution)/shard_map/ppermute | solution.py:21
  25.4 10.7 %collective-permute-start.8 = (bf16[1,256,256]{2,1,0:T(8,128)(2,1)S(1)}, bf16[1,256,256]{2,1,0:T(8,128)(2,1)S(1)}, u32[]{:S(2)}, u32[]{:S(2)}) collective-permute-start(bf16[1,256,256]{2,1,0:T(8,128)(2,1)S(1)} %get-tuple-element.48), channel_id=1, source_target_pairs={{16,8},{20,12},{17,9},{21,13},{18,10},{22,14},{19,11},{23,15}} | collective-permute-start | bytes 393224 | tf_op jit(solution)/shard_map/ppermute | solution.py:324
  26.1 10.0 %collective-permute-start.7 = (bf16[1,256,256]{2,1,0:T(8,128)(2,1)S(1)}, bf16[1,256,256]{2,1,0:T(8,128)(2,1)S(1)}, u32[]{:S(2)}, u32[]{:S(2)}) collective-permute-start(bf16[1,256,256]{2,1,0:T(8,128)(2,1)S(1)} %get-tuple-element.48), channel_id=1, source_target_pairs={{16,0},{20,4},{17,1},{21,5},{18,2},{22,6},{19,3},{23,7}} | collective-permute-start | bytes 393224 | tf_op jit(solution)/shard_map/ppermute | solution.py:324
  36.2 6.6 %collective-permute-start.9 = (bf16[3,256,128]{2,1,0:T(8,128)(2,1)}, bf16[3,256,128]{2,1,0:T(8,128)(2,1)S(1)}, u32[]{:S(2)}, u32[]{:S(2)}) collective-permute-start(bf16[3,256,128]{2,1,0:T(8,128)(2,1)} %get-tuple-element.53), channel_id=1, source_target_pairs={{0,2},{1,3},{2,0},{3,1},{4,6},{5,7},{6,4},{7,5},{8,10},{9,11},{10,... | collective-permute-start | bytes 589832 | tf_op jit(solution)/shard_map/ppermute | solution.py:21
  38.0 10.0 %collective-permute-start.11 = (bf16[3,256,256]{2,1,0:T(8,128)(2,1)S(1)}, bf16[3,256,256]{2,1,0:T(8,128)(2,1)S(1)}, u32[]{:S(2)}, u32[]{:S(2)}) collective-permute-start(bf16[3,256,256]{2,1,0:T(8,128)(2,1)S(1)} %get-tuple-element.47.mine), channel_id=1, source_target_pairs={{0,8},{4,12},{8,0},{12,4},{16,24},{20,28},{24,16},{28,20},{1,9},{5... | collective-permute-start | bytes 1179656 | tf_op jit(solution)/shard_map/ppermute | solution.py:21
  39.7 0.7 copy-start.6
  43.8 5.7 %collective-permute-start.10 = (bf16[3,256,128]{2,1,0:T(8,128)(2,1)S(1)}, bf16[3,256,128]{2,1,0:T(8,128)(2,1)S(1)}, u32[]{:S(2)}, u32[]{:S(2)}) collective-permute-start(bf16[3,256,128]{2,1,0:T(8,128)(2,1)S(1)} %add_convert_fusion.mine), channel_id=1, source_target_pairs={{0,4},{4,0},{8,12},{12,8},{16,20},{20,16},{24,28},{28,24},{1,5},{5... | collective-permute-start | bytes 589832 | tf_op jit(solution)/shard_map/ppermute | solution.py:21
  45.3 5.1 %copy-start.1 = (bf16[5,256,256]{2,1,0:T(8,128)(2,1)}, bf16[5,256,256]{2,1,0:T(8,128)(2,1)S(1)}, u32[]{:S(2)}) copy-start(bf16[5,256,256]{2,1,0:T(8,128)(2,1)S(1)} %sort.7.factors) | copy-start | bytes 1966084
  48.0 3.1 %copy-start.4 = (bf16[1,256,256]{2,1,0:T(8,128)(2,1)}, bf16[1,256,256]{2,1,0:T(8,128)(2,1)S(1)}, u32[]{:S(2)}) copy-start(bf16[1,256,256]{2,1,0:T(8,128)(2,1)S(1)} %sort.6.refs_1_) | copy-start | bytes 393220
  50.4 0.6 copy-start.16
  51.0 22.4 %collective-permute-start.13 = (bf16[8,3,256,256]{3,2,1,0:T(8,128)(2,1)}, bf16[8,3,256,256]{3,2,1,0:T(8,128)(2,1)S(1)}, u32[]{:S(2)}, u32[]{:S(2)}) collective-permute-start(bf16[8,3,256,256]{3,2,1,0:T(8,128)(2,1)} %panels.5), channel_id=1, source_target_pairs={{0,1},{1,0},{2,3},{3,2},{4,5},{5,4},{6,7},{7,6},{8,9},{9,8},{10,11... | collective-permute-start | bytes 9437192 | tf_op jit(solution)/shard_map/ppermute | solution.py:21
  51.0 22.3 %collective-permute-start.12 = (bf16[8,256,256]{2,1,0:T(8,128)(2,1)}, bf16[8,256,256]{2,1,0:T(8,128)(2,1)}, u32[]{:S(2)}, u32[]{:S(2)}) collective-permute-start(bf16[8,256,256]{2,1,0:T(8,128)(2,1)} %inv.5), channel_id=1, source_target_pairs={{0,1},{1,0},{2,3},{3,2},{4,5},{5,4},{6,7},{7,6},{8,9},{9,8},{10,11... | collective-permute-start | bytes 3145736 | tf_op jit(solution)/shard_map/ppermute | solution.py:21
  51.5 6.2 %collective-permute-start.14 = (bf16[2,256,128]{2,1,0:T(8,128)(2,1)}, bf16[2,256,128]{2,1,0:T(8,128)(2,1)}, u32[]{:S(2)}, u32[]{:S(2)}) collective-permute-start(bf16[2,256,128]{2,1,0:T(8,128)(2,1)} %get-tuple-element.58.mine), channel_id=1, source_target_pairs={{0,8},{4,12},{8,0},{12,4},{16,24},{20,28},{24,16},{28,20},{1,9},{5... | collective-permute-start | bytes 393224 | tf_op jit(solution)/shard_map/ppermute | solution.py:21
  53.0 0.9 copy-start.5
  53.9 0.9 copy-start.7
  54.8 8.6 %copy-start.17 = (bf16[1,256,128]{2,1,0:T(8,128)(2,1)S(1)}, bf16[1,256,128]{2,1,0:T(8,128)(2,1)}, u32[]{:S(2)}) copy-start(bf16[1,256,128]{2,1,0:T(8,128)(2,1)} %copy-done.16) | copy-start | bytes 196612
  55.0 8.1 %collective-permute-start.18 = (bf16[1,256,128]{2,1,0:T(8,128)(2,1)}, bf16[1,256,128]{2,1,0:T(8,128)(2,1)S(1)}, u32[]{:S(2)}, u32[]{:S(2)}) collective-permute-start(bf16[1,256,128]{2,1,0:T(8,128)(2,1)} %copy-done.16), channel_id=1, source_target_pairs={{0,2},{1,3},{2,0},{3,1},{4,6},{5,7},{6,4},{7,5},{8,10},{9,11},{10,... | collective-permute-start | bytes 196616 | tf_op jit(solution)/shard_map/ppermute | solution.py:21
  56.6 1.1 %copy-start.2 = (bf16[5,256,256]{2,1,0:T(8,128)(2,1)S(1)}, bf16[5,256,256]{2,1,0:T(8,128)(2,1)}, u32[]{:S(2)}) copy-start(bf16[5,256,256]{2,1,0:T(8,128)(2,1)} %copy-done.1) | copy-start | bytes 1966084
  57.7 12.1 %copy-start.3 = (bf16[8,256,256]{2,1,0:T(8,128)(2,1)S(1)}, bf16[8,256,256]{2,1,0:T(8,128)(2,1)}, u32[]{:S(2)}) copy-start(bf16[8,256,256]{2,1,0:T(8,128)(2,1)} %get-tuple-element.73.value) | copy-start | bytes 3145732
  57.7 12.1 %copy-start.15 = (s32[8,3]{1,0:T(8,128)S(1)}, s32[8,3]{1,0:T(8,128)}, u32[]{:S(2)}) copy-start(s32[8,3]{1,0:T(8,128)} %copy-done.14) | copy-start | bytes 292
  59.0 10.2 %collective-permute-start.15 = (bf16[2,256,128]{2,1,0:T(8,128)(2,1)S(1)}, bf16[2,256,128]{2,1,0:T(8,128)(2,1)S(1)}, u32[]{:S(2)}, u32[]{:S(2)}) collective-permute-start(bf16[2,256,128]{2,1,0:T(8,128)(2,1)S(1)} %get-tuple-element.64.own), channel_id=1, source_target_pairs={{0,2},{1,3},{2,0},{3,1},{4,6},{5,7},{6,4},{7,5},{8,10},{9,11},{10,... | collective-permute-start | bytes 393224 | tf_op jit(solution)/shard_map/ppermute | solution.py:21
  59.9 6.5 %collective-permute-start.17 = (bf16[1,256,128]{2,1,0:T(8,128)(2,1)S(1)}, bf16[1,256,128]{2,1,0:T(8,128)(2,1)S(1)}, u32[]{:S(2)}, u32[]{:S(2)}) collective-permute-start(bf16[1,256,128]{2,1,0:T(8,128)(2,1)S(1)} %get-tuple-element.65), channel_id=1, source_target_pairs={{0,18},{1,19},{2,16},{3,17},{4,22},{5,23},{6,20},{7,21},{8,26},{9,... | collective-permute-start | bytes 196616 | tf_op jit(solution)/shard_map/ppermute | solution.py:515
  63.1 6.1 %collective-permute-start.16 = (bf16[1,256,128]{2,1,0:T(8,128)(2,1)S(1)}, bf16[1,256,128]{2,1,0:T(8,128)(2,1)S(1)}, u32[]{:S(2)}, u32[]{:S(2)}) collective-permute-start(bf16[1,256,128]{2,1,0:T(8,128)(2,1)S(1)} %get-tuple-element.65), channel_id=1, source_target_pairs={{0,16},{4,20},{8,24},{12,28},{16,0},{20,4},{24,8},{28,12},{1,17},{... | collective-permute-start | bytes 196616 | tf_op jit(solution)/shard_map/ppermute | solution.py:21
  69.8 3.6 %copy-start = (bf16[8,256,256]{2,1,0:T(8,128)(2,1)S(1)}, bf16[8,256,256]{2,1,0:T(8,128)(2,1)}, u32[]{:S(2)}) copy-start(bf16[8,256,256]{2,1,0:T(8,128)(2,1)} %get-tuple-element.50.value) | copy-start | bytes 3145732
  69.8 3.6 %copy-start.13 = (s32[8,3]{1,0:T(8,128)S(1)}, s32[8,3]{1,0:T(8,128)}, u32[]{:S(2)}) copy-start(s32[8,3]{1,0:T(8,128)} %copy-done.12) | copy-start | bytes 292
  73.1 14.9 %collective-permute-start.21 = (bf16[8,256,128]{2,1,0:T(8,128)(2,1)S(1)}, bf16[8,256,128]{2,1,0:T(8,128)(2,1)S(1)}, u32[]{:S(2)}, u32[]{:S(2)}) collective-permute-start(bf16[8,256,128]{2,1,0:T(8,128)(2,1)S(1)} %solve_far.5), channel_id=1, source_target_pairs={{0,2},{1,3},{2,0},{3,1},{4,6},{5,7},{6,4},{7,5},{8,10},{9,11},{10,... | collective-permute-start | bytes 1572872 | tf_op jit(solution)/shard_map/ppermute | solution.py:21
  75.3 4.0 %copy-start.18 = (s32[5]{0:T(128)S(1)}, s32[5]{0:T(128)}, u32[]{:S(2)}) copy-start(s32[5]{0:T(128)} %stack.23.scalars) | copy-start | bytes 64
  75.3 18.4 %collective-permute-start.20 = (bf16[4,256,128]{2,1,0:T(8,128)(2,1)S(1)}, bf16[4,256,128]{2,1,0:T(8,128)(2,1)S(1)}, u32[]{:S(2)}, u32[]{:S(2)}) collective-permute-start(bf16[4,256,128]{2,1,0:T(8,128)(2,1)S(1)} %solve_far.4), channel_id=1, source_target_pairs={{0,2},{1,3},{2,0},{3,1},{4,6},{5,7},{6,4},{7,5},{8,10},{9,11},{10,... | collective-permute-start | bytes 786440 | tf_op jit(solution)/shard_map/ppermute | solution.py:21
  79.1 18.1 %collective-permute-start.19 = (bf16[4,256,128]{2,1,0:T(8,128)(2,1)S(1)}, bf16[4,256,128]{2,1,0:T(8,128)(2,1)S(1)}, u32[]{:S(2)}, u32[]{:S(2)}) collective-permute-start(bf16[4,256,128]{2,1,0:T(8,128)(2,1)S(1)} %solve_far.3), channel_id=1, source_target_pairs={{0,2},{1,3},{2,0},{3,1},{4,6},{5,7},{6,4},{7,5},{8,10},{9,11},{10,... | collective-permute-start | bytes 786440 | tf_op jit(solution)/shard_map/ppermute | solution.py:21

commit v4 on v3

--- a/solution.py
+++ b/solution.py
@@ -29,15 +29,15 @@
     return pl.CostEstimate(flops=flops, bytes_accessed=moved, transcendentals=0)
 
 
-def forward_kernel(first, last, scalars, ancestors, rhs, far, inv, panels, start, *refs):
-    if last:
-        value, own_total, far_total, solved, held, sems = refs
-    else:
-        value, total, solved, held, sems = refs
+def forward_kernel(own, far, first, scalars, ancestors, *refs):
+    sides = own + far
+    columns_in, (inv, panels, start) = refs[:sides], refs[sides : sides + 3]
+    value, *totals = refs[sides + 3 : -3]
+    solved, held, sems = refs[-3:]
     step, steps = pl.program_id(0), pl.num_programs(0)
     batch, slots = panels.shape[:2]
-    levels, _, both = held.shape
-    cols = both // 2
+    levels = held.shape[0]
+    cols = start.shape[2]
 
     def leaving(leaf):
         return pltpu.make_async_copy(solved.at[leaf], value.at[leaf], sems.at[leaf])
@@ -46,14 +46,16 @@
     def _():
         if first:
             for level in range(levels):
-                held[level, :, :cols] = start[0].astype(F32) * -(scalars[2] == level + 1).astype(F32)
-                held[level, :, cols:] = jnp.zeros((held.shape[1], cols), F32)
+                held[level] = start[0].astype(F32) * -(scalars[2] == level + 1).astype(F32)
         else:
-            held[...] = start[...]
+            held[:, :, :cols] = start[...]
+            if sides == 2:
+                held[:, :, cols:] = jnp.zeros((levels, held.shape[1], cols), F32)
 
     values = []
     for leaf in range(batch):
-        columns = jnp.concatenate([rhs[leaf], far[leaf]], axis=1)
+        columns = [array[leaf] for array in columns_in]
+        columns = jnp.concatenate(columns, axis=1) if sides == 2 else columns[0]
         values.append(dot(inv[leaf], columns).astype(BF16))
         solved[step * batch + leaf] = values[leaf]
         leaving(step * batch + leaf).start()
@@ -70,49 +72,48 @@
 
     @pl.when(step == steps - 1)
     def _():
-        if last:
-            own_total[...] = held[:, :, :cols].astype(BF16)
-            far_total[...] = held[:, :, cols:].astype(BF16)
-        else:
-            total[...] = held[...]
+        for side, total in enumerate(totals):
+            total[...] = held[:, :, side * cols : (side + 1) * cols].astype(total.dtype)
         for leaf in range(solved.shape[0]):
             leaving(leaf).wait()
 
 
-def forward(levels, scalars, which, ancestors, inv, panels, rhs, far, start, first, last):
+def forward(levels, scalars, which, ancestors, inv, panels, rhs, far, start, first, types):
     count, size, _ = inv.shape
-    cols = rhs.shape[2]
+    cols = start.shape[2]
     slots = panels.shape[1]
     batch = min(BATCH, count)
     whole = lambda i, *_: (0, 0, 0)
-    if last:
-        sums = [jax.ShapeDtypeStruct((levels, size, cols), BF16)] * 2
-    else:
-        sums = [jax.ShapeDtypeStruct((levels, size, 2 * cols), F32)]
-    return pl.pallas_call(
-        functools.partial(forward_kernel, first, last),
+    sides = [array for array in (rhs, far) if array is not None]
+    specs = []
+    if rhs is not None:
+        specs.append(pl.BlockSpec((batch, size, cols), lambda i, scalars, _: (scalars[which] // batch + i, 0, 0)))
+    if far is not None:
+        specs.append(pl.BlockSpec((batch, size, cols), lambda i, *_: (i, 0, 0)))
+    sums = [jax.ShapeDtypeStruct((levels, size, cols), kind) for kind in types]
+    return pl.pallas_call(
+        functools.partial(forward_kernel, rhs is not None, far is not None, first),
         grid_spec=pltpu.PrefetchScalarGridSpec(
             num_scalar_prefetch=2,
             grid=(count // batch,),
-            in_specs=[
-                pl.BlockSpec((batch, size, cols), lambda i, scalars, _: (scalars[which] // batch + i, 0, 0)),
-                pl.BlockSpec((batch, size, cols), lambda i, *_: (i, 0, 0)),
+            in_specs=specs
+            + [
                 pl.BlockSpec((batch, size, size), lambda i, *_: (i, 0, 0)),
                 pl.BlockSpec((batch, slots, size, size), lambda i, *_: (i, 0, 0, 0)),
                 pl.BlockSpec(start.shape, whole),
             ],
             out_specs=[pl.BlockSpec(memory_space=pl.ANY)] + [pl.BlockSpec(part.shape, whole) for part in sums],
             scratch_shapes=[
-                pltpu.VMEM((count, size, 2 * cols), BF16),
-                pltpu.VMEM((levels, size, 2 * cols), F32),
+                pltpu.VMEM((count, size, len(sides) * cols), BF16),
+                pltpu.VMEM((levels, size, len(sides) * cols), F32),
                 pltpu.SemaphoreType.DMA((count,)),
             ],
         ),
-        out_shape=[jax.ShapeDtypeStruct((count, size, 2 * cols), BF16)] + sums,
+        out_shape=[jax.ShapeDtypeStruct((count, size, len(sides) * cols), BF16)] + sums,
         compiler_params=pltpu.CompilerParams(vmem_limit_bytes=FORWARD_VMEM),
         cost_estimate=cost(0, 0),
         name="leaf_forward",
-    )(scalars, ancestors, rhs, far, inv, panels, start)
+    )(scalars, ancestors, *sides, inv, panels, start)
 
 
 def solve_leaves(base, step, batch, ancestors, value, inv, panels, paths):
@@ -140,7 +141,7 @@
 
 def solve_far(ancestors, inv, panels, value, paths, base, count):
     levels, size, cols = paths.shape[0], paths.shape[1], paths.shape[2] // 2
-    batch = min(BATCH, count)
+    batch = max(leaves for leaves in range(1, BATCH + 1) if count % leaves == 0 and base % leaves == 0)
     ahead = base // batch
 
     def part(array):
@@ -152,7 +153,7 @@
         grid=(count // batch,),
         in_specs=[
             pl.BlockSpec(memory_space=pltpu.SMEM),
-            pl.BlockSpec((batch, size, cols), lambda i: (ahead + i, 0, 1)),
+            pl.BlockSpec((batch, size, cols), lambda i: (ahead + i, 0, value.shape[2] // cols - 1)),
             part(inv),
             part(panels),
             pl.BlockSpec((levels, size, cols), lambda i: (0, 0, 1)),
@@ -217,13 +218,19 @@
 
 def place_rows(scalars, which, offset, part, whole):
     count, size, cols = part.shape
+    batch = max(leaves for leaves in (8, 4, 2, 1) if count % leaves == 0 and offset % leaves == 0)
     return pl.pallas_call(
         place_kernel,
         grid_spec=pltpu.PrefetchScalarGridSpec(
             num_scalar_prefetch=1,
-            grid=(1,),
-            in_specs=[pl.BlockSpec(part.shape, lambda i, _: (0, 0, 0)), pl.BlockSpec(memory_space=pl.ANY)],
-            out_specs=pl.BlockSpec(part.shape, lambda i, scalars: ((scalars[which] + offset) // count, 0, 0)),
+            grid=(count // batch,),
+            in_specs=[
+                pl.BlockSpec((batch, size, cols), lambda i, _: (i, 0, 0)),
+                pl.BlockSpec(memory_space=pl.ANY),
+            ],
+            out_specs=pl.BlockSpec(
+                (batch, size, cols), lambda i, scalars: ((scalars[which] + offset) // batch + i, 0, 0)
+            ),
         ),
         out_shape=jax.ShapeDtypeStruct(whole.shape, whole.dtype),
         input_output_aliases={2: 0},
@@ -462,20 +469,21 @@
     far_rhs = [swap(part, "col", 2) for part in sent]
 
     near_ancestors = swap(ancestors, "col", 1)
-    near_lower_inv = swap(leaf_lower_inv, "col", 1)
-    near_lower_panels = swap(leaf_lower_panels, "col", 1)
+    near_lower_inv = swap(after(leaf_lower_inv, sent[0]), "col", 1)
+    near_lower_panels = swap(after(leaf_lower_panels, sent[0]), "col", 1)
     local = (ancestors, leaf_lower_inv, leaf_lower_panels)
     near = (near_ancestors, near_lower_inv, near_lower_panels)
 
     blocks, pieces = combine(after(sep_lower_inv, *sent), sep_lower_panels, sep_upper_inv, sep_upper_panels)
 
     start = after(sep_rhs, *near)
-    value_1, total = forward(levels, scalars, 0, *local, leaf_rhs, far_rhs[0], start, True, False)
+    value_2_own, total = forward(levels, scalars, 1, *near, leaf_rhs, None, start, True, [F32])
+    value_1, own_total, total = forward(levels, scalars, 0, *local, leaf_rhs, far_rhs[0], total, False, [BF16, F32])
     arrived = [swap(piece, "leaf", 1) for piece in pieces]
     count_above = blocks.shape[0] - 2
     onward = sort(device % 2, 0, blocks, after(arrived, total), (count_above, 1)) if levels > 1 else []
     total = after(total, *onward)
-    value_2, own_total, far_total = forward(levels, scalars, 1, *near, leaf_rhs, far_rhs[1], total, False, True)
+    value_2_far, far_total = forward(levels, scalars, 1, *near, None, far_rhs[1], total, False, [BF16])
 
     if levels == 3:
         from_top = [from_owners(onward[1], levels, hop) for hop in (4, 6)]
@@ -522,12 +530,14 @@
     local = (ancestors, leaf_upper_inv, leaf_upper_panels)
     near = (near_ancestors, near_upper_inv, near_upper_panels)
     leaf_solution = solve_own(scalars, 0, *local, value_1, paths, rows)
+    quarter = half // 2
     returning = [
-        (3, 0, solve_far(*local, value_1, paths, 0, count)),
-        (4, 0, solve_far(*near, value_2, paths, 0, half)),
-        (4, half, solve_far(*near, value_2, paths, half, half)),
+        (3, 0, solve_far(*local, value_1, paths, 0, count - quarter)),
+        (4, 0, solve_far(*near, value_2_far, paths, 0, half)),
+        (4, half, solve_far(*near, value_2_far, paths, half, half)),
+        (3, count - quarter, solve_far(*local, value_1, paths, count - quarter, quarter)),
     ]
-    leaf_solution = solve_own(scalars, 1, *near, value_2, paths, rows, leaf_solution)
+    leaf_solution = solve_own(scalars, 1, *near, value_2_own, paths, rows, leaf_solution)
     for which, offset, part in returning:
         leaf_solution = place_rows(scalars, which, offset, swap(part, "col", 2), leaf_solution)
     return (leaf_solution, own_solution[None])

time: 98.9 us -> 95 us (0.961)
  waiting for transfers between devices: 29.2 us -> 12.8 us
  Pallas kernels: 34.3 us -> 40.9 us
  local copies, waits for them, and re-layouts: 8.74 us -> 12.2 us
  starting transfers between devices: 23.5 us -> 26.7 us
    ppermute x19 -> x20, waiting for transfers between devices: 26.4 us -> 9.44 us  [swap(): return lax.ppermute(value, axis, pairs)]
    ppermute x19 -> x20, starting transfers between devices: 18.4 us -> 23.4 us  [swap(): return lax.ppermute(value, axis, pairs)]
    pallas_call x2 -> x3, Pallas kernels: 12.5 us -> 17.1 us  [forward(): pl.pallas_call(functools.partial(forward_kernel, rhs is not None, far is...]
    unnamed x43 -> x61, local copies, waits for them, and re-layouts: 4.34 us -> 7.74 us
    ppermute x1, starting transfers between devices: 3.2 us -> 1.3 us  [on_device(): across = lax.ppermute(mine, ('leaf', 'col'), pairs)]
    pallas_call x3 -> x4, Pallas kernels: 7.03 us -> 8.9 us  [solve_far(): pl.pallas_call(functools.partial(send_kernel, base), grid=(count // batch...]
    pallas_call x3 -> x4, Pallas kernels: 3.88 us -> 5.63 us  [place_rows(): pl.pallas_call(place_kernel, grid_spec=pltpu.PrefetchScalarGridSpec(num_s...]
    pallas_call x2, Pallas kernels: 2.1 us -> 0.4 us  [climb(): pl.pallas_call(climb_kernel, in_specs=[vmem] * 3, out_specs=[vmem] * 2, o...]
  transfers between devices with their start and end apart: 22 -> 23, of which waited for: 11 -> 10; matrix products, arithmetic and copies ran while one was open for 6% -> 3% of each run, Pallas kernels for 33% -> 42%
where the time goes in v4:
time: 95 us; the launch traced here: 94.4 us
  Pallas kernels  40.9 us (43%)
  starting transfers between devices  26.7 us (28%)
  waiting for transfers between devices  12.8 us (13%)
  local copies, waits for them, and re-layouts  12.2 us (13%)
  between operations  1.16 us (1%)
    ppermute x20, starting transfers between devices, swap(): return lax.ppermute(value, axis, pairs)  23.4 us
    pallas_call x3, Pallas kernels, forward(): pl.pallas_call(functools.partial(forward_kernel, rhs is not None, far is...  17.1 us
    ppermute x20, waiting for transfers between devices, swap(): return lax.ppermute(value, axis, pairs)  9.44 us
    pallas_call x4, Pallas kernels, solve_far(): pl.pallas_call(functools.partial(send_kernel, base), grid=(count // batch...  8.9 us
    unnamed x61, local copies, waits for them, and re-layouts  7.74 us
    pallas_call x2, Pallas kernels, solve_own(): pl.pallas_call(functools.partial(keep_kernel, which), grid=(count // batc...  7.31 us
    pallas_call x4, Pallas kernels, place_rows(): pl.pallas_call(place_kernel, grid_spec=pltpu.PrefetchScalarGridSpec(num_s...  5.63 us
    ppermute x1, waiting for transfers between devices, on_device(): across = lax.ppermute(mine, ('leaf', 'col'), pairs)  2.66 us
  transfers between devices with their start and end apart: 23, of which 10 were waited for; matrix products, arithmetic and copies ran while one was open for 3% of the time, Pallas kernels for 42%

profile of v4, /device:TPU:0, one launch (start us, length us, event | category | flops | bytes accessed | tf_op | source)
XLA Modules:
  0.0 94.4 jit_solution(16151800052034930469)
XLA Ops:
  0.7 1.9 %constant_dynamic-slice_fusion.1 = bf16[8,256,128]{2,1,0:T(8,128)(2,1)} fusion(bf16[32,256,128]{2,1,0:T(8,128)(2,1)} %refs_0_.3, s32[]{:T(128)S(6)} %select_n.94), kind=kLoop, calls=%fused_computation.5 | loop fusion | bytes 1048580 | tf_op jit(solution)/shard_map/dynamic_slice | solution.py:467
  3.2 3.0 %collective-permute-start = (bf16[8,256,128]{2,1,0:T(8,128)(2,1)}, bf16[8,256,128]{2,1,0:T(8,128)(2,1)}, u32[]{:S(2)}, u32[]{:S(2)}) collective-permute-start(bf16[8,256,128]{2,1,0:T(8,128)(2,1)} %constant_dynamic-slice_fusion.1), channel_id=1, source_target_pairs={{0,2},{1,3},{2,0},{3,1},{4,6},{5,7},{6,4},{7,5},{8,10},{9,11},{10,... | collective-permute-start | bytes 1572872 | tf_op jit(solution)/shard_map/ppermute | solution.py:21
  6.1 1.9 %constant_dynamic-slice_fusion = bf16[8,256,128]{2,1,0:T(8,128)(2,1)} fusion(bf16[32,256,128]{2,1,0:T(8,128)(2,1)} %refs_0_.3, s32[]{:T(128)S(6)} %select_n.95), kind=kLoop, calls=%fused_computation.4 | loop fusion | bytes 1048580 | tf_op jit(solution)/shard_map/dynamic_slice | solution.py:468
  8.4 1.6 %collective-permute-start.5 = (bf16[3,256,256]{2,1,0:T(8,128)(2,1)S(1)}, bf16[3,256,256]{2,1,0:T(8,128)(2,1)S(1)}, u32[]{:S(2)}, u32[]{:S(2)}) collective-permute-start(bf16[3,256,256]{2,1,0:T(8,128)(2,1)S(1)} %get-tuple-element.52), channel_id=1, source_target_pairs={{0,4},{4,0},{8,12},{12,8},{16,20},{20,16},{24,28},{28,24},{1,5},{5... | collective-permute-start | bytes 1179656 | tf_op jit(solution)/shard_map/ppermute | solution.py:21
  10.0 1.2 %collective-permute-done.1.ancestors = s32[8,3]{1,0:T(8,128)S(1)} collective-permute-done((s32[8,3]{1,0:T(8,128)S(1)}, s32[8,3]{1,0:T(8,128)S(1)}, u32[]{:S(2)}, u32[]{:S(2)}) %collective-permute-start.1) | collective-permute-done | bytes 128 | tf_op jit(solution)/shard_map/ppermute | solution.py:21
  11.2 1.6 %collective-permute-start.4 = (bf16[8,256,128]{2,1,0:T(8,128)(2,1)}, bf16[8,256,128]{2,1,0:T(8,128)(2,1)}, u32[]{:S(2)}, u32[]{:S(2)}) collective-permute-start(bf16[8,256,128]{2,1,0:T(8,128)(2,1)} %constant_dynamic-slice_fusion), channel_id=1, source_target_pairs={{0,2},{1,3},{2,0},{3,1},{4,6},{5,7},{6,4},{7,5},{8,10},{9,11},{10,... | collective-permute-start | bytes 1572872 | tf_op jit(solution)/shard_map/ppermute | solution.py:21
  12.8 1.5 %collective-permute-start.6 = (bf16[2,256,256]{2,1,0:T(8,128)(2,1)S(1)}, bf16[2,256,256]{2,1,0:T(8,128)(2,1)S(1)}, u32[]{:S(2)}, u32[]{:S(2)}) collective-permute-start(bf16[2,256,256]{2,1,0:T(8,128)(2,1)S(1)} %get-tuple-element.53), channel_id=1, source_target_pairs={{0,4},{4,0},{8,12},{12,8},{16,20},{20,16},{24,28},{28,24},{1,5},{5... | collective-permute-start | bytes 786440 | tf_op jit(solution)/shard_map/ppermute | solution.py:21
  14.9 5.4 %leaf_forward.3 = (bf16[8,256,128]{2,1,0:T(8,128)(2,1)}, f32[3,256,128]{2,1,0:T(8,128)}) custom-call(s32[5]{0:T(128)} %stack.23.scalars, s32[8,3]{1,0:T(8,128)} %copy-done.24, bf16[32,256,128]{2,1,0:T(8,128)(2,1)} %refs_0_.3, bf16[8,256,256]{2,1,0:T(8,128)(2,1)} %copy-done.27, bf16[8,3,256,256]{3,2,1,0:T(8,128)(2,1)} %collective-permute-done.3.refs_2_, ...), custom_call_target="tpu_custom_call" | custom-call | tf_op jit(solution)/shard_map/leaf_forward/pallas_call | solution.py:94
  20.4 6.2 %leaf_forward.4 = (bf16[8,256,256]{2,1,0:T(8,128)(2,1)}, bf16[3,256,128]{2,1,0:T(8,128)(2,1)}, f32[3,256,128]{2,1,0:T(8,128)}) custom-call(s32[5]{0:T(128)} %stack.23.scalars, s32[8,3]{1,0:T(8,128)} %copy-done.22, bf16[32,256,128]{2,1,0:T(8,128)(2,1)} %refs_0_.3, bf16[8,256,128]{2,1,0:T(8,128)(2,1)} %collective-permute-done.refs_1_, ...), custom_call_target="tpu_custom_call" | custom-call | tf_op jit(solution)/shard_map/leaf_forward/pallas_call | solution.py:94
  26.7 1.3 %collective-permute-start.7 = (bf16[1,256,256]{2,1,0:T(8,128)(2,1)S(1)}, bf16[1,256,256]{2,1,0:T(8,128)(2,1)S(1)}, u32[]{:S(2)}, u32[]{:S(2)}) collective-permute-start(bf16[1,256,256]{2,1,0:T(8,128)(2,1)S(1)} %get-tuple-element.57), channel_id=1, source_target_pairs={{16,0},{20,4},{17,1},{21,5},{18,2},{22,6},{19,3},{23,7}} | collective-permute-start | bytes 393224 | tf_op jit(solution)/shard_map/ppermute | solution.py:331
  28.0 0.7 collective-permute-start.8
  28.7 1.1 %collective-permute-done.4.refs_0_ = bf16[8,256,128]{2,1,0:T(8,128)(2,1)} collective-permute-done((bf16[8,256,128]{2,1,0:T(8,128)(2,1)}, bf16[8,256,128]{2,1,0:T(8,128)(2,1)}, u32[]{:S(2)}, u32[]{:S(2)}) %collective-permute-start.4) | collective-permute-done | bytes 524320 | tf_op jit(solution)/shard_map/ppermute | solution.py:21
  29.8 5.5 %leaf_forward.5 = (bf16[8,256,128]{2,1,0:T(8,128)(2,1)}, bf16[3,256,128]{2,1,0:T(8,128)(2,1)}) custom-call(s32[5]{0:T(128)} %stack.23.scalars, s32[8,3]{1,0:T(8,128)} %copy-done.24, bf16[8,256,128]{2,1,0:T(8,128)(2,1)} %collective-permute-done.4.refs_0_, bf16[8,256,256]{2,1,0:T(8,128)(2,1)} %copy-done.27, ...), custom_call_target="tpu_custom_call" | custom-call | tf_op jit(solution)/shard_map/leaf_forward/pallas_call | solution.py:94
  35.3 0.6 collective-permute-done.7.refs_0_
  35.9 1.2 %collective-permute-start.9 = (bf16[3,256,128]{2,1,0:T(8,128)(2,1)}, bf16[3,256,128]{2,1,0:T(8,128)(2,1)S(1)}, u32[]{:S(2)}, u32[]{:S(2)}) collective-permute-start(bf16[3,256,128]{2,1,0:T(8,128)(2,1)} %get-tuple-element.60), channel_id=1, source_target_pairs={{0,2},{1,3},{2,0},{3,1},{4,6},{5,7},{6,4},{7,5},{8,10},{9,11},{10,... | collective-permute-start | bytes 589832 | tf_op jit(solution)/shard_map/ppermute | solution.py:21
  37.1 1.6 %collective-permute-start.11 = (bf16[3,256,256]{2,1,0:T(8,128)(2,1)S(1)}, bf16[3,256,256]{2,1,0:T(8,128)(2,1)S(1)}, u32[]{:S(2)}, u32[]{:S(2)}) collective-permute-start(bf16[3,256,256]{2,1,0:T(8,128)(2,1)S(1)} %get-tuple-element.56.mine), channel_id=1, source_target_pairs={{0,8},{4,12},{8,0},{12,4},{16,24},{20,28},{24,16},{28,20},{1,9},{5... | collective-permute-start | bytes 1179656 | tf_op jit(solution)/shard_map/ppermute | solution.py:21
  39.5 2.4 %collective-permute-done.9 = bf16[3,256,128]{2,1,0:T(8,128)(2,1)S(1)} collective-permute-done((bf16[3,256,128]{2,1,0:T(8,128)(2,1)}, bf16[3,256,128]{2,1,0:T(8,128)(2,1)S(1)}, u32[]{:S(2)}, u32[]{:S(2)}) %collective-permute-start.9) | collective-permute-done | bytes 196640 | tf_op jit(solution)/shard_map/ppermute | solution.py:21
  41.9 1.5 %collective-permute-start.10 = (bf16[3,256,128]{2,1,0:T(8,128)(2,1)S(1)}, bf16[3,256,128]{2,1,0:T(8,128)(2,1)S(1)}, u32[]{:S(2)}, u32[]{:S(2)}) collective-permute-start(bf16[3,256,128]{2,1,0:T(8,128)(2,1)S(1)} %add_convert_fusion.mine), channel_id=1, source_target_pairs={{0,4},{4,0},{8,12},{12,8},{16,20},{20,16},{24,28},{28,24},{1,5},{5... | collective-permute-start | bytes 589832 | tf_op jit(solution)/shard_map/ppermute | solution.py:21
  43.4 1.1 %copy-done.5 = bf16[5,256,256]{2,1,0:T(8,128)(2,1)S(1)} copy-done((bf16[5,256,256]{2,1,0:T(8,128)(2,1)S(1)}, bf16[5,256,256]{2,1,0:T(8,128)(2,1)}, u32[]{:S(2)}) %copy-start.5) | copy-done | bytes 655384
  44.5 1.0 %copy-done.8 = bf16[3,256,256]{2,1,0:T(8,128)(2,1)S(1)} copy-done((bf16[3,256,256]{2,1,0:T(8,128)(2,1)S(1)}, bf16[3,256,256]{2,1,0:T(8,128)(2,1)}, u32[]{:S(2)}) %copy-start.8) | copy-done | bytes 393240
  45.4 0.9 %copy-done.12 = bf16[2,256,256]{2,1,0:T(8,128)(2,1)S(1)} copy-done((bf16[2,256,256]{2,1,0:T(8,128)(2,1)S(1)}, bf16[2,256,256]{2,1,0:T(8,128)(2,1)}, u32[]{:S(2)}) %copy-start.12) | copy-done | bytes 262168
  48.5 1.9 %collective-permute-start.12 = (bf16[2,256,128]{2,1,0:T(8,128)(2,1)S(1)}, bf16[2,256,128]{2,1,0:T(8,128)(2,1)S(1)}, u32[]{:S(2)}, u32[]{:S(2)}) collective-permute-start(bf16[2,256,128]{2,1,0:T(8,128)(2,1)S(1)} %get-tuple-element.65.mine), channel_id=1, source_target_pairs={{0,8},{4,12},{8,0},{12,4},{16,24},{20,28},{24,16},{28,20},{1,9},{5... | collective-permute-start | bytes 393224 | tf_op jit(solution)/shard_map/ppermute | solution.py:21
  50.4 0.9 copy-done.15
  51.3 0.9 copy-done.17
  52.4 1.1 %collective-permute-start.16 = (bf16[1,256,128]{2,1,0:T(8,128)(2,1)S(1)}, bf16[1,256,128]{2,1,0:T(8,128)(2,1)S(1)}, u32[]{:S(2)}, u32[]{:S(2)}) collective-permute-start(bf16[1,256,128]{2,1,0:T(8,128)(2,1)S(1)} %get-tuple-element.74.refs_2_), channel_id=1, source_target_pairs={{0,2},{1,3},{2,0},{3,1},{4,6},{5,7},{6,4},{7,5},{8,10},{9,11},{10,... | collective-permute-start | bytes 196616 | tf_op jit(solution)/shard_map/ppermute | solution.py:21
  53.5 1.1 %copy-done.3 = bf16[5,256,256]{2,1,0:T(8,128)(2,1)S(1)} copy-done((bf16[5,256,256]{2,1,0:T(8,128)(2,1)S(1)}, bf16[5,256,256]{2,1,0:T(8,128)(2,1)}, u32[]{:S(2)}) %copy-start.3) | copy-done | bytes 655384
  54.6 1.0 %copy-done.10 = bf16[3,256,256]{2,1,0:T(8,128)(2,1)S(1)} copy-done((bf16[3,256,256]{2,1,0:T(8,128)(2,1)S(1)}, bf16[3,256,256]{2,1,0:T(8,128)(2,1)}, u32[]{:S(2)}) %copy-start.10) | copy-done | bytes 393240
  55.9 1.0 %collective-permute-start.13 = (bf16[2,256,128]{2,1,0:T(8,128)(2,1)S(1)}, bf16[2,256,128]{2,1,0:T(8,128)(2,1)S(1)}, u32[]{:S(2)}, u32[]{:S(2)}) collective-permute-start(bf16[2,256,128]{2,1,0:T(8,128)(2,1)S(1)} %get-tuple-element.69.own), channel_id=1, source_target_pairs={{0,2},{1,3},{2,0},{3,1},{4,6},{5,7},{6,4},{7,5},{8,10},{9,11},{10,... | collective-permute-start | bytes 393224 | tf_op jit(solution)/shard_map/ppermute | solution.py:21
  56.9 2.1 %collective-permute-start.14 = (bf16[1,256,128]{2,1,0:T(8,128)(2,1)S(1)}, bf16[1,256,128]{2,1,0:T(8,128)(2,1)S(1)}, u32[]{:S(2)}, u32[]{:S(2)}) collective-permute-start(bf16[1,256,128]{2,1,0:T(8,128)(2,1)S(1)} %get-tuple-element.70), channel_id=1, source_target_pairs={{0,16},{4,20},{8,24},{12,28},{16,0},{20,4},{24,8},{28,12},{1,17},{... | collective-permute-start | bytes 196616 | tf_op jit(solution)/shard_map/ppermute | solution.py:21
  59.0 1.3 %collective-permute-start.15 = (bf16[1,256,128]{2,1,0:T(8,128)(2,1)S(1)}, bf16[1,256,128]{2,1,0:T(8,128)(2,1)S(1)}, u32[]{:S(2)}, u32[]{:S(2)}) collective-permute-start(bf16[1,256,128]{2,1,0:T(8,128)(2,1)S(1)} %get-tuple-element.70), channel_id=1, source_target_pairs={{0,18},{1,19},{2,16},{3,17},{4,22},{5,23},{6,20},{7,21},{8,26},{9,... | collective-permute-start | bytes 196616 | tf_op jit(solution)/shard_map/ppermute | solution.py:523
  60.4 2.9 %collective-permute-done.14.theirs = bf16[1,256,128]{2,1,0:T(8,128)(2,1)S(1)} collective-permute-done((bf16[1,256,128]{2,1,0:T(8,128)(2,1)S(1)}, bf16[1,256,128]{2,1,0:T(8,128)(2,1)S(1)}, u32[]{:S(2)}, u32[]{:S(2)}) %collective-permute-start.14) | collective-permute-done | bytes 65568 | tf_op jit(solution)/shard_map/ppermute | solution.py:21
  63.3 2.7 %collective-permute-done.15.across = bf16[1,256,128]{2,1,0:T(8,128)(2,1)S(1)} collective-permute-done((bf16[1,256,128]{2,1,0:T(8,128)(2,1)S(1)}, bf16[1,256,128]{2,1,0:T(8,128)(2,1)S(1)}, u32[]{:S(2)}, u32[]{:S(2)}) %collective-permute-start.15) | collective-permute-done | bytes 65568 | tf_op jit(solution)/shard_map/ppermute | solution.py:523
  66.6 2.7 %solve_far.7 = bf16[6,256,128]{2,1,0:T(8,128)(2,1)S(1)} custom-call(s32[8,3]{1,0:T(8,128)S(1)} %copy-done.23, bf16[8,256,256]{2,1,0:T(8,128)(2,1)S(1)} %copy-done.1, bf16[8,256,256]{2,1,0:T(8,128)(2,1)} %inv.5, bf16[8,3,256,256]{3,2,1,0:T(8,128)(2,1)S(1)} %copy-done, bf16[3,256,256]{2,1,0:T(8,128)(2,1)S(1)} %descend.1.paths), custom_call_target="tpu_custom_call" | custom-call | tf_op jit(solution)/shard_map/solve_far/pallas_call | solution.py:151
  69.3 1.3 %collective-permute-start.22 = (bf16[6,256,128]{2,1,0:T(8,128)(2,1)S(1)}, bf16[6,256,128]{2,1,0:T(8,128)(2,1)S(1)}, u32[]{:S(2)}, u32[]{:S(2)}) collective-permute-start(bf16[6,256,128]{2,1,0:T(8,128)(2,1)S(1)} %solve_far.7), channel_id=1, source_target_pairs={{0,2},{1,3},{2,0},{3,1},{4,6},{5,7},{6,4},{7,5},{8,10},{9,11},{10,... | collective-permute-start | bytes 1179656 | tf_op jit(solution)/shard_map/ppermute | solution.py:21
  70.6 2.4 %solve_far.6 = bf16[4,256,128]{2,1,0:T(8,128)(2,1)S(1)} custom-call(s32[8,3]{1,0:T(8,128)S(1)} %copy-done.25, bf16[8,256,128]{2,1,0:T(8,128)(2,1)S(1)} %copy-done.6, bf16[8,256,256]{2,1,0:T(8,128)(2,1)} %collective-permute-done.18.inv, bf16[8,3,256,256]{3,2,1,0:T(8,128)(2,1)} %collective-permute-done.19.panels, bf16[3,256,256]{2,1,0:T(8,128)(2,1)S(1)} %descend.1.paths), custom_call_target="tpu_custom_call" | custom-call | tf_op jit(solution)/shard_map/solve_far/pallas_call | solution.py:151
  73.0 0.9 collective-permute-start.21
  73.8 2.4 %solve_far.5 = bf16[4,256,128]{2,1,0:T(8,128)(2,1)S(1)} custom-call(s32[8,3]{1,0:T(8,128)S(1)} %copy-done.25, bf16[8,256,128]{2,1,0:T(8,128)(2,1)S(1)} %copy-done.6, bf16[8,256,256]{2,1,0:T(8,128)(2,1)} %collective-permute-done.18.inv, bf16[8,3,256,256]{3,2,1,0:T(8,128)(2,1)} %collective-permute-done.19.panels, bf16[3,256,256]{2,1,0:T(8,128)(2,1)S(1)} %descend.1.paths), custom_call_target="tpu_custom_call" | custom-call | tf_op jit(solution)/shard_map/solve_far/pallas_call | solution.py:151
  76.2 1.3 %collective-permute-start.20 = (bf16[4,256,128]{2,1,0:T(8,128)(2,1)S(1)}, bf16[4,256,128]{2,1,0:T(8,128)(2,1)S(1)}, u32[]{:S(2)}, u32[]{:S(2)}) collective-permute-start(bf16[4,256,128]{2,1,0:T(8,128)(2,1)S(1)} %solve_far.5), channel_id=1, source_target_pairs={{0,2},{1,3},{2,0},{3,1},{4,6},{5,7},{6,4},{7,5},{8,10},{9,11},{10,... | collective-permute-start | bytes 786440 | tf_op jit(solution)/shard_map/ppermute | solution.py:21
  77.5 1.5 %solve_far.4 = bf16[2,256,128]{2,1,0:T(8,128)(2,1)S(1)} custom-call(s32[8,3]{1,0:T(8,128)S(1)} %copy-done.23, bf16[8,256,256]{2,1,0:T(8,128)(2,1)S(1)} %copy-done.1, bf16[8,256,256]{2,1,0:T(8,128)(2,1)} %inv.5, bf16[8,3,256,256]{3,2,1,0:T(8,128)(2,1)S(1)} %copy-done, bf16[3,256,256]{2,1,0:T(8,128)(2,1)S(1)} %descend.1.paths), custom_call_target="tpu_custom_call" | custom-call | tf_op jit(solution)/shard_map/solve_far/pallas_call | solution.py:151
  79.0 3.4 %solve_own.2.refs_0_ = bf16[32,256,128]{2,1,0:T(8,128)(2,1)} custom-call(s32[5]{0:T(128)S(1)} %copy-done.26, s32[8,3]{1,0:T(8,128)S(1)} %copy-done.23, bf16[8,256,256]{2,1,0:T(8,128)(2,1)S(1)} %copy-done.1, bf16[8,256,256]{2,1,0:T(8,128)(2,1)} %inv.5, bf16[8,3,256,256]{3,2,1,0:T(8,128)(2,1)S(1)} %copy-done, bf16[3,256,256]{2,1,0:T(8,128)(2,1)S(1)} %descend.1.paths), custom_call_target="tpu_custom_call" | custom-call | tf_op jit(solution)/shard_map/solve_own/pallas_call | solution.py:193
  82.5 0.9 collective-permute-start.17
  83.3 0.6 fusion.1
  84.0 3.9 %solve_own.3.whole = bf16[32,256,128]{2,1,0:T(8,128)(2,1)} custom-call(s32[5]{0:T(128)S(1)} %copy-done.26, s32[8,3]{1,0:T(8,128)S(1)} %copy-done.25, bf16[8,256,128]{2,1,0:T(8,128)(2,1)S(1)} %copy-done.13, bf16[8,256,256]{2,1,0:T(8,128)(2,1)} %collective-permute-done.18.inv, ...), custom_call_target="tpu_custom_call", output_to_operand_aliasing={{}: (6, {})} | custom-call | tf_op jit(solution)/shard_map/solve_own/pallas_call | solution.py:193
  87.9 1.9 %place_rows.4.whole = bf16[32,256,128]{2,1,0:T(8,128)(2,1)} custom-call(s32[5]{0:T(128)S(1)} %copy-done.26, bf16[6,256,128]{2,1,0:T(8,128)(2,1)S(1)} %collective-permute-done.22.part, bf16[32,256,128]{2,1,0:T(8,128)(2,1)} %solve_own.3.whole), custom_call_target="tpu_custom_call", output_to_operand_aliasing={{}: (2, {})} | custom-call | tf_op jit(solution)/shard_map/place_rows/pallas_call | solution.py:222
  89.8 1.3 %place_rows.5.whole = bf16[32,256,128]{2,1,0:T(8,128)(2,1)} custom-call(s32[5]{0:T(128)S(1)} %copy-done.26, bf16[4,256,128]{2,1,0:T(8,128)(2,1)S(1)} %collective-permute-done.21.part, bf16[32,256,128]{2,1,0:T(8,128)(2,1)} %place_rows.4.whole), custom_call_target="tpu_custom_call", output_to_operand_aliasing={{}: (2, {})} | custom-call | tf_op jit(solution)/shard_map/place_rows/pallas_call | solution.py:222
  91.1 0.7 collective-permute-done.20.part
  91.8 1.3 %place_rows.6.whole = bf16[32,256,128]{2,1,0:T(8,128)(2,1)} custom-call(s32[5]{0:T(128)S(1)} %copy-done.26, bf16[4,256,128]{2,1,0:T(8,128)(2,1)S(1)} %collective-permute-done.20.part, bf16[32,256,128]{2,1,0:T(8,128)(2,1)} %place_rows.5.whole), custom_call_target="tpu_custom_call", output_to_operand_aliasing={{}: (2, {})} | custom-call | tf_op jit(solution)/shard_map/place_rows/pallas_call | solution.py:222
  93.2 1.2 %place_rows.7 = bf16[32,256,128]{2,1,0:T(8,128)(2,1)} custom-call(s32[5]{0:T(128)S(1)} %copy-done.26, bf16[2,256,128]{2,1,0:T(8,128)(2,1)S(1)} %collective-permute-done.17.part, bf16[32,256,128]{2,1,0:T(8,128)(2,1)} %place_rows.6.whole), custom_call_target="tpu_custom_call", output_to_operand_aliasing={{}: (2, {})} | custom-call | tf_op jit(solution)/shard_map/place_rows/pallas_call | solution.py:222
  (89 shorter events, 5.8 us)
Async XLA Ops:
  0.6 7.4 %copy-start.20 = (bf16[1,256,256]{2,1,0:T(8,128)(2,1)S(1)}, bf16[1,256,256]{2,1,0:T(8,128)(2,1)}, u32[]{:S(2)}) copy-start(bf16[1,256,256]{2,1,0:T(8,128)(2,1)} %lower_inv) | copy-start | bytes 393220
  0.6 7.4 %copy-start.18 = (bf16[1,2,256,256]{3,2,1,0:T(8,128)(2,1)S(1)}, bf16[1,2,256,256]{3,2,1,0:T(8,128)(2,1)}, u32[]{:S(2)}) copy-start(bf16[1,2,256,256]{3,2,1,0:T(8,128)(2,1)} %lower_panels.1) | copy-start | bytes 786436
  0.7 7.4 %copy-start.21 = (bf16[1,256,256]{2,1,0:T(8,128)(2,1)S(1)}, bf16[1,256,256]{2,1,0:T(8,128)(2,1)}, u32[]{:S(2)}) copy-start(bf16[1,256,256]{2,1,0:T(8,128)(2,1)} %upper_inv.1) | copy-start | bytes 393220
  0.7 7.4 %copy-start.19 = (bf16[1,2,256,256]{3,2,1,0:T(8,128)(2,1)S(1)}, bf16[1,2,256,256]{3,2,1,0:T(8,128)(2,1)}, u32[]{:S(2)}) copy-start(bf16[1,2,256,256]{3,2,1,0:T(8,128)(2,1)} %upper_panels.1) | copy-start | bytes 786436
  0.7 9.3 %copy-start.29 = (s32[8,3]{0,1:T(4,128)S(1)}, s32[8,3]{0,1:T(4,128)}, u32[]{:S(2)}) copy-start(s32[8,3]{0,1:T(4,128)} %param.16) | copy-start | bytes 292
  2.6 12.3 %collective-permute-start.3 = (bf16[8,3,256,256]{3,2,1,0:T(8,128)(2,1)}, bf16[8,3,256,256]{3,2,1,0:T(8,128)(2,1)}, u32[]{:S(2)}, u32[]{:S(2)}) collective-permute-start(bf16[8,3,256,256]{3,2,1,0:T(8,128)(2,1)} %refs_3_.2), channel_id=1, source_target_pairs={{0,1},{1,0},{2,3},{3,2},{4,5},{5,4},{6,7},{7,6},{8,9},{9,8},{10,11... | collective-permute-start | bytes 9437192 | tf_op jit(solution)/shard_map/ppermute | solution.py:21
  3.1 9.7 %collective-permute-start.2 = (bf16[8,256,256]{2,1,0:T(8,128)(2,1)}, bf16[8,256,256]{2,1,0:T(8,128)(2,1)S(1)}, u32[]{:S(2)}, u32[]{:S(2)}) collective-permute-start(bf16[8,256,256]{2,1,0:T(8,128)(2,1)} %refs_2_.1), channel_id=1, source_target_pairs={{0,1},{1,0},{2,3},{3,2},{4,5},{5,4},{6,7},{7,6},{8,9},{9,8},{10,11... | collective-permute-start | bytes 3145736 | tf_op jit(solution)/shard_map/ppermute | solution.py:21
  3.2 17.2 %collective-permute-start = (bf16[8,256,128]{2,1,0:T(8,128)(2,1)}, bf16[8,256,128]{2,1,0:T(8,128)(2,1)}, u32[]{:S(2)}, u32[]{:S(2)}) collective-permute-start(bf16[8,256,128]{2,1,0:T(8,128)(2,1)} %constant_dynamic-slice_fusion.1), channel_id=1, source_target_pairs={{0,2},{1,3},{2,0},{3,1},{4,6},{5,7},{6,4},{7,5},{8,10},{9,11},{10,... | collective-permute-start | bytes 1572872 | tf_op jit(solution)/shard_map/ppermute | solution.py:21
  8.4 18.3 %copy-start.4 = (bf16[5,256,256]{2,1,0:T(8,128)(2,1)}, bf16[5,256,256]{2,1,0:T(8,128)(2,1)S(1)}, u32[]{:S(2)}) copy-start(bf16[5,256,256]{2,1,0:T(8,128)(2,1)S(1)} %get-tuple-element.51.mine) | copy-start | bytes 1966084
  8.4 18.3 %collective-permute-start.5 = (bf16[3,256,256]{2,1,0:T(8,128)(2,1)S(1)}, bf16[3,256,256]{2,1,0:T(8,128)(2,1)S(1)}, u32[]{:S(2)}, u32[]{:S(2)}) collective-permute-start(bf16[3,256,256]{2,1,0:T(8,128)(2,1)S(1)} %get-tuple-element.52), channel_id=1, source_target_pairs={{0,4},{4,0},{8,12},{12,8},{16,20},{20,16},{24,28},{28,24},{1,5},{5... | collective-permute-start | bytes 1179656 | tf_op jit(solution)/shard_map/ppermute | solution.py:21
  10.0 10.3 %copy-start.22 = (s32[8,3]{1,0:T(8,128)}, s32[8,3]{1,0:T(8,128)S(1)}, u32[]{:S(2)}) copy-start(s32[8,3]{1,0:T(8,128)S(1)} %copy.20.ancestors) | copy-start | bytes 292
  10.0 1.2 %collective-permute-start.1 = (s32[8,3]{1,0:T(8,128)S(1)}, s32[8,3]{1,0:T(8,128)S(1)}, u32[]{:S(2)}, u32[]{:S(2)}) collective-permute-start(s32[8,3]{1,0:T(8,128)S(1)} %copy.20.ancestors), channel_id=1, source_target_pairs={{0,1},{1,0},{2,3},{3,2},{4,5},{5,4},{6,7},{7,6},{8,9},{9,8},{10,11... | collective-permute-start | bytes 296 | tf_op jit(solution)/shard_map/ppermute | solution.py:21
  11.2 3.7 %copy-start.24 = (s32[8,3]{1,0:T(8,128)}, s32[8,3]{1,0:T(8,128)S(1)}, u32[]{:S(2)}) copy-start(s32[8,3]{1,0:T(8,128)S(1)} %collective-permute-done.1.ancestors) | copy-start | bytes 292
  11.2 18.6 %collective-permute-start.4 = (bf16[8,256,128]{2,1,0:T(8,128)(2,1)}, bf16[8,256,128]{2,1,0:T(8,128)(2,1)}, u32[]{:S(2)}, u32[]{:S(2)}) collective-permute-start(bf16[8,256,128]{2,1,0:T(8,128)(2,1)} %constant_dynamic-slice_fusion), channel_id=1, source_target_pairs={{0,2},{1,3},{2,0},{3,1},{4,6},{5,7},{6,4},{7,5},{8,10},{9,11},{10,... | collective-permute-start | bytes 1572872 | tf_op jit(solution)/shard_map/ppermute | solution.py:21
  12.8 2.1 %copy-start.27 = (bf16[8,256,256]{2,1,0:T(8,128)(2,1)}, bf16[8,256,256]{2,1,0:T(8,128)(2,1)S(1)}, u32[]{:S(2)}) copy-start(bf16[8,256,256]{2,1,0:T(8,128)(2,1)S(1)} %collective-permute-done.2.refs_1_) | copy-start | bytes 3145732
  12.8 13.8 %collective-permute-start.6 = (bf16[2,256,256]{2,1,0:T(8,128)(2,1)S(1)}, bf16[2,256,256]{2,1,0:T(8,128)(2,1)S(1)}, u32[]{:S(2)}, u32[]{:S(2)}) collective-permute-start(bf16[2,256,256]{2,1,0:T(8,128)(2,1)S(1)} %get-tuple-element.53), channel_id=1, source_target_pairs={{0,4},{4,0},{8,12},{12,8},{16,20},{20,16},{24,28},{28,24},{1,5},{5... | collective-permute-start | bytes 786440 | tf_op jit(solution)/shard_map/ppermute | solution.py:21
  26.6 8.6 %copy-start.11 = (bf16[2,256,256]{2,1,0:T(8,128)(2,1)}, bf16[2,256,256]{2,1,0:T(8,128)(2,1)S(1)}, u32[]{:S(2)}) copy-start(bf16[2,256,256]{2,1,0:T(8,128)(2,1)S(1)} %collective-permute-done.6.refs_1_) | copy-start | bytes 786436
  26.7 8.6 %copy-start.7 = (bf16[3,256,256]{2,1,0:T(8,128)(2,1)}, bf16[3,256,256]{2,1,0:T(8,128)(2,1)S(1)}, u32[]{:S(2)}) copy-start(bf16[3,256,256]{2,1,0:T(8,128)(2,1)S(1)} %collective-permute-done.5.refs_0_) | copy-start | bytes 1179652
  26.7 9.2 %collective-permute-start.7 = (bf16[1,256,256]{2,1,0:T(8,128)(2,1)S(1)}, bf16[1,256,256]{2,1,0:T(8,128)(2,1)S(1)}, u32[]{:S(2)}, u32[]{:S(2)}) collective-permute-start(bf16[1,256,256]{2,1,0:T(8,128)(2,1)S(1)} %get-tuple-element.57), channel_id=1, source_target_pairs={{16,0},{20,4},{17,1},{21,5},{18,2},{22,6},{19,3},{23,7}} | collective-permute-start | bytes 393224 | tf_op jit(solution)/shard_map/ppermute | solution.py:331
  28.0 7.9 %collective-permute-start.8 = (bf16[1,256,256]{2,1,0:T(8,128)(2,1)S(1)}, bf16[1,256,256]{2,1,0:T(8,128)(2,1)S(1)}, u32[]{:S(2)}, u32[]{:S(2)}) collective-permute-start(bf16[1,256,256]{2,1,0:T(8,128)(2,1)S(1)} %get-tuple-element.57), channel_id=1, source_target_pairs={{16,8},{20,12},{17,9},{21,13},{18,10},{22,14},{19,11},{23,15}} | collective-permute-start | bytes 393224 | tf_op jit(solution)/shard_map/ppermute | solution.py:331
  28.7 13.1 %copy-start.28 = (bf16[3,256,128]{2,1,0:T(8,128)(2,1)S(1)}, bf16[3,256,128]{2,1,0:T(8,128)(2,1)}, u32[]{:S(2)}) copy-start(bf16[3,256,128]{2,1,0:T(8,128)(2,1)} %get-tuple-element.47) | copy-start | bytes 589828
  35.9 5.9 %collective-permute-start.9 = (bf16[3,256,128]{2,1,0:T(8,128)(2,1)}, bf16[3,256,128]{2,1,0:T(8,128)(2,1)S(1)}, u32[]{:S(2)}, u32[]{:S(2)}) collective-permute-start(bf16[3,256,128]{2,1,0:T(8,128)(2,1)} %get-tuple-element.60), channel_id=1, source_target_pairs={{0,2},{1,3},{2,0},{3,1},{4,6},{5,7},{6,4},{7,5},{8,10},{9,11},{10,... | collective-permute-start | bytes 589832 | tf_op jit(solution)/shard_map/ppermute | solution.py:21
  37.1 9.9 %collective-permute-start.11 = (bf16[3,256,256]{2,1,0:T(8,128)(2,1)S(1)}, bf16[3,256,256]{2,1,0:T(8,128)(2,1)S(1)}, u32[]{:S(2)}, u32[]{:S(2)}) collective-permute-start(bf16[3,256,256]{2,1,0:T(8,128)(2,1)S(1)} %get-tuple-element.56.mine), channel_id=1, source_target_pairs={{0,8},{4,12},{8,0},{12,4},{16,24},{20,28},{24,16},{28,20},{1,9},{5... | collective-permute-start | bytes 1179656 | tf_op jit(solution)/shard_map/ppermute | solution.py:21
  41.9 6.0 %copy-start = (bf16[8,3,256,256]{3,2,1,0:T(8,128)(2,1)S(1)}, bf16[8,3,256,256]{3,2,1,0:T(8,128)(2,1)}, u32[]{:S(2)}) copy-start(bf16[8,3,256,256]{3,2,1,0:T(8,128)(2,1)} %panels.5) | copy-start | bytes 9437188
  41.9 5.7 %collective-permute-start.10 = (bf16[3,256,128]{2,1,0:T(8,128)(2,1)S(1)}, bf16[3,256,128]{2,1,0:T(8,128)(2,1)S(1)}, u32[]{:S(2)}, u32[]{:S(2)}) collective-permute-start(bf16[3,256,128]{2,1,0:T(8,128)(2,1)S(1)} %add_convert_fusion.mine), channel_id=1, source_target_pairs={{0,4},{4,0},{8,12},{12,8},{16,20},{20,16},{24,28},{28,24},{1,5},{5... | collective-permute-start | bytes 589832 | tf_op jit(solution)/shard_map/ppermute | solution.py:21
  43.4 1.1 %copy-start.5 = (bf16[5,256,256]{2,1,0:T(8,128)(2,1)S(1)}, bf16[5,256,256]{2,1,0:T(8,128)(2,1)}, u32[]{:S(2)}) copy-start(bf16[5,256,256]{2,1,0:T(8,128)(2,1)} %copy-done.4) | copy-start | bytes 1966084
  44.5 1.0 %copy-start.8 = (bf16[3,256,256]{2,1,0:T(8,128)(2,1)S(1)}, bf16[3,256,256]{2,1,0:T(8,128)(2,1)}, u32[]{:S(2)}) copy-start(bf16[3,256,256]{2,1,0:T(8,128)(2,1)} %copy-done.7) | copy-start | bytes 1179652
  45.4 0.9 %copy-start.12 = (bf16[2,256,256]{2,1,0:T(8,128)(2,1)S(1)}, bf16[2,256,256]{2,1,0:T(8,128)(2,1)}, u32[]{:S(2)}) copy-start(bf16[2,256,256]{2,1,0:T(8,128)(2,1)} %copy-done.11) | copy-start | bytes 786436
  46.4 1.4 %copy-start.2 = (bf16[5,256,256]{2,1,0:T(8,128)(2,1)}, bf16[5,256,256]{2,1,0:T(8,128)(2,1)S(1)}, u32[]{:S(2)}) copy-start(bf16[5,256,256]{2,1,0:T(8,128)(2,1)S(1)} %sort.7.factors) | copy-start | bytes 1966084
  47.9 22.7 %collective-permute-start.19 = (bf16[8,3,256,256]{3,2,1,0:T(8,128)(2,1)S(1)}, bf16[8,3,256,256]{3,2,1,0:T(8,128)(2,1)}, u32[]{:S(2)}, u32[]{:S(2)}) collective-permute-start(bf16[8,3,256,256]{3,2,1,0:T(8,128)(2,1)S(1)} %copy-done), channel_id=1, source_target_pairs={{0,1},{1,0},{2,3},{3,2},{4,5},{5,4},{6,7},{7,6},{8,9},{9,8},{10,11... | collective-permute-start | bytes 9437192 | tf_op jit(solution)/shard_map/ppermute | solution.py:21
  48.0 22.6 %collective-permute-start.18 = (bf16[8,256,256]{2,1,0:T(8,128)(2,1)}, bf16[8,256,256]{2,1,0:T(8,128)(2,1)}, u32[]{:S(2)}, u32[]{:S(2)}) collective-permute-start(bf16[8,256,256]{2,1,0:T(8,128)(2,1)} %inv.5), channel_id=1, source_target_pairs={{0,1},{1,0},{2,3},{3,2},{4,5},{5,4},{6,7},{7,6},{8,9},{9,8},{10,11... | collective-permute-start | bytes 3145736 | tf_op jit(solution)/shard_map/ppermute | solution.py:21
  48.5 7.2 %collective-permute-start.12 = (bf16[2,256,128]{2,1,0:T(8,128)(2,1)S(1)}, bf16[2,256,128]{2,1,0:T(8,128)(2,1)S(1)}, u32[]{:S(2)}, u32[]{:S(2)}) collective-permute-start(bf16[2,256,128]{2,1,0:T(8,128)(2,1)S(1)} %get-tuple-element.65.mine), channel_id=1, source_target_pairs={{0,8},{4,12},{8,0},{12,4},{16,24},{20,28},{24,16},{28,20},{1,9},{5... | collective-permute-start | bytes 393224 | tf_op jit(solution)/shard_map/ppermute | solution.py:21
  52.4 14.2 %copy-start.1 = (bf16[8,256,256]{2,1,0:T(8,128)(2,1)S(1)}, bf16[8,256,256]{2,1,0:T(8,128)(2,1)}, u32[]{:S(2)}) copy-start(bf16[8,256,256]{2,1,0:T(8,128)(2,1)} %get-tuple-element.46.value) | copy-start | bytes 3145732
  52.4 6.7 %collective-permute-start.16 = (bf16[1,256,128]{2,1,0:T(8,128)(2,1)S(1)}, bf16[1,256,128]{2,1,0:T(8,128)(2,1)S(1)}, u32[]{:S(2)}, u32[]{:S(2)}) collective-permute-start(bf16[1,256,128]{2,1,0:T(8,128)(2,1)S(1)} %get-tuple-element.74.refs_2_), channel_id=1, source_target_pairs={{0,2},{1,3},{2,0},{3,1},{4,6},{5,7},{6,4},{7,5},{8,10},{9,11},{10,... | collective-permute-start | bytes 196616 | tf_op jit(solution)/shard_map/ppermute | solution.py:21
  53.5 1.1 %copy-start.3 = (bf16[5,256,256]{2,1,0:T(8,128)(2,1)S(1)}, bf16[5,256,256]{2,1,0:T(8,128)(2,1)}, u32[]{:S(2)}) copy-start(bf16[5,256,256]{2,1,0:T(8,128)(2,1)} %copy-done.2) | copy-start | bytes 1966084
  54.6 1.0 %copy-start.10 = (bf16[3,256,256]{2,1,0:T(8,128)(2,1)S(1)}, bf16[3,256,256]{2,1,0:T(8,128)(2,1)}, u32[]{:S(2)}) copy-start(bf16[3,256,256]{2,1,0:T(8,128)(2,1)} %copy-done.9) | copy-start | bytes 1179652
  55.6 11.0 %copy-start.23 = (s32[8,3]{1,0:T(8,128)S(1)}, s32[8,3]{1,0:T(8,128)}, u32[]{:S(2)}) copy-start(s32[8,3]{1,0:T(8,128)} %copy-done.22) | copy-start | bytes 292
  55.9 10.1 %collective-permute-start.13 = (bf16[2,256,128]{2,1,0:T(8,128)(2,1)S(1)}, bf16[2,256,128]{2,1,0:T(8,128)(2,1)S(1)}, u32[]{:S(2)}, u32[]{:S(2)}) collective-permute-start(bf16[2,256,128]{2,1,0:T(8,128)(2,1)S(1)} %get-tuple-element.69.own), channel_id=1, source_target_pairs={{0,2},{1,3},{2,0},{3,1},{4,6},{5,7},{6,4},{7,5},{8,10},{9,11},{10,... | collective-permute-start | bytes 393224 | tf_op jit(solution)/shard_map/ppermute | solution.py:21
  56.9 6.4 %collective-permute-start.14 = (bf16[1,256,128]{2,1,0:T(8,128)(2,1)S(1)}, bf16[1,256,128]{2,1,0:T(8,128)(2,1)S(1)}, u32[]{:S(2)}, u32[]{:S(2)}) collective-permute-start(bf16[1,256,128]{2,1,0:T(8,128)(2,1)S(1)} %get-tuple-element.70), channel_id=1, source_target_pairs={{0,16},{4,20},{8,24},{12,28},{16,0},{20,4},{24,8},{28,12},{1,17},{... | collective-permute-start | bytes 196616 | tf_op jit(solution)/shard_map/ppermute | solution.py:21
  59.0 6.9 %collective-permute-start.15 = (bf16[1,256,128]{2,1,0:T(8,128)(2,1)S(1)}, bf16[1,256,128]{2,1,0:T(8,128)(2,1)S(1)}, u32[]{:S(2)}, u32[]{:S(2)}) collective-permute-start(bf16[1,256,128]{2,1,0:T(8,128)(2,1)S(1)} %get-tuple-element.70), channel_id=1, source_target_pairs={{0,18},{1,19},{2,16},{3,17},{4,22},{5,23},{6,20},{7,21},{8,26},{9,... | collective-permute-start | bytes 196616 | tf_op jit(solution)/shard_map/ppermute | solution.py:523
  66.6 4.0 %copy-start.6 = (bf16[8,256,128]{2,1,0:T(8,128)(2,1)S(1)}, bf16[8,256,128]{2,1,0:T(8,128)(2,1)}, u32[]{:S(2)}) copy-start(bf16[8,256,128]{2,1,0:T(8,128)(2,1)} %get-tuple-element.78.value) | copy-start | bytes 1572868
  66.6 4.0 %copy-start.25 = (s32[8,3]{1,0:T(8,128)S(1)}, s32[8,3]{1,0:T(8,128)}, u32[]{:S(2)}) copy-start(s32[8,3]{1,0:T(8,128)} %copy-done.24) | copy-start | bytes 292
  69.3 18.6 %collective-permute-start.22 = (bf16[6,256,128]{2,1,0:T(8,128)(2,1)S(1)}, bf16[6,256,128]{2,1,0:T(8,128)(2,1)S(1)}, u32[]{:S(2)}, u32[]{:S(2)}) collective-permute-start(bf16[6,256,128]{2,1,0:T(8,128)(2,1)S(1)} %solve_far.7), channel_id=1, source_target_pairs={{0,2},{1,3},{2,0},{3,1},{4,6},{5,7},{6,4},{7,5},{8,10},{9,11},{10,... | collective-permute-start | bytes 1179656 | tf_op jit(solution)/shard_map/ppermute | solution.py:21
  73.0 16.8 %collective-permute-start.21 = (bf16[4,256,128]{2,1,0:T(8,128)(2,1)S(1)}, bf16[4,256,128]{2,1,0:T(8,128)(2,1)S(1)}, u32[]{:S(2)}, u32[]{:S(2)}) collective-permute-start(bf16[4,256,128]{2,1,0:T(8,128)(2,1)S(1)} %solve_far.6), channel_id=1, source_target_pairs={{0,2},{1,3},{2,0},{3,1},{4,6},{5,7},{6,4},{7,5},{8,10},{9,11},{10,... | collective-permute-start | bytes 786440 | tf_op jit(solution)/shard_map/ppermute | solution.py:21
  76.2 2.9 %copy-start.26 = (s32[5]{0:T(128)S(1)}, s32[5]{0:T(128)}, u32[]{:S(2)}) copy-start(s32[5]{0:T(128)} %stack.23.scalars) | copy-start | bytes 64
  76.2 15.6 %collective-permute-start.20 = (bf16[4,256,128]{2,1,0:T(8,128)(2,1)S(1)}, bf16[4,256,128]{2,1,0:T(8,128)(2,1)S(1)}, u32[]{:S(2)}, u32[]{:S(2)}) collective-permute-start(bf16[4,256,128]{2,1,0:T(8,128)(2,1)S(1)} %solve_far.5), channel_id=1, source_target_pairs={{0,2},{1,3},{2,0},{3,1},{4,6},{5,7},{6,4},{7,5},{8,10},{9,11},{10,... | collective-permute-start | bytes 786440 | tf_op jit(solution)/shard_map/ppermute | solution.py:21
  79.0 5.0 %copy-start.13 = (bf16[8,256,128]{2,1,0:T(8,128)(2,1)S(1)}, bf16[8,256,128]{2,1,0:T(8,128)(2,1)}, u32[]{:S(2)}) copy-start(bf16[8,256,128]{2,1,0:T(8,128)(2,1)} %get-tuple-element.81.value) | copy-start | bytes 1572868
  82.5 10.7 %collective-permute-start.17 = (bf16[2,256,128]{2,1,0:T(8,128)(2,1)S(1)}, bf16[2,256,128]{2,1,0:T(8,128)(2,1)S(1)}, u32[]{:S(2)}, u32[]{:S(2)}) collective-permute-start(bf16[2,256,128]{2,1,0:T(8,128)(2,1)S(1)} %solve_far.4), channel_id=1, source_target_pairs={{0,2},{1,3},{2,0},{3,1},{4,6},{5,7},{6,4},{7,5},{8,10},{9,11},{10,... | collective-permute-start | bytes 393224 | tf_op jit(solution)/shard_map/ppermute | solution.py:21
  (5 other events, 4.2 us)

commit v5 on v4

--- a/solution.py
+++ b/solution.py
@@ -225,7 +225,9 @@
             num_scalar_prefetch=1,
             grid=(count // batch,),
             in_specs=[
-                pl.BlockSpec((batch, size, cols), lambda i, _: (i, 0, 0)),
+                pl.BlockSpec(memory_space=pltpu.VMEM)
+                if count == batch
+                else pl.BlockSpec((batch, size, cols), lambda i, _: (i, 0, 0)),
                 pl.BlockSpec(memory_space=pl.ANY),
             ],
             out_specs=pl.BlockSpec(
@@ -315,7 +317,7 @@
         out_specs=pl.BlockSpec(memory_space=pltpu.VMEM),
         out_shape=jax.ShapeDtypeStruct((1,) + sources[0].shape[1:], BF16),
         scratch_shapes=[pltpu.SemaphoreType.DMA],
-        compiler_params=pltpu.CompilerParams(vmem_limit_bytes=TREE_VMEM),
+        compiler_params=pltpu.CompilerParams(vmem_limit_bytes=FORWARD_VMEM),
         cost_estimate=cost(2**20, 2**20),
         name="pick",
     )(jnp.reshape(index, (1,)).astype(jnp.int32), *sources)
@@ -335,14 +337,12 @@
     return lax.optimization_barrier((value, *earlier))[0]
 
 
-def climb_kernel(mine, theirs, factors, passed, entered, *both):
+def climb_kernel(mine, theirs, factors, passed, entered):
     here = (-(mine[0].astype(F32) + theirs[0].astype(F32))).astype(BF16)
     for above in range(passed.shape[0]):
         carried = mine[above + 1].astype(F32) + theirs[above + 1].astype(F32)
         passed[above] = (carried + dot(factors[1 + 2 * above], here)).astype(BF16)
     entered[0] = here
-    if passed.shape[0] == 1:
-        entered[1] = passed[0]
 
 
 def climb(mine, theirs, factors):
@@ -354,7 +354,7 @@
         out_specs=[vmem] * 2,
         out_shape=[
             jax.ShapeDtypeStruct((levels - 1, size, cols), BF16),
-            jax.ShapeDtypeStruct((2 if levels == 2 else 1, size, cols), BF16),
+            jax.ShapeDtypeStruct((1, size, cols), BF16),
         ],
         compiler_params=pltpu.CompilerParams(vmem_limit_bytes=TREE_VMEM),
         cost_estimate=cost(2**20, 2**20),
@@ -403,11 +403,26 @@
     return held, onward
 
 
-def descend_kernel(own, far, theirs, across, top, kept, inputs, paths):
+def enter_kernel(mine, theirs, entered):
+    entered[0] = (-(mine[0].astype(F32) + theirs[0].astype(F32))).astype(BF16)
+
+
+def enter(mine, theirs):
+    vmem = pl.BlockSpec(memory_space=pltpu.VMEM)
+    return pl.pallas_call(
+        enter_kernel,
+        in_specs=[vmem] * 2,
+        out_specs=vmem,
+        out_shape=jax.ShapeDtypeStruct(mine.shape, BF16),
+        compiler_params=pltpu.CompilerParams(vmem_limit_bytes=TREE_VMEM),
+        cost_estimate=cost(2**20, 2**20),
+        name="enter",
+    )(mine, theirs)
+
+
+def descend_kernel(own, far, own_top, far_top, top, kept, inputs, paths):
     levels = paths.shape[0]
-    entered = [own[1].astype(F32) + theirs[0].astype(F32), far[1].astype(F32) + across[0].astype(F32)]
-    entered = (-jnp.concatenate(entered, axis=1)).astype(BF16)
-    paths[levels - 1] = dot(top[0], entered).astype(BF16)
+    paths[levels - 1] = dot(top[0], jnp.concatenate([own_top[0], far_top[0]], axis=1)).astype(BF16)
     end = kept.shape[0]
     for level in range(levels - 2, -1, -1):
         count = levels - 1 - level
@@ -422,7 +437,7 @@
         paths[level] = rest.astype(BF16)
 
 
-def descend(levels, own, far, theirs, across, top, kept, inputs):
+def descend(levels, own, far, own_top, far_top, top, kept, inputs):
     _, size, cols = own.shape
     vmem = pl.BlockSpec(memory_space=pltpu.VMEM)
     return pl.pallas_call(
@@ -433,7 +448,7 @@
         compiler_params=pltpu.CompilerParams(vmem_limit_bytes=TREE_VMEM),
         cost_estimate=cost(2**20, 2**20),
         name="descend",
-    )(own, far, theirs, across, top, kept, inputs)
+    )(own, far, own_top, far_top, top, kept, inputs)
 
 
 def on_device(
@@ -512,16 +527,14 @@
         else:
             theirs = after(theirs, following)
         passed, entered = climb(mine, theirs, factors)
-        if level == 1:
+        if level == levels - 1:
             near_upper_inv = swap(after(leaf_upper_inv, passed), "col", 1)
             near_upper_panels = swap(after(leaf_upper_panels, passed), "col", 1)
         held, following = hold(level, after(factors, passed), following, [*held, own, far] if level > 1 else [])
         mine, factors, own, far = passed, following, entered, swap(entered, "col", 2)
     theirs = swap(mine, "leaf", 2 ** (levels - 1))
-    hop = 2 ** (levels - 1) * lax.axis_size("col") + 2
-    pairs = [(source, source ^ hop) for source in range(lax.axis_size("leaf") * lax.axis_size("col"))]
-    across = lax.ppermute(mine, ("leaf", "col"), pairs)
-    paths = descend(levels, own, far, theirs, across, factors, *held)
+    own_top = enter(mine, theirs)
+    paths = descend(levels, own, far, own_top, swap(own_top, "col", 2), factors, *held)
 
     own_solution = jnp.zeros((size, cols), BF16)
     for level in range(levels):

time: 95 us -> 92.5 us (0.974)
  local copies, waits for them, and re-layouts: 12.2 us -> 8.7 us
  waiting for transfers between devices: 12.8 us -> 15.7 us
  Pallas kernels: 40.9 us -> 39.4 us
    ppermute x20 -> x21, waiting for transfers between devices: 9.44 us -> 15.1 us  [swap(): return lax.ppermute(value, axis, pairs)]
    unnamed x61 -> x51, local copies, waits for them, and re-layouts: 7.74 us -> 4.28 us
    pallas_call x2, Pallas kernels: 0.3 us -> 3.13 us  [pick(): pl.pallas_call(pick_kernel, in_specs=[pl.BlockSpec(memory_space=pltpu.SME...]
    pallas_call x4, Pallas kernels: 8.9 us -> 6.14 us  [solve_far(): pl.pallas_call(functools.partial(send_kernel, base), grid=(count // batch...]
    ppermute x1 -> x0, waiting for transfers between devices: 2.66 us -> none  [on_device(): across = lax.ppermute(mine, ('leaf', 'col'), pairs)]
    pallas_call x2, Pallas kernels: 7.31 us -> 5.8 us  [solve_own(): pl.pallas_call(functools.partial(keep_kernel, which), grid=(count // batc...]
    ppermute x1 -> x0, starting transfers between devices: 1.3 us -> none  [on_device(): across = lax.ppermute(mine, ('leaf', 'col'), pairs)]
    ppermute x20 -> x21, starting transfers between devices: 23.4 us -> 24.5 us  [swap(): return lax.ppermute(value, axis, pairs)]
  transfers between devices with their start and end apart: 23 -> 23, of which waited for: 10 -> 11; matrix products, arithmetic and copies ran while one was open for 3% -> 4% of each run, Pallas kernels for 42% -> 41%
where the time goes in v5:
time: 92.5 us; the launch traced here: 92 us
  Pallas kernels  39.4 us (43%)
  starting transfers between devices  26.4 us (29%)
  waiting for transfers between devices  15.7 us (17%)
  local copies, waits for them, and re-layouts  8.7 us (9%)
  between operations  1.09 us (1%)
    ppermute x21, starting transfers between devices, swap(): return lax.ppermute(value, axis, pairs)  24.5 us
    pallas_call x3, Pallas kernels, forward(): pl.pallas_call(functools.partial(forward_kernel, rhs is not None, far is...  17.1 us
    ppermute x21, waiting for transfers between devices, swap(): return lax.ppermute(value, axis, pairs)  15.1 us
    pallas_call x4, Pallas kernels, solve_far(): pl.pallas_call(functools.partial(send_kernel, base), grid=(count // batch...  6.14 us
    pallas_call x2, Pallas kernels, solve_own(): pl.pallas_call(functools.partial(keep_kernel, which), grid=(count // batc...  5.8 us
    pallas_call x4, Pallas kernels, place_rows(): pl.pallas_call(place_kernel, grid_spec=pltpu.PrefetchScalarGridSpec(num_s...  5.63 us
    unnamed x51, local copies, waits for them, and re-layouts  4.28 us
    pallas_call x2, Pallas kernels, pick(): pl.pallas_call(pick_kernel, in_specs=[pl.BlockSpec(memory_space=pltpu.SME...  3.13 us
  transfers between devices with their start and end apart: 23, of which 11 were waited for; matrix products, arithmetic and copies ran while one was open for 4% of the time, Pallas kernels for 41%

profile of v5, /device:TPU:0, one launch (start us, length us, event | category | flops | bytes accessed | tf_op | source)
XLA Modules:
  0.0 92.0 jit_solution(16235627908327122757)
XLA Ops:
  0.7 1.9 %constant_dynamic-slice_fusion.1 = bf16[8,256,128]{2,1,0:T(8,128)(2,1)} fusion(bf16[32,256,128]{2,1,0:T(8,128)(2,1)} %refs_0_.3, s32[]{:T(128)S(6)} %select_n.94), kind=kLoop, calls=%fused_computation.5 | loop fusion | bytes 1048580 | tf_op jit(solution)/shard_map/dynamic_slice | solution.py:482
  3.2 3.0 %collective-permute-start = (bf16[8,256,128]{2,1,0:T(8,128)(2,1)}, bf16[8,256,128]{2,1,0:T(8,128)(2,1)}, u32[]{:S(2)}, u32[]{:S(2)}) collective-permute-start(bf16[8,256,128]{2,1,0:T(8,128)(2,1)} %constant_dynamic-slice_fusion.1), channel_id=1, source_target_pairs={{0,2},{1,3},{2,0},{3,1},{4,6},{5,7},{6,4},{7,5},{8,10},{9,11},{10,... | collective-permute-start | bytes 1572872 | tf_op jit(solution)/shard_map/ppermute | solution.py:21
  6.1 1.9 %constant_dynamic-slice_fusion = bf16[8,256,128]{2,1,0:T(8,128)(2,1)} fusion(bf16[32,256,128]{2,1,0:T(8,128)(2,1)} %refs_0_.3, s32[]{:T(128)S(6)} %select_n.95), kind=kLoop, calls=%fused_computation.4 | loop fusion | bytes 1048580 | tf_op jit(solution)/shard_map/dynamic_slice | solution.py:483
  8.4 1.6 %collective-permute-start.5 = (bf16[3,256,256]{2,1,0:T(8,128)(2,1)S(1)}, bf16[3,256,256]{2,1,0:T(8,128)(2,1)S(1)}, u32[]{:S(2)}, u32[]{:S(2)}) collective-permute-start(bf16[3,256,256]{2,1,0:T(8,128)(2,1)S(1)} %get-tuple-element.52), channel_id=1, source_target_pairs={{0,4},{4,0},{8,12},{12,8},{16,20},{20,16},{24,28},{28,24},{1,5},{5... | collective-permute-start | bytes 1179656 | tf_op jit(solution)/shard_map/ppermute | solution.py:21
  10.0 1.2 %collective-permute-done.1.ancestors = s32[8,3]{1,0:T(8,128)S(1)} collective-permute-done((s32[8,3]{1,0:T(8,128)S(1)}, s32[8,3]{1,0:T(8,128)S(1)}, u32[]{:S(2)}, u32[]{:S(2)}) %collective-permute-start.1) | collective-permute-done | bytes 128 | tf_op jit(solution)/shard_map/ppermute | solution.py:21
  11.2 1.6 %collective-permute-start.4 = (bf16[8,256,128]{2,1,0:T(8,128)(2,1)}, bf16[8,256,128]{2,1,0:T(8,128)(2,1)}, u32[]{:S(2)}, u32[]{:S(2)}) collective-permute-start(bf16[8,256,128]{2,1,0:T(8,128)(2,1)} %constant_dynamic-slice_fusion), channel_id=1, source_target_pairs={{0,2},{1,3},{2,0},{3,1},{4,6},{5,7},{6,4},{7,5},{8,10},{9,11},{10,... | collective-permute-start | bytes 1572872 | tf_op jit(solution)/shard_map/ppermute | solution.py:21
  12.8 1.5 %collective-permute-start.6 = (bf16[2,256,256]{2,1,0:T(8,128)(2,1)S(1)}, bf16[2,256,256]{2,1,0:T(8,128)(2,1)S(1)}, u32[]{:S(2)}, u32[]{:S(2)}) collective-permute-start(bf16[2,256,256]{2,1,0:T(8,128)(2,1)S(1)} %get-tuple-element.53), channel_id=1, source_target_pairs={{0,4},{4,0},{8,12},{12,8},{16,20},{20,16},{24,28},{28,24},{1,5},{5... | collective-permute-start | bytes 786440 | tf_op jit(solution)/shard_map/ppermute | solution.py:21
  14.9 5.4 %leaf_forward.3 = (bf16[8,256,128]{2,1,0:T(8,128)(2,1)}, f32[3,256,128]{2,1,0:T(8,128)}) custom-call(s32[5]{0:T(128)} %stack.23.scalars, s32[8,3]{1,0:T(8,128)} %copy-done.17, bf16[32,256,128]{2,1,0:T(8,128)(2,1)} %refs_0_.3, bf16[8,256,256]{2,1,0:T(8,128)(2,1)} %copy-done.20, bf16[8,3,256,256]{3,2,1,0:T(8,128)(2,1)} %collective-permute-done.3.refs_2_, ...), custom_call_target="tpu_custom_call" | custom-call | tf_op jit(solution)/shard_map/leaf_forward/pallas_call | solution.py:94
  20.3 6.2 %leaf_forward.4 = (bf16[8,256,256]{2,1,0:T(8,128)(2,1)}, bf16[3,256,128]{2,1,0:T(8,128)(2,1)}, f32[3,256,128]{2,1,0:T(8,128)}) custom-call(s32[5]{0:T(128)} %stack.23.scalars, s32[8,3]{1,0:T(8,128)} %copy-done.15, bf16[32,256,128]{2,1,0:T(8,128)(2,1)} %refs_0_.3, bf16[8,256,128]{2,1,0:T(8,128)(2,1)} %collective-permute-done.refs_1_, ...), custom_call_target="tpu_custom_call" | custom-call | tf_op jit(solution)/shard_map/leaf_forward/pallas_call | solution.py:94
  26.6 1.3 %collective-permute-start.7 = (bf16[1,256,256]{2,1,0:T(8,128)(2,1)S(1)}, bf16[1,256,256]{2,1,0:T(8,128)(2,1)S(1)}, u32[]{:S(2)}, u32[]{:S(2)}) collective-permute-start(bf16[1,256,256]{2,1,0:T(8,128)(2,1)S(1)} %get-tuple-element.57), channel_id=1, source_target_pairs={{16,0},{20,4},{17,1},{21,5},{18,2},{22,6},{19,3},{23,7}} | collective-permute-start | bytes 393224 | tf_op jit(solution)/shard_map/ppermute | solution.py:333
  27.9 0.7 collective-permute-start.8
  28.6 1.1 %collective-permute-done.4.refs_0_ = bf16[8,256,128]{2,1,0:T(8,128)(2,1)} collective-permute-done((bf16[8,256,128]{2,1,0:T(8,128)(2,1)}, bf16[8,256,128]{2,1,0:T(8,128)(2,1)}, u32[]{:S(2)}, u32[]{:S(2)}) %collective-permute-start.4) | collective-permute-done | bytes 524320 | tf_op jit(solution)/shard_map/ppermute | solution.py:21
  29.8 5.4 %leaf_forward.5 = (bf16[8,256,128]{2,1,0:T(8,128)(2,1)}, bf16[3,256,128]{2,1,0:T(8,128)(2,1)}) custom-call(s32[5]{0:T(128)} %stack.23.scalars, s32[8,3]{1,0:T(8,128)} %copy-done.17, bf16[8,256,128]{2,1,0:T(8,128)(2,1)} %collective-permute-done.4.refs_0_, bf16[8,256,256]{2,1,0:T(8,128)(2,1)} %copy-done.20, ...), custom_call_target="tpu_custom_call" | custom-call | tf_op jit(solution)/shard_map/leaf_forward/pallas_call | solution.py:94
  35.8 1.2 %collective-permute-start.9 = (bf16[3,256,128]{2,1,0:T(8,128)(2,1)}, bf16[3,256,128]{2,1,0:T(8,128)(2,1)S(1)}, u32[]{:S(2)}, u32[]{:S(2)}) collective-permute-start(bf16[3,256,128]{2,1,0:T(8,128)(2,1)} %get-tuple-element.60), channel_id=1, source_target_pairs={{0,2},{1,3},{2,0},{3,1},{4,6},{5,7},{6,4},{7,5},{8,10},{9,11},{10,... | collective-permute-start | bytes 589832 | tf_op jit(solution)/shard_map/ppermute | solution.py:21
  37.1 1.6 %collective-permute-start.11 = (bf16[3,256,256]{2,1,0:T(8,128)(2,1)S(1)}, bf16[3,256,256]{2,1,0:T(8,128)(2,1)S(1)}, u32[]{:S(2)}, u32[]{:S(2)}) collective-permute-start(bf16[3,256,256]{2,1,0:T(8,128)(2,1)S(1)} %get-tuple-element.56.mine), channel_id=1, source_target_pairs={{0,8},{4,12},{8,0},{12,4},{16,24},{20,28},{24,16},{28,20},{1,9},{5... | collective-permute-start | bytes 1179656 | tf_op jit(solution)/shard_map/ppermute | solution.py:21
  38.7 1.6 %pick.2.refs_0_ = bf16[1,256,256]{2,1,0:T(8,128)(2,1)} custom-call(s32[1]{0:T(128)} %bitcast.6.flags, bf16[1,256,256]{2,1,0:T(8,128)(2,1)} %copy-done.22, bf16[1,256,256]{2,1,0:T(8,128)(2,1)} %copy-done.23), custom_call_target="tpu_custom_call" | custom-call | flops 1048576 | bytes 1048576 | tf_op jit(solution)/shard_map/pick/pallas_call | solution.py:314
  40.2 1.6 %collective-permute-done.9 = bf16[3,256,128]{2,1,0:T(8,128)(2,1)S(1)} collective-permute-done((bf16[3,256,128]{2,1,0:T(8,128)(2,1)}, bf16[3,256,128]{2,1,0:T(8,128)(2,1)S(1)}, u32[]{:S(2)}, u32[]{:S(2)}) %collective-permute-start.9) | collective-permute-done | bytes 196640 | tf_op jit(solution)/shard_map/ppermute | solution.py:21
  41.9 1.5 %collective-permute-start.10 = (bf16[3,256,128]{2,1,0:T(8,128)(2,1)S(1)}, bf16[3,256,128]{2,1,0:T(8,128)(2,1)S(1)}, u32[]{:S(2)}, u32[]{:S(2)}) collective-permute-start(bf16[3,256,128]{2,1,0:T(8,128)(2,1)S(1)} %add_convert_fusion.mine), channel_id=1, source_target_pairs={{0,4},{4,0},{8,12},{12,8},{16,20},{20,16},{24,28},{28,24},{1,5},{5... | collective-permute-start | bytes 589832 | tf_op jit(solution)/shard_map/ppermute | solution.py:21
  43.4 3.6 %collective-permute-done.11.refs_0_ = bf16[3,256,256]{2,1,0:T(8,128)(2,1)S(1)} collective-permute-done((bf16[3,256,256]{2,1,0:T(8,128)(2,1)S(1)}, bf16[3,256,256]{2,1,0:T(8,128)(2,1)S(1)}, u32[]{:S(2)}, u32[]{:S(2)}) %collective-permute-start.11) | collective-permute-done | bytes 393248 | tf_op jit(solution)/shard_map/ppermute | solution.py:21
  47.0 0.7 copy-done.6
  48.4 1.6 %collective-permute-start.12 = (bf16[2,256,128]{2,1,0:T(8,128)(2,1)S(1)}, bf16[2,256,128]{2,1,0:T(8,128)(2,1)S(1)}, u32[]{:S(2)}, u32[]{:S(2)}) collective-permute-start(bf16[2,256,128]{2,1,0:T(8,128)(2,1)S(1)} %get-tuple-element.65.mine), channel_id=1, source_target_pairs={{0,8},{4,12},{8,0},{12,4},{16,24},{20,28},{24,16},{28,20},{1,9},{5... | collective-permute-start | bytes 393224 | tf_op jit(solution)/shard_map/ppermute | solution.py:21
  50.0 1.6 %pick.3.next_factors = bf16[1,256,256]{2,1,0:T(8,128)(2,1)} custom-call(s32[1]{0:T(128)} %bitcast.7.flags, bf16[1,256,256]{2,1,0:T(8,128)(2,1)} %pick.2.refs_0_, bf16[1,256,256]{2,1,0:T(8,128)(2,1)} %copy-done.9), custom_call_target="tpu_custom_call" | custom-call | flops 1048576 | bytes 1048576 | tf_op jit(solution)/shard_map/pick/pallas_call | solution.py:314
  51.6 1.1 %copy-done.4 = bf16[5,256,256]{2,1,0:T(8,128)(2,1)S(1)} copy-done((bf16[5,256,256]{2,1,0:T(8,128)(2,1)S(1)}, bf16[5,256,256]{2,1,0:T(8,128)(2,1)}, u32[]{:S(2)}) %copy-start.4) | copy-done | bytes 655384
  52.7 1.0 %copy-done.7 = bf16[3,256,256]{2,1,0:T(8,128)(2,1)S(1)} copy-done((bf16[3,256,256]{2,1,0:T(8,128)(2,1)S(1)}, bf16[3,256,256]{2,1,0:T(8,128)(2,1)}, u32[]{:S(2)}) %copy-start.7) | copy-done | bytes 393240
  54.5 2.6 %collective-permute-start.14 = (bf16[1,256,128]{2,1,0:T(8,128)(2,1)S(1)}, bf16[1,256,128]{2,1,0:T(8,128)(2,1)S(1)}, u32[]{:S(2)}, u32[]{:S(2)}) collective-permute-start(bf16[1,256,128]{2,1,0:T(8,128)(2,1)S(1)} %get-tuple-element.70.mine), channel_id=1, source_target_pairs={{0,16},{4,20},{8,24},{12,28},{16,0},{20,4},{24,8},{28,12},{1,17},{... | collective-permute-start | bytes 196616 | tf_op jit(solution)/shard_map/ppermute | solution.py:21
  57.1 0.9 collective-permute-start.16
  58.0 1.1 %collective-permute-start.13 = (bf16[1,256,128]{2,1,0:T(8,128)(2,1)S(1)}, bf16[1,256,128]{2,1,0:T(8,128)(2,1)S(1)}, u32[]{:S(2)}, u32[]{:S(2)}) collective-permute-start(bf16[1,256,128]{2,1,0:T(8,128)(2,1)S(1)} %get-tuple-element.69.own), channel_id=1, source_target_pairs={{0,2},{1,3},{2,0},{3,1},{4,6},{5,7},{6,4},{7,5},{8,10},{9,11},{10,... | collective-permute-start | bytes 196616 | tf_op jit(solution)/shard_map/ppermute | solution.py:21
  59.1 1.8 %collective-permute-done.14.theirs = bf16[1,256,128]{2,1,0:T(8,128)(2,1)S(1)} collective-permute-done((bf16[1,256,128]{2,1,0:T(8,128)(2,1)S(1)}, bf16[1,256,128]{2,1,0:T(8,128)(2,1)S(1)}, u32[]{:S(2)}, u32[]{:S(2)}) %collective-permute-start.14) | collective-permute-done | bytes 65568 | tf_op jit(solution)/shard_map/ppermute | solution.py:21
  60.9 1.0 %collective-permute-start.15 = (bf16[1,256,128]{2,1,0:T(8,128)(2,1)S(1)}, bf16[1,256,128]{2,1,0:T(8,128)(2,1)S(1)}, u32[]{:S(2)}, u32[]{:S(2)}) collective-permute-start(bf16[1,256,128]{2,1,0:T(8,128)(2,1)S(1)} %enter.1.own_top), channel_id=1, source_target_pairs={{0,2},{1,3},{2,0},{3,1},{4,6},{5,7},{6,4},{7,5},{8,10},{9,11},{10,... | collective-permute-start | bytes 196616 | tf_op jit(solution)/shard_map/ppermute | solution.py:21
  61.9 0.9 copy-done.10
  63.0 2.2 %collective-permute-done.15.far_top = bf16[1,256,128]{2,1,0:T(8,128)(2,1)S(1)} collective-permute-done((bf16[1,256,128]{2,1,0:T(8,128)(2,1)S(1)}, bf16[1,256,128]{2,1,0:T(8,128)(2,1)S(1)}, u32[]{:S(2)}, u32[]{:S(2)}) %collective-permute-start.15) | collective-permute-done | bytes 65568 | tf_op jit(solution)/shard_map/ppermute | solution.py:21
  65.9 2.3 %solve_far.7 = bf16[6,256,128]{2,1,0:T(8,128)(2,1)S(1)} custom-call(s32[8,3]{1,0:T(8,128)S(1)} %copy-done.16, bf16[8,256,256]{2,1,0:T(8,128)(2,1)S(1)} %copy-done.2, bf16[8,256,256]{2,1,0:T(8,128)(2,1)S(1)} %copy-done.1, bf16[8,3,256,256]{3,2,1,0:T(8,128)(2,1)S(1)} %copy-done, bf16[3,256,256]{2,1,0:T(8,128)(2,1)S(1)} %descend.1.paths), custom_call_target="tpu_custom_call" | custom-call | tf_op jit(solution)/shard_map/solve_far/pallas_call | solution.py:151
  68.2 1.0 %collective-permute-start.22 = (bf16[6,256,128]{2,1,0:T(8,128)(2,1)S(1)}, bf16[6,256,128]{2,1,0:T(8,128)(2,1)S(1)}, u32[]{:S(2)}, u32[]{:S(2)}) collective-permute-start(bf16[6,256,128]{2,1,0:T(8,128)(2,1)S(1)} %solve_far.7), channel_id=1, source_target_pairs={{0,2},{1,3},{2,0},{3,1},{4,6},{5,7},{6,4},{7,5},{8,10},{9,11},{10,... | collective-permute-start | bytes 1179656 | tf_op jit(solution)/shard_map/ppermute | solution.py:21
  69.2 1.4 %solve_far.6 = bf16[4,256,128]{2,1,0:T(8,128)(2,1)S(1)} custom-call(s32[8,3]{1,0:T(8,128)S(1)} %copy-done.18, bf16[8,256,128]{2,1,0:T(8,128)(2,1)S(1)} %copy-done.5, bf16[8,256,256]{2,1,0:T(8,128)(2,1)S(1)} %collective-permute-done.18.inv, bf16[8,3,256,256]{3,2,1,0:T(8,128)(2,1)S(1)} %collective-permute-done.19.panels, bf16[3,256,256]{2,1,0:T(8,128)(2,1)S(1)} %descend.1.paths), custom_call_target="tpu_custom_call" | custom-call | tf_op jit(solution)/shard_map/solve_far/pallas_call | solution.py:151
  70.5 1.2 %collective-permute-start.21 = (bf16[4,256,128]{2,1,0:T(8,128)(2,1)S(1)}, bf16[4,256,128]{2,1,0:T(8,128)(2,1)S(1)}, u32[]{:S(2)}, u32[]{:S(2)}) collective-permute-start(bf16[4,256,128]{2,1,0:T(8,128)(2,1)S(1)} %solve_far.6), channel_id=1, source_target_pairs={{0,2},{1,3},{2,0},{3,1},{4,6},{5,7},{6,4},{7,5},{8,10},{9,11},{10,... | collective-permute-start | bytes 786440 | tf_op jit(solution)/shard_map/ppermute | solution.py:21
  71.7 1.4 %solve_far.5 = bf16[4,256,128]{2,1,0:T(8,128)(2,1)S(1)} custom-call(s32[8,3]{1,0:T(8,128)S(1)} %copy-done.18, bf16[8,256,128]{2,1,0:T(8,128)(2,1)S(1)} %copy-done.5, bf16[8,256,256]{2,1,0:T(8,128)(2,1)S(1)} %collective-permute-done.18.inv, bf16[8,3,256,256]{3,2,1,0:T(8,128)(2,1)S(1)} %collective-permute-done.19.panels, bf16[3,256,256]{2,1,0:T(8,128)(2,1)S(1)} %descend.1.paths), custom_call_target="tpu_custom_call" | custom-call | tf_op jit(solution)/shard_map/solve_far/pallas_call | solution.py:151
  73.1 1.0 %collective-permute-start.20 = (bf16[4,256,128]{2,1,0:T(8,128)(2,1)S(1)}, bf16[4,256,128]{2,1,0:T(8,128)(2,1)S(1)}, u32[]{:S(2)}, u32[]{:S(2)}) collective-permute-start(bf16[4,256,128]{2,1,0:T(8,128)(2,1)S(1)} %solve_far.5), channel_id=1, source_target_pairs={{0,2},{1,3},{2,0},{3,1},{4,6},{5,7},{6,4},{7,5},{8,10},{9,11},{10,... | collective-permute-start | bytes 786440 | tf_op jit(solution)/shard_map/ppermute | solution.py:21
  74.1 1.2 %solve_far.4 = bf16[2,256,128]{2,1,0:T(8,128)(2,1)S(1)} custom-call(s32[8,3]{1,0:T(8,128)S(1)} %copy-done.16, bf16[8,256,256]{2,1,0:T(8,128)(2,1)S(1)} %copy-done.2, bf16[8,256,256]{2,1,0:T(8,128)(2,1)S(1)} %copy-done.1, bf16[8,3,256,256]{3,2,1,0:T(8,128)(2,1)S(1)} %copy-done, bf16[3,256,256]{2,1,0:T(8,128)(2,1)S(1)} %descend.1.paths), custom_call_target="tpu_custom_call" | custom-call | tf_op jit(solution)/shard_map/solve_far/pallas_call | solution.py:151
  75.3 2.9 %solve_own.2.refs_0_ = bf16[32,256,128]{2,1,0:T(8,128)(2,1)} custom-call(s32[5]{0:T(128)S(1)} %copy-done.19, s32[8,3]{1,0:T(8,128)S(1)} %copy-done.16, bf16[8,256,256]{2,1,0:T(8,128)(2,1)S(1)} %copy-done.2, bf16[8,256,256]{2,1,0:T(8,128)(2,1)S(1)} %copy-done.1, bf16[8,3,256,256]{3,2,1,0:T(8,128)(2,1)S(1)} %copy-done, bf16[3,256,256]{2,1,0:T(8,128)(2,1)S(1)} %descend.1.paths), custom_call_target="tpu_custom_call" | custom-call | tf_op jit(solution)/shard_map/solve_own/pallas_call | solution.py:193
  78.2 1.2 %collective-permute-start.17 = (bf16[2,256,128]{2,1,0:T(8,128)(2,1)S(1)}, bf16[2,256,128]{2,1,0:T(8,128)(2,1)S(1)}, u32[]{:S(2)}, u32[]{:S(2)}) collective-permute-start(bf16[2,256,128]{2,1,0:T(8,128)(2,1)S(1)} %solve_far.4), channel_id=1, source_target_pairs={{0,2},{1,3},{2,0},{3,1},{4,6},{5,7},{6,4},{7,5},{8,10},{9,11},{10,... | collective-permute-start | bytes 393224 | tf_op jit(solution)/shard_map/ppermute | solution.py:21
  79.4 0.6 fusion.1
  80.0 2.9 %solve_own.3.whole = bf16[32,256,128]{2,1,0:T(8,128)(2,1)} custom-call(s32[5]{0:T(128)S(1)} %copy-done.19, s32[8,3]{1,0:T(8,128)S(1)} %copy-done.18, bf16[8,256,128]{2,1,0:T(8,128)(2,1)S(1)} %copy-done.8, bf16[8,256,256]{2,1,0:T(8,128)(2,1)S(1)} %collective-permute-done.18.inv, ...), custom_call_target="tpu_custom_call", output_to_operand_aliasing={{}: (6, {})} | custom-call | tf_op jit(solution)/shard_map/solve_own/pallas_call | solution.py:193
  82.9 1.9 %place_rows.4.whole = bf16[32,256,128]{2,1,0:T(8,128)(2,1)} custom-call(s32[5]{0:T(128)S(1)} %copy-done.19, bf16[6,256,128]{2,1,0:T(8,128)(2,1)S(1)} %collective-permute-done.22.part, bf16[32,256,128]{2,1,0:T(8,128)(2,1)} %solve_own.3.whole), custom_call_target="tpu_custom_call", output_to_operand_aliasing={{}: (2, {})} | custom-call | tf_op jit(solution)/shard_map/place_rows/pallas_call | solution.py:222
  84.8 1.1 %collective-permute-done.21.part = bf16[4,256,128]{2,1,0:T(8,128)(2,1)S(1)} collective-permute-done((bf16[4,256,128]{2,1,0:T(8,128)(2,1)S(1)}, bf16[4,256,128]{2,1,0:T(8,128)(2,1)S(1)}, u32[]{:S(2)}, u32[]{:S(2)}) %collective-permute-start.21) | collective-permute-done | bytes 262176 | tf_op jit(solution)/shard_map/ppermute | solution.py:21
  85.9 1.3 %place_rows.5.whole = bf16[32,256,128]{2,1,0:T(8,128)(2,1)} custom-call(s32[5]{0:T(128)S(1)} %copy-done.19, bf16[4,256,128]{2,1,0:T(8,128)(2,1)S(1)} %collective-permute-done.21.part, bf16[32,256,128]{2,1,0:T(8,128)(2,1)} %place_rows.4.whole), custom_call_target="tpu_custom_call", output_to_operand_aliasing={{}: (2, {})} | custom-call | tf_op jit(solution)/shard_map/place_rows/pallas_call | solution.py:222
  87.2 2.3 %collective-permute-done.20.part = bf16[4,256,128]{2,1,0:T(8,128)(2,1)S(1)} collective-permute-done((bf16[4,256,128]{2,1,0:T(8,128)(2,1)S(1)}, bf16[4,256,128]{2,1,0:T(8,128)(2,1)S(1)}, u32[]{:S(2)}, u32[]{:S(2)}) %collective-permute-start.20) | collective-permute-done | bytes 262176 | tf_op jit(solution)/shard_map/ppermute | solution.py:21
  89.4 1.3 %place_rows.6.whole = bf16[32,256,128]{2,1,0:T(8,128)(2,1)} custom-call(s32[5]{0:T(128)S(1)} %copy-done.19, bf16[4,256,128]{2,1,0:T(8,128)(2,1)S(1)} %collective-permute-done.20.part, bf16[32,256,128]{2,1,0:T(8,128)(2,1)} %place_rows.5.whole), custom_call_target="tpu_custom_call", output_to_operand_aliasing={{}: (2, {})} | custom-call | tf_op jit(solution)/shard_map/place_rows/pallas_call | solution.py:222
  90.8 1.2 %place_rows.7 = bf16[32,256,128]{2,1,0:T(8,128)(2,1)} custom-call(s32[5]{0:T(128)S(1)} %copy-done.19, bf16[2,256,128]{2,1,0:T(8,128)(2,1)S(1)} %collective-permute-done.17.part, bf16[32,256,128]{2,1,0:T(8,128)(2,1)} %place_rows.6.whole), custom_call_target="tpu_custom_call", output_to_operand_aliasing={{}: (2, {})} | custom-call | tf_op jit(solution)/shard_map/place_rows/pallas_call | solution.py:222
  (80 shorter events, 4.8 us)
Async XLA Ops:
  0.6 7.4 %copy-start.13 = (bf16[1,256,256]{2,1,0:T(8,128)(2,1)S(1)}, bf16[1,256,256]{2,1,0:T(8,128)(2,1)}, u32[]{:S(2)}) copy-start(bf16[1,256,256]{2,1,0:T(8,128)(2,1)} %lower_inv) | copy-start | bytes 393220
  0.6 7.4 %copy-start.11 = (bf16[1,2,256,256]{3,2,1,0:T(8,128)(2,1)S(1)}, bf16[1,2,256,256]{3,2,1,0:T(8,128)(2,1)}, u32[]{:S(2)}) copy-start(bf16[1,2,256,256]{3,2,1,0:T(8,128)(2,1)} %lower_panels.1) | copy-start | bytes 786436
  0.7 7.4 %copy-start.14 = (bf16[1,256,256]{2,1,0:T(8,128)(2,1)S(1)}, bf16[1,256,256]{2,1,0:T(8,128)(2,1)}, u32[]{:S(2)}) copy-start(bf16[1,256,256]{2,1,0:T(8,128)(2,1)} %upper_inv.1) | copy-start | bytes 393220
  0.7 7.4 %copy-start.12 = (bf16[1,2,256,256]{3,2,1,0:T(8,128)(2,1)S(1)}, bf16[1,2,256,256]{3,2,1,0:T(8,128)(2,1)}, u32[]{:S(2)}) copy-start(bf16[1,2,256,256]{3,2,1,0:T(8,128)(2,1)} %upper_panels.1) | copy-start | bytes 786436
  0.7 9.3 %copy-start.24 = (s32[8,3]{0,1:T(4,128)S(1)}, s32[8,3]{0,1:T(4,128)}, u32[]{:S(2)}) copy-start(s32[8,3]{0,1:T(4,128)} %param.16) | copy-start | bytes 292
  2.6 12.2 %collective-permute-start.3 = (bf16[8,3,256,256]{3,2,1,0:T(8,128)(2,1)}, bf16[8,3,256,256]{3,2,1,0:T(8,128)(2,1)}, u32[]{:S(2)}, u32[]{:S(2)}) collective-permute-start(bf16[8,3,256,256]{3,2,1,0:T(8,128)(2,1)} %refs_3_.2), channel_id=1, source_target_pairs={{0,1},{1,0},{2,3},{3,2},{4,5},{5,4},{6,7},{7,6},{8,9},{9,8},{10,11... | collective-permute-start | bytes 9437192 | tf_op jit(solution)/shard_map/ppermute | solution.py:21
  3.1 9.7 %collective-permute-start.2 = (bf16[8,256,256]{2,1,0:T(8,128)(2,1)}, bf16[8,256,256]{2,1,0:T(8,128)(2,1)S(1)}, u32[]{:S(2)}, u32[]{:S(2)}) collective-permute-start(bf16[8,256,256]{2,1,0:T(8,128)(2,1)} %refs_2_.1), channel_id=1, source_target_pairs={{0,1},{1,0},{2,3},{3,2},{4,5},{5,4},{6,7},{7,6},{8,9},{9,8},{10,11... | collective-permute-start | bytes 3145736 | tf_op jit(solution)/shard_map/ppermute | solution.py:21
  3.2 17.2 %collective-permute-start = (bf16[8,256,128]{2,1,0:T(8,128)(2,1)}, bf16[8,256,128]{2,1,0:T(8,128)(2,1)}, u32[]{:S(2)}, u32[]{:S(2)}) collective-permute-start(bf16[8,256,128]{2,1,0:T(8,128)(2,1)} %constant_dynamic-slice_fusion.1), channel_id=1, source_target_pairs={{0,2},{1,3},{2,0},{3,1},{4,6},{5,7},{6,4},{7,5},{8,10},{9,11},{10,... | collective-permute-start | bytes 1572872 | tf_op jit(solution)/shard_map/ppermute | solution.py:21
  8.4 18.2 %collective-permute-start.5 = (bf16[3,256,256]{2,1,0:T(8,128)(2,1)S(1)}, bf16[3,256,256]{2,1,0:T(8,128)(2,1)S(1)}, u32[]{:S(2)}, u32[]{:S(2)}) collective-permute-start(bf16[3,256,256]{2,1,0:T(8,128)(2,1)S(1)} %get-tuple-element.52), channel_id=1, source_target_pairs={{0,4},{4,0},{8,12},{12,8},{16,20},{20,16},{24,28},{28,24},{1,5},{5... | collective-permute-start | bytes 1179656 | tf_op jit(solution)/shard_map/ppermute | solution.py:21
  10.0 10.3 %copy-start.15 = (s32[8,3]{1,0:T(8,128)}, s32[8,3]{1,0:T(8,128)S(1)}, u32[]{:S(2)}) copy-start(s32[8,3]{1,0:T(8,128)S(1)} %copy.20.ancestors) | copy-start | bytes 292
  10.0 1.2 %collective-permute-start.1 = (s32[8,3]{1,0:T(8,128)S(1)}, s32[8,3]{1,0:T(8,128)S(1)}, u32[]{:S(2)}, u32[]{:S(2)}) collective-permute-start(s32[8,3]{1,0:T(8,128)S(1)} %copy.20.ancestors), channel_id=1, source_target_pairs={{0,1},{1,0},{2,3},{3,2},{4,5},{5,4},{6,7},{7,6},{8,9},{9,8},{10,11... | collective-permute-start | bytes 296 | tf_op jit(solution)/shard_map/ppermute | solution.py:21
  11.2 3.7 %copy-start.17 = (s32[8,3]{1,0:T(8,128)}, s32[8,3]{1,0:T(8,128)S(1)}, u32[]{:S(2)}) copy-start(s32[8,3]{1,0:T(8,128)S(1)} %collective-permute-done.1.ancestors) | copy-start | bytes 292
  11.2 18.6 %collective-permute-start.4 = (bf16[8,256,128]{2,1,0:T(8,128)(2,1)}, bf16[8,256,128]{2,1,0:T(8,128)(2,1)}, u32[]{:S(2)}, u32[]{:S(2)}) collective-permute-start(bf16[8,256,128]{2,1,0:T(8,128)(2,1)} %constant_dynamic-slice_fusion), channel_id=1, source_target_pairs={{0,2},{1,3},{2,0},{3,1},{4,6},{5,7},{6,4},{7,5},{8,10},{9,11},{10,... | collective-permute-start | bytes 1572872 | tf_op jit(solution)/shard_map/ppermute | solution.py:21
  12.8 2.1 %copy-start.20 = (bf16[8,256,256]{2,1,0:T(8,128)(2,1)}, bf16[8,256,256]{2,1,0:T(8,128)(2,1)S(1)}, u32[]{:S(2)}) copy-start(bf16[8,256,256]{2,1,0:T(8,128)(2,1)S(1)} %collective-permute-done.2.refs_1_) | copy-start | bytes 3145732
  12.8 13.8 %collective-permute-start.6 = (bf16[2,256,256]{2,1,0:T(8,128)(2,1)S(1)}, bf16[2,256,256]{2,1,0:T(8,128)(2,1)S(1)}, u32[]{:S(2)}, u32[]{:S(2)}) collective-permute-start(bf16[2,256,256]{2,1,0:T(8,128)(2,1)S(1)} %get-tuple-element.53), channel_id=1, source_target_pairs={{0,4},{4,0},{8,12},{12,8},{16,20},{20,16},{24,28},{28,24},{1,5},{5... | collective-permute-start | bytes 786440 | tf_op jit(solution)/shard_map/ppermute | solution.py:21
  26.6 9.2 %collective-permute-start.7 = (bf16[1,256,256]{2,1,0:T(8,128)(2,1)S(1)}, bf16[1,256,256]{2,1,0:T(8,128)(2,1)S(1)}, u32[]{:S(2)}, u32[]{:S(2)}) collective-permute-start(bf16[1,256,256]{2,1,0:T(8,128)(2,1)S(1)} %get-tuple-element.57), channel_id=1, source_target_pairs={{16,0},{20,4},{17,1},{21,5},{18,2},{22,6},{19,3},{23,7}} | collective-permute-start | bytes 393224 | tf_op jit(solution)/shard_map/ppermute | solution.py:333
  27.9 7.9 %collective-permute-start.8 = (bf16[1,256,256]{2,1,0:T(8,128)(2,1)S(1)}, bf16[1,256,256]{2,1,0:T(8,128)(2,1)S(1)}, u32[]{:S(2)}, u32[]{:S(2)}) collective-permute-start(bf16[1,256,256]{2,1,0:T(8,128)(2,1)S(1)} %get-tuple-element.57), channel_id=1, source_target_pairs={{16,8},{20,12},{17,9},{21,13},{18,10},{22,14},{19,11},{23,15}} | collective-permute-start | bytes 393224 | tf_op jit(solution)/shard_map/ppermute | solution.py:333
  28.6 13.2 %copy-start.21 = (bf16[3,256,128]{2,1,0:T(8,128)(2,1)S(1)}, bf16[3,256,128]{2,1,0:T(8,128)(2,1)}, u32[]{:S(2)}) copy-start(bf16[3,256,128]{2,1,0:T(8,128)(2,1)} %get-tuple-element.47) | copy-start | bytes 589828
  35.8 2.8 %copy-start.22 = (bf16[1,256,256]{2,1,0:T(8,128)(2,1)}, bf16[1,256,256]{2,1,0:T(8,128)(2,1)S(1)}, u32[]{:S(2)}) copy-start(bf16[1,256,256]{2,1,0:T(8,128)(2,1)S(1)} %collective-permute-done.7.refs_0_) | copy-start | bytes 393220
  35.8 2.8 %copy-start.23 = (bf16[1,256,256]{2,1,0:T(8,128)(2,1)}, bf16[1,256,256]{2,1,0:T(8,128)(2,1)S(1)}, u32[]{:S(2)}) copy-start(bf16[1,256,256]{2,1,0:T(8,128)(2,1)S(1)} %collective-permute-done.8.refs_1_) | copy-start | bytes 393220
  35.8 6.0 %collective-permute-start.9 = (bf16[3,256,128]{2,1,0:T(8,128)(2,1)}, bf16[3,256,128]{2,1,0:T(8,128)(2,1)S(1)}, u32[]{:S(2)}, u32[]{:S(2)}) collective-permute-start(bf16[3,256,128]{2,1,0:T(8,128)(2,1)} %get-tuple-element.60), channel_id=1, source_target_pairs={{0,2},{1,3},{2,0},{3,1},{4,6},{5,7},{6,4},{7,5},{8,10},{9,11},{10,... | collective-permute-start | bytes 589832 | tf_op jit(solution)/shard_map/ppermute | solution.py:21
  37.1 9.9 %collective-permute-start.11 = (bf16[3,256,256]{2,1,0:T(8,128)(2,1)S(1)}, bf16[3,256,256]{2,1,0:T(8,128)(2,1)S(1)}, u32[]{:S(2)}, u32[]{:S(2)}) collective-permute-start(bf16[3,256,256]{2,1,0:T(8,128)(2,1)S(1)} %get-tuple-element.56.mine), channel_id=1, source_target_pairs={{0,8},{4,12},{8,0},{12,4},{16,24},{20,28},{24,16},{28,20},{1,9},{5... | collective-permute-start | bytes 1179656 | tf_op jit(solution)/shard_map/ppermute | solution.py:21
  41.9 5.9 %collective-permute-start.10 = (bf16[3,256,128]{2,1,0:T(8,128)(2,1)S(1)}, bf16[3,256,128]{2,1,0:T(8,128)(2,1)S(1)}, u32[]{:S(2)}, u32[]{:S(2)}) collective-permute-start(bf16[3,256,128]{2,1,0:T(8,128)(2,1)S(1)} %add_convert_fusion.mine), channel_id=1, source_target_pairs={{0,4},{4,0},{8,12},{12,8},{16,20},{20,16},{24,28},{28,24},{1,5},{5... | collective-permute-start | bytes 589832 | tf_op jit(solution)/shard_map/ppermute | solution.py:21
  43.4 4.4 %copy-start.3 = (bf16[5,256,256]{2,1,0:T(8,128)(2,1)}, bf16[5,256,256]{2,1,0:T(8,128)(2,1)S(1)}, u32[]{:S(2)}) copy-start(bf16[5,256,256]{2,1,0:T(8,128)(2,1)S(1)} %sort.7.factors) | copy-start | bytes 1966084
  47.0 0.8 copy-start.6
  47.0 6.9 %copy-start = (bf16[8,3,256,256]{3,2,1,0:T(8,128)(2,1)S(1)}, bf16[8,3,256,256]{3,2,1,0:T(8,128)(2,1)}, u32[]{:S(2)}) copy-start(bf16[8,3,256,256]{3,2,1,0:T(8,128)(2,1)} %panels.5) | copy-start | bytes 9437188
  47.8 0.7 copy-start.9
  48.4 5.3 %collective-permute-start.12 = (bf16[2,256,128]{2,1,0:T(8,128)(2,1)S(1)}, bf16[2,256,128]{2,1,0:T(8,128)(2,1)S(1)}, u32[]{:S(2)}, u32[]{:S(2)}) collective-permute-start(bf16[2,256,128]{2,1,0:T(8,128)(2,1)S(1)} %get-tuple-element.65.mine), channel_id=1, source_target_pairs={{0,8},{4,12},{8,0},{12,4},{16,24},{20,28},{24,16},{28,20},{1,9},{5... | collective-permute-start | bytes 393224 | tf_op jit(solution)/shard_map/ppermute | solution.py:21
  51.6 1.1 %copy-start.4 = (bf16[5,256,256]{2,1,0:T(8,128)(2,1)S(1)}, bf16[5,256,256]{2,1,0:T(8,128)(2,1)}, u32[]{:S(2)}) copy-start(bf16[5,256,256]{2,1,0:T(8,128)(2,1)} %copy-done.3) | copy-start | bytes 1966084
  52.7 1.0 %copy-start.7 = (bf16[3,256,256]{2,1,0:T(8,128)(2,1)S(1)}, bf16[3,256,256]{2,1,0:T(8,128)(2,1)}, u32[]{:S(2)}) copy-start(bf16[3,256,256]{2,1,0:T(8,128)(2,1)} %copy-done.6) | copy-start | bytes 1179652
  53.7 12.2 %copy-start.1 = (bf16[8,256,256]{2,1,0:T(8,128)(2,1)S(1)}, bf16[8,256,256]{2,1,0:T(8,128)(2,1)}, u32[]{:S(2)}) copy-start(bf16[8,256,256]{2,1,0:T(8,128)(2,1)} %inv.5) | copy-start | bytes 3145732
  53.7 12.2 %copy-start.2 = (bf16[8,256,256]{2,1,0:T(8,128)(2,1)S(1)}, bf16[8,256,256]{2,1,0:T(8,128)(2,1)}, u32[]{:S(2)}) copy-start(bf16[8,256,256]{2,1,0:T(8,128)(2,1)} %get-tuple-element.46.value) | copy-start | bytes 3145732
  53.9 15.2 %collective-permute-start.19 = (bf16[8,3,256,256]{3,2,1,0:T(8,128)(2,1)S(1)}, bf16[8,3,256,256]{3,2,1,0:T(8,128)(2,1)S(1)}, u32[]{:S(2)}, u32[]{:S(2)}) collective-permute-start(bf16[8,3,256,256]{3,2,1,0:T(8,128)(2,1)S(1)} %copy-done), channel_id=1, source_target_pairs={{0,1},{1,0},{2,3},{3,2},{4,5},{5,4},{6,7},{7,6},{8,9},{9,8},{10,11... | collective-permute-start | bytes 9437192 | tf_op jit(solution)/shard_map/ppermute | solution.py:21
  54.0 15.1 %collective-permute-start.18 = (bf16[8,256,256]{2,1,0:T(8,128)(2,1)}, bf16[8,256,256]{2,1,0:T(8,128)(2,1)S(1)}, u32[]{:S(2)}, u32[]{:S(2)}) collective-permute-start(bf16[8,256,256]{2,1,0:T(8,128)(2,1)} %inv.5), channel_id=1, source_target_pairs={{0,1},{1,0},{2,3},{3,2},{4,5},{5,4},{6,7},{7,6},{8,9},{9,8},{10,11... | collective-permute-start | bytes 3145736 | tf_op jit(solution)/shard_map/ppermute | solution.py:21
  54.5 6.4 %collective-permute-start.14 = (bf16[1,256,128]{2,1,0:T(8,128)(2,1)S(1)}, bf16[1,256,128]{2,1,0:T(8,128)(2,1)S(1)}, u32[]{:S(2)}, u32[]{:S(2)}) collective-permute-start(bf16[1,256,128]{2,1,0:T(8,128)(2,1)S(1)} %get-tuple-element.70.mine), channel_id=1, source_target_pairs={{0,16},{4,20},{8,24},{12,28},{16,0},{20,4},{24,8},{28,12},{1,17},{... | collective-permute-start | bytes 196616 | tf_op jit(solution)/shard_map/ppermute | solution.py:21
  57.1 4.8 %collective-permute-start.16 = (bf16[1,256,128]{2,1,0:T(8,128)(2,1)S(1)}, bf16[1,256,128]{2,1,0:T(8,128)(2,1)S(1)}, u32[]{:S(2)}, u32[]{:S(2)}) collective-permute-start(bf16[1,256,128]{2,1,0:T(8,128)(2,1)S(1)} %get-tuple-element.74.refs_2_), channel_id=1, source_target_pairs={{0,2},{1,3},{2,0},{3,1},{4,6},{5,7},{6,4},{7,5},{8,10},{9,11},{10,... | collective-permute-start | bytes 196616 | tf_op jit(solution)/shard_map/ppermute | solution.py:21
  58.0 5.0 %collective-permute-start.13 = (bf16[1,256,128]{2,1,0:T(8,128)(2,1)S(1)}, bf16[1,256,128]{2,1,0:T(8,128)(2,1)S(1)}, u32[]{:S(2)}, u32[]{:S(2)}) collective-permute-start(bf16[1,256,128]{2,1,0:T(8,128)(2,1)S(1)} %get-tuple-element.69.own), channel_id=1, source_target_pairs={{0,2},{1,3},{2,0},{3,1},{4,6},{5,7},{6,4},{7,5},{8,10},{9,11},{10,... | collective-permute-start | bytes 196616 | tf_op jit(solution)/shard_map/ppermute | solution.py:21
  60.9 4.3 %collective-permute-start.15 = (bf16[1,256,128]{2,1,0:T(8,128)(2,1)S(1)}, bf16[1,256,128]{2,1,0:T(8,128)(2,1)S(1)}, u32[]{:S(2)}, u32[]{:S(2)}) collective-permute-start(bf16[1,256,128]{2,1,0:T(8,128)(2,1)S(1)} %enter.1.own_top), channel_id=1, source_target_pairs={{0,2},{1,3},{2,0},{3,1},{4,6},{5,7},{6,4},{7,5},{8,10},{9,11},{10,... | collective-permute-start | bytes 196616 | tf_op jit(solution)/shard_map/ppermute | solution.py:21
  61.9 0.9 copy-start.10
  62.8 3.0 %copy-start.16 = (s32[8,3]{1,0:T(8,128)S(1)}, s32[8,3]{1,0:T(8,128)}, u32[]{:S(2)}) copy-start(s32[8,3]{1,0:T(8,128)} %copy-done.15) | copy-start | bytes 292
  65.9 3.3 %copy-start.5 = (bf16[8,256,128]{2,1,0:T(8,128)(2,1)S(1)}, bf16[8,256,128]{2,1,0:T(8,128)(2,1)}, u32[]{:S(2)}) copy-start(bf16[8,256,128]{2,1,0:T(8,128)(2,1)} %get-tuple-element.78.value) | copy-start | bytes 1572868
  65.9 3.3 %copy-start.18 = (s32[8,3]{1,0:T(8,128)S(1)}, s32[8,3]{1,0:T(8,128)}, u32[]{:S(2)}) copy-start(s32[8,3]{1,0:T(8,128)} %copy-done.17) | copy-start | bytes 292
  68.2 14.7 %collective-permute-start.22 = (bf16[6,256,128]{2,1,0:T(8,128)(2,1)S(1)}, bf16[6,256,128]{2,1,0:T(8,128)(2,1)S(1)}, u32[]{:S(2)}, u32[]{:S(2)}) collective-permute-start(bf16[6,256,128]{2,1,0:T(8,128)(2,1)S(1)} %solve_far.7), channel_id=1, source_target_pairs={{0,2},{1,3},{2,0},{3,1},{4,6},{5,7},{6,4},{7,5},{8,10},{9,11},{10,... | collective-permute-start | bytes 1179656 | tf_op jit(solution)/shard_map/ppermute | solution.py:21
  70.5 15.4 %collective-permute-start.21 = (bf16[4,256,128]{2,1,0:T(8,128)(2,1)S(1)}, bf16[4,256,128]{2,1,0:T(8,128)(2,1)S(1)}, u32[]{:S(2)}, u32[]{:S(2)}) collective-permute-start(bf16[4,256,128]{2,1,0:T(8,128)(2,1)S(1)} %solve_far.6), channel_id=1, source_target_pairs={{0,2},{1,3},{2,0},{3,1},{4,6},{5,7},{6,4},{7,5},{8,10},{9,11},{10,... | collective-permute-start | bytes 786440 | tf_op jit(solution)/shard_map/ppermute | solution.py:21
  73.1 2.2 %copy-start.19 = (s32[5]{0:T(128)S(1)}, s32[5]{0:T(128)}, u32[]{:S(2)}) copy-start(s32[5]{0:T(128)} %stack.23.scalars) | copy-start | bytes 64
  73.1 16.3 %collective-permute-start.20 = (bf16[4,256,128]{2,1,0:T(8,128)(2,1)S(1)}, bf16[4,256,128]{2,1,0:T(8,128)(2,1)S(1)}, u32[]{:S(2)}, u32[]{:S(2)}) collective-permute-start(bf16[4,256,128]{2,1,0:T(8,128)(2,1)S(1)} %solve_far.5), channel_id=1, source_target_pairs={{0,2},{1,3},{2,0},{3,1},{4,6},{5,7},{6,4},{7,5},{8,10},{9,11},{10,... | collective-permute-start | bytes 786440 | tf_op jit(solution)/shard_map/ppermute | solution.py:21
  75.2 4.8 %copy-start.8 = (bf16[8,256,128]{2,1,0:T(8,128)(2,1)S(1)}, bf16[8,256,128]{2,1,0:T(8,128)(2,1)}, u32[]{:S(2)}) copy-start(bf16[8,256,128]{2,1,0:T(8,128)(2,1)} %get-tuple-element.81.value) | copy-start | bytes 1572868
  78.2 12.6 %collective-permute-start.17 = (bf16[2,256,128]{2,1,0:T(8,128)(2,1)S(1)}, bf16[2,256,128]{2,1,0:T(8,128)(2,1)S(1)}, u32[]{:S(2)}, u32[]{:S(2)}) collective-permute-start(bf16[2,256,128]{2,1,0:T(8,128)(2,1)S(1)} %solve_far.4), channel_id=1, source_target_pairs={{0,2},{1,3},{2,0},{3,1},{4,6},{5,7},{6,4},{7,5},{8,10},{9,11},{10,... | collective-permute-start | bytes 393224 | tf_op jit(solution)/shard_map/ppermute | solution.py:21

commit v6 on v5

--- a/solution.py
+++ b/solution.py
@@ -13,6 +13,7 @@
 LEAF_VMEM = 10 * 2**20
 TREE_VMEM = 6 * 2**20
 BATCH = 4
+SOLVE_BATCH = 6
 PART = 3
 
 
@@ -141,7 +142,7 @@
 
 def solve_far(ancestors, inv, panels, value, paths, base, count):
     levels, size, cols = paths.shape[0], paths.shape[1], paths.shape[2] // 2
-    batch = max(leaves for leaves in range(1, BATCH + 1) if count % leaves == 0 and base % leaves == 0)
+    batch = max(leaves for leaves in range(1, SOLVE_BATCH + 1) if count % leaves == 0 and base % leaves == 0)
     ahead = base // batch
 
     def part(array):

time: 92.5 us -> 91.8 us (level)
  no operation moved by 1% of the time
where the time goes in v6:
time: 91.8 us; the launch traced here: 91.3 us
  Pallas kernels  38.8 us (42%)
  starting transfers between devices  26.4 us (29%)
  waiting for transfers between devices  15.7 us (17%)
  local copies, waits for them, and re-layouts  8.7 us (9%)
  between operations  1.09 us (1%)
    ppermute x21, starting transfers between devices, swap(): return lax.ppermute(value, axis, pairs)  24.5 us
    pallas_call x3, Pallas kernels, forward(): pl.pallas_call(functools.partial(forward_kernel, rhs is not None, far is...  17.1 us
    ppermute x21, waiting for transfers between devices, swap(): return lax.ppermute(value, axis, pairs)  15.1 us
    pallas_call x2, Pallas kernels, solve_own(): pl.pallas_call(functools.partial(keep_kernel, which), grid=(count // batc...  5.8 us
    pallas_call x4, Pallas kernels, place_rows(): pl.pallas_call(place_kernel, grid_spec=pltpu.PrefetchScalarGridSpec(num_s...  5.63 us
    pallas_call x4, Pallas kernels, solve_far(): pl.pallas_call(functools.partial(send_kernel, base), grid=(count // batch...  5.47 us
    unnamed x51, local copies, waits for them, and re-layouts  4.28 us
    pallas_call x2, Pallas kernels, pick(): pl.pallas_call(pick_kernel, in_specs=[pl.BlockSpec(memory_space=pltpu.SME...  3.13 us
  transfers between devices with their start and end apart: 23, of which 11 were waited for; matrix products, arithmetic and copies ran while one was open for 4% of the time, Pallas kernels for 41%

profile of v6, /device:TPU:0, one launch (start us, length us, event | category | flops | bytes accessed | tf_op | source)
XLA Modules:
  0.0 91.3 jit_solution(11277801440421353302)
XLA Ops:
  0.7 1.9 %constant_dynamic-slice_fusion.1 = bf16[8,256,128]{2,1,0:T(8,128)(2,1)} fusion(bf16[32,256,128]{2,1,0:T(8,128)(2,1)} %refs_0_.3, s32[]{:T(128)S(6)} %select_n.94), kind=kLoop, calls=%fused_computation.5 | loop fusion | bytes 1048580 | tf_op jit(solution)/shard_map/dynamic_slice | solution.py:483
  3.2 3.0 %collective-permute-start = (bf16[8,256,128]{2,1,0:T(8,128)(2,1)}, bf16[8,256,128]{2,1,0:T(8,128)(2,1)}, u32[]{:S(2)}, u32[]{:S(2)}) collective-permute-start(bf16[8,256,128]{2,1,0:T(8,128)(2,1)} %constant_dynamic-slice_fusion.1), channel_id=1, source_target_pairs={{0,2},{1,3},{2,0},{3,1},{4,6},{5,7},{6,4},{7,5},{8,10},{9,11},{10,... | collective-permute-start | bytes 1572872 | tf_op jit(solution)/shard_map/ppermute | solution.py:22
  6.1 1.9 %constant_dynamic-slice_fusion = bf16[8,256,128]{2,1,0:T(8,128)(2,1)} fusion(bf16[32,256,128]{2,1,0:T(8,128)(2,1)} %refs_0_.3, s32[]{:T(128)S(6)} %select_n.95), kind=kLoop, calls=%fused_computation.4 | loop fusion | bytes 1048580 | tf_op jit(solution)/shard_map/dynamic_slice | solution.py:484
  8.4 1.6 %collective-permute-start.5 = (bf16[3,256,256]{2,1,0:T(8,128)(2,1)S(1)}, bf16[3,256,256]{2,1,0:T(8,128)(2,1)S(1)}, u32[]{:S(2)}, u32[]{:S(2)}) collective-permute-start(bf16[3,256,256]{2,1,0:T(8,128)(2,1)S(1)} %get-tuple-element.52), channel_id=1, source_target_pairs={{0,4},{4,0},{8,12},{12,8},{16,20},{20,16},{24,28},{28,24},{1,5},{5... | collective-permute-start | bytes 1179656 | tf_op jit(solution)/shard_map/ppermute | solution.py:22
  10.0 1.2 %collective-permute-done.1.ancestors = s32[8,3]{1,0:T(8,128)S(1)} collective-permute-done((s32[8,3]{1,0:T(8,128)S(1)}, s32[8,3]{1,0:T(8,128)S(1)}, u32[]{:S(2)}, u32[]{:S(2)}) %collective-permute-start.1) | collective-permute-done | bytes 128 | tf_op jit(solution)/shard_map/ppermute | solution.py:22
  11.2 1.6 %collective-permute-start.4 = (bf16[8,256,128]{2,1,0:T(8,128)(2,1)}, bf16[8,256,128]{2,1,0:T(8,128)(2,1)}, u32[]{:S(2)}, u32[]{:S(2)}) collective-permute-start(bf16[8,256,128]{2,1,0:T(8,128)(2,1)} %constant_dynamic-slice_fusion), channel_id=1, source_target_pairs={{0,2},{1,3},{2,0},{3,1},{4,6},{5,7},{6,4},{7,5},{8,10},{9,11},{10,... | collective-permute-start | bytes 1572872 | tf_op jit(solution)/shard_map/ppermute | solution.py:22
  12.8 1.5 %collective-permute-start.6 = (bf16[2,256,256]{2,1,0:T(8,128)(2,1)S(1)}, bf16[2,256,256]{2,1,0:T(8,128)(2,1)S(1)}, u32[]{:S(2)}, u32[]{:S(2)}) collective-permute-start(bf16[2,256,256]{2,1,0:T(8,128)(2,1)S(1)} %get-tuple-element.53), channel_id=1, source_target_pairs={{0,4},{4,0},{8,12},{12,8},{16,20},{20,16},{24,28},{28,24},{1,5},{5... | collective-permute-start | bytes 786440 | tf_op jit(solution)/shard_map/ppermute | solution.py:22
  14.9 5.4 %leaf_forward.3 = (bf16[8,256,128]{2,1,0:T(8,128)(2,1)}, f32[3,256,128]{2,1,0:T(8,128)}) custom-call(s32[5]{0:T(128)} %stack.23.scalars, s32[8,3]{1,0:T(8,128)} %copy-done.17, bf16[32,256,128]{2,1,0:T(8,128)(2,1)} %refs_0_.3, bf16[8,256,256]{2,1,0:T(8,128)(2,1)} %copy-done.20, bf16[8,3,256,256]{3,2,1,0:T(8,128)(2,1)} %collective-permute-done.3.refs_2_, ...), custom_call_target="tpu_custom_call" | custom-call | tf_op jit(solution)/shard_map/leaf_forward/pallas_call | solution.py:95
  20.3 6.2 %leaf_forward.4 = (bf16[8,256,256]{2,1,0:T(8,128)(2,1)}, bf16[3,256,128]{2,1,0:T(8,128)(2,1)}, f32[3,256,128]{2,1,0:T(8,128)}) custom-call(s32[5]{0:T(128)} %stack.23.scalars, s32[8,3]{1,0:T(8,128)} %copy-done.15, bf16[32,256,128]{2,1,0:T(8,128)(2,1)} %refs_0_.3, bf16[8,256,128]{2,1,0:T(8,128)(2,1)} %collective-permute-done.refs_1_, ...), custom_call_target="tpu_custom_call" | custom-call | tf_op jit(solution)/shard_map/leaf_forward/pallas_call | solution.py:95
  26.6 1.3 %collective-permute-start.7 = (bf16[1,256,256]{2,1,0:T(8,128)(2,1)S(1)}, bf16[1,256,256]{2,1,0:T(8,128)(2,1)S(1)}, u32[]{:S(2)}, u32[]{:S(2)}) collective-permute-start(bf16[1,256,256]{2,1,0:T(8,128)(2,1)S(1)} %get-tuple-element.57), channel_id=1, source_target_pairs={{16,0},{20,4},{17,1},{21,5},{18,2},{22,6},{19,3},{23,7}} | collective-permute-start | bytes 393224 | tf_op jit(solution)/shard_map/ppermute | solution.py:334
  27.9 0.7 collective-permute-start.8
  28.6 1.1 %collective-permute-done.4.refs_0_ = bf16[8,256,128]{2,1,0:T(8,128)(2,1)} collective-permute-done((bf16[8,256,128]{2,1,0:T(8,128)(2,1)}, bf16[8,256,128]{2,1,0:T(8,128)(2,1)}, u32[]{:S(2)}, u32[]{:S(2)}) %collective-permute-start.4) | collective-permute-done | bytes 524320 | tf_op jit(solution)/shard_map/ppermute | solution.py:22
  29.8 5.4 %leaf_forward.5 = (bf16[8,256,128]{2,1,0:T(8,128)(2,1)}, bf16[3,256,128]{2,1,0:T(8,128)(2,1)}) custom-call(s32[5]{0:T(128)} %stack.23.scalars, s32[8,3]{1,0:T(8,128)} %copy-done.17, bf16[8,256,128]{2,1,0:T(8,128)(2,1)} %collective-permute-done.4.refs_0_, bf16[8,256,256]{2,1,0:T(8,128)(2,1)} %copy-done.20, ...), custom_call_target="tpu_custom_call" | custom-call | tf_op jit(solution)/shard_map/leaf_forward/pallas_call | solution.py:95
  35.8 1.2 %collective-permute-start.9 = (bf16[3,256,128]{2,1,0:T(8,128)(2,1)}, bf16[3,256,128]{2,1,0:T(8,128)(2,1)S(1)}, u32[]{:S(2)}, u32[]{:S(2)}) collective-permute-start(bf16[3,256,128]{2,1,0:T(8,128)(2,1)} %get-tuple-element.60), channel_id=1, source_target_pairs={{0,2},{1,3},{2,0},{3,1},{4,6},{5,7},{6,4},{7,5},{8,10},{9,11},{10,... | collective-permute-start | bytes 589832 | tf_op jit(solution)/shard_map/ppermute | solution.py:22
  37.1 1.6 %collective-permute-start.11 = (bf16[3,256,256]{2,1,0:T(8,128)(2,1)S(1)}, bf16[3,256,256]{2,1,0:T(8,128)(2,1)S(1)}, u32[]{:S(2)}, u32[]{:S(2)}) collective-permute-start(bf16[3,256,256]{2,1,0:T(8,128)(2,1)S(1)} %get-tuple-element.56.mine), channel_id=1, source_target_pairs={{0,8},{4,12},{8,0},{12,4},{16,24},{20,28},{24,16},{28,20},{1,9},{5... | collective-permute-start | bytes 1179656 | tf_op jit(solution)/shard_map/ppermute | solution.py:22
  38.7 1.6 %pick.2.refs_0_ = bf16[1,256,256]{2,1,0:T(8,128)(2,1)} custom-call(s32[1]{0:T(128)} %bitcast.6.flags, bf16[1,256,256]{2,1,0:T(8,128)(2,1)} %copy-done.22, bf16[1,256,256]{2,1,0:T(8,128)(2,1)} %copy-done.23), custom_call_target="tpu_custom_call" | custom-call | flops 1048576 | bytes 1048576 | tf_op jit(solution)/shard_map/pick/pallas_call | solution.py:315
  40.2 1.6 %collective-permute-done.9 = bf16[3,256,128]{2,1,0:T(8,128)(2,1)S(1)} collective-permute-done((bf16[3,256,128]{2,1,0:T(8,128)(2,1)}, bf16[3,256,128]{2,1,0:T(8,128)(2,1)S(1)}, u32[]{:S(2)}, u32[]{:S(2)}) %collective-permute-start.9) | collective-permute-done | bytes 196640 | tf_op jit(solution)/shard_map/ppermute | solution.py:22
  41.9 1.5 %collective-permute-start.10 = (bf16[3,256,128]{2,1,0:T(8,128)(2,1)S(1)}, bf16[3,256,128]{2,1,0:T(8,128)(2,1)S(1)}, u32[]{:S(2)}, u32[]{:S(2)}) collective-permute-start(bf16[3,256,128]{2,1,0:T(8,128)(2,1)S(1)} %add_convert_fusion.mine), channel_id=1, source_target_pairs={{0,4},{4,0},{8,12},{12,8},{16,20},{20,16},{24,28},{28,24},{1,5},{5... | collective-permute-start | bytes 589832 | tf_op jit(solution)/shard_map/ppermute | solution.py:22
  43.4 3.6 %collective-permute-done.11.refs_0_ = bf16[3,256,256]{2,1,0:T(8,128)(2,1)S(1)} collective-permute-done((bf16[3,256,256]{2,1,0:T(8,128)(2,1)S(1)}, bf16[3,256,256]{2,1,0:T(8,128)(2,1)S(1)}, u32[]{:S(2)}, u32[]{:S(2)}) %collective-permute-start.11) | collective-permute-done | bytes 393248 | tf_op jit(solution)/shard_map/ppermute | solution.py:22
  47.0 0.7 copy-done.6
  48.4 1.6 %collective-permute-start.12 = (bf16[2,256,128]{2,1,0:T(8,128)(2,1)S(1)}, bf16[2,256,128]{2,1,0:T(8,128)(2,1)S(1)}, u32[]{:S(2)}, u32[]{:S(2)}) collective-permute-start(bf16[2,256,128]{2,1,0:T(8,128)(2,1)S(1)} %get-tuple-element.65.mine), channel_id=1, source_target_pairs={{0,8},{4,12},{8,0},{12,4},{16,24},{20,28},{24,16},{28,20},{1,9},{5... | collective-permute-start | bytes 393224 | tf_op jit(solution)/shard_map/ppermute | solution.py:22
  50.0 1.6 %pick.3.next_factors = bf16[1,256,256]{2,1,0:T(8,128)(2,1)} custom-call(s32[1]{0:T(128)} %bitcast.7.flags, bf16[1,256,256]{2,1,0:T(8,128)(2,1)} %pick.2.refs_0_, bf16[1,256,256]{2,1,0:T(8,128)(2,1)} %copy-done.9), custom_call_target="tpu_custom_call" | custom-call | flops 1048576 | bytes 1048576 | tf_op jit(solution)/shard_map/pick/pallas_call | solution.py:315
  51.6 1.1 %copy-done.4 = bf16[5,256,256]{2,1,0:T(8,128)(2,1)S(1)} copy-done((bf16[5,256,256]{2,1,0:T(8,128)(2,1)S(1)}, bf16[5,256,256]{2,1,0:T(8,128)(2,1)}, u32[]{:S(2)}) %copy-start.4) | copy-done | bytes 655384
  52.7 1.0 %copy-done.7 = bf16[3,256,256]{2,1,0:T(8,128)(2,1)S(1)} copy-done((bf16[3,256,256]{2,1,0:T(8,128)(2,1)S(1)}, bf16[3,256,256]{2,1,0:T(8,128)(2,1)}, u32[]{:S(2)}) %copy-start.7) | copy-done | bytes 393240
  54.5 2.6 %collective-permute-start.14 = (bf16[1,256,128]{2,1,0:T(8,128)(2,1)S(1)}, bf16[1,256,128]{2,1,0:T(8,128)(2,1)S(1)}, u32[]{:S(2)}, u32[]{:S(2)}) collective-permute-start(bf16[1,256,128]{2,1,0:T(8,128)(2,1)S(1)} %get-tuple-element.70.mine), channel_id=1, source_target_pairs={{0,16},{4,20},{8,24},{12,28},{16,0},{20,4},{24,8},{28,12},{1,17},{... | collective-permute-start | bytes 196616 | tf_op jit(solution)/shard_map/ppermute | solution.py:22
  57.1 0.9 %collective-permute-start.16 = (bf16[1,256,128]{2,1,0:T(8,128)(2,1)S(1)}, bf16[1,256,128]{2,1,0:T(8,128)(2,1)S(1)}, u32[]{:S(2)}, u32[]{:S(2)}) collective-permute-start(bf16[1,256,128]{2,1,0:T(8,128)(2,1)S(1)} %get-tuple-element.74.refs_2_), channel_id=1, source_target_pairs={{0,2},{1,3},{2,0},{3,1},{4,6},{5,7},{6,4},{7,5},{8,10},{9,11},{10,... | collective-permute-start | bytes 196616 | tf_op jit(solution)/shard_map/ppermute | solution.py:22
  58.0 1.1 %collective-permute-start.13 = (bf16[1,256,128]{2,1,0:T(8,128)(2,1)S(1)}, bf16[1,256,128]{2,1,0:T(8,128)(2,1)S(1)}, u32[]{:S(2)}, u32[]{:S(2)}) collective-permute-start(bf16[1,256,128]{2,1,0:T(8,128)(2,1)S(1)} %get-tuple-element.69.own), channel_id=1, source_target_pairs={{0,2},{1,3},{2,0},{3,1},{4,6},{5,7},{6,4},{7,5},{8,10},{9,11},{10,... | collective-permute-start | bytes 196616 | tf_op jit(solution)/shard_map/ppermute | solution.py:22
  59.1 1.8 %collective-permute-done.14.theirs = bf16[1,256,128]{2,1,0:T(8,128)(2,1)S(1)} collective-permute-done((bf16[1,256,128]{2,1,0:T(8,128)(2,1)S(1)}, bf16[1,256,128]{2,1,0:T(8,128)(2,1)S(1)}, u32[]{:S(2)}, u32[]{:S(2)}) %collective-permute-start.14) | collective-permute-done | bytes 65568 | tf_op jit(solution)/shard_map/ppermute | solution.py:22
  60.9 1.0 %collective-permute-start.15 = (bf16[1,256,128]{2,1,0:T(8,128)(2,1)S(1)}, bf16[1,256,128]{2,1,0:T(8,128)(2,1)S(1)}, u32[]{:S(2)}, u32[]{:S(2)}) collective-permute-start(bf16[1,256,128]{2,1,0:T(8,128)(2,1)S(1)} %enter.1.own_top), channel_id=1, source_target_pairs={{0,2},{1,3},{2,0},{3,1},{4,6},{5,7},{6,4},{7,5},{8,10},{9,11},{10,... | collective-permute-start | bytes 196616 | tf_op jit(solution)/shard_map/ppermute | solution.py:22
  61.9 0.9 copy-done.10
  63.0 2.2 %collective-permute-done.15.far_top = bf16[1,256,128]{2,1,0:T(8,128)(2,1)S(1)} collective-permute-done((bf16[1,256,128]{2,1,0:T(8,128)(2,1)S(1)}, bf16[1,256,128]{2,1,0:T(8,128)(2,1)S(1)}, u32[]{:S(2)}, u32[]{:S(2)}) %collective-permute-start.15) | collective-permute-done | bytes 65568 | tf_op jit(solution)/shard_map/ppermute | solution.py:22
  65.9 1.6 %solve_far.7 = bf16[6,256,128]{2,1,0:T(8,128)(2,1)S(1)} custom-call(s32[8,3]{1,0:T(8,128)S(1)} %copy-done.16, bf16[8,256,256]{2,1,0:T(8,128)(2,1)S(1)} %copy-done.2, bf16[8,256,256]{2,1,0:T(8,128)(2,1)S(1)} %copy-done.1, bf16[8,3,256,256]{3,2,1,0:T(8,128)(2,1)S(1)} %copy-done, bf16[3,256,256]{2,1,0:T(8,128)(2,1)S(1)} %descend.1.paths), custom_call_target="tpu_custom_call" | custom-call | tf_op jit(solution)/shard_map/solve_far/pallas_call | solution.py:152
  67.5 1.0 %collective-permute-start.22 = (bf16[6,256,128]{2,1,0:T(8,128)(2,1)S(1)}, bf16[6,256,128]{2,1,0:T(8,128)(2,1)S(1)}, u32[]{:S(2)}, u32[]{:S(2)}) collective-permute-start(bf16[6,256,128]{2,1,0:T(8,128)(2,1)S(1)} %solve_far.7), channel_id=1, source_target_pairs={{0,2},{1,3},{2,0},{3,1},{4,6},{5,7},{6,4},{7,5},{8,10},{9,11},{10,... | collective-permute-start | bytes 1179656 | tf_op jit(solution)/shard_map/ppermute | solution.py:22
  68.5 1.4 %solve_far.6 = bf16[4,256,128]{2,1,0:T(8,128)(2,1)S(1)} custom-call(s32[8,3]{1,0:T(8,128)S(1)} %copy-done.18, bf16[8,256,128]{2,1,0:T(8,128)(2,1)S(1)} %copy-done.5, bf16[8,256,256]{2,1,0:T(8,128)(2,1)S(1)} %collective-permute-done.18.inv, bf16[8,3,256,256]{3,2,1,0:T(8,128)(2,1)S(1)} %collective-permute-done.19.panels, bf16[3,256,256]{2,1,0:T(8,128)(2,1)S(1)} %descend.1.paths), custom_call_target="tpu_custom_call" | custom-call | tf_op jit(solution)/shard_map/solve_far/pallas_call | solution.py:152
  69.9 1.2 %collective-permute-start.21 = (bf16[4,256,128]{2,1,0:T(8,128)(2,1)S(1)}, bf16[4,256,128]{2,1,0:T(8,128)(2,1)S(1)}, u32[]{:S(2)}, u32[]{:S(2)}) collective-permute-start(bf16[4,256,128]{2,1,0:T(8,128)(2,1)S(1)} %solve_far.6), channel_id=1, source_target_pairs={{0,2},{1,3},{2,0},{3,1},{4,6},{5,7},{6,4},{7,5},{8,10},{9,11},{10,... | collective-permute-start | bytes 786440 | tf_op jit(solution)/shard_map/ppermute | solution.py:22
  71.0 1.4 %solve_far.5 = bf16[4,256,128]{2,1,0:T(8,128)(2,1)S(1)} custom-call(s32[8,3]{1,0:T(8,128)S(1)} %copy-done.18, bf16[8,256,128]{2,1,0:T(8,128)(2,1)S(1)} %copy-done.5, bf16[8,256,256]{2,1,0:T(8,128)(2,1)S(1)} %collective-permute-done.18.inv, bf16[8,3,256,256]{3,2,1,0:T(8,128)(2,1)S(1)} %collective-permute-done.19.panels, bf16[3,256,256]{2,1,0:T(8,128)(2,1)S(1)} %descend.1.paths), custom_call_target="tpu_custom_call" | custom-call | tf_op jit(solution)/shard_map/solve_far/pallas_call | solution.py:152
  72.4 1.0 %collective-permute-start.20 = (bf16[4,256,128]{2,1,0:T(8,128)(2,1)S(1)}, bf16[4,256,128]{2,1,0:T(8,128)(2,1)S(1)}, u32[]{:S(2)}, u32[]{:S(2)}) collective-permute-start(bf16[4,256,128]{2,1,0:T(8,128)(2,1)S(1)} %solve_far.5), channel_id=1, source_target_pairs={{0,2},{1,3},{2,0},{3,1},{4,6},{5,7},{6,4},{7,5},{8,10},{9,11},{10,... | collective-permute-start | bytes 786440 | tf_op jit(solution)/shard_map/ppermute | solution.py:22
  73.4 1.2 %solve_far.4 = bf16[2,256,128]{2,1,0:T(8,128)(2,1)S(1)} custom-call(s32[8,3]{1,0:T(8,128)S(1)} %copy-done.16, bf16[8,256,256]{2,1,0:T(8,128)(2,1)S(1)} %copy-done.2, bf16[8,256,256]{2,1,0:T(8,128)(2,1)S(1)} %copy-done.1, bf16[8,3,256,256]{3,2,1,0:T(8,128)(2,1)S(1)} %copy-done, bf16[3,256,256]{2,1,0:T(8,128)(2,1)S(1)} %descend.1.paths), custom_call_target="tpu_custom_call" | custom-call | tf_op jit(solution)/shard_map/solve_far/pallas_call | solution.py:152
  74.6 2.9 %solve_own.2.refs_0_ = bf16[32,256,128]{2,1,0:T(8,128)(2,1)} custom-call(s32[5]{0:T(128)S(1)} %copy-done.19, s32[8,3]{1,0:T(8,128)S(1)} %copy-done.16, bf16[8,256,256]{2,1,0:T(8,128)(2,1)S(1)} %copy-done.2, bf16[8,256,256]{2,1,0:T(8,128)(2,1)S(1)} %copy-done.1, bf16[8,3,256,256]{3,2,1,0:T(8,128)(2,1)S(1)} %copy-done, bf16[3,256,256]{2,1,0:T(8,128)(2,1)S(1)} %descend.1.paths), custom_call_target="tpu_custom_call" | custom-call | tf_op jit(solution)/shard_map/solve_own/pallas_call | solution.py:194
  77.5 1.2 %collective-permute-start.17 = (bf16[2,256,128]{2,1,0:T(8,128)(2,1)S(1)}, bf16[2,256,128]{2,1,0:T(8,128)(2,1)S(1)}, u32[]{:S(2)}, u32[]{:S(2)}) collective-permute-start(bf16[2,256,128]{2,1,0:T(8,128)(2,1)S(1)} %solve_far.4), channel_id=1, source_target_pairs={{0,2},{1,3},{2,0},{3,1},{4,6},{5,7},{6,4},{7,5},{8,10},{9,11},{10,... | collective-permute-start | bytes 393224 | tf_op jit(solution)/shard_map/ppermute | solution.py:22
  78.7 0.6 fusion.1
  79.4 2.9 %solve_own.3.whole = bf16[32,256,128]{2,1,0:T(8,128)(2,1)} custom-call(s32[5]{0:T(128)S(1)} %copy-done.19, s32[8,3]{1,0:T(8,128)S(1)} %copy-done.18, bf16[8,256,128]{2,1,0:T(8,128)(2,1)S(1)} %copy-done.8, bf16[8,256,256]{2,1,0:T(8,128)(2,1)S(1)} %collective-permute-done.18.inv, ...), custom_call_target="tpu_custom_call", output_to_operand_aliasing={{}: (6, {})} | custom-call | tf_op jit(solution)/shard_map/solve_own/pallas_call | solution.py:194
  82.2 1.9 %place_rows.4.whole = bf16[32,256,128]{2,1,0:T(8,128)(2,1)} custom-call(s32[5]{0:T(128)S(1)} %copy-done.19, bf16[6,256,128]{2,1,0:T(8,128)(2,1)S(1)} %collective-permute-done.22.part, bf16[32,256,128]{2,1,0:T(8,128)(2,1)} %solve_own.3.whole), custom_call_target="tpu_custom_call", output_to_operand_aliasing={{}: (2, {})} | custom-call | tf_op jit(solution)/shard_map/place_rows/pallas_call | solution.py:223
  84.1 1.1 %collective-permute-done.21.part = bf16[4,256,128]{2,1,0:T(8,128)(2,1)S(1)} collective-permute-done((bf16[4,256,128]{2,1,0:T(8,128)(2,1)S(1)}, bf16[4,256,128]{2,1,0:T(8,128)(2,1)S(1)}, u32[]{:S(2)}, u32[]{:S(2)}) %collective-permute-start.21) | collective-permute-done | bytes 262176 | tf_op jit(solution)/shard_map/ppermute | solution.py:22
  85.2 1.3 %place_rows.5.whole = bf16[32,256,128]{2,1,0:T(8,128)(2,1)} custom-call(s32[5]{0:T(128)S(1)} %copy-done.19, bf16[4,256,128]{2,1,0:T(8,128)(2,1)S(1)} %collective-permute-done.21.part, bf16[32,256,128]{2,1,0:T(8,128)(2,1)} %place_rows.4.whole), custom_call_target="tpu_custom_call", output_to_operand_aliasing={{}: (2, {})} | custom-call | tf_op jit(solution)/shard_map/place_rows/pallas_call | solution.py:223
  86.5 2.3 %collective-permute-done.20.part = bf16[4,256,128]{2,1,0:T(8,128)(2,1)S(1)} collective-permute-done((bf16[4,256,128]{2,1,0:T(8,128)(2,1)S(1)}, bf16[4,256,128]{2,1,0:T(8,128)(2,1)S(1)}, u32[]{:S(2)}, u32[]{:S(2)}) %collective-permute-start.20) | collective-permute-done | bytes 262176 | tf_op jit(solution)/shard_map/ppermute | solution.py:22
  88.7 1.3 %place_rows.6.whole = bf16[32,256,128]{2,1,0:T(8,128)(2,1)} custom-call(s32[5]{0:T(128)S(1)} %copy-done.19, bf16[4,256,128]{2,1,0:T(8,128)(2,1)S(1)} %collective-permute-done.20.part, bf16[32,256,128]{2,1,0:T(8,128)(2,1)} %place_rows.5.whole), custom_call_target="tpu_custom_call", output_to_operand_aliasing={{}: (2, {})} | custom-call | tf_op jit(solution)/shard_map/place_rows/pallas_call | solution.py:223
  90.1 1.2 %place_rows.7 = bf16[32,256,128]{2,1,0:T(8,128)(2,1)} custom-call(s32[5]{0:T(128)S(1)} %copy-done.19, bf16[2,256,128]{2,1,0:T(8,128)(2,1)S(1)} %collective-permute-done.17.part, bf16[32,256,128]{2,1,0:T(8,128)(2,1)} %place_rows.6.whole), custom_call_target="tpu_custom_call", output_to_operand_aliasing={{}: (2, {})} | custom-call | tf_op jit(solution)/shard_map/place_rows/pallas_call | solution.py:223
  (80 shorter events, 4.8 us)
Async XLA Ops:
  0.6 7.4 %copy-start.13 = (bf16[1,256,256]{2,1,0:T(8,128)(2,1)S(1)}, bf16[1,256,256]{2,1,0:T(8,128)(2,1)}, u32[]{:S(2)}) copy-start(bf16[1,256,256]{2,1,0:T(8,128)(2,1)} %lower_inv) | copy-start | bytes 393220
  0.6 7.4 %copy-start.11 = (bf16[1,2,256,256]{3,2,1,0:T(8,128)(2,1)S(1)}, bf16[1,2,256,256]{3,2,1,0:T(8,128)(2,1)}, u32[]{:S(2)}) copy-start(bf16[1,2,256,256]{3,2,1,0:T(8,128)(2,1)} %lower_panels.1) | copy-start | bytes 786436
  0.7 7.4 %copy-start.14 = (bf16[1,256,256]{2,1,0:T(8,128)(2,1)S(1)}, bf16[1,256,256]{2,1,0:T(8,128)(2,1)}, u32[]{:S(2)}) copy-start(bf16[1,256,256]{2,1,0:T(8,128)(2,1)} %upper_inv.1) | copy-start | bytes 393220
  0.7 7.4 %copy-start.12 = (bf16[1,2,256,256]{3,2,1,0:T(8,128)(2,1)S(1)}, bf16[1,2,256,256]{3,2,1,0:T(8,128)(2,1)}, u32[]{:S(2)}) copy-start(bf16[1,2,256,256]{3,2,1,0:T(8,128)(2,1)} %upper_panels.1) | copy-start | bytes 786436
  0.7 9.3 %copy-start.24 = (s32[8,3]{0,1:T(4,128)S(1)}, s32[8,3]{0,1:T(4,128)}, u32[]{:S(2)}) copy-start(s32[8,3]{0,1:T(4,128)} %param.16) | copy-start | bytes 292
  2.6 12.2 %collective-permute-start.3 = (bf16[8,3,256,256]{3,2,1,0:T(8,128)(2,1)}, bf16[8,3,256,256]{3,2,1,0:T(8,128)(2,1)}, u32[]{:S(2)}, u32[]{:S(2)}) collective-permute-start(bf16[8,3,256,256]{3,2,1,0:T(8,128)(2,1)} %refs_3_.2), channel_id=1, source_target_pairs={{0,1},{1,0},{2,3},{3,2},{4,5},{5,4},{6,7},{7,6},{8,9},{9,8},{10,11... | collective-permute-start | bytes 9437192 | tf_op jit(solution)/shard_map/ppermute | solution.py:22
  3.1 9.7 %collective-permute-start.2 = (bf16[8,256,256]{2,1,0:T(8,128)(2,1)}, bf16[8,256,256]{2,1,0:T(8,128)(2,1)S(1)}, u32[]{:S(2)}, u32[]{:S(2)}) collective-permute-start(bf16[8,256,256]{2,1,0:T(8,128)(2,1)} %refs_2_.1), channel_id=1, source_target_pairs={{0,1},{1,0},{2,3},{3,2},{4,5},{5,4},{6,7},{7,6},{8,9},{9,8},{10,11... | collective-permute-start | bytes 3145736 | tf_op jit(solution)/shard_map/ppermute | solution.py:22
  3.2 17.2 %collective-permute-start = (bf16[8,256,128]{2,1,0:T(8,128)(2,1)}, bf16[8,256,128]{2,1,0:T(8,128)(2,1)}, u32[]{:S(2)}, u32[]{:S(2)}) collective-permute-start(bf16[8,256,128]{2,1,0:T(8,128)(2,1)} %constant_dynamic-slice_fusion.1), channel_id=1, source_target_pairs={{0,2},{1,3},{2,0},{3,1},{4,6},{5,7},{6,4},{7,5},{8,10},{9,11},{10,... | collective-permute-start | bytes 1572872 | tf_op jit(solution)/shard_map/ppermute | solution.py:22
  8.4 18.2 %collective-permute-start.5 = (bf16[3,256,256]{2,1,0:T(8,128)(2,1)S(1)}, bf16[3,256,256]{2,1,0:T(8,128)(2,1)S(1)}, u32[]{:S(2)}, u32[]{:S(2)}) collective-permute-start(bf16[3,256,256]{2,1,0:T(8,128)(2,1)S(1)} %get-tuple-element.52), channel_id=1, source_target_pairs={{0,4},{4,0},{8,12},{12,8},{16,20},{20,16},{24,28},{28,24},{1,5},{5... | collective-permute-start | bytes 1179656 | tf_op jit(solution)/shard_map/ppermute | solution.py:22
  10.0 10.3 %copy-start.15 = (s32[8,3]{1,0:T(8,128)}, s32[8,3]{1,0:T(8,128)S(1)}, u32[]{:S(2)}) copy-start(s32[8,3]{1,0:T(8,128)S(1)} %copy.20.ancestors) | copy-start | bytes 292
  10.0 1.2 %collective-permute-start.1 = (s32[8,3]{1,0:T(8,128)S(1)}, s32[8,3]{1,0:T(8,128)S(1)}, u32[]{:S(2)}, u32[]{:S(2)}) collective-permute-start(s32[8,3]{1,0:T(8,128)S(1)} %copy.20.ancestors), channel_id=1, source_target_pairs={{0,1},{1,0},{2,3},{3,2},{4,5},{5,4},{6,7},{7,6},{8,9},{9,8},{10,11... | collective-permute-start | bytes 296 | tf_op jit(solution)/shard_map/ppermute | solution.py:22
  11.2 3.7 %copy-start.17 = (s32[8,3]{1,0:T(8,128)}, s32[8,3]{1,0:T(8,128)S(1)}, u32[]{:S(2)}) copy-start(s32[8,3]{1,0:T(8,128)S(1)} %collective-permute-done.1.ancestors) | copy-start | bytes 292
  11.2 18.6 %collective-permute-start.4 = (bf16[8,256,128]{2,1,0:T(8,128)(2,1)}, bf16[8,256,128]{2,1,0:T(8,128)(2,1)}, u32[]{:S(2)}, u32[]{:S(2)}) collective-permute-start(bf16[8,256,128]{2,1,0:T(8,128)(2,1)} %constant_dynamic-slice_fusion), channel_id=1, source_target_pairs={{0,2},{1,3},{2,0},{3,1},{4,6},{5,7},{6,4},{7,5},{8,10},{9,11},{10,... | collective-permute-start | bytes 1572872 | tf_op jit(solution)/shard_map/ppermute | solution.py:22
  12.8 2.1 %copy-start.20 = (bf16[8,256,256]{2,1,0:T(8,128)(2,1)}, bf16[8,256,256]{2,1,0:T(8,128)(2,1)S(1)}, u32[]{:S(2)}) copy-start(bf16[8,256,256]{2,1,0:T(8,128)(2,1)S(1)} %collective-permute-done.2.refs_1_) | copy-start | bytes 3145732
  12.8 13.8 %collective-permute-start.6 = (bf16[2,256,256]{2,1,0:T(8,128)(2,1)S(1)}, bf16[2,256,256]{2,1,0:T(8,128)(2,1)S(1)}, u32[]{:S(2)}, u32[]{:S(2)}) collective-permute-start(bf16[2,256,256]{2,1,0:T(8,128)(2,1)S(1)} %get-tuple-element.53), channel_id=1, source_target_pairs={{0,4},{4,0},{8,12},{12,8},{16,20},{20,16},{24,28},{28,24},{1,5},{5... | collective-permute-start | bytes 786440 | tf_op jit(solution)/shard_map/ppermute | solution.py:22
  26.6 9.2 %collective-permute-start.7 = (bf16[1,256,256]{2,1,0:T(8,128)(2,1)S(1)}, bf16[1,256,256]{2,1,0:T(8,128)(2,1)S(1)}, u32[]{:S(2)}, u32[]{:S(2)}) collective-permute-start(bf16[1,256,256]{2,1,0:T(8,128)(2,1)S(1)} %get-tuple-element.57), channel_id=1, source_target_pairs={{16,0},{20,4},{17,1},{21,5},{18,2},{22,6},{19,3},{23,7}} | collective-permute-start | bytes 393224 | tf_op jit(solution)/shard_map/ppermute | solution.py:334
  27.9 7.9 %collective-permute-start.8 = (bf16[1,256,256]{2,1,0:T(8,128)(2,1)S(1)}, bf16[1,256,256]{2,1,0:T(8,128)(2,1)S(1)}, u32[]{:S(2)}, u32[]{:S(2)}) collective-permute-start(bf16[1,256,256]{2,1,0:T(8,128)(2,1)S(1)} %get-tuple-element.57), channel_id=1, source_target_pairs={{16,8},{20,12},{17,9},{21,13},{18,10},{22,14},{19,11},{23,15}} | collective-permute-start | bytes 393224 | tf_op jit(solution)/shard_map/ppermute | solution.py:334
  28.6 13.2 %copy-start.21 = (bf16[3,256,128]{2,1,0:T(8,128)(2,1)S(1)}, bf16[3,256,128]{2,1,0:T(8,128)(2,1)}, u32[]{:S(2)}) copy-start(bf16[3,256,128]{2,1,0:T(8,128)(2,1)} %get-tuple-element.47) | copy-start | bytes 589828
  35.8 2.8 %copy-start.22 = (bf16[1,256,256]{2,1,0:T(8,128)(2,1)}, bf16[1,256,256]{2,1,0:T(8,128)(2,1)S(1)}, u32[]{:S(2)}) copy-start(bf16[1,256,256]{2,1,0:T(8,128)(2,1)S(1)} %collective-permute-done.7.refs_0_) | copy-start | bytes 393220
  35.8 2.8 %copy-start.23 = (bf16[1,256,256]{2,1,0:T(8,128)(2,1)}, bf16[1,256,256]{2,1,0:T(8,128)(2,1)S(1)}, u32[]{:S(2)}) copy-start(bf16[1,256,256]{2,1,0:T(8,128)(2,1)S(1)} %collective-permute-done.8.refs_1_) | copy-start | bytes 393220
  35.8 6.0 %collective-permute-start.9 = (bf16[3,256,128]{2,1,0:T(8,128)(2,1)}, bf16[3,256,128]{2,1,0:T(8,128)(2,1)S(1)}, u32[]{:S(2)}, u32[]{:S(2)}) collective-permute-start(bf16[3,256,128]{2,1,0:T(8,128)(2,1)} %get-tuple-element.60), channel_id=1, source_target_pairs={{0,2},{1,3},{2,0},{3,1},{4,6},{5,7},{6,4},{7,5},{8,10},{9,11},{10,... | collective-permute-start | bytes 589832 | tf_op jit(solution)/shard_map/ppermute | solution.py:22
  37.1 9.9 %collective-permute-start.11 = (bf16[3,256,256]{2,1,0:T(8,128)(2,1)S(1)}, bf16[3,256,256]{2,1,0:T(8,128)(2,1)S(1)}, u32[]{:S(2)}, u32[]{:S(2)}) collective-permute-start(bf16[3,256,256]{2,1,0:T(8,128)(2,1)S(1)} %get-tuple-element.56.mine), channel_id=1, source_target_pairs={{0,8},{4,12},{8,0},{12,4},{16,24},{20,28},{24,16},{28,20},{1,9},{5... | collective-permute-start | bytes 1179656 | tf_op jit(solution)/shard_map/ppermute | solution.py:22
  41.9 5.9 %collective-permute-start.10 = (bf16[3,256,128]{2,1,0:T(8,128)(2,1)S(1)}, bf16[3,256,128]{2,1,0:T(8,128)(2,1)S(1)}, u32[]{:S(2)}, u32[]{:S(2)}) collective-permute-start(bf16[3,256,128]{2,1,0:T(8,128)(2,1)S(1)} %add_convert_fusion.mine), channel_id=1, source_target_pairs={{0,4},{4,0},{8,12},{12,8},{16,20},{20,16},{24,28},{28,24},{1,5},{5... | collective-permute-start | bytes 589832 | tf_op jit(solution)/shard_map/ppermute | solution.py:22
  43.4 4.4 %copy-start.3 = (bf16[5,256,256]{2,1,0:T(8,128)(2,1)}, bf16[5,256,256]{2,1,0:T(8,128)(2,1)S(1)}, u32[]{:S(2)}) copy-start(bf16[5,256,256]{2,1,0:T(8,128)(2,1)S(1)} %sort.7.factors) | copy-start | bytes 1966084
  47.0 0.8 copy-start.6
  47.0 6.9 %copy-start = (bf16[8,3,256,256]{3,2,1,0:T(8,128)(2,1)S(1)}, bf16[8,3,256,256]{3,2,1,0:T(8,128)(2,1)}, u32[]{:S(2)}) copy-start(bf16[8,3,256,256]{3,2,1,0:T(8,128)(2,1)} %panels.5) | copy-start | bytes 9437188
  47.8 0.7 copy-start.9
  48.4 5.3 %collective-permute-start.12 = (bf16[2,256,128]{2,1,0:T(8,128)(2,1)S(1)}, bf16[2,256,128]{2,1,0:T(8,128)(2,1)S(1)}, u32[]{:S(2)}, u32[]{:S(2)}) collective-permute-start(bf16[2,256,128]{2,1,0:T(8,128)(2,1)S(1)} %get-tuple-element.65.mine), channel_id=1, source_target_pairs={{0,8},{4,12},{8,0},{12,4},{16,24},{20,28},{24,16},{28,20},{1,9},{5... | collective-permute-start | bytes 393224 | tf_op jit(solution)/shard_map/ppermute | solution.py:22
  51.6 1.1 %copy-start.4 = (bf16[5,256,256]{2,1,0:T(8,128)(2,1)S(1)}, bf16[5,256,256]{2,1,0:T(8,128)(2,1)}, u32[]{:S(2)}) copy-start(bf16[5,256,256]{2,1,0:T(8,128)(2,1)} %copy-done.3) | copy-start | bytes 1966084
  52.7 1.0 %copy-start.7 = (bf16[3,256,256]{2,1,0:T(8,128)(2,1)S(1)}, bf16[3,256,256]{2,1,0:T(8,128)(2,1)}, u32[]{:S(2)}) copy-start(bf16[3,256,256]{2,1,0:T(8,128)(2,1)} %copy-done.6) | copy-start | bytes 1179652
  53.7 12.2 %copy-start.1 = (bf16[8,256,256]{2,1,0:T(8,128)(2,1)S(1)}, bf16[8,256,256]{2,1,0:T(8,128)(2,1)}, u32[]{:S(2)}) copy-start(bf16[8,256,256]{2,1,0:T(8,128)(2,1)} %inv.5) | copy-start | bytes 3145732
  53.7 12.2 %copy-start.2 = (bf16[8,256,256]{2,1,0:T(8,128)(2,1)S(1)}, bf16[8,256,256]{2,1,0:T(8,128)(2,1)}, u32[]{:S(2)}) copy-start(bf16[8,256,256]{2,1,0:T(8,128)(2,1)} %get-tuple-element.46.value) | copy-start | bytes 3145732
  53.9 14.5 %collective-permute-start.19 = (bf16[8,3,256,256]{3,2,1,0:T(8,128)(2,1)S(1)}, bf16[8,3,256,256]{3,2,1,0:T(8,128)(2,1)S(1)}, u32[]{:S(2)}, u32[]{:S(2)}) collective-permute-start(bf16[8,3,256,256]{3,2,1,0:T(8,128)(2,1)S(1)} %copy-done), channel_id=1, source_target_pairs={{0,1},{1,0},{2,3},{3,2},{4,5},{5,4},{6,7},{7,6},{8,9},{9,8},{10,11... | collective-permute-start | bytes 9437192 | tf_op jit(solution)/shard_map/ppermute | solution.py:22
  54.0 14.5 %collective-permute-start.18 = (bf16[8,256,256]{2,1,0:T(8,128)(2,1)}, bf16[8,256,256]{2,1,0:T(8,128)(2,1)S(1)}, u32[]{:S(2)}, u32[]{:S(2)}) collective-permute-start(bf16[8,256,256]{2,1,0:T(8,128)(2,1)} %inv.5), channel_id=1, source_target_pairs={{0,1},{1,0},{2,3},{3,2},{4,5},{5,4},{6,7},{7,6},{8,9},{9,8},{10,11... | collective-permute-start | bytes 3145736 | tf_op jit(solution)/shard_map/ppermute | solution.py:22
  54.5 6.4 %collective-permute-start.14 = (bf16[1,256,128]{2,1,0:T(8,128)(2,1)S(1)}, bf16[1,256,128]{2,1,0:T(8,128)(2,1)S(1)}, u32[]{:S(2)}, u32[]{:S(2)}) collective-permute-start(bf16[1,256,128]{2,1,0:T(8,128)(2,1)S(1)} %get-tuple-element.70.mine), channel_id=1, source_target_pairs={{0,16},{4,20},{8,24},{12,28},{16,0},{20,4},{24,8},{28,12},{1,17},{... | collective-permute-start | bytes 196616 | tf_op jit(solution)/shard_map/ppermute | solution.py:22
  57.1 4.8 %collective-permute-start.16 = (bf16[1,256,128]{2,1,0:T(8,128)(2,1)S(1)}, bf16[1,256,128]{2,1,0:T(8,128)(2,1)S(1)}, u32[]{:S(2)}, u32[]{:S(2)}) collective-permute-start(bf16[1,256,128]{2,1,0:T(8,128)(2,1)S(1)} %get-tuple-element.74.refs_2_), channel_id=1, source_target_pairs={{0,2},{1,3},{2,0},{3,1},{4,6},{5,7},{6,4},{7,5},{8,10},{9,11},{10,... | collective-permute-start | bytes 196616 | tf_op jit(solution)/shard_map/ppermute | solution.py:22
  58.0 5.0 %collective-permute-start.13 = (bf16[1,256,128]{2,1,0:T(8,128)(2,1)S(1)}, bf16[1,256,128]{2,1,0:T(8,128)(2,1)S(1)}, u32[]{:S(2)}, u32[]{:S(2)}) collective-permute-start(bf16[1,256,128]{2,1,0:T(8,128)(2,1)S(1)} %get-tuple-element.69.own), channel_id=1, source_target_pairs={{0,2},{1,3},{2,0},{3,1},{4,6},{5,7},{6,4},{7,5},{8,10},{9,11},{10,... | collective-permute-start | bytes 196616 | tf_op jit(solution)/shard_map/ppermute | solution.py:22
  60.9 4.3 %collective-permute-start.15 = (bf16[1,256,128]{2,1,0:T(8,128)(2,1)S(1)}, bf16[1,256,128]{2,1,0:T(8,128)(2,1)S(1)}, u32[]{:S(2)}, u32[]{:S(2)}) collective-permute-start(bf16[1,256,128]{2,1,0:T(8,128)(2,1)S(1)} %enter.1.own_top), channel_id=1, source_target_pairs={{0,2},{1,3},{2,0},{3,1},{4,6},{5,7},{6,4},{7,5},{8,10},{9,11},{10,... | collective-permute-start | bytes 196616 | tf_op jit(solution)/shard_map/ppermute | solution.py:22
  61.9 0.9 copy-start.10
  62.8 3.0 %copy-start.16 = (s32[8,3]{1,0:T(8,128)S(1)}, s32[8,3]{1,0:T(8,128)}, u32[]{:S(2)}) copy-start(s32[8,3]{1,0:T(8,128)} %copy-done.15) | copy-start | bytes 292
  65.9 2.6 %copy-start.5 = (bf16[8,256,128]{2,1,0:T(8,128)(2,1)S(1)}, bf16[8,256,128]{2,1,0:T(8,128)(2,1)}, u32[]{:S(2)}) copy-start(bf16[8,256,128]{2,1,0:T(8,128)(2,1)} %get-tuple-element.78.value) | copy-start | bytes 1572868
  65.9 2.6 %copy-start.18 = (s32[8,3]{1,0:T(8,128)S(1)}, s32[8,3]{1,0:T(8,128)}, u32[]{:S(2)}) copy-start(s32[8,3]{1,0:T(8,128)} %copy-done.17) | copy-start | bytes 292
  67.5 14.7 %collective-permute-start.22 = (bf16[6,256,128]{2,1,0:T(8,128)(2,1)S(1)}, bf16[6,256,128]{2,1,0:T(8,128)(2,1)S(1)}, u32[]{:S(2)}, u32[]{:S(2)}) collective-permute-start(bf16[6,256,128]{2,1,0:T(8,128)(2,1)S(1)} %solve_far.7), channel_id=1, source_target_pairs={{0,2},{1,3},{2,0},{3,1},{4,6},{5,7},{6,4},{7,5},{8,10},{9,11},{10,... | collective-permute-start | bytes 1179656 | tf_op jit(solution)/shard_map/ppermute | solution.py:22
  69.9 15.4 %collective-permute-start.21 = (bf16[4,256,128]{2,1,0:T(8,128)(2,1)S(1)}, bf16[4,256,128]{2,1,0:T(8,128)(2,1)S(1)}, u32[]{:S(2)}, u32[]{:S(2)}) collective-permute-start(bf16[4,256,128]{2,1,0:T(8,128)(2,1)S(1)} %solve_far.6), channel_id=1, source_target_pairs={{0,2},{1,3},{2,0},{3,1},{4,6},{5,7},{6,4},{7,5},{8,10},{9,11},{10,... | collective-permute-start | bytes 786440 | tf_op jit(solution)/shard_map/ppermute | solution.py:22
  72.4 2.2 %copy-start.19 = (s32[5]{0:T(128)S(1)}, s32[5]{0:T(128)}, u32[]{:S(2)}) copy-start(s32[5]{0:T(128)} %stack.23.scalars) | copy-start | bytes 64
  72.4 16.3 %collective-permute-start.20 = (bf16[4,256,128]{2,1,0:T(8,128)(2,1)S(1)}, bf16[4,256,128]{2,1,0:T(8,128)(2,1)S(1)}, u32[]{:S(2)}, u32[]{:S(2)}) collective-permute-start(bf16[4,256,128]{2,1,0:T(8,128)(2,1)S(1)} %solve_far.5), channel_id=1, source_target_pairs={{0,2},{1,3},{2,0},{3,1},{4,6},{5,7},{6,4},{7,5},{8,10},{9,11},{10,... | collective-permute-start | bytes 786440 | tf_op jit(solution)/shard_map/ppermute | solution.py:22
  74.6 4.8 %copy-start.8 = (bf16[8,256,128]{2,1,0:T(8,128)(2,1)S(1)}, bf16[8,256,128]{2,1,0:T(8,128)(2,1)}, u32[]{:S(2)}) copy-start(bf16[8,256,128]{2,1,0:T(8,128)(2,1)} %get-tuple-element.81.value) | copy-start | bytes 1572868
  77.5 12.6 %collective-permute-start.17 = (bf16[2,256,128]{2,1,0:T(8,128)(2,1)S(1)}, bf16[2,256,128]{2,1,0:T(8,128)(2,1)S(1)}, u32[]{:S(2)}, u32[]{:S(2)}) collective-permute-start(bf16[2,256,128]{2,1,0:T(8,128)(2,1)S(1)} %solve_far.4), channel_id=1, source_target_pairs={{0,2},{1,3},{2,0},{3,1},{4,6},{5,7},{6,4},{7,5},{8,10},{9,11},{10,... | collective-permute-start | bytes 393224 | tf_op jit(solution)/shard_map/ppermute | solution.py:22

commit v7 on v6

--- a/solution.py
+++ b/solution.py
@@ -213,34 +213,27 @@
     )(scalars, ancestors, value, inv, panels, paths, *extra)
 
 
-def place_kernel(scalars, part, whole, result):
-    result[...] = part[...]
-
-
-def place_rows(scalars, which, offset, part, whole):
-    count, size, cols = part.shape
-    batch = max(leaves for leaves in (8, 4, 2, 1) if count % leaves == 0 and offset % leaves == 0)
-    return pl.pallas_call(
-        place_kernel,
-        grid_spec=pltpu.PrefetchScalarGridSpec(
-            num_scalar_prefetch=1,
-            grid=(count // batch,),
-            in_specs=[
-                pl.BlockSpec(memory_space=pltpu.VMEM)
-                if count == batch
-                else pl.BlockSpec((batch, size, cols), lambda i, _: (i, 0, 0)),
-                pl.BlockSpec(memory_space=pl.ANY),
-            ],
-            out_specs=pl.BlockSpec(
-                (batch, size, cols), lambda i, scalars: ((scalars[which] + offset) // batch + i, 0, 0)
-            ),
-        ),
+def place_kernel(group, leaves, offset, part, whole, result, sem):
+    place = lax.axis_index("col")
+    row = (1 - place // 2) * 2 * leaves + (place + group) % 2 * leaves + offset
+    copy = pltpu.make_async_copy(part, result.at[pl.ds(row, part.shape[0])], sem)
+    copy.start()
+    copy.wait()
+
+
+def place_rows(group, leaves, offset, part, whole):
+    hbm = pl.BlockSpec(memory_space=pl.ANY)
+    return pl.pallas_call(
+        functools.partial(place_kernel, group, leaves, offset),
+        in_specs=[pl.BlockSpec(memory_space=pltpu.VMEM), hbm],
+        out_specs=hbm,
         out_shape=jax.ShapeDtypeStruct(whole.shape, whole.dtype),
-        input_output_aliases={2: 0},
+        scratch_shapes=[pltpu.SemaphoreType.DMA],
+        input_output_aliases={1: 0},
         compiler_params=pltpu.CompilerParams(vmem_limit_bytes=LEAF_VMEM),
         cost_estimate=cost(0, 0),
         name="place_rows",
-    )(scalars, part, whole)
+    )(part, whole)
 
 
 def combine_kernel(lower_inv, lower_panels, upper_inv, upper_panels, blocks, *parts):
@@ -478,7 +471,7 @@
     own_level = sum(jnp.where(is_owner, level, 0) for level, is_owner in enumerate(owned, 1))
 
     away = (1 - high) * 2 * count
-    scalars = jnp.stack([first, second, own_level, away + low * count, away + (1 - low) * count]).astype(jnp.int32)
+    scalars = jnp.stack([first, second, own_level]).astype(jnp.int32)
     half = count // 2
     sent = [lax.dynamic_slice_in_dim(leaf_rhs, away + low * count, count, 0)]
     sent.append(lax.dynamic_slice_in_dim(after(leaf_rhs, sent[0]), away + (1 - low) * count, count, 0))
@@ -546,14 +539,14 @@
     leaf_solution = solve_own(scalars, 0, *local, value_1, paths, rows)
     quarter = half // 2
     returning = [
-        (3, 0, solve_far(*local, value_1, paths, 0, count - quarter)),
-        (4, 0, solve_far(*near, value_2_far, paths, 0, half)),
-        (4, half, solve_far(*near, value_2_far, paths, half, half)),
-        (3, count - quarter, solve_far(*local, value_1, paths, count - quarter, quarter)),
+        (0, 0, solve_far(*local, value_1, paths, 0, count - quarter)),
+        (1, 0, solve_far(*near, value_2_far, paths, 0, half)),
+        (1, half, solve_far(*near, value_2_far, paths, half, half)),
+        (0, count - quarter, solve_far(*local, value_1, paths, count - quarter, quarter)),
     ]
     leaf_solution = solve_own(scalars, 1, *near, value_2_own, paths, rows, leaf_solution)
-    for which, offset, part in returning:
-        leaf_solution = place_rows(scalars, which, offset, swap(part, "col", 2), leaf_solution)
+    for group, offset, part in returning:
+        leaf_solution = place_rows(group, count, offset, swap(part, "col", 2), leaf_solution)
     return (leaf_solution, own_solution[None])
 
 

time: 91.8 us -> 91.3 us (level)
  Pallas kernels: 38.8 us -> 36 us
  waiting for transfers between devices: 15.7 us -> 17.9 us
    pallas_call x4, Pallas kernels: 5.63 us -> 2.86 us  [place_rows(): pl.pallas_call(functools.partial(place_kernel, group, leaves, offset), in...]
    ppermute x21, waiting for transfers between devices: 15.1 us -> 17.3 us  [swap(): return lax.ppermute(value, axis, pairs)]
  transfers between devices with their start and end apart: 23 -> 23, of which waited for: 11 -> 12; matrix products, arithmetic and copies ran while one was open for 4% -> 4% of each run, Pallas kernels for 41% -> 38%
where the time goes in v7:
time: 91.3 us; the launch traced here: 90.8 us
  Pallas kernels  36 us (39%)
  starting transfers between devices  26.4 us (29%)
  waiting for transfers between devices  17.9 us (20%)
  local copies, waits for them, and re-layouts  8.1 us (9%)
  other arithmetic  1.29 us (1%)
  between operations  1.11 us (1%)
    ppermute x21, starting transfers between devices, swap(): return lax.ppermute(value, axis, pairs)  24.5 us
    ppermute x21, waiting for transfers between devices, swap(): return lax.ppermute(value, axis, pairs)  17.3 us
    pallas_call x3, Pallas kernels, forward(): pl.pallas_call(functools.partial(forward_kernel, rhs is not None, far is...  17.1 us
    pallas_call x2, Pallas kernels, solve_own(): pl.pallas_call(functools.partial(keep_kernel, which), grid=(count // batc...  5.81 us
    pallas_call x4, Pallas kernels, solve_far(): pl.pallas_call(functools.partial(send_kernel, base), grid=(count // batch...  5.47 us
    unnamed x51, local copies, waits for them, and re-layouts  4.28 us
    pallas_call x2, Pallas kernels, pick(): pl.pallas_call(pick_kernel, in_specs=[pl.BlockSpec(memory_space=pltpu.SME...  3.13 us
    pallas_call x4, Pallas kernels, place_rows(): pl.pallas_call(functools.partial(place_kernel, group, leaves, offset), in...  2.86 us
  transfers between devices with their start and end apart: 23, of which 12 were waited for; matrix products, arithmetic and copies ran while one was open for 4% of the time, Pallas kernels for 38%

profile of v7, /device:TPU:0, one launch (start us, length us, event | category | flops | bytes accessed | tf_op | source)
XLA Modules:
  0.0 90.8 jit_solution(4947243962717632361)
XLA Ops:
  0.7 1.9 %constant_dynamic-slice_fusion.1 = bf16[8,256,128]{2,1,0:T(8,128)(2,1)} fusion(bf16[32,256,128]{2,1,0:T(8,128)(2,1)} %refs_0_.3, s32[]{:T(128)S(6)} %select_n.94), kind=kLoop, calls=%fused_computation.6 | loop fusion | bytes 1048580 | tf_op jit(solution)/shard_map/dynamic_slice | solution.py:476
  3.2 3.0 %collective-permute-start = (bf16[8,256,128]{2,1,0:T(8,128)(2,1)}, bf16[8,256,128]{2,1,0:T(8,128)(2,1)}, u32[]{:S(2)}, u32[]{:S(2)}) collective-permute-start(bf16[8,256,128]{2,1,0:T(8,128)(2,1)} %constant_dynamic-slice_fusion.1), channel_id=1, source_target_pairs={{0,2},{1,3},{2,0},{3,1},{4,6},{5,7},{6,4},{7,5},{8,10},{9,11},{10,... | collective-permute-start | bytes 1572872 | tf_op jit(solution)/shard_map/ppermute | solution.py:22
  6.1 1.9 %constant_dynamic-slice_fusion = bf16[8,256,128]{2,1,0:T(8,128)(2,1)} fusion(bf16[32,256,128]{2,1,0:T(8,128)(2,1)} %refs_0_.3, s32[]{:T(128)S(6)} %select_n.95), kind=kLoop, calls=%fused_computation.5 | loop fusion | bytes 1048580 | tf_op jit(solution)/shard_map/dynamic_slice | solution.py:477
  8.4 1.6 %collective-permute-start.5 = (bf16[3,256,256]{2,1,0:T(8,128)(2,1)S(1)}, bf16[3,256,256]{2,1,0:T(8,128)(2,1)S(1)}, u32[]{:S(2)}, u32[]{:S(2)}) collective-permute-start(bf16[3,256,256]{2,1,0:T(8,128)(2,1)S(1)} %get-tuple-element.52), channel_id=1, source_target_pairs={{0,4},{4,0},{8,12},{12,8},{16,20},{20,16},{24,28},{28,24},{1,5},{5... | collective-permute-start | bytes 1179656 | tf_op jit(solution)/shard_map/ppermute | solution.py:22
  10.0 1.2 %collective-permute-done.1.ancestors = s32[8,3]{1,0:T(8,128)S(1)} collective-permute-done((s32[8,3]{1,0:T(8,128)S(1)}, s32[8,3]{1,0:T(8,128)S(1)}, u32[]{:S(2)}, u32[]{:S(2)}) %collective-permute-start.1) | collective-permute-done | bytes 128 | tf_op jit(solution)/shard_map/ppermute | solution.py:22
  11.2 1.6 %collective-permute-start.4 = (bf16[8,256,128]{2,1,0:T(8,128)(2,1)}, bf16[8,256,128]{2,1,0:T(8,128)(2,1)}, u32[]{:S(2)}, u32[]{:S(2)}) collective-permute-start(bf16[8,256,128]{2,1,0:T(8,128)(2,1)} %constant_dynamic-slice_fusion), channel_id=1, source_target_pairs={{0,2},{1,3},{2,0},{3,1},{4,6},{5,7},{6,4},{7,5},{8,10},{9,11},{10,... | collective-permute-start | bytes 1572872 | tf_op jit(solution)/shard_map/ppermute | solution.py:22
  12.8 1.5 %collective-permute-start.6 = (bf16[2,256,256]{2,1,0:T(8,128)(2,1)S(1)}, bf16[2,256,256]{2,1,0:T(8,128)(2,1)S(1)}, u32[]{:S(2)}, u32[]{:S(2)}) collective-permute-start(bf16[2,256,256]{2,1,0:T(8,128)(2,1)S(1)} %get-tuple-element.53), channel_id=1, source_target_pairs={{0,4},{4,0},{8,12},{12,8},{16,20},{20,16},{24,28},{28,24},{1,5},{5... | collective-permute-start | bytes 786440 | tf_op jit(solution)/shard_map/ppermute | solution.py:22
  14.9 5.4 %leaf_forward.3 = (bf16[8,256,128]{2,1,0:T(8,128)(2,1)}, f32[3,256,128]{2,1,0:T(8,128)}) custom-call(s32[3]{0:T(128)} %pad_add_fusion.scalars, s32[8,3]{1,0:T(8,128)} %copy-done.17, bf16[32,256,128]{2,1,0:T(8,128)(2,1)} %refs_0_.3, bf16[8,256,256]{2,1,0:T(8,128)(2,1)} %copy-done.20, bf16[8,3,256,256]{3,2,1,0:T(8,128)(2,1)} %collective-permute-done.3.refs_2_, ...), custom_call_target="tpu_custom_call" | custom-call | tf_op jit(solution)/shard_map/leaf_forward/pallas_call | solution.py:95
  20.3 6.2 %leaf_forward.4 = (bf16[8,256,256]{2,1,0:T(8,128)(2,1)}, bf16[3,256,128]{2,1,0:T(8,128)(2,1)}, f32[3,256,128]{2,1,0:T(8,128)}) custom-call(s32[3]{0:T(128)} %pad_add_fusion.scalars, s32[8,3]{1,0:T(8,128)} %copy-done.15, bf16[32,256,128]{2,1,0:T(8,128)(2,1)} %refs_0_.3, bf16[8,256,128]{2,1,0:T(8,128)(2,1)} %collective-permute-done.refs_1_, ...), custom_call_target="tpu_custom_call" | custom-call | tf_op jit(solution)/shard_map/leaf_forward/pallas_call | solution.py:95
  26.6 1.3 %collective-permute-start.7 = (bf16[1,256,256]{2,1,0:T(8,128)(2,1)S(1)}, bf16[1,256,256]{2,1,0:T(8,128)(2,1)S(1)}, u32[]{:S(2)}, u32[]{:S(2)}) collective-permute-start(bf16[1,256,256]{2,1,0:T(8,128)(2,1)S(1)} %get-tuple-element.57), channel_id=1, source_target_pairs={{16,0},{20,4},{17,1},{21,5},{18,2},{22,6},{19,3},{23,7}} | collective-permute-start | bytes 393224 | tf_op jit(solution)/shard_map/ppermute | solution.py:327
  27.9 0.7 collective-permute-start.8
  28.6 1.2 %collective-permute-done.4.refs_0_ = bf16[8,256,128]{2,1,0:T(8,128)(2,1)} collective-permute-done((bf16[8,256,128]{2,1,0:T(8,128)(2,1)}, bf16[8,256,128]{2,1,0:T(8,128)(2,1)}, u32[]{:S(2)}, u32[]{:S(2)}) %collective-permute-start.4) | collective-permute-done | bytes 524320 | tf_op jit(solution)/shard_map/ppermute | solution.py:22
  29.8 5.5 %leaf_forward.5 = (bf16[8,256,128]{2,1,0:T(8,128)(2,1)}, bf16[3,256,128]{2,1,0:T(8,128)(2,1)}) custom-call(s32[3]{0:T(128)} %pad_add_fusion.scalars, s32[8,3]{1,0:T(8,128)} %copy-done.17, bf16[8,256,128]{2,1,0:T(8,128)(2,1)} %collective-permute-done.4.refs_0_, bf16[8,256,256]{2,1,0:T(8,128)(2,1)} %copy-done.20, ...), custom_call_target="tpu_custom_call" | custom-call | tf_op jit(solution)/shard_map/leaf_forward/pallas_call | solution.py:95
  35.8 1.3 %collective-permute-start.9 = (bf16[3,256,128]{2,1,0:T(8,128)(2,1)}, bf16[3,256,128]{2,1,0:T(8,128)(2,1)S(1)}, u32[]{:S(2)}, u32[]{:S(2)}) collective-permute-start(bf16[3,256,128]{2,1,0:T(8,128)(2,1)} %get-tuple-element.60), channel_id=1, source_target_pairs={{0,2},{1,3},{2,0},{3,1},{4,6},{5,7},{6,4},{7,5},{8,10},{9,11},{10,... | collective-permute-start | bytes 589832 | tf_op jit(solution)/shard_map/ppermute | solution.py:22
  37.1 1.6 %collective-permute-start.11 = (bf16[3,256,256]{2,1,0:T(8,128)(2,1)S(1)}, bf16[3,256,256]{2,1,0:T(8,128)(2,1)S(1)}, u32[]{:S(2)}, u32[]{:S(2)}) collective-permute-start(bf16[3,256,256]{2,1,0:T(8,128)(2,1)S(1)} %get-tuple-element.56.mine), channel_id=1, source_target_pairs={{0,8},{4,12},{8,0},{12,4},{16,24},{20,28},{24,16},{28,20},{1,9},{5... | collective-permute-start | bytes 1179656 | tf_op jit(solution)/shard_map/ppermute | solution.py:22
  38.7 1.6 %pick.2.refs_0_ = bf16[1,256,256]{2,1,0:T(8,128)(2,1)} custom-call(s32[1]{0:T(128)} %bitcast.4.flags, bf16[1,256,256]{2,1,0:T(8,128)(2,1)} %copy-done.22, bf16[1,256,256]{2,1,0:T(8,128)(2,1)} %copy-done.23), custom_call_target="tpu_custom_call" | custom-call | flops 1048576 | bytes 1048576 | tf_op jit(solution)/shard_map/pick/pallas_call | solution.py:308
  40.2 1.6 %collective-permute-done.9 = bf16[3,256,128]{2,1,0:T(8,128)(2,1)S(1)} collective-permute-done((bf16[3,256,128]{2,1,0:T(8,128)(2,1)}, bf16[3,256,128]{2,1,0:T(8,128)(2,1)S(1)}, u32[]{:S(2)}, u32[]{:S(2)}) %collective-permute-start.9) | collective-permute-done | bytes 196640 | tf_op jit(solution)/shard_map/ppermute | solution.py:22
  41.9 1.5 %collective-permute-start.10 = (bf16[3,256,128]{2,1,0:T(8,128)(2,1)S(1)}, bf16[3,256,128]{2,1,0:T(8,128)(2,1)S(1)}, u32[]{:S(2)}, u32[]{:S(2)}) collective-permute-start(bf16[3,256,128]{2,1,0:T(8,128)(2,1)S(1)} %add_convert_fusion.mine), channel_id=1, source_target_pairs={{0,4},{4,0},{8,12},{12,8},{16,20},{20,16},{24,28},{28,24},{1,5},{5... | collective-permute-start | bytes 589832 | tf_op jit(solution)/shard_map/ppermute | solution.py:22
  43.4 3.6 %collective-permute-done.11.refs_0_ = bf16[3,256,256]{2,1,0:T(8,128)(2,1)S(1)} collective-permute-done((bf16[3,256,256]{2,1,0:T(8,128)(2,1)S(1)}, bf16[3,256,256]{2,1,0:T(8,128)(2,1)S(1)}, u32[]{:S(2)}, u32[]{:S(2)}) %collective-permute-start.11) | collective-permute-done | bytes 393248 | tf_op jit(solution)/shard_map/ppermute | solution.py:22
  47.1 0.7 copy-done.6
  48.4 1.6 %collective-permute-start.12 = (bf16[2,256,128]{2,1,0:T(8,128)(2,1)S(1)}, bf16[2,256,128]{2,1,0:T(8,128)(2,1)S(1)}, u32[]{:S(2)}, u32[]{:S(2)}) collective-permute-start(bf16[2,256,128]{2,1,0:T(8,128)(2,1)S(1)} %get-tuple-element.65.mine), channel_id=1, source_target_pairs={{0,8},{4,12},{8,0},{12,4},{16,24},{20,28},{24,16},{28,20},{1,9},{5... | collective-permute-start | bytes 393224 | tf_op jit(solution)/shard_map/ppermute | solution.py:22
  50.0 1.6 %pick.3.next_factors = bf16[1,256,256]{2,1,0:T(8,128)(2,1)} custom-call(s32[1]{0:T(128)} %bitcast.5.flags, bf16[1,256,256]{2,1,0:T(8,128)(2,1)} %pick.2.refs_0_, bf16[1,256,256]{2,1,0:T(8,128)(2,1)} %copy-done.9), custom_call_target="tpu_custom_call" | custom-call | flops 1048576 | bytes 1048576 | tf_op jit(solution)/shard_map/pick/pallas_call | solution.py:308
  51.6 1.1 %copy-done.4 = bf16[5,256,256]{2,1,0:T(8,128)(2,1)S(1)} copy-done((bf16[5,256,256]{2,1,0:T(8,128)(2,1)S(1)}, bf16[5,256,256]{2,1,0:T(8,128)(2,1)}, u32[]{:S(2)}) %copy-start.4) | copy-done | bytes 655384
  52.7 1.0 %copy-done.7 = bf16[3,256,256]{2,1,0:T(8,128)(2,1)S(1)} copy-done((bf16[3,256,256]{2,1,0:T(8,128)(2,1)S(1)}, bf16[3,256,256]{2,1,0:T(8,128)(2,1)}, u32[]{:S(2)}) %copy-start.7) | copy-done | bytes 393240
  54.5 2.6 %collective-permute-start.14 = (bf16[1,256,128]{2,1,0:T(8,128)(2,1)S(1)}, bf16[1,256,128]{2,1,0:T(8,128)(2,1)S(1)}, u32[]{:S(2)}, u32[]{:S(2)}) collective-permute-start(bf16[1,256,128]{2,1,0:T(8,128)(2,1)S(1)} %get-tuple-element.70.mine), channel_id=1, source_target_pairs={{0,16},{4,20},{8,24},{12,28},{16,0},{20,4},{24,8},{28,12},{1,17},{... | collective-permute-start | bytes 196616 | tf_op jit(solution)/shard_map/ppermute | solution.py:22
  57.1 0.9 %collective-permute-start.16 = (bf16[1,256,128]{2,1,0:T(8,128)(2,1)S(1)}, bf16[1,256,128]{2,1,0:T(8,128)(2,1)S(1)}, u32[]{:S(2)}, u32[]{:S(2)}) collective-permute-start(bf16[1,256,128]{2,1,0:T(8,128)(2,1)S(1)} %get-tuple-element.74.refs_2_), channel_id=1, source_target_pairs={{0,2},{1,3},{2,0},{3,1},{4,6},{5,7},{6,4},{7,5},{8,10},{9,11},{10,... | collective-permute-start | bytes 196616 | tf_op jit(solution)/shard_map/ppermute | solution.py:22
  58.0 1.1 %collective-permute-start.13 = (bf16[1,256,128]{2,1,0:T(8,128)(2,1)S(1)}, bf16[1,256,128]{2,1,0:T(8,128)(2,1)S(1)}, u32[]{:S(2)}, u32[]{:S(2)}) collective-permute-start(bf16[1,256,128]{2,1,0:T(8,128)(2,1)S(1)} %get-tuple-element.69.own), channel_id=1, source_target_pairs={{0,2},{1,3},{2,0},{3,1},{4,6},{5,7},{6,4},{7,5},{8,10},{9,11},{10,... | collective-permute-start | bytes 196616 | tf_op jit(solution)/shard_map/ppermute | solution.py:22
  59.1 1.8 %collective-permute-done.14.theirs = bf16[1,256,128]{2,1,0:T(8,128)(2,1)S(1)} collective-permute-done((bf16[1,256,128]{2,1,0:T(8,128)(2,1)S(1)}, bf16[1,256,128]{2,1,0:T(8,128)(2,1)S(1)}, u32[]{:S(2)}, u32[]{:S(2)}) %collective-permute-start.14) | collective-permute-done | bytes 65568 | tf_op jit(solution)/shard_map/ppermute | solution.py:22
  60.9 1.0 %collective-permute-start.15 = (bf16[1,256,128]{2,1,0:T(8,128)(2,1)S(1)}, bf16[1,256,128]{2,1,0:T(8,128)(2,1)S(1)}, u32[]{:S(2)}, u32[]{:S(2)}) collective-permute-start(bf16[1,256,128]{2,1,0:T(8,128)(2,1)S(1)} %enter.1.own_top), channel_id=1, source_target_pairs={{0,2},{1,3},{2,0},{3,1},{4,6},{5,7},{6,4},{7,5},{8,10},{9,11},{10,... | collective-permute-start | bytes 196616 | tf_op jit(solution)/shard_map/ppermute | solution.py:22
  62.0 0.9 copy-done.10
  63.0 2.2 %collective-permute-done.15.far_top = bf16[1,256,128]{2,1,0:T(8,128)(2,1)S(1)} collective-permute-done((bf16[1,256,128]{2,1,0:T(8,128)(2,1)S(1)}, bf16[1,256,128]{2,1,0:T(8,128)(2,1)S(1)}, u32[]{:S(2)}, u32[]{:S(2)}) %collective-permute-start.15) | collective-permute-done | bytes 65568 | tf_op jit(solution)/shard_map/ppermute | solution.py:22
  65.9 1.6 %solve_far.7 = bf16[6,256,128]{2,1,0:T(8,128)(2,1)S(1)} custom-call(s32[8,3]{1,0:T(8,128)S(1)} %copy-done.16, bf16[8,256,256]{2,1,0:T(8,128)(2,1)S(1)} %copy-done.2, bf16[8,256,256]{2,1,0:T(8,128)(2,1)S(1)} %copy-done.1, bf16[8,3,256,256]{3,2,1,0:T(8,128)(2,1)S(1)} %copy-done, bf16[3,256,256]{2,1,0:T(8,128)(2,1)S(1)} %descend.1.paths), custom_call_target="tpu_custom_call" | custom-call | tf_op jit(solution)/shard_map/solve_far/pallas_call | solution.py:152
  67.5 1.0 %collective-permute-start.22 = (bf16[6,256,128]{2,1,0:T(8,128)(2,1)S(1)}, bf16[6,256,128]{2,1,0:T(8,128)(2,1)S(1)}, u32[]{:S(2)}, u32[]{:S(2)}) collective-permute-start(bf16[6,256,128]{2,1,0:T(8,128)(2,1)S(1)} %solve_far.7), channel_id=1, source_target_pairs={{0,2},{1,3},{2,0},{3,1},{4,6},{5,7},{6,4},{7,5},{8,10},{9,11},{10,... | collective-permute-start | bytes 1179656 | tf_op jit(solution)/shard_map/ppermute | solution.py:22
  68.5 1.4 %solve_far.6 = bf16[4,256,128]{2,1,0:T(8,128)(2,1)S(1)} custom-call(s32[8,3]{1,0:T(8,128)S(1)} %copy-done.18, bf16[8,256,128]{2,1,0:T(8,128)(2,1)S(1)} %copy-done.5, bf16[8,256,256]{2,1,0:T(8,128)(2,1)S(1)} %collective-permute-done.18.inv, bf16[8,3,256,256]{3,2,1,0:T(8,128)(2,1)S(1)} %collective-permute-done.19.panels, bf16[3,256,256]{2,1,0:T(8,128)(2,1)S(1)} %descend.1.paths), custom_call_target="tpu_custom_call" | custom-call | tf_op jit(solution)/shard_map/solve_far/pallas_call | solution.py:152
  69.9 1.2 %collective-permute-start.21 = (bf16[4,256,128]{2,1,0:T(8,128)(2,1)S(1)}, bf16[4,256,128]{2,1,0:T(8,128)(2,1)S(1)}, u32[]{:S(2)}, u32[]{:S(2)}) collective-permute-start(bf16[4,256,128]{2,1,0:T(8,128)(2,1)S(1)} %solve_far.6), channel_id=1, source_target_pairs={{0,2},{1,3},{2,0},{3,1},{4,6},{5,7},{6,4},{7,5},{8,10},{9,11},{10,... | collective-permute-start | bytes 786440 | tf_op jit(solution)/shard_map/ppermute | solution.py:22
  71.0 1.4 %solve_far.5 = bf16[4,256,128]{2,1,0:T(8,128)(2,1)S(1)} custom-call(s32[8,3]{1,0:T(8,128)S(1)} %copy-done.18, bf16[8,256,128]{2,1,0:T(8,128)(2,1)S(1)} %copy-done.5, bf16[8,256,256]{2,1,0:T(8,128)(2,1)S(1)} %collective-permute-done.18.inv, bf16[8,3,256,256]{3,2,1,0:T(8,128)(2,1)S(1)} %collective-permute-done.19.panels, bf16[3,256,256]{2,1,0:T(8,128)(2,1)S(1)} %descend.1.paths), custom_call_target="tpu_custom_call" | custom-call | tf_op jit(solution)/shard_map/solve_far/pallas_call | solution.py:152
  72.4 1.0 %collective-permute-start.20 = (bf16[4,256,128]{2,1,0:T(8,128)(2,1)S(1)}, bf16[4,256,128]{2,1,0:T(8,128)(2,1)S(1)}, u32[]{:S(2)}, u32[]{:S(2)}) collective-permute-start(bf16[4,256,128]{2,1,0:T(8,128)(2,1)S(1)} %solve_far.5), channel_id=1, source_target_pairs={{0,2},{1,3},{2,0},{3,1},{4,6},{5,7},{6,4},{7,5},{8,10},{9,11},{10,... | collective-permute-start | bytes 786440 | tf_op jit(solution)/shard_map/ppermute | solution.py:22
  73.4 1.1 %solve_far.4 = bf16[2,256,128]{2,1,0:T(8,128)(2,1)S(1)} custom-call(s32[8,3]{1,0:T(8,128)S(1)} %copy-done.16, bf16[8,256,256]{2,1,0:T(8,128)(2,1)S(1)} %copy-done.2, bf16[8,256,256]{2,1,0:T(8,128)(2,1)S(1)} %copy-done.1, bf16[8,3,256,256]{3,2,1,0:T(8,128)(2,1)S(1)} %copy-done, bf16[3,256,256]{2,1,0:T(8,128)(2,1)S(1)} %descend.1.paths), custom_call_target="tpu_custom_call" | custom-call | tf_op jit(solution)/shard_map/solve_far/pallas_call | solution.py:152
  74.6 2.9 %solve_own.2.refs_0_ = bf16[32,256,128]{2,1,0:T(8,128)(2,1)} custom-call(s32[3]{0:T(128)S(1)} %copy-done.19, s32[8,3]{1,0:T(8,128)S(1)} %copy-done.16, bf16[8,256,256]{2,1,0:T(8,128)(2,1)S(1)} %copy-done.2, bf16[8,256,256]{2,1,0:T(8,128)(2,1)S(1)} %copy-done.1, bf16[8,3,256,256]{3,2,1,0:T(8,128)(2,1)S(1)} %copy-done, bf16[3,256,256]{2,1,0:T(8,128)(2,1)S(1)} %descend.1.paths), custom_call_target="tpu_custom_call" | custom-call | tf_op jit(solution)/shard_map/solve_own/pallas_call | solution.py:194
  77.5 1.2 %collective-permute-start.17 = (bf16[2,256,128]{2,1,0:T(8,128)(2,1)S(1)}, bf16[2,256,128]{2,1,0:T(8,128)(2,1)S(1)}, u32[]{:S(2)}, u32[]{:S(2)}) collective-permute-start(bf16[2,256,128]{2,1,0:T(8,128)(2,1)S(1)} %solve_far.4), channel_id=1, source_target_pairs={{0,2},{1,3},{2,0},{3,1},{4,6},{5,7},{6,4},{7,5},{8,10},{9,11},{10,... | collective-permute-start | bytes 393224 | tf_op jit(solution)/shard_map/ppermute | solution.py:22
  79.4 2.9 %solve_own.3.whole = bf16[32,256,128]{2,1,0:T(8,128)(2,1)} custom-call(s32[3]{0:T(128)S(1)} %copy-done.19, s32[8,3]{1,0:T(8,128)S(1)} %copy-done.18, bf16[8,256,128]{2,1,0:T(8,128)(2,1)S(1)} %copy-done.8, bf16[8,256,256]{2,1,0:T(8,128)(2,1)S(1)} %collective-permute-done.18.inv, ...), custom_call_target="tpu_custom_call", output_to_operand_aliasing={{}: (6, {})} | custom-call | tf_op jit(solution)/shard_map/solve_own/pallas_call | solution.py:194
  82.2 0.8 place_rows.4.whole
  83.0 2.2 %collective-permute-done.21.part = bf16[4,256,128]{2,1,0:T(8,128)(2,1)S(1)} collective-permute-done((bf16[4,256,128]{2,1,0:T(8,128)(2,1)S(1)}, bf16[4,256,128]{2,1,0:T(8,128)(2,1)S(1)}, u32[]{:S(2)}, u32[]{:S(2)}) %collective-permute-start.21) | collective-permute-done | bytes 262176 | tf_op jit(solution)/shard_map/ppermute | solution.py:22
  85.2 0.7 place_rows.5.whole
  85.9 2.8 %collective-permute-done.20.part = bf16[4,256,128]{2,1,0:T(8,128)(2,1)S(1)} collective-permute-done((bf16[4,256,128]{2,1,0:T(8,128)(2,1)S(1)}, bf16[4,256,128]{2,1,0:T(8,128)(2,1)S(1)}, u32[]{:S(2)}, u32[]{:S(2)}) %collective-permute-start.20) | collective-permute-done | bytes 262176 | tf_op jit(solution)/shard_map/ppermute | solution.py:22
  88.7 0.7 place_rows.6.whole
  89.5 0.7 collective-permute-done.17.part
  90.1 0.7 place_rows.7
  (80 shorter events, 5.3 us)
Async XLA Ops:
  0.6 7.4 %copy-start.13 = (bf16[1,256,256]{2,1,0:T(8,128)(2,1)S(1)}, bf16[1,256,256]{2,1,0:T(8,128)(2,1)}, u32[]{:S(2)}) copy-start(bf16[1,256,256]{2,1,0:T(8,128)(2,1)} %lower_inv) | copy-start | bytes 393220
  0.6 7.4 %copy-start.11 = (bf16[1,2,256,256]{3,2,1,0:T(8,128)(2,1)S(1)}, bf16[1,2,256,256]{3,2,1,0:T(8,128)(2,1)}, u32[]{:S(2)}) copy-start(bf16[1,2,256,256]{3,2,1,0:T(8,128)(2,1)} %lower_panels.1) | copy-start | bytes 786436
  0.7 7.4 %copy-start.14 = (bf16[1,256,256]{2,1,0:T(8,128)(2,1)S(1)}, bf16[1,256,256]{2,1,0:T(8,128)(2,1)}, u32[]{:S(2)}) copy-start(bf16[1,256,256]{2,1,0:T(8,128)(2,1)} %upper_inv.1) | copy-start | bytes 393220
  0.7 7.4 %copy-start.12 = (bf16[1,2,256,256]{3,2,1,0:T(8,128)(2,1)S(1)}, bf16[1,2,256,256]{3,2,1,0:T(8,128)(2,1)}, u32[]{:S(2)}) copy-start(bf16[1,2,256,256]{3,2,1,0:T(8,128)(2,1)} %upper_panels.1) | copy-start | bytes 786436
  0.7 9.3 %copy-start.24 = (s32[8,3]{0,1:T(4,128)S(1)}, s32[8,3]{0,1:T(4,128)}, u32[]{:S(2)}) copy-start(s32[8,3]{0,1:T(4,128)} %param.16) | copy-start | bytes 292
  2.6 12.2 %collective-permute-start.3 = (bf16[8,3,256,256]{3,2,1,0:T(8,128)(2,1)}, bf16[8,3,256,256]{3,2,1,0:T(8,128)(2,1)}, u32[]{:S(2)}, u32[]{:S(2)}) collective-permute-start(bf16[8,3,256,256]{3,2,1,0:T(8,128)(2,1)} %refs_3_.2), channel_id=1, source_target_pairs={{0,1},{1,0},{2,3},{3,2},{4,5},{5,4},{6,7},{7,6},{8,9},{9,8},{10,11... | collective-permute-start | bytes 9437192 | tf_op jit(solution)/shard_map/ppermute | solution.py:22
  3.1 9.7 %collective-permute-start.2 = (bf16[8,256,256]{2,1,0:T(8,128)(2,1)}, bf16[8,256,256]{2,1,0:T(8,128)(2,1)S(1)}, u32[]{:S(2)}, u32[]{:S(2)}) collective-permute-start(bf16[8,256,256]{2,1,0:T(8,128)(2,1)} %refs_2_.1), channel_id=1, source_target_pairs={{0,1},{1,0},{2,3},{3,2},{4,5},{5,4},{6,7},{7,6},{8,9},{9,8},{10,11... | collective-permute-start | bytes 3145736 | tf_op jit(solution)/shard_map/ppermute | solution.py:22
  3.2 17.2 %collective-permute-start = (bf16[8,256,128]{2,1,0:T(8,128)(2,1)}, bf16[8,256,128]{2,1,0:T(8,128)(2,1)}, u32[]{:S(2)}, u32[]{:S(2)}) collective-permute-start(bf16[8,256,128]{2,1,0:T(8,128)(2,1)} %constant_dynamic-slice_fusion.1), channel_id=1, source_target_pairs={{0,2},{1,3},{2,0},{3,1},{4,6},{5,7},{6,4},{7,5},{8,10},{9,11},{10,... | collective-permute-start | bytes 1572872 | tf_op jit(solution)/shard_map/ppermute | solution.py:22
  8.4 18.2 %collective-permute-start.5 = (bf16[3,256,256]{2,1,0:T(8,128)(2,1)S(1)}, bf16[3,256,256]{2,1,0:T(8,128)(2,1)S(1)}, u32[]{:S(2)}, u32[]{:S(2)}) collective-permute-start(bf16[3,256,256]{2,1,0:T(8,128)(2,1)S(1)} %get-tuple-element.52), channel_id=1, source_target_pairs={{0,4},{4,0},{8,12},{12,8},{16,20},{20,16},{24,28},{28,24},{1,5},{5... | collective-permute-start | bytes 1179656 | tf_op jit(solution)/shard_map/ppermute | solution.py:22
  10.0 10.3 %copy-start.15 = (s32[8,3]{1,0:T(8,128)}, s32[8,3]{1,0:T(8,128)S(1)}, u32[]{:S(2)}) copy-start(s32[8,3]{1,0:T(8,128)S(1)} %copy.20.ancestors) | copy-start | bytes 292
  10.0 1.2 %collective-permute-start.1 = (s32[8,3]{1,0:T(8,128)S(1)}, s32[8,3]{1,0:T(8,128)S(1)}, u32[]{:S(2)}, u32[]{:S(2)}) collective-permute-start(s32[8,3]{1,0:T(8,128)S(1)} %copy.20.ancestors), channel_id=1, source_target_pairs={{0,1},{1,0},{2,3},{3,2},{4,5},{5,4},{6,7},{7,6},{8,9},{9,8},{10,11... | collective-permute-start | bytes 296 | tf_op jit(solution)/shard_map/ppermute | solution.py:22
  11.2 3.7 %copy-start.17 = (s32[8,3]{1,0:T(8,128)}, s32[8,3]{1,0:T(8,128)S(1)}, u32[]{:S(2)}) copy-start(s32[8,3]{1,0:T(8,128)S(1)} %collective-permute-done.1.ancestors) | copy-start | bytes 292
  11.2 18.6 %collective-permute-start.4 = (bf16[8,256,128]{2,1,0:T(8,128)(2,1)}, bf16[8,256,128]{2,1,0:T(8,128)(2,1)}, u32[]{:S(2)}, u32[]{:S(2)}) collective-permute-start(bf16[8,256,128]{2,1,0:T(8,128)(2,1)} %constant_dynamic-slice_fusion), channel_id=1, source_target_pairs={{0,2},{1,3},{2,0},{3,1},{4,6},{5,7},{6,4},{7,5},{8,10},{9,11},{10,... | collective-permute-start | bytes 1572872 | tf_op jit(solution)/shard_map/ppermute | solution.py:22
  12.8 2.1 %copy-start.20 = (bf16[8,256,256]{2,1,0:T(8,128)(2,1)}, bf16[8,256,256]{2,1,0:T(8,128)(2,1)S(1)}, u32[]{:S(2)}) copy-start(bf16[8,256,256]{2,1,0:T(8,128)(2,1)S(1)} %collective-permute-done.2.refs_1_) | copy-start | bytes 3145732
  12.8 13.8 %collective-permute-start.6 = (bf16[2,256,256]{2,1,0:T(8,128)(2,1)S(1)}, bf16[2,256,256]{2,1,0:T(8,128)(2,1)S(1)}, u32[]{:S(2)}, u32[]{:S(2)}) collective-permute-start(bf16[2,256,256]{2,1,0:T(8,128)(2,1)S(1)} %get-tuple-element.53), channel_id=1, source_target_pairs={{0,4},{4,0},{8,12},{12,8},{16,20},{20,16},{24,28},{28,24},{1,5},{5... | collective-permute-start | bytes 786440 | tf_op jit(solution)/shard_map/ppermute | solution.py:22
  26.6 9.2 %collective-permute-start.7 = (bf16[1,256,256]{2,1,0:T(8,128)(2,1)S(1)}, bf16[1,256,256]{2,1,0:T(8,128)(2,1)S(1)}, u32[]{:S(2)}, u32[]{:S(2)}) collective-permute-start(bf16[1,256,256]{2,1,0:T(8,128)(2,1)S(1)} %get-tuple-element.57), channel_id=1, source_target_pairs={{16,0},{20,4},{17,1},{21,5},{18,2},{22,6},{19,3},{23,7}} | collective-permute-start | bytes 393224 | tf_op jit(solution)/shard_map/ppermute | solution.py:327
  27.9 7.9 %collective-permute-start.8 = (bf16[1,256,256]{2,1,0:T(8,128)(2,1)S(1)}, bf16[1,256,256]{2,1,0:T(8,128)(2,1)S(1)}, u32[]{:S(2)}, u32[]{:S(2)}) collective-permute-start(bf16[1,256,256]{2,1,0:T(8,128)(2,1)S(1)} %get-tuple-element.57), channel_id=1, source_target_pairs={{16,8},{20,12},{17,9},{21,13},{18,10},{22,14},{19,11},{23,15}} | collective-permute-start | bytes 393224 | tf_op jit(solution)/shard_map/ppermute | solution.py:327
  28.6 13.2 %copy-start.21 = (bf16[3,256,128]{2,1,0:T(8,128)(2,1)S(1)}, bf16[3,256,128]{2,1,0:T(8,128)(2,1)}, u32[]{:S(2)}) copy-start(bf16[3,256,128]{2,1,0:T(8,128)(2,1)} %get-tuple-element.47) | copy-start | bytes 589828
  35.8 2.9 %copy-start.22 = (bf16[1,256,256]{2,1,0:T(8,128)(2,1)}, bf16[1,256,256]{2,1,0:T(8,128)(2,1)S(1)}, u32[]{:S(2)}) copy-start(bf16[1,256,256]{2,1,0:T(8,128)(2,1)S(1)} %collective-permute-done.7.refs_0_) | copy-start | bytes 393220
  35.8 2.9 %copy-start.23 = (bf16[1,256,256]{2,1,0:T(8,128)(2,1)}, bf16[1,256,256]{2,1,0:T(8,128)(2,1)S(1)}, u32[]{:S(2)}) copy-start(bf16[1,256,256]{2,1,0:T(8,128)(2,1)S(1)} %collective-permute-done.8.refs_1_) | copy-start | bytes 393220
  35.8 6.0 %collective-permute-start.9 = (bf16[3,256,128]{2,1,0:T(8,128)(2,1)}, bf16[3,256,128]{2,1,0:T(8,128)(2,1)S(1)}, u32[]{:S(2)}, u32[]{:S(2)}) collective-permute-start(bf16[3,256,128]{2,1,0:T(8,128)(2,1)} %get-tuple-element.60), channel_id=1, source_target_pairs={{0,2},{1,3},{2,0},{3,1},{4,6},{5,7},{6,4},{7,5},{8,10},{9,11},{10,... | collective-permute-start | bytes 589832 | tf_op jit(solution)/shard_map/ppermute | solution.py:22
  37.1 9.9 %collective-permute-start.11 = (bf16[3,256,256]{2,1,0:T(8,128)(2,1)S(1)}, bf16[3,256,256]{2,1,0:T(8,128)(2,1)S(1)}, u32[]{:S(2)}, u32[]{:S(2)}) collective-permute-start(bf16[3,256,256]{2,1,0:T(8,128)(2,1)S(1)} %get-tuple-element.56.mine), channel_id=1, source_target_pairs={{0,8},{4,12},{8,0},{12,4},{16,24},{20,28},{24,16},{28,20},{1,9},{5... | collective-permute-start | bytes 1179656 | tf_op jit(solution)/shard_map/ppermute | solution.py:22
  41.9 5.9 %collective-permute-start.10 = (bf16[3,256,128]{2,1,0:T(8,128)(2,1)S(1)}, bf16[3,256,128]{2,1,0:T(8,128)(2,1)S(1)}, u32[]{:S(2)}, u32[]{:S(2)}) collective-permute-start(bf16[3,256,128]{2,1,0:T(8,128)(2,1)S(1)} %add_convert_fusion.mine), channel_id=1, source_target_pairs={{0,4},{4,0},{8,12},{12,8},{16,20},{20,16},{24,28},{28,24},{1,5},{5... | collective-permute-start | bytes 589832 | tf_op jit(solution)/shard_map/ppermute | solution.py:22
  43.4 4.4 %copy-start.3 = (bf16[5,256,256]{2,1,0:T(8,128)(2,1)}, bf16[5,256,256]{2,1,0:T(8,128)(2,1)S(1)}, u32[]{:S(2)}) copy-start(bf16[5,256,256]{2,1,0:T(8,128)(2,1)S(1)} %sort.7.factors) | copy-start | bytes 1966084
  47.0 0.8 copy-start.6
  47.0 6.9 %copy-start = (bf16[8,3,256,256]{3,2,1,0:T(8,128)(2,1)S(1)}, bf16[8,3,256,256]{3,2,1,0:T(8,128)(2,1)}, u32[]{:S(2)}) copy-start(bf16[8,3,256,256]{3,2,1,0:T(8,128)(2,1)} %panels.5) | copy-start | bytes 9437188
  47.8 0.7 copy-start.9
  48.4 5.3 %collective-permute-start.12 = (bf16[2,256,128]{2,1,0:T(8,128)(2,1)S(1)}, bf16[2,256,128]{2,1,0:T(8,128)(2,1)S(1)}, u32[]{:S(2)}, u32[]{:S(2)}) collective-permute-start(bf16[2,256,128]{2,1,0:T(8,128)(2,1)S(1)} %get-tuple-element.65.mine), channel_id=1, source_target_pairs={{0,8},{4,12},{8,0},{12,4},{16,24},{20,28},{24,16},{28,20},{1,9},{5... | collective-permute-start | bytes 393224 | tf_op jit(solution)/shard_map/ppermute | solution.py:22
  51.6 1.1 %copy-start.4 = (bf16[5,256,256]{2,1,0:T(8,128)(2,1)S(1)}, bf16[5,256,256]{2,1,0:T(8,128)(2,1)}, u32[]{:S(2)}) copy-start(bf16[5,256,256]{2,1,0:T(8,128)(2,1)} %copy-done.3) | copy-start | bytes 1966084
  52.7 1.0 %copy-start.7 = (bf16[3,256,256]{2,1,0:T(8,128)(2,1)S(1)}, bf16[3,256,256]{2,1,0:T(8,128)(2,1)}, u32[]{:S(2)}) copy-start(bf16[3,256,256]{2,1,0:T(8,128)(2,1)} %copy-done.6) | copy-start | bytes 1179652
  53.7 12.2 %copy-start.1 = (bf16[8,256,256]{2,1,0:T(8,128)(2,1)S(1)}, bf16[8,256,256]{2,1,0:T(8,128)(2,1)}, u32[]{:S(2)}) copy-start(bf16[8,256,256]{2,1,0:T(8,128)(2,1)} %inv.5) | copy-start | bytes 3145732
  53.7 12.2 %copy-start.2 = (bf16[8,256,256]{2,1,0:T(8,128)(2,1)S(1)}, bf16[8,256,256]{2,1,0:T(8,128)(2,1)}, u32[]{:S(2)}) copy-start(bf16[8,256,256]{2,1,0:T(8,128)(2,1)} %get-tuple-element.46.value) | copy-start | bytes 3145732
  53.9 14.5 %collective-permute-start.19 = (bf16[8,3,256,256]{3,2,1,0:T(8,128)(2,1)S(1)}, bf16[8,3,256,256]{3,2,1,0:T(8,128)(2,1)S(1)}, u32[]{:S(2)}, u32[]{:S(2)}) collective-permute-start(bf16[8,3,256,256]{3,2,1,0:T(8,128)(2,1)S(1)} %copy-done), channel_id=1, source_target_pairs={{0,1},{1,0},{2,3},{3,2},{4,5},{5,4},{6,7},{7,6},{8,9},{9,8},{10,11... | collective-permute-start | bytes 9437192 | tf_op jit(solution)/shard_map/ppermute | solution.py:22
  54.0 14.5 %collective-permute-start.18 = (bf16[8,256,256]{2,1,0:T(8,128)(2,1)}, bf16[8,256,256]{2,1,0:T(8,128)(2,1)S(1)}, u32[]{:S(2)}, u32[]{:S(2)}) collective-permute-start(bf16[8,256,256]{2,1,0:T(8,128)(2,1)} %inv.5), channel_id=1, source_target_pairs={{0,1},{1,0},{2,3},{3,2},{4,5},{5,4},{6,7},{7,6},{8,9},{9,8},{10,11... | collective-permute-start | bytes 3145736 | tf_op jit(solution)/shard_map/ppermute | solution.py:22
  54.5 6.4 %collective-permute-start.14 = (bf16[1,256,128]{2,1,0:T(8,128)(2,1)S(1)}, bf16[1,256,128]{2,1,0:T(8,128)(2,1)S(1)}, u32[]{:S(2)}, u32[]{:S(2)}) collective-permute-start(bf16[1,256,128]{2,1,0:T(8,128)(2,1)S(1)} %get-tuple-element.70.mine), channel_id=1, source_target_pairs={{0,16},{4,20},{8,24},{12,28},{16,0},{20,4},{24,8},{28,12},{1,17},{... | collective-permute-start | bytes 196616 | tf_op jit(solution)/shard_map/ppermute | solution.py:22
  57.1 4.8 %collective-permute-start.16 = (bf16[1,256,128]{2,1,0:T(8,128)(2,1)S(1)}, bf16[1,256,128]{2,1,0:T(8,128)(2,1)S(1)}, u32[]{:S(2)}, u32[]{:S(2)}) collective-permute-start(bf16[1,256,128]{2,1,0:T(8,128)(2,1)S(1)} %get-tuple-element.74.refs_2_), channel_id=1, source_target_pairs={{0,2},{1,3},{2,0},{3,1},{4,6},{5,7},{6,4},{7,5},{8,10},{9,11},{10,... | collective-permute-start | bytes 196616 | tf_op jit(solution)/shard_map/ppermute | solution.py:22
  58.0 5.0 %collective-permute-start.13 = (bf16[1,256,128]{2,1,0:T(8,128)(2,1)S(1)}, bf16[1,256,128]{2,1,0:T(8,128)(2,1)S(1)}, u32[]{:S(2)}, u32[]{:S(2)}) collective-permute-start(bf16[1,256,128]{2,1,0:T(8,128)(2,1)S(1)} %get-tuple-element.69.own), channel_id=1, source_target_pairs={{0,2},{1,3},{2,0},{3,1},{4,6},{5,7},{6,4},{7,5},{8,10},{9,11},{10,... | collective-permute-start | bytes 196616 | tf_op jit(solution)/shard_map/ppermute | solution.py:22
  60.9 4.3 %collective-permute-start.15 = (bf16[1,256,128]{2,1,0:T(8,128)(2,1)S(1)}, bf16[1,256,128]{2,1,0:T(8,128)(2,1)S(1)}, u32[]{:S(2)}, u32[]{:S(2)}) collective-permute-start(bf16[1,256,128]{2,1,0:T(8,128)(2,1)S(1)} %enter.1.own_top), channel_id=1, source_target_pairs={{0,2},{1,3},{2,0},{3,1},{4,6},{5,7},{6,4},{7,5},{8,10},{9,11},{10,... | collective-permute-start | bytes 196616 | tf_op jit(solution)/shard_map/ppermute | solution.py:22
  62.0 0.9 copy-start.10
  62.9 3.0 %copy-start.16 = (s32[8,3]{1,0:T(8,128)S(1)}, s32[8,3]{1,0:T(8,128)}, u32[]{:S(2)}) copy-start(s32[8,3]{1,0:T(8,128)} %copy-done.15) | copy-start | bytes 292
  65.9 2.6 %copy-start.5 = (bf16[8,256,128]{2,1,0:T(8,128)(2,1)S(1)}, bf16[8,256,128]{2,1,0:T(8,128)(2,1)}, u32[]{:S(2)}) copy-start(bf16[8,256,128]{2,1,0:T(8,128)(2,1)} %get-tuple-element.78.value) | copy-start | bytes 1572868
  65.9 2.6 %copy-start.18 = (s32[8,3]{1,0:T(8,128)S(1)}, s32[8,3]{1,0:T(8,128)}, u32[]{:S(2)}) copy-start(s32[8,3]{1,0:T(8,128)} %copy-done.17) | copy-start | bytes 292
  67.5 14.7 %collective-permute-start.22 = (bf16[6,256,128]{2,1,0:T(8,128)(2,1)S(1)}, bf16[6,256,128]{2,1,0:T(8,128)(2,1)S(1)}, u32[]{:S(2)}, u32[]{:S(2)}) collective-permute-start(bf16[6,256,128]{2,1,0:T(8,128)(2,1)S(1)} %solve_far.7), channel_id=1, source_target_pairs={{0,2},{1,3},{2,0},{3,1},{4,6},{5,7},{6,4},{7,5},{8,10},{9,11},{10,... | collective-permute-start | bytes 1179656 | tf_op jit(solution)/shard_map/ppermute | solution.py:22
  69.9 15.4 %collective-permute-start.21 = (bf16[4,256,128]{2,1,0:T(8,128)(2,1)S(1)}, bf16[4,256,128]{2,1,0:T(8,128)(2,1)S(1)}, u32[]{:S(2)}, u32[]{:S(2)}) collective-permute-start(bf16[4,256,128]{2,1,0:T(8,128)(2,1)S(1)} %solve_far.6), channel_id=1, source_target_pairs={{0,2},{1,3},{2,0},{3,1},{4,6},{5,7},{6,4},{7,5},{8,10},{9,11},{10,... | collective-permute-start | bytes 786440 | tf_op jit(solution)/shard_map/ppermute | solution.py:22
  72.4 2.1 %copy-start.19 = (s32[3]{0:T(128)S(1)}, s32[3]{0:T(128)}, u32[]{:S(2)}) copy-start(s32[3]{0:T(128)} %pad_add_fusion.scalars) | copy-start | bytes 40
  72.4 16.3 %collective-permute-start.20 = (bf16[4,256,128]{2,1,0:T(8,128)(2,1)S(1)}, bf16[4,256,128]{2,1,0:T(8,128)(2,1)S(1)}, u32[]{:S(2)}, u32[]{:S(2)}) collective-permute-start(bf16[4,256,128]{2,1,0:T(8,128)(2,1)S(1)} %solve_far.5), channel_id=1, source_target_pairs={{0,2},{1,3},{2,0},{3,1},{4,6},{5,7},{6,4},{7,5},{8,10},{9,11},{10,... | collective-permute-start | bytes 786440 | tf_op jit(solution)/shard_map/ppermute | solution.py:22
  74.6 4.8 %copy-start.8 = (bf16[8,256,128]{2,1,0:T(8,128)(2,1)S(1)}, bf16[8,256,128]{2,1,0:T(8,128)(2,1)}, u32[]{:S(2)}) copy-start(bf16[8,256,128]{2,1,0:T(8,128)(2,1)} %get-tuple-element.81.value) | copy-start | bytes 1572868
  77.5 12.6 %collective-permute-start.17 = (bf16[2,256,128]{2,1,0:T(8,128)(2,1)S(1)}, bf16[2,256,128]{2,1,0:T(8,128)(2,1)S(1)}, u32[]{:S(2)}, u32[]{:S(2)}) collective-permute-start(bf16[2,256,128]{2,1,0:T(8,128)(2,1)S(1)} %solve_far.4), channel_id=1, source_target_pairs={{0,2},{1,3},{2,0},{3,1},{4,6},{5,7},{6,4},{7,5},{8,10},{9,11},{10,... | collective-permute-start | bytes 393224 | tf_op jit(solution)/shard_map/ppermute | solution.py:22

commit v8 on v7

--- a/solution.py
+++ b/solution.py
@@ -537,12 +537,12 @@
     local = (ancestors, leaf_upper_inv, leaf_upper_panels)
     near = (near_ancestors, near_upper_inv, near_upper_panels)
     leaf_solution = solve_own(scalars, 0, *local, value_1, paths, rows)
-    quarter = half // 2
+    rest = half - 1
     returning = [
-        (0, 0, solve_far(*local, value_1, paths, 0, count - quarter)),
+        (0, 0, solve_far(*local, value_1, paths, 0, count - rest)),
         (1, 0, solve_far(*near, value_2_far, paths, 0, half)),
         (1, half, solve_far(*near, value_2_far, paths, half, half)),
-        (0, count - quarter, solve_far(*local, value_1, paths, count - quarter, quarter)),
+        (0, count - rest, solve_far(*local, value_1, paths, count - rest, rest)),
     ]
     leaf_solution = solve_own(scalars, 1, *near, value_2_own, paths, rows, leaf_solution)
     for group, offset, part in returning:

time: 91.3 us -> 91.2 us (level)
  waiting for transfers between devices: 17.9 us -> 16.9 us
    ppermute x21, waiting for transfers between devices: 17.3 us -> 16.3 us  [swap(): return lax.ppermute(value, axis, pairs)]
  transfers between devices with their start and end apart: 23 -> 23, of which waited for: 12 -> 11; matrix products, arithmetic and copies ran while one was open for 4% -> 4% of each run, Pallas kernels for 38% -> 39%
where the time goes in v8:
time: 91.2 us; the launch traced here: 90.7 us
  Pallas kernels  36.9 us (40%)
  starting transfers between devices  26.4 us (29%)
  waiting for transfers between devices  16.9 us (19%)
  local copies, waits for them, and re-layouts  8.1 us (9%)
  other arithmetic  1.29 us (1%)
  between operations  1.12 us (1%)
    ppermute x21, starting transfers between devices, swap(): return lax.ppermute(value, axis, pairs)  24.5 us
    pallas_call x3, Pallas kernels, forward(): pl.pallas_call(functools.partial(forward_kernel, rhs is not None, far is...  17.1 us
    ppermute x21, waiting for transfers between devices, swap(): return lax.ppermute(value, axis, pairs)  16.3 us
    pallas_call x4, Pallas kernels, solve_far(): pl.pallas_call(functools.partial(send_kernel, base), grid=(count // batch...  6.36 us
    pallas_call x2, Pallas kernels, solve_own(): pl.pallas_call(functools.partial(keep_kernel, which), grid=(count // batc...  5.81 us
    unnamed x51, local copies, waits for them, and re-layouts  4.28 us
    pallas_call x2, Pallas kernels, pick(): pl.pallas_call(pick_kernel, in_specs=[pl.BlockSpec(memory_space=pltpu.SME...  3.13 us
    pallas_call x4, Pallas kernels, place_rows(): pl.pallas_call(functools.partial(place_kernel, group, leaves, offset), in...  2.88 us
  transfers between devices with their start and end apart: 23, of which 11 were waited for; matrix products, arithmetic and copies ran while one was open for 4% of the time, Pallas kernels for 39%

profile of v8, /device:TPU:0, one launch (start us, length us, event | category | flops | bytes accessed | tf_op | source)
XLA Modules:
  0.0 90.7 jit_solution(5125431692554513771)
XLA Ops:
  0.7 1.9 %constant_dynamic-slice_fusion.1 = bf16[8,256,128]{2,1,0:T(8,128)(2,1)} fusion(bf16[32,256,128]{2,1,0:T(8,128)(2,1)} %refs_0_.3, s32[]{:T(128)S(6)} %select_n.94), kind=kLoop, calls=%fused_computation.6 | loop fusion | bytes 1048580 | tf_op jit(solution)/shard_map/dynamic_slice | solution.py:476
  3.2 3.0 %collective-permute-start = (bf16[8,256,128]{2,1,0:T(8,128)(2,1)}, bf16[8,256,128]{2,1,0:T(8,128)(2,1)}, u32[]{:S(2)}, u32[]{:S(2)}) collective-permute-start(bf16[8,256,128]{2,1,0:T(8,128)(2,1)} %constant_dynamic-slice_fusion.1), channel_id=1, source_target_pairs={{0,2},{1,3},{2,0},{3,1},{4,6},{5,7},{6,4},{7,5},{8,10},{9,11},{10,... | collective-permute-start | bytes 1572872 | tf_op jit(solution)/shard_map/ppermute | solution.py:22
  6.1 1.9 %constant_dynamic-slice_fusion = bf16[8,256,128]{2,1,0:T(8,128)(2,1)} fusion(bf16[32,256,128]{2,1,0:T(8,128)(2,1)} %refs_0_.3, s32[]{:T(128)S(6)} %select_n.95), kind=kLoop, calls=%fused_computation.5 | loop fusion | bytes 1048580 | tf_op jit(solution)/shard_map/dynamic_slice | solution.py:477
  8.4 1.6 %collective-permute-start.5 = (bf16[3,256,256]{2,1,0:T(8,128)(2,1)S(1)}, bf16[3,256,256]{2,1,0:T(8,128)(2,1)S(1)}, u32[]{:S(2)}, u32[]{:S(2)}) collective-permute-start(bf16[3,256,256]{2,1,0:T(8,128)(2,1)S(1)} %get-tuple-element.52), channel_id=1, source_target_pairs={{0,4},{4,0},{8,12},{12,8},{16,20},{20,16},{24,28},{28,24},{1,5},{5... | collective-permute-start | bytes 1179656 | tf_op jit(solution)/shard_map/ppermute | solution.py:22
  10.0 1.2 %collective-permute-done.1.ancestors = s32[8,3]{1,0:T(8,128)S(1)} collective-permute-done((s32[8,3]{1,0:T(8,128)S(1)}, s32[8,3]{1,0:T(8,128)S(1)}, u32[]{:S(2)}, u32[]{:S(2)}) %collective-permute-start.1) | collective-permute-done | bytes 128 | tf_op jit(solution)/shard_map/ppermute | solution.py:22
  11.2 1.6 %collective-permute-start.4 = (bf16[8,256,128]{2,1,0:T(8,128)(2,1)}, bf16[8,256,128]{2,1,0:T(8,128)(2,1)}, u32[]{:S(2)}, u32[]{:S(2)}) collective-permute-start(bf16[8,256,128]{2,1,0:T(8,128)(2,1)} %constant_dynamic-slice_fusion), channel_id=1, source_target_pairs={{0,2},{1,3},{2,0},{3,1},{4,6},{5,7},{6,4},{7,5},{8,10},{9,11},{10,... | collective-permute-start | bytes 1572872 | tf_op jit(solution)/shard_map/ppermute | solution.py:22
  12.8 1.5 %collective-permute-start.6 = (bf16[2,256,256]{2,1,0:T(8,128)(2,1)S(1)}, bf16[2,256,256]{2,1,0:T(8,128)(2,1)S(1)}, u32[]{:S(2)}, u32[]{:S(2)}) collective-permute-start(bf16[2,256,256]{2,1,0:T(8,128)(2,1)S(1)} %get-tuple-element.53), channel_id=1, source_target_pairs={{0,4},{4,0},{8,12},{12,8},{16,20},{20,16},{24,28},{28,24},{1,5},{5... | collective-permute-start | bytes 786440 | tf_op jit(solution)/shard_map/ppermute | solution.py:22
  14.9 5.4 %leaf_forward.3 = (bf16[8,256,128]{2,1,0:T(8,128)(2,1)}, f32[3,256,128]{2,1,0:T(8,128)}) custom-call(s32[3]{0:T(128)} %pad_add_fusion.scalars, s32[8,3]{1,0:T(8,128)} %copy-done.17, bf16[32,256,128]{2,1,0:T(8,128)(2,1)} %refs_0_.3, bf16[8,256,256]{2,1,0:T(8,128)(2,1)} %copy-done.20, bf16[8,3,256,256]{3,2,1,0:T(8,128)(2,1)} %collective-permute-done.3.refs_2_, ...), custom_call_target="tpu_custom_call" | custom-call | tf_op jit(solution)/shard_map/leaf_forward/pallas_call | solution.py:95
  20.3 6.2 %leaf_forward.4 = (bf16[8,256,256]{2,1,0:T(8,128)(2,1)}, bf16[3,256,128]{2,1,0:T(8,128)(2,1)}, f32[3,256,128]{2,1,0:T(8,128)}) custom-call(s32[3]{0:T(128)} %pad_add_fusion.scalars, s32[8,3]{1,0:T(8,128)} %copy-done.15, bf16[32,256,128]{2,1,0:T(8,128)(2,1)} %refs_0_.3, bf16[8,256,128]{2,1,0:T(8,128)(2,1)} %collective-permute-done.refs_1_, ...), custom_call_target="tpu_custom_call" | custom-call | tf_op jit(solution)/shard_map/leaf_forward/pallas_call | solution.py:95
  26.6 1.3 %collective-permute-start.7 = (bf16[1,256,256]{2,1,0:T(8,128)(2,1)S(1)}, bf16[1,256,256]{2,1,0:T(8,128)(2,1)S(1)}, u32[]{:S(2)}, u32[]{:S(2)}) collective-permute-start(bf16[1,256,256]{2,1,0:T(8,128)(2,1)S(1)} %get-tuple-element.57), channel_id=1, source_target_pairs={{16,0},{20,4},{17,1},{21,5},{18,2},{22,6},{19,3},{23,7}} | collective-permute-start | bytes 393224 | tf_op jit(solution)/shard_map/ppermute | solution.py:327
  27.9 0.7 collective-permute-start.8
  28.6 1.2 %collective-permute-done.4.refs_0_ = bf16[8,256,128]{2,1,0:T(8,128)(2,1)} collective-permute-done((bf16[8,256,128]{2,1,0:T(8,128)(2,1)}, bf16[8,256,128]{2,1,0:T(8,128)(2,1)}, u32[]{:S(2)}, u32[]{:S(2)}) %collective-permute-start.4) | collective-permute-done | bytes 524320 | tf_op jit(solution)/shard_map/ppermute | solution.py:22
  29.8 5.5 %leaf_forward.5 = (bf16[8,256,128]{2,1,0:T(8,128)(2,1)}, bf16[3,256,128]{2,1,0:T(8,128)(2,1)}) custom-call(s32[3]{0:T(128)} %pad_add_fusion.scalars, s32[8,3]{1,0:T(8,128)} %copy-done.17, bf16[8,256,128]{2,1,0:T(8,128)(2,1)} %collective-permute-done.4.refs_0_, bf16[8,256,256]{2,1,0:T(8,128)(2,1)} %copy-done.20, ...), custom_call_target="tpu_custom_call" | custom-call | tf_op jit(solution)/shard_map/leaf_forward/pallas_call | solution.py:95
  35.8 1.3 %collective-permute-start.9 = (bf16[3,256,128]{2,1,0:T(8,128)(2,1)}, bf16[3,256,128]{2,1,0:T(8,128)(2,1)S(1)}, u32[]{:S(2)}, u32[]{:S(2)}) collective-permute-start(bf16[3,256,128]{2,1,0:T(8,128)(2,1)} %get-tuple-element.60), channel_id=1, source_target_pairs={{0,2},{1,3},{2,0},{3,1},{4,6},{5,7},{6,4},{7,5},{8,10},{9,11},{10,... | collective-permute-start | bytes 589832 | tf_op jit(solution)/shard_map/ppermute | solution.py:22
  37.1 1.6 %collective-permute-start.11 = (bf16[3,256,256]{2,1,0:T(8,128)(2,1)S(1)}, bf16[3,256,256]{2,1,0:T(8,128)(2,1)S(1)}, u32[]{:S(2)}, u32[]{:S(2)}) collective-permute-start(bf16[3,256,256]{2,1,0:T(8,128)(2,1)S(1)} %get-tuple-element.56.mine), channel_id=1, source_target_pairs={{0,8},{4,12},{8,0},{12,4},{16,24},{20,28},{24,16},{28,20},{1,9},{5... | collective-permute-start | bytes 1179656 | tf_op jit(solution)/shard_map/ppermute | solution.py:22
  38.7 1.6 %pick.2.refs_0_ = bf16[1,256,256]{2,1,0:T(8,128)(2,1)} custom-call(s32[1]{0:T(128)} %bitcast.4.flags, bf16[1,256,256]{2,1,0:T(8,128)(2,1)} %copy-done.22, bf16[1,256,256]{2,1,0:T(8,128)(2,1)} %copy-done.23), custom_call_target="tpu_custom_call" | custom-call | flops 1048576 | bytes 1048576 | tf_op jit(solution)/shard_map/pick/pallas_call | solution.py:308
  40.2 1.6 %collective-permute-done.9 = bf16[3,256,128]{2,1,0:T(8,128)(2,1)S(1)} collective-permute-done((bf16[3,256,128]{2,1,0:T(8,128)(2,1)}, bf16[3,256,128]{2,1,0:T(8,128)(2,1)S(1)}, u32[]{:S(2)}, u32[]{:S(2)}) %collective-permute-start.9) | collective-permute-done | bytes 196640 | tf_op jit(solution)/shard_map/ppermute | solution.py:22
  41.9 1.5 %collective-permute-start.10 = (bf16[3,256,128]{2,1,0:T(8,128)(2,1)S(1)}, bf16[3,256,128]{2,1,0:T(8,128)(2,1)S(1)}, u32[]{:S(2)}, u32[]{:S(2)}) collective-permute-start(bf16[3,256,128]{2,1,0:T(8,128)(2,1)S(1)} %add_convert_fusion.mine), channel_id=1, source_target_pairs={{0,4},{4,0},{8,12},{12,8},{16,20},{20,16},{24,28},{28,24},{1,5},{5... | collective-permute-start | bytes 589832 | tf_op jit(solution)/shard_map/ppermute | solution.py:22
  43.4 3.6 %collective-permute-done.11.refs_0_ = bf16[3,256,256]{2,1,0:T(8,128)(2,1)S(1)} collective-permute-done((bf16[3,256,256]{2,1,0:T(8,128)(2,1)S(1)}, bf16[3,256,256]{2,1,0:T(8,128)(2,1)S(1)}, u32[]{:S(2)}, u32[]{:S(2)}) %collective-permute-start.11) | collective-permute-done | bytes 393248 | tf_op jit(solution)/shard_map/ppermute | solution.py:22
  47.1 0.7 copy-done.6
  48.4 1.6 %collective-permute-start.12 = (bf16[2,256,128]{2,1,0:T(8,128)(2,1)S(1)}, bf16[2,256,128]{2,1,0:T(8,128)(2,1)S(1)}, u32[]{:S(2)}, u32[]{:S(2)}) collective-permute-start(bf16[2,256,128]{2,1,0:T(8,128)(2,1)S(1)} %get-tuple-element.65.mine), channel_id=1, source_target_pairs={{0,8},{4,12},{8,0},{12,4},{16,24},{20,28},{24,16},{28,20},{1,9},{5... | collective-permute-start | bytes 393224 | tf_op jit(solution)/shard_map/ppermute | solution.py:22
  50.0 1.6 %pick.3.next_factors = bf16[1,256,256]{2,1,0:T(8,128)(2,1)} custom-call(s32[1]{0:T(128)} %bitcast.5.flags, bf16[1,256,256]{2,1,0:T(8,128)(2,1)} %pick.2.refs_0_, bf16[1,256,256]{2,1,0:T(8,128)(2,1)} %copy-done.9), custom_call_target="tpu_custom_call" | custom-call | flops 1048576 | bytes 1048576 | tf_op jit(solution)/shard_map/pick/pallas_call | solution.py:308
  51.6 1.1 %copy-done.4 = bf16[5,256,256]{2,1,0:T(8,128)(2,1)S(1)} copy-done((bf16[5,256,256]{2,1,0:T(8,128)(2,1)S(1)}, bf16[5,256,256]{2,1,0:T(8,128)(2,1)}, u32[]{:S(2)}) %copy-start.4) | copy-done | bytes 655384
  52.7 1.0 %copy-done.7 = bf16[3,256,256]{2,1,0:T(8,128)(2,1)S(1)} copy-done((bf16[3,256,256]{2,1,0:T(8,128)(2,1)S(1)}, bf16[3,256,256]{2,1,0:T(8,128)(2,1)}, u32[]{:S(2)}) %copy-start.7) | copy-done | bytes 393240
  54.5 2.6 %collective-permute-start.14 = (bf16[1,256,128]{2,1,0:T(8,128)(2,1)S(1)}, bf16[1,256,128]{2,1,0:T(8,128)(2,1)S(1)}, u32[]{:S(2)}, u32[]{:S(2)}) collective-permute-start(bf16[1,256,128]{2,1,0:T(8,128)(2,1)S(1)} %get-tuple-element.70.mine), channel_id=1, source_target_pairs={{0,16},{4,20},{8,24},{12,28},{16,0},{20,4},{24,8},{28,12},{1,17},{... | collective-permute-start | bytes 196616 | tf_op jit(solution)/shard_map/ppermute | solution.py:22
  57.1 0.9 %collective-permute-start.16 = (bf16[1,256,128]{2,1,0:T(8,128)(2,1)S(1)}, bf16[1,256,128]{2,1,0:T(8,128)(2,1)S(1)}, u32[]{:S(2)}, u32[]{:S(2)}) collective-permute-start(bf16[1,256,128]{2,1,0:T(8,128)(2,1)S(1)} %get-tuple-element.74.refs_2_), channel_id=1, source_target_pairs={{0,2},{1,3},{2,0},{3,1},{4,6},{5,7},{6,4},{7,5},{8,10},{9,11},{10,... | collective-permute-start | bytes 196616 | tf_op jit(solution)/shard_map/ppermute | solution.py:22
  58.0 1.1 %collective-permute-start.13 = (bf16[1,256,128]{2,1,0:T(8,128)(2,1)S(1)}, bf16[1,256,128]{2,1,0:T(8,128)(2,1)S(1)}, u32[]{:S(2)}, u32[]{:S(2)}) collective-permute-start(bf16[1,256,128]{2,1,0:T(8,128)(2,1)S(1)} %get-tuple-element.69.own), channel_id=1, source_target_pairs={{0,2},{1,3},{2,0},{3,1},{4,6},{5,7},{6,4},{7,5},{8,10},{9,11},{10,... | collective-permute-start | bytes 196616 | tf_op jit(solution)/shard_map/ppermute | solution.py:22
  59.1 1.8 %collective-permute-done.14.theirs = bf16[1,256,128]{2,1,0:T(8,128)(2,1)S(1)} collective-permute-done((bf16[1,256,128]{2,1,0:T(8,128)(2,1)S(1)}, bf16[1,256,128]{2,1,0:T(8,128)(2,1)S(1)}, u32[]{:S(2)}, u32[]{:S(2)}) %collective-permute-start.14) | collective-permute-done | bytes 65568 | tf_op jit(solution)/shard_map/ppermute | solution.py:22
  60.9 1.0 %collective-permute-start.15 = (bf16[1,256,128]{2,1,0:T(8,128)(2,1)S(1)}, bf16[1,256,128]{2,1,0:T(8,128)(2,1)S(1)}, u32[]{:S(2)}, u32[]{:S(2)}) collective-permute-start(bf16[1,256,128]{2,1,0:T(8,128)(2,1)S(1)} %enter.1.own_top), channel_id=1, source_target_pairs={{0,2},{1,3},{2,0},{3,1},{4,6},{5,7},{6,4},{7,5},{8,10},{9,11},{10,... | collective-permute-start | bytes 196616 | tf_op jit(solution)/shard_map/ppermute | solution.py:22
  62.0 0.9 copy-done.10
  63.0 2.2 %collective-permute-done.15.far_top = bf16[1,256,128]{2,1,0:T(8,128)(2,1)S(1)} collective-permute-done((bf16[1,256,128]{2,1,0:T(8,128)(2,1)S(1)}, bf16[1,256,128]{2,1,0:T(8,128)(2,1)S(1)}, u32[]{:S(2)}, u32[]{:S(2)}) %collective-permute-start.15) | collective-permute-done | bytes 65568 | tf_op jit(solution)/shard_map/ppermute | solution.py:22
  65.9 1.5 %solve_far.7 = bf16[5,256,128]{2,1,0:T(8,128)(2,1)S(1)} custom-call(s32[8,3]{1,0:T(8,128)S(1)} %copy-done.16, bf16[8,256,256]{2,1,0:T(8,128)(2,1)S(1)} %copy-done.2, bf16[8,256,256]{2,1,0:T(8,128)(2,1)S(1)} %copy-done.1, bf16[8,3,256,256]{3,2,1,0:T(8,128)(2,1)S(1)} %copy-done, bf16[3,256,256]{2,1,0:T(8,128)(2,1)S(1)} %descend.1.paths), custom_call_target="tpu_custom_call" | custom-call | tf_op jit(solution)/shard_map/solve_far/pallas_call | solution.py:152
  67.4 1.0 %collective-permute-start.22 = (bf16[5,256,128]{2,1,0:T(8,128)(2,1)S(1)}, bf16[5,256,128]{2,1,0:T(8,128)(2,1)S(1)}, u32[]{:S(2)}, u32[]{:S(2)}) collective-permute-start(bf16[5,256,128]{2,1,0:T(8,128)(2,1)S(1)} %solve_far.7), channel_id=1, source_target_pairs={{0,2},{1,3},{2,0},{3,1},{4,6},{5,7},{6,4},{7,5},{8,10},{9,11},{10,... | collective-permute-start | bytes 983048 | tf_op jit(solution)/shard_map/ppermute | solution.py:22
  68.4 1.4 %solve_far.6 = bf16[4,256,128]{2,1,0:T(8,128)(2,1)S(1)} custom-call(s32[8,3]{1,0:T(8,128)S(1)} %copy-done.18, bf16[8,256,128]{2,1,0:T(8,128)(2,1)S(1)} %copy-done.5, bf16[8,256,256]{2,1,0:T(8,128)(2,1)S(1)} %collective-permute-done.18.inv, bf16[8,3,256,256]{3,2,1,0:T(8,128)(2,1)S(1)} %collective-permute-done.19.panels, bf16[3,256,256]{2,1,0:T(8,128)(2,1)S(1)} %descend.1.paths), custom_call_target="tpu_custom_call" | custom-call | tf_op jit(solution)/shard_map/solve_far/pallas_call | solution.py:152
  69.8 1.2 %collective-permute-start.21 = (bf16[4,256,128]{2,1,0:T(8,128)(2,1)S(1)}, bf16[4,256,128]{2,1,0:T(8,128)(2,1)S(1)}, u32[]{:S(2)}, u32[]{:S(2)}) collective-permute-start(bf16[4,256,128]{2,1,0:T(8,128)(2,1)S(1)} %solve_far.6), channel_id=1, source_target_pairs={{0,2},{1,3},{2,0},{3,1},{4,6},{5,7},{6,4},{7,5},{8,10},{9,11},{10,... | collective-permute-start | bytes 786440 | tf_op jit(solution)/shard_map/ppermute | solution.py:22
  70.9 1.4 %solve_far.5 = bf16[4,256,128]{2,1,0:T(8,128)(2,1)S(1)} custom-call(s32[8,3]{1,0:T(8,128)S(1)} %copy-done.18, bf16[8,256,128]{2,1,0:T(8,128)(2,1)S(1)} %copy-done.5, bf16[8,256,256]{2,1,0:T(8,128)(2,1)S(1)} %collective-permute-done.18.inv, bf16[8,3,256,256]{3,2,1,0:T(8,128)(2,1)S(1)} %collective-permute-done.19.panels, bf16[3,256,256]{2,1,0:T(8,128)(2,1)S(1)} %descend.1.paths), custom_call_target="tpu_custom_call" | custom-call | tf_op jit(solution)/shard_map/solve_far/pallas_call | solution.py:152
  72.3 1.0 %collective-permute-start.20 = (bf16[4,256,128]{2,1,0:T(8,128)(2,1)S(1)}, bf16[4,256,128]{2,1,0:T(8,128)(2,1)S(1)}, u32[]{:S(2)}, u32[]{:S(2)}) collective-permute-start(bf16[4,256,128]{2,1,0:T(8,128)(2,1)S(1)} %solve_far.5), channel_id=1, source_target_pairs={{0,2},{1,3},{2,0},{3,1},{4,6},{5,7},{6,4},{7,5},{8,10},{9,11},{10,... | collective-permute-start | bytes 786440 | tf_op jit(solution)/shard_map/ppermute | solution.py:22
  73.3 2.1 %solve_far.4 = bf16[3,256,128]{2,1,0:T(8,128)(2,1)S(1)} custom-call(s32[8,3]{1,0:T(8,128)S(1)} %copy-done.16, bf16[8,256,256]{2,1,0:T(8,128)(2,1)S(1)} %copy-done.2, bf16[8,256,256]{2,1,0:T(8,128)(2,1)S(1)} %copy-done.1, bf16[8,3,256,256]{3,2,1,0:T(8,128)(2,1)S(1)} %copy-done, bf16[3,256,256]{2,1,0:T(8,128)(2,1)S(1)} %descend.1.paths), custom_call_target="tpu_custom_call" | custom-call | tf_op jit(solution)/shard_map/solve_far/pallas_call | solution.py:152
  75.5 2.9 %solve_own.2.refs_0_ = bf16[32,256,128]{2,1,0:T(8,128)(2,1)} custom-call(s32[3]{0:T(128)S(1)} %copy-done.19, s32[8,3]{1,0:T(8,128)S(1)} %copy-done.16, bf16[8,256,256]{2,1,0:T(8,128)(2,1)S(1)} %copy-done.2, bf16[8,256,256]{2,1,0:T(8,128)(2,1)S(1)} %copy-done.1, bf16[8,3,256,256]{3,2,1,0:T(8,128)(2,1)S(1)} %copy-done, bf16[3,256,256]{2,1,0:T(8,128)(2,1)S(1)} %descend.1.paths), custom_call_target="tpu_custom_call" | custom-call | tf_op jit(solution)/shard_map/solve_own/pallas_call | solution.py:194
  78.4 1.2 %collective-permute-start.17 = (bf16[3,256,128]{2,1,0:T(8,128)(2,1)S(1)}, bf16[3,256,128]{2,1,0:T(8,128)(2,1)S(1)}, u32[]{:S(2)}, u32[]{:S(2)}) collective-permute-start(bf16[3,256,128]{2,1,0:T(8,128)(2,1)S(1)} %solve_far.4), channel_id=1, source_target_pairs={{0,2},{1,3},{2,0},{3,1},{4,6},{5,7},{6,4},{7,5},{8,10},{9,11},{10,... | collective-permute-start | bytes 589832 | tf_op jit(solution)/shard_map/ppermute | solution.py:22
  79.6 0.6 fusion.1
  80.2 2.9 %solve_own.3.whole = bf16[32,256,128]{2,1,0:T(8,128)(2,1)} custom-call(s32[3]{0:T(128)S(1)} %copy-done.19, s32[8,3]{1,0:T(8,128)S(1)} %copy-done.18, bf16[8,256,128]{2,1,0:T(8,128)(2,1)S(1)} %copy-done.8, bf16[8,256,256]{2,1,0:T(8,128)(2,1)S(1)} %collective-permute-done.18.inv, ...), custom_call_target="tpu_custom_call", output_to_operand_aliasing={{}: (6, {})} | custom-call | tf_op jit(solution)/shard_map/solve_own/pallas_call | solution.py:194
  83.1 0.8 place_rows.4.whole
  83.9 0.7 place_rows.5.whole
  84.6 3.3 %collective-permute-done.20.part = bf16[4,256,128]{2,1,0:T(8,128)(2,1)S(1)} collective-permute-done((bf16[4,256,128]{2,1,0:T(8,128)(2,1)S(1)}, bf16[4,256,128]{2,1,0:T(8,128)(2,1)S(1)}, u32[]{:S(2)}, u32[]{:S(2)}) %collective-permute-start.20) | collective-permute-done | bytes 262176 | tf_op jit(solution)/shard_map/ppermute | solution.py:22
  87.9 0.7 place_rows.6.whole
  88.7 1.4 %collective-permute-done.17.part = bf16[3,256,128]{2,1,0:T(8,128)(2,1)S(1)} collective-permute-done((bf16[3,256,128]{2,1,0:T(8,128)(2,1)S(1)}, bf16[3,256,128]{2,1,0:T(8,128)(2,1)S(1)}, u32[]{:S(2)}, u32[]{:S(2)}) %collective-permute-start.17) | collective-permute-done | bytes 196640 | tf_op jit(solution)/shard_map/ppermute | solution.py:22
  90.0 0.7 place_rows.7
  (80 shorter events, 4.7 us)
Async XLA Ops:
  0.6 7.4 %copy-start.13 = (bf16[1,256,256]{2,1,0:T(8,128)(2,1)S(1)}, bf16[1,256,256]{2,1,0:T(8,128)(2,1)}, u32[]{:S(2)}) copy-start(bf16[1,256,256]{2,1,0:T(8,128)(2,1)} %lower_inv) | copy-start | bytes 393220
  0.6 7.4 %copy-start.11 = (bf16[1,2,256,256]{3,2,1,0:T(8,128)(2,1)S(1)}, bf16[1,2,256,256]{3,2,1,0:T(8,128)(2,1)}, u32[]{:S(2)}) copy-start(bf16[1,2,256,256]{3,2,1,0:T(8,128)(2,1)} %lower_panels.1) | copy-start | bytes 786436
  0.7 7.4 %copy-start.14 = (bf16[1,256,256]{2,1,0:T(8,128)(2,1)S(1)}, bf16[1,256,256]{2,1,0:T(8,128)(2,1)}, u32[]{:S(2)}) copy-start(bf16[1,256,256]{2,1,0:T(8,128)(2,1)} %upper_inv.1) | copy-start | bytes 393220
  0.7 7.4 %copy-start.12 = (bf16[1,2,256,256]{3,2,1,0:T(8,128)(2,1)S(1)}, bf16[1,2,256,256]{3,2,1,0:T(8,128)(2,1)}, u32[]{:S(2)}) copy-start(bf16[1,2,256,256]{3,2,1,0:T(8,128)(2,1)} %upper_panels.1) | copy-start | bytes 786436
  0.7 9.3 %copy-start.24 = (s32[8,3]{0,1:T(4,128)S(1)}, s32[8,3]{0,1:T(4,128)}, u32[]{:S(2)}) copy-start(s32[8,3]{0,1:T(4,128)} %param.16) | copy-start | bytes 292
  2.6 12.2 %collective-permute-start.3 = (bf16[8,3,256,256]{3,2,1,0:T(8,128)(2,1)}, bf16[8,3,256,256]{3,2,1,0:T(8,128)(2,1)}, u32[]{:S(2)}, u32[]{:S(2)}) collective-permute-start(bf16[8,3,256,256]{3,2,1,0:T(8,128)(2,1)} %refs_3_.2), channel_id=1, source_target_pairs={{0,1},{1,0},{2,3},{3,2},{4,5},{5,4},{6,7},{7,6},{8,9},{9,8},{10,11... | collective-permute-start | bytes 9437192 | tf_op jit(solution)/shard_map/ppermute | solution.py:22
  3.1 9.7 %collective-permute-start.2 = (bf16[8,256,256]{2,1,0:T(8,128)(2,1)}, bf16[8,256,256]{2,1,0:T(8,128)(2,1)S(1)}, u32[]{:S(2)}, u32[]{:S(2)}) collective-permute-start(bf16[8,256,256]{2,1,0:T(8,128)(2,1)} %refs_2_.1), channel_id=1, source_target_pairs={{0,1},{1,0},{2,3},{3,2},{4,5},{5,4},{6,7},{7,6},{8,9},{9,8},{10,11... | collective-permute-start | bytes 3145736 | tf_op jit(solution)/shard_map/ppermute | solution.py:22
  3.2 17.2 %collective-permute-start = (bf16[8,256,128]{2,1,0:T(8,128)(2,1)}, bf16[8,256,128]{2,1,0:T(8,128)(2,1)}, u32[]{:S(2)}, u32[]{:S(2)}) collective-permute-start(bf16[8,256,128]{2,1,0:T(8,128)(2,1)} %constant_dynamic-slice_fusion.1), channel_id=1, source_target_pairs={{0,2},{1,3},{2,0},{3,1},{4,6},{5,7},{6,4},{7,5},{8,10},{9,11},{10,... | collective-permute-start | bytes 1572872 | tf_op jit(solution)/shard_map/ppermute | solution.py:22
  8.4 18.2 %collective-permute-start.5 = (bf16[3,256,256]{2,1,0:T(8,128)(2,1)S(1)}, bf16[3,256,256]{2,1,0:T(8,128)(2,1)S(1)}, u32[]{:S(2)}, u32[]{:S(2)}) collective-permute-start(bf16[3,256,256]{2,1,0:T(8,128)(2,1)S(1)} %get-tuple-element.52), channel_id=1, source_target_pairs={{0,4},{4,0},{8,12},{12,8},{16,20},{20,16},{24,28},{28,24},{1,5},{5... | collective-permute-start | bytes 1179656 | tf_op jit(solution)/shard_map/ppermute | solution.py:22
  10.0 10.3 %copy-start.15 = (s32[8,3]{1,0:T(8,128)}, s32[8,3]{1,0:T(8,128)S(1)}, u32[]{:S(2)}) copy-start(s32[8,3]{1,0:T(8,128)S(1)} %copy.20.ancestors) | copy-start | bytes 292
  10.0 1.2 %collective-permute-start.1 = (s32[8,3]{1,0:T(8,128)S(1)}, s32[8,3]{1,0:T(8,128)S(1)}, u32[]{:S(2)}, u32[]{:S(2)}) collective-permute-start(s32[8,3]{1,0:T(8,128)S(1)} %copy.20.ancestors), channel_id=1, source_target_pairs={{0,1},{1,0},{2,3},{3,2},{4,5},{5,4},{6,7},{7,6},{8,9},{9,8},{10,11... | collective-permute-start | bytes 296 | tf_op jit(solution)/shard_map/ppermute | solution.py:22
  11.2 3.7 %copy-start.17 = (s32[8,3]{1,0:T(8,128)}, s32[8,3]{1,0:T(8,128)S(1)}, u32[]{:S(2)}) copy-start(s32[8,3]{1,0:T(8,128)S(1)} %collective-permute-done.1.ancestors) | copy-start | bytes 292
  11.2 18.6 %collective-permute-start.4 = (bf16[8,256,128]{2,1,0:T(8,128)(2,1)}, bf16[8,256,128]{2,1,0:T(8,128)(2,1)}, u32[]{:S(2)}, u32[]{:S(2)}) collective-permute-start(bf16[8,256,128]{2,1,0:T(8,128)(2,1)} %constant_dynamic-slice_fusion), channel_id=1, source_target_pairs={{0,2},{1,3},{2,0},{3,1},{4,6},{5,7},{6,4},{7,5},{8,10},{9,11},{10,... | collective-permute-start | bytes 1572872 | tf_op jit(solution)/shard_map/ppermute | solution.py:22
  12.8 2.1 %copy-start.20 = (bf16[8,256,256]{2,1,0:T(8,128)(2,1)}, bf16[8,256,256]{2,1,0:T(8,128)(2,1)S(1)}, u32[]{:S(2)}) copy-start(bf16[8,256,256]{2,1,0:T(8,128)(2,1)S(1)} %collective-permute-done.2.refs_1_) | copy-start | bytes 3145732
  12.8 13.8 %collective-permute-start.6 = (bf16[2,256,256]{2,1,0:T(8,128)(2,1)S(1)}, bf16[2,256,256]{2,1,0:T(8,128)(2,1)S(1)}, u32[]{:S(2)}, u32[]{:S(2)}) collective-permute-start(bf16[2,256,256]{2,1,0:T(8,128)(2,1)S(1)} %get-tuple-element.53), channel_id=1, source_target_pairs={{0,4},{4,0},{8,12},{12,8},{16,20},{20,16},{24,28},{28,24},{1,5},{5... | collective-permute-start | bytes 786440 | tf_op jit(solution)/shard_map/ppermute | solution.py:22
  26.6 9.2 %collective-permute-start.7 = (bf16[1,256,256]{2,1,0:T(8,128)(2,1)S(1)}, bf16[1,256,256]{2,1,0:T(8,128)(2,1)S(1)}, u32[]{:S(2)}, u32[]{:S(2)}) collective-permute-start(bf16[1,256,256]{2,1,0:T(8,128)(2,1)S(1)} %get-tuple-element.57), channel_id=1, source_target_pairs={{16,0},{20,4},{17,1},{21,5},{18,2},{22,6},{19,3},{23,7}} | collective-permute-start | bytes 393224 | tf_op jit(solution)/shard_map/ppermute | solution.py:327
  27.9 7.9 %collective-permute-start.8 = (bf16[1,256,256]{2,1,0:T(8,128)(2,1)S(1)}, bf16[1,256,256]{2,1,0:T(8,128)(2,1)S(1)}, u32[]{:S(2)}, u32[]{:S(2)}) collective-permute-start(bf16[1,256,256]{2,1,0:T(8,128)(2,1)S(1)} %get-tuple-element.57), channel_id=1, source_target_pairs={{16,8},{20,12},{17,9},{21,13},{18,10},{22,14},{19,11},{23,15}} | collective-permute-start | bytes 393224 | tf_op jit(solution)/shard_map/ppermute | solution.py:327
  28.6 13.2 %copy-start.21 = (bf16[3,256,128]{2,1,0:T(8,128)(2,1)S(1)}, bf16[3,256,128]{2,1,0:T(8,128)(2,1)}, u32[]{:S(2)}) copy-start(bf16[3,256,128]{2,1,0:T(8,128)(2,1)} %get-tuple-element.47) | copy-start | bytes 589828
  35.8 2.9 %copy-start.22 = (bf16[1,256,256]{2,1,0:T(8,128)(2,1)}, bf16[1,256,256]{2,1,0:T(8,128)(2,1)S(1)}, u32[]{:S(2)}) copy-start(bf16[1,256,256]{2,1,0:T(8,128)(2,1)S(1)} %collective-permute-done.7.refs_0_) | copy-start | bytes 393220
  35.8 2.9 %copy-start.23 = (bf16[1,256,256]{2,1,0:T(8,128)(2,1)}, bf16[1,256,256]{2,1,0:T(8,128)(2,1)S(1)}, u32[]{:S(2)}) copy-start(bf16[1,256,256]{2,1,0:T(8,128)(2,1)S(1)} %collective-permute-done.8.refs_1_) | copy-start | bytes 393220
  35.8 6.0 %collective-permute-start.9 = (bf16[3,256,128]{2,1,0:T(8,128)(2,1)}, bf16[3,256,128]{2,1,0:T(8,128)(2,1)S(1)}, u32[]{:S(2)}, u32[]{:S(2)}) collective-permute-start(bf16[3,256,128]{2,1,0:T(8,128)(2,1)} %get-tuple-element.60), channel_id=1, source_target_pairs={{0,2},{1,3},{2,0},{3,1},{4,6},{5,7},{6,4},{7,5},{8,10},{9,11},{10,... | collective-permute-start | bytes 589832 | tf_op jit(solution)/shard_map/ppermute | solution.py:22
  37.1 9.9 %collective-permute-start.11 = (bf16[3,256,256]{2,1,0:T(8,128)(2,1)S(1)}, bf16[3,256,256]{2,1,0:T(8,128)(2,1)S(1)}, u32[]{:S(2)}, u32[]{:S(2)}) collective-permute-start(bf16[3,256,256]{2,1,0:T(8,128)(2,1)S(1)} %get-tuple-element.56.mine), channel_id=1, source_target_pairs={{0,8},{4,12},{8,0},{12,4},{16,24},{20,28},{24,16},{28,20},{1,9},{5... | collective-permute-start | bytes 1179656 | tf_op jit(solution)/shard_map/ppermute | solution.py:22
  41.9 5.9 %collective-permute-start.10 = (bf16[3,256,128]{2,1,0:T(8,128)(2,1)S(1)}, bf16[3,256,128]{2,1,0:T(8,128)(2,1)S(1)}, u32[]{:S(2)}, u32[]{:S(2)}) collective-permute-start(bf16[3,256,128]{2,1,0:T(8,128)(2,1)S(1)} %add_convert_fusion.mine), channel_id=1, source_target_pairs={{0,4},{4,0},{8,12},{12,8},{16,20},{20,16},{24,28},{28,24},{1,5},{5... | collective-permute-start | bytes 589832 | tf_op jit(solution)/shard_map/ppermute | solution.py:22
  43.4 4.4 %copy-start.3 = (bf16[5,256,256]{2,1,0:T(8,128)(2,1)}, bf16[5,256,256]{2,1,0:T(8,128)(2,1)S(1)}, u32[]{:S(2)}) copy-start(bf16[5,256,256]{2,1,0:T(8,128)(2,1)S(1)} %sort.7.factors) | copy-start | bytes 1966084
  47.0 0.8 copy-start.6
  47.0 6.9 %copy-start = (bf16[8,3,256,256]{3,2,1,0:T(8,128)(2,1)S(1)}, bf16[8,3,256,256]{3,2,1,0:T(8,128)(2,1)}, u32[]{:S(2)}) copy-start(bf16[8,3,256,256]{3,2,1,0:T(8,128)(2,1)} %panels.5) | copy-start | bytes 9437188
  47.8 0.7 copy-start.9
  48.4 5.3 %collective-permute-start.12 = (bf16[2,256,128]{2,1,0:T(8,128)(2,1)S(1)}, bf16[2,256,128]{2,1,0:T(8,128)(2,1)S(1)}, u32[]{:S(2)}, u32[]{:S(2)}) collective-permute-start(bf16[2,256,128]{2,1,0:T(8,128)(2,1)S(1)} %get-tuple-element.65.mine), channel_id=1, source_target_pairs={{0,8},{4,12},{8,0},{12,4},{16,24},{20,28},{24,16},{28,20},{1,9},{5... | collective-permute-start | bytes 393224 | tf_op jit(solution)/shard_map/ppermute | solution.py:22
  51.6 1.1 %copy-start.4 = (bf16[5,256,256]{2,1,0:T(8,128)(2,1)S(1)}, bf16[5,256,256]{2,1,0:T(8,128)(2,1)}, u32[]{:S(2)}) copy-start(bf16[5,256,256]{2,1,0:T(8,128)(2,1)} %copy-done.3) | copy-start | bytes 1966084
  52.7 1.0 %copy-start.7 = (bf16[3,256,256]{2,1,0:T(8,128)(2,1)S(1)}, bf16[3,256,256]{2,1,0:T(8,128)(2,1)}, u32[]{:S(2)}) copy-start(bf16[3,256,256]{2,1,0:T(8,128)(2,1)} %copy-done.6) | copy-start | bytes 1179652
  53.7 12.2 %copy-start.1 = (bf16[8,256,256]{2,1,0:T(8,128)(2,1)S(1)}, bf16[8,256,256]{2,1,0:T(8,128)(2,1)}, u32[]{:S(2)}) copy-start(bf16[8,256,256]{2,1,0:T(8,128)(2,1)} %inv.5) | copy-start | bytes 3145732
  53.7 12.2 %copy-start.2 = (bf16[8,256,256]{2,1,0:T(8,128)(2,1)S(1)}, bf16[8,256,256]{2,1,0:T(8,128)(2,1)}, u32[]{:S(2)}) copy-start(bf16[8,256,256]{2,1,0:T(8,128)(2,1)} %get-tuple-element.46.value) | copy-start | bytes 3145732
  53.9 14.4 %collective-permute-start.19 = (bf16[8,3,256,256]{3,2,1,0:T(8,128)(2,1)S(1)}, bf16[8,3,256,256]{3,2,1,0:T(8,128)(2,1)S(1)}, u32[]{:S(2)}, u32[]{:S(2)}) collective-permute-start(bf16[8,3,256,256]{3,2,1,0:T(8,128)(2,1)S(1)} %copy-done), channel_id=1, source_target_pairs={{0,1},{1,0},{2,3},{3,2},{4,5},{5,4},{6,7},{7,6},{8,9},{9,8},{10,11... | collective-permute-start | bytes 9437192 | tf_op jit(solution)/shard_map/ppermute | solution.py:22
  54.0 14.4 %collective-permute-start.18 = (bf16[8,256,256]{2,1,0:T(8,128)(2,1)}, bf16[8,256,256]{2,1,0:T(8,128)(2,1)S(1)}, u32[]{:S(2)}, u32[]{:S(2)}) collective-permute-start(bf16[8,256,256]{2,1,0:T(8,128)(2,1)} %inv.5), channel_id=1, source_target_pairs={{0,1},{1,0},{2,3},{3,2},{4,5},{5,4},{6,7},{7,6},{8,9},{9,8},{10,11... | collective-permute-start | bytes 3145736 | tf_op jit(solution)/shard_map/ppermute | solution.py:22
  54.5 6.4 %collective-permute-start.14 = (bf16[1,256,128]{2,1,0:T(8,128)(2,1)S(1)}, bf16[1,256,128]{2,1,0:T(8,128)(2,1)S(1)}, u32[]{:S(2)}, u32[]{:S(2)}) collective-permute-start(bf16[1,256,128]{2,1,0:T(8,128)(2,1)S(1)} %get-tuple-element.70.mine), channel_id=1, source_target_pairs={{0,16},{4,20},{8,24},{12,28},{16,0},{20,4},{24,8},{28,12},{1,17},{... | collective-permute-start | bytes 196616 | tf_op jit(solution)/shard_map/ppermute | solution.py:22
  57.1 4.8 %collective-permute-start.16 = (bf16[1,256,128]{2,1,0:T(8,128)(2,1)S(1)}, bf16[1,256,128]{2,1,0:T(8,128)(2,1)S(1)}, u32[]{:S(2)}, u32[]{:S(2)}) collective-permute-start(bf16[1,256,128]{2,1,0:T(8,128)(2,1)S(1)} %get-tuple-element.74.refs_2_), channel_id=1, source_target_pairs={{0,2},{1,3},{2,0},{3,1},{4,6},{5,7},{6,4},{7,5},{8,10},{9,11},{10,... | collective-permute-start | bytes 196616 | tf_op jit(solution)/shard_map/ppermute | solution.py:22
  58.0 5.0 %collective-permute-start.13 = (bf16[1,256,128]{2,1,0:T(8,128)(2,1)S(1)}, bf16[1,256,128]{2,1,0:T(8,128)(2,1)S(1)}, u32[]{:S(2)}, u32[]{:S(2)}) collective-permute-start(bf16[1,256,128]{2,1,0:T(8,128)(2,1)S(1)} %get-tuple-element.69.own), channel_id=1, source_target_pairs={{0,2},{1,3},{2,0},{3,1},{4,6},{5,7},{6,4},{7,5},{8,10},{9,11},{10,... | collective-permute-start | bytes 196616 | tf_op jit(solution)/shard_map/ppermute | solution.py:22
  60.9 4.3 %collective-permute-start.15 = (bf16[1,256,128]{2,1,0:T(8,128)(2,1)S(1)}, bf16[1,256,128]{2,1,0:T(8,128)(2,1)S(1)}, u32[]{:S(2)}, u32[]{:S(2)}) collective-permute-start(bf16[1,256,128]{2,1,0:T(8,128)(2,1)S(1)} %enter.1.own_top), channel_id=1, source_target_pairs={{0,2},{1,3},{2,0},{3,1},{4,6},{5,7},{6,4},{7,5},{8,10},{9,11},{10,... | collective-permute-start | bytes 196616 | tf_op jit(solution)/shard_map/ppermute | solution.py:22
  62.0 0.9 copy-start.10
  62.9 3.0 %copy-start.16 = (s32[8,3]{1,0:T(8,128)S(1)}, s32[8,3]{1,0:T(8,128)}, u32[]{:S(2)}) copy-start(s32[8,3]{1,0:T(8,128)} %copy-done.15) | copy-start | bytes 292
  65.9 2.5 %copy-start.5 = (bf16[8,256,128]{2,1,0:T(8,128)(2,1)S(1)}, bf16[8,256,128]{2,1,0:T(8,128)(2,1)}, u32[]{:S(2)}) copy-start(bf16[8,256,128]{2,1,0:T(8,128)(2,1)} %get-tuple-element.78.value) | copy-start | bytes 1572868
  65.9 2.5 %copy-start.18 = (s32[8,3]{1,0:T(8,128)S(1)}, s32[8,3]{1,0:T(8,128)}, u32[]{:S(2)}) copy-start(s32[8,3]{1,0:T(8,128)} %copy-done.17) | copy-start | bytes 292
  67.4 15.7 %collective-permute-start.22 = (bf16[5,256,128]{2,1,0:T(8,128)(2,1)S(1)}, bf16[5,256,128]{2,1,0:T(8,128)(2,1)S(1)}, u32[]{:S(2)}, u32[]{:S(2)}) collective-permute-start(bf16[5,256,128]{2,1,0:T(8,128)(2,1)S(1)} %solve_far.7), channel_id=1, source_target_pairs={{0,2},{1,3},{2,0},{3,1},{4,6},{5,7},{6,4},{7,5},{8,10},{9,11},{10,... | collective-permute-start | bytes 983048 | tf_op jit(solution)/shard_map/ppermute | solution.py:22
  69.8 14.1 %collective-permute-start.21 = (bf16[4,256,128]{2,1,0:T(8,128)(2,1)S(1)}, bf16[4,256,128]{2,1,0:T(8,128)(2,1)S(1)}, u32[]{:S(2)}, u32[]{:S(2)}) collective-permute-start(bf16[4,256,128]{2,1,0:T(8,128)(2,1)S(1)} %solve_far.6), channel_id=1, source_target_pairs={{0,2},{1,3},{2,0},{3,1},{4,6},{5,7},{6,4},{7,5},{8,10},{9,11},{10,... | collective-permute-start | bytes 786440 | tf_op jit(solution)/shard_map/ppermute | solution.py:22
  72.3 3.1 %copy-start.19 = (s32[3]{0:T(128)S(1)}, s32[3]{0:T(128)}, u32[]{:S(2)}) copy-start(s32[3]{0:T(128)} %pad_add_fusion.scalars) | copy-start | bytes 40
  72.3 15.6 %collective-permute-start.20 = (bf16[4,256,128]{2,1,0:T(8,128)(2,1)S(1)}, bf16[4,256,128]{2,1,0:T(8,128)(2,1)S(1)}, u32[]{:S(2)}, u32[]{:S(2)}) collective-permute-start(bf16[4,256,128]{2,1,0:T(8,128)(2,1)S(1)} %solve_far.5), channel_id=1, source_target_pairs={{0,2},{1,3},{2,0},{3,1},{4,6},{5,7},{6,4},{7,5},{8,10},{9,11},{10,... | collective-permute-start | bytes 786440 | tf_op jit(solution)/shard_map/ppermute | solution.py:22
  75.5 4.8 %copy-start.8 = (bf16[8,256,128]{2,1,0:T(8,128)(2,1)S(1)}, bf16[8,256,128]{2,1,0:T(8,128)(2,1)}, u32[]{:S(2)}) copy-start(bf16[8,256,128]{2,1,0:T(8,128)(2,1)} %get-tuple-element.81.value) | copy-start | bytes 1572868
  78.4 11.6 %collective-permute-start.17 = (bf16[3,256,128]{2,1,0:T(8,128)(2,1)S(1)}, bf16[3,256,128]{2,1,0:T(8,128)(2,1)S(1)}, u32[]{:S(2)}, u32[]{:S(2)}) collective-permute-start(bf16[3,256,128]{2,1,0:T(8,128)(2,1)S(1)} %solve_far.4), channel_id=1, source_target_pairs={{0,2},{1,3},{2,0},{3,1},{4,6},{5,7},{6,4},{7,5},{8,10},{9,11},{10,... | collective-permute-start | bytes 589832 | tf_op jit(solution)/shard_map/ppermute | solution.py:22
